TPU v7x, 256 devices: a whole 4x4x8 slice. The times are simulated.
256 devices in a mesh: unit: 4 (over x), samp: 64 (over z, y, core).
Axes of the slice: x: 4, y: 4, z: 8, core: 2. Of those that a mesh axis runs over, the one named last changes fastest.
Arguments:
- states: float32 [65536, 8192], P('samp', 'unit'), may hold values from -0.0234375 to 0.0234375
- targets: float32 [65536, 64], P('samp'), may hold values from -6 to 6
Outputs:
- readout: float32 [8192, 64], P('unit')
- residual: float32 [65536, 64], P('samp')
All inputs are finite; a program needn't handle non-finite values.
Results may differ from a plain program's by a relative error of at most 0.0003.
Values sent between devices are 32-bit elements; how exact they have to be, the bound alone decides.
No kernel may reach another device: no remote copies, remote signals or barrier semaphores. Data moves between devices by JAX's collectives and lax.ppermute only.
A program may use at most 64 MiB of HBM per device.

v0:
```python
import jax
import jax.numpy as jnp
from jax import lax
from jax.sharding import PartitionSpec as P

ITERS = 3


ridge = 0.5


def transposed(states, residual):
    return lax.dot_general(
        states,
        residual,
        (((0,), (0,)), ((), ())),
        precision=lax.Precision.HIGHEST,
        preferred_element_type=jnp.float32,
    )


def shards(states, targets):
    unit_local = states.shape[1]
    outputs = targets.shape[1]
    samp_count = lax.axis_size("samp")
    readout = jnp.zeros((unit_local, outputs), jnp.float32)

    def gradient_of(residual, readout):
        summed = lax.psum(transposed(states, residual), "samp")
        return summed - ridge * readout

    def norm_of(gradient):
        return lax.psum(jnp.sum(gradient * gradient) / samp_count, ("unit", "samp"))

    residual = targets
    gradient = gradient_of(residual, readout)
    direction = gradient
    gamma = norm_of(gradient)
    for step in range(ITERS):
        whole_direction = direction
        partial_image = jnp.dot(
            states,
            whole_direction,
            precision=lax.Precision.HIGHEST,
            preferred_element_type=jnp.float32,
        )
        image = lax.psum(partial_image, "unit")
        image_sq = lax.psum(jnp.sum(image * image), "samp")
        direction_sq = lax.psum(jnp.sum(direction * direction) / samp_count, ("unit", "samp"))
        delta = image_sq + ridge * direction_sq
        alpha = gamma / delta
        readout = readout + alpha * direction
        residual = residual - alpha * image
        if step + 1 < ITERS:
            gradient = gradient_of(residual, readout)
            gamma_next = norm_of(gradient)
            direction = gradient + gamma_next / gamma * direction
            gamma = gamma_next
    return (readout, residual)


def solution(mesh):
    return jax.shard_map(
        shards,
        mesh=mesh,
        in_specs=(P("samp", "unit"), P("samp", None)),
        out_specs=(P("unit", None), P("samp", None)),
        check_vma=False,
    )
```

profile of v0, /device:TPU:1, one launch (start us, length us, event | category | flops | bytes accessed | tf_op | source)
XLA Modules:
  0.0 1392.4 jit_solution(6348653614439952410)
XLA Ops:
  7.2 0.0 copy-start.2
  7.2 0.0 all-reduce.7.cloned.1.call-start
  7.2 9.6 fusion
  16.8 0.0 all-reduce.7.cloned.1.call-update
  16.9 0.0 all-reduce.9.cloned.1.call-start
  16.9 183.3 %all-reduce.7.cloned.1.call-done = f32[2048,64]{0,1:T(8,128)} async-done(((f32[2048,64]{0,1:T(8,128)}), f32[2048,64]{0,1:T(8,128)}) %all-reduce.7.cloned.1.call-update) | async-done | bytes 524304 | tf_op jit(solution)/shard_map/psum | solution.py:29
  200.2 0.0 copy-start
  200.2 12.3 convolution_bitcast_fusion.4
  212.5 0.0 all-reduce.9.cloned.1.call-update
  212.5 0.0 all-reduce.11.cloned.1.call-start
  212.6 0.0 copy-done
  212.6 0.7 multiply_reduce_fusion.4
  213.9 77.6 %psum.102 = f32[]{:T(128)} all-reduce(f32[]{:T(128)S(6)} %div.31), channel_id=1, replica_groups=mesh['unit'=4,'samp'=64] {'unit','samp'}, use_global_device_ids=true, to_apply=%region_2.0 | all-reduce | flops 1 | bytes 8 | tf_op jit(solution)/shard_map/psum | solution.py:33
  291.6 0.0 all-reduce.9.cloned.1.call-done
  291.6 1.6 multiply_reduce_fusion.7
  293.8 124.7 %psum.104 = f32[]{:T(128)} all-reduce(f32[]{:T(128)} %multiply_reduce_fusion.7), channel_id=1, replica_groups=mesh['unit'=4,'samp'=64] {'samp'}, use_global_device_ids=true, to_apply=%region_5.0 | all-reduce | flops 1 | bytes 8 | tf_op jit(solution)/shard_map/psum | solution.py:48
  419.8 0.0 copy-done.2
  419.8 9.4 convolution_bitcast_fusion.1
  429.2 0.0 copy-start.3
  429.2 0.0 all-reduce.11.cloned.1.call-update
  429.3 0.0 all-reduce.13.cloned.1.call-start
  429.3 175.1 %all-reduce.11.cloned.1.call-done = f32[2048,64]{0,1:T(8,128)} async-done(((f32[2048,64]{0,1:T(8,128)}), f32[2048,64]{0,1:T(8,128)}) %all-reduce.11.cloned.1.call-update) | async-done | bytes 524304 | tf_op jit(solution)/shard_map/psum | solution.py:29
  604.4 1.9 multiply_reduce_fusion.3
  606.9 77.0 %psum.106 = f32[]{:T(128)} all-reduce(f32[]{:T(128)S(6)} %div.33), channel_id=1, replica_groups=mesh['unit'=4,'samp'=64] {'unit','samp'}, use_global_device_ids=true, to_apply=%region_8.0 | all-reduce | flops 1 | bytes 8 | tf_op jit(solution)/shard_map/psum | solution.py:33
  685.3 12.3 convolution_bitcast_fusion.3
  697.6 0.0 all-reduce.13.cloned.1.call-update
  697.6 0.0 all-reduce.15.cloned.1.call-start
  697.7 0.0 copy-done.1
  697.7 0.7 multiply_reduce_fusion.2
  699.1 72.9 %psum.109 = f32[]{:T(128)} all-reduce(f32[]{:T(128)S(6)} %div.35), channel_id=1, replica_groups=mesh['unit'=4,'samp'=64] {'unit','samp'}, use_global_device_ids=true, to_apply=%region_13.0 | all-reduce | flops 1 | bytes 8 | tf_op jit(solution)/shard_map/psum | solution.py:49
  771.9 1.6 multiply_reduce_fusion.6
  774.2 124.7 %psum.108 = f32[]{:T(128)} all-reduce(f32[]{:T(128)} %multiply_reduce_fusion.6), channel_id=1, replica_groups=mesh['unit'=4,'samp'=64] {'samp'}, use_global_device_ids=true, to_apply=%region_11.0 | all-reduce | flops 1 | bytes 8 | tf_op jit(solution)/shard_map/psum | solution.py:48
  900.3 0.0 copy-done.3
  900.3 1.0 multiply_subtract_fusion.3
  901.3 8.3 convolution_bitcast_fusion
  909.5 0.0 all-reduce.15.cloned.1.call-update
  909.6 0.0 all-reduce.17.cloned.1.call-start
  909.6 177.6 %all-reduce.15.cloned.1.call-done = f32[2048,64]{0,1:T(8,128)} async-done(((f32[2048,64]{0,1:T(8,128)}), f32[2048,64]{0,1:T(8,128)}) %all-reduce.15.cloned.1.call-update) | async-done | bytes 524304 | tf_op jit(solution)/shard_map/psum | solution.py:29
  1087.2 1.8 multiply_reduce_fusion.1
  1089.7 77.3 %psum.111 = f32[]{:T(128)} all-reduce(f32[]{:T(128)S(6)} %div.37), channel_id=1, replica_groups=mesh['unit'=4,'samp'=64] {'unit','samp'}, use_global_device_ids=true, to_apply=%region_16.0 | all-reduce | flops 1 | bytes 8 | tf_op jit(solution)/shard_map/psum | solution.py:33
  1168.3 2.0 multiply_reduce_fusion
  1170.3 11.1 convolution_bitcast_fusion.2
  1181.4 0.0 all-reduce.17.cloned.1.call-update
  1182.1 72.6 %psum.114 = f32[]{:T(128)} all-reduce(f32[]{:T(128)S(6)} %div.39), channel_id=1, replica_groups=mesh['unit'=4,'samp'=64] {'unit','samp'}, use_global_device_ids=true, to_apply=%region_21.0 | all-reduce | flops 1 | bytes 8 | tf_op jit(solution)/shard_map/psum | solution.py:49
  1254.7 1.6 multiply_reduce_fusion.5
  1256.9 124.7 %psum.113 = f32[]{:T(128)} all-reduce(f32[]{:T(128)} %multiply_reduce_fusion.5), channel_id=1, replica_groups=mesh['unit'=4,'samp'=64] {'samp'}, use_global_device_ids=true, to_apply=%region_19.0 | all-reduce | flops 1 | bytes 8 | tf_op jit(solution)/shard_map/psum | solution.py:48
  1382.9 1.7 multiply_subtract_fusion.2
  1384.6 1.0 multiply_add_fusion
  (3 shorter events, 0.0 us)
Async XLA Ops:
  7.2 412.7 %copy-start.2 = (f32[1024,64]{0,1:T(8,128)S(1)}, f32[1024,64]{0,1:T(8,128)}, u32[]{:S(2)}) copy-start(f32[1024,64]{0,1:T(8,128)} %param.3) | copy-start | bytes 786436
  7.2 193.0 %all-reduce.7.cloned.1.call-start = ((), (), s32[]{:S(2)}) async-start(), calls=%async_computation | async-start | bytes 1048576 | tf_op jit(solution)/shard_map/psum | solution.py:29
  16.9 274.7 %all-reduce.9.cloned.1.call-start = ((), (), s32[]{:S(2)}) async-start(), calls=%async_computation.1 | async-start | bytes 524288 | tf_op jit(solution)/shard_map/psum | solution.py:47
  200.2 12.4 copy-start
  212.5 391.9 %all-reduce.11.cloned.1.call-start = ((), (), s32[]{:S(2)}) async-start(), calls=%async_computation.2 | async-start | bytes 1048576 | tf_op jit(solution)/shard_map/psum | solution.py:29
  429.2 471.0 %copy-start.3 = (f32[1024,64]{0,1:T(8,128)S(1)}, f32[1024,64]{0,1:T(8,128)}, u32[]{:S(2)}) copy-start(f32[1024,64]{0,1:T(8,128)} %all-reduce.9.cloned.1.call-done) | copy-start | bytes 786436
  429.3 342.7 %all-reduce.13.cloned.1.call-start = ((), (), s32[]{:S(2)}) async-start(), calls=%async_computation.3 | async-start | bytes 524288 | tf_op jit(solution)/shard_map/psum | solution.py:47
  604.4 93.3 %copy-start.1 = (f32[2048,64]{0,1:T(8,128)S(1)}, f32[2048,64]{0,1:T(8,128)}, u32[]{:S(2)}) copy-start(f32[2048,64]{0,1:T(8,128)} %all-reduce.11.cloned.1.call-done) | copy-start | bytes 1572868
  697.6 389.6 %all-reduce.15.cloned.1.call-start = ((), (), s32[]{:S(2)}) async-start(), calls=%async_computation.4 | async-start | bytes 1048576 | tf_op jit(solution)/shard_map/psum | solution.py:29
  909.6 345.1 %all-reduce.17.cloned.1.call-start = ((), (), s32[]{:S(2)}) async-start(), calls=%async_computation.5 | async-start | bytes 524288 | tf_op jit(solution)/shard_map/psum | solution.py:47
Sparse Core Ops, SparseCore 0:
  17.0 183.1 all-reduce.6
  212.6 43.8 all-reduce.8
  429.4 174.9 all-reduce.10
  697.7 40.4 all-reduce.12
  909.7 177.4 all-reduce.14
  1181.5 40.3 all-reduce.16
where the time goes:
time: 1390 us
  blocking collectives  751 us (54%)
  waiting for transfers between devices  536 us (39%)
  matrix products  63 us (5%)
  between operations  26.1 us (2%)
  other arithmetic  15.6 us (1%)
    psum x3, waiting for transfers between devices, gradient_of(): summed = lax.psum(transposed(states, residual), 'samp')  536 us
    psum x3, blocking collectives, shards(): image_sq = lax.psum(jnp.sum(image * image), 'samp')  374 us
    psum x3, blocking collectives, norm_of(): return lax.psum(jnp.sum(gradient * gradient) / samp_count, ('unit', 'samp'))  232 us
    psum x2, blocking collectives, shards(): lax.psum(jnp.sum(direction * direction) / samp_count, ('unit', 'samp'))  145 us
    dot_general x3, matrix products, shards(): jnp.dot(states, whole_direction, precision=lax.Precision.HIGHEST, preferr...  35.7 us
  transfers between devices with their start and end apart: 6, of which 3 were waited for; matrix products, arithmetic and copies ran while one was open for 0% of the time, Pallas kernels for 0%

commit v1 on v0

v1 whole, which is shorter than its diff:
```python
import jax
import jax.numpy as jnp
from jax import lax
from jax.sharding import PartitionSpec as P

ITERS = 3
ridge = 0.5
Y, CORES, LANES = 4, 2, 128


def rounded(values):
    return lax.reduce_precision(values, 8, 7)


def split2(values):
    high = rounded(values)
    return high.astype(jnp.bfloat16), rounded(values - high).astype(jnp.bfloat16)


def split3(values):
    high = rounded(values)
    rest = values - high
    middle = rounded(rest)
    parts = [high, middle, rounded(rest - middle)]
    return jnp.concatenate(parts, axis=0).astype(jnp.bfloat16)


def product(rows, states_parts, contract):
    stacked = split3(rows)
    total = 0.0
    for part in states_parts[::-1]:
        p = lax.dot_general(
            stacked,
            part,
            (((1,), (contract,)), ((), ())),
            preferred_element_type=jnp.float32,
        )
        n = rows.shape[0]
        total = total + (p[2 * n :] + p[n : 2 * n] + p[:n])
    return total


def shards(states, targets):
    units = states.shape[1]
    samples, outputs = targets.shape
    samp_count = lax.axis_size("samp")
    chips = samp_count // CORES
    half = outputs // CORES
    core = lax.axis_index("samp") % CORES

    swap_cores = [(i, i ^ 1) for i in range(samp_count)]
    groups = [[chip * CORES + c for chip in range(chips)] for c in range(CORES)]

    def swap(x):
        return lax.ppermute(x, "samp", swap_cores)

    def exchange(x):
        return lax.all_to_all(x, "samp", 0, 0, axis_index_groups=groups, tiled=True)

    def unit_hop(x, mask):
        return lax.ppermute(x, "unit", [(i, i ^ mask) for i in range(lax.axis_size("unit"))])

    def unit_sum(a, b):
        a, b = a + unit_hop(a, 1), b + unit_hop(b, 3)
        return a + unit_hop(a, 3), b + unit_hop(b, 1)

    def turn(x):
        return jnp.where(core == 0, x, jnp.concatenate([x[half:], x[:half]], axis=0))

    parts = split2(states)

    def scatter_sum(residual, scalar):
        g = product(residual, parts, 0).reshape(outputs, units // LANES, LANES)
        extra = jnp.broadcast_to(scalar, (half, 1, LANES))
        mine = jnp.concatenate([g[:half], extra], axis=1)
        theirs = jnp.concatenate([g[half:], extra], axis=1)
        mine = mine + swap(theirs)
        rows = mine.shape[1]
        got = exchange(mine.reshape(half * rows, 1, LANES)).reshape(half, rows, LANES)
        got = jnp.sum(got, axis=0)
        return got[: rows - 1], got[rows - 1, 0]

    def gather(shard):
        mine = exchange(jnp.broadcast_to(shard[None], (half,) + shard.shape))
        return jnp.concatenate([mine, swap(mine)], axis=0).reshape(outputs, units)

    def image_sum(g, scalars):
        p = product(g, parts, 1).reshape(outputs * samples // LANES, LANES)
        n = p.shape[0] // 2
        tile = jnp.concatenate(
            [jnp.broadcast_to(s, (1, LANES)) for s in scalars]
            + [jnp.zeros((8 - len(scalars), LANES), jnp.float32)],
            axis=0,
        )
        a, b = unit_sum(jnp.concatenate([p[:n], tile], axis=0), p[n:])
        image = jnp.concatenate([a[:n], b], axis=0).reshape(outputs, samples)
        return image, [a[n + i, 0] for i in range(len(scalars))]

    residual = turn(targets.T)
    shard, _ = scatter_sum(residual, jnp.float32(0))
    gradient = gather(shard)
    readout = jnp.zeros_like(gradient)
    direction = gradient
    shard_direction = shard
    for step in range(ITERS):
        square = jnp.sum(gradient * gradient)
        if step == 0:
            image, (gamma,) = image_sum(gradient, [square])
            direction_sq = gamma
        else:
            cross = jnp.sum(gradient * direction)
            new_image, (gamma_next, cross) = image_sum(gradient, [square, cross])
            beta = gamma_next / gamma
            gamma = gamma_next
            image = new_image + beta * image
            direction = gradient + beta * direction
            shard_direction = shard + beta * shard_direction
            direction_sq = gamma + beta * (2.0 * cross + beta * direction_sq)
        image_sq = jnp.sum(image * image)
        if step + 1 < ITERS:
            back, image_sq = scatter_sum(image, image_sq)
            alpha = gamma / (image_sq + ridge * direction_sq)
            shard = shard - alpha * (back + ridge * shard_direction)
            gradient = gather(shard)
        else:
            tile = jnp.broadcast_to(image_sq, (chips, 1, LANES))
            got = exchange(tile + swap(tile))
            image_sq = jnp.sum(got[:, 0, 0])
            alpha = gamma / (image_sq + ridge * direction_sq)
        readout = readout + alpha * direction
        residual = residual - alpha * image
    return turn(readout).T, turn(residual).T


def solution(mesh):
    return jax.shard_map(
        shards,
        mesh=mesh,
        in_specs=(P("samp", "unit"), P("samp", None)),
        out_specs=(P("unit", None), P("samp", None)),
        check_vma=False,
    )
```

time: 1390 us -> 241 us (0.17)
  blocking collectives: 751 us -> 65.5 us
  waiting for transfers between devices: 536 us -> 57.2 us
  starting transfers between devices: 0.25 us -> 45.1 us
  matrix products: 63 us -> 22.2 us
  local copies, waits for them, and re-layouts: 0.02 us -> 15.4 us
  between operations: 26.1 us -> 11.4 us
    psum x8 -> x0, blocking collectives: 751 us -> none  [the longest x3 374 us: shards(): image_sq = lax.psum(jnp.sum(image * image), 'samp')]
    psum x6 -> x0, waiting for transfers between devices: 536 us -> none  [the longest x3 536 us: gradient_of(): summed = lax.psum(transposed(states, residual), 'samp')]
    all_to_all x0 -> x4, blocking collectives: none -> 65.5 us  [exchange(): return lax.all_to_all(x, 'samp', 0, 0, axis_index_groups=groups, tiled=True)]
    dot_general x6 -> x12, matrix products: 63 us -> 22.2 us  [product(): lax.dot_general(stacked, part, (((1,), (contract,)), ((), ())), preferred...]
    ppermute x0 -> x19, starting transfers between devices: none -> 33.6 us  [the longest x7 21.3 us: swap(): return lax.ppermute(x, 'samp', swap_cores)]
    ppermute x0 -> x19, waiting for transfers between devices: none -> 28.6 us  [the longest x12 20.6 us: unit_hop(): lax.ppermute(x, 'unit', [(i, i ^ mask) for i in range(lax.axis_size('unit...]
    all_to_all x0 -> x3, waiting for transfers between devices: none -> 28.6 us  [exchange(): return lax.all_to_all(x, 'samp', 0, 0, axis_index_groups=groups, tiled=True)]
  transfers between devices with their start and end apart: 6 -> 22, of which waited for: 3 -> 16; matrix products, arithmetic and copies ran while one was open for 0% -> 1% of each run, Pallas kernels for 0% -> 0%
where the time goes in v1:
time: 241 us; the launch traced here: 240 us
  blocking collectives  65.5 us (27%)
  waiting for transfers between devices  57.2 us (24%)
  starting transfers between devices  45.1 us (19%)
  other arithmetic  23.5 us (10%)
  matrix products  22.2 us (9%)
  local copies, waits for them, and re-layouts  15.4 us (6%)
  between operations  11.4 us (5%)
    all_to_all x4, blocking collectives, exchange(): return lax.all_to_all(x, 'samp', 0, 0, axis_index_groups=groups, tiled=True)  65.5 us
    all_to_all x3, waiting for transfers between devices, exchange(): return lax.all_to_all(x, 'samp', 0, 0, axis_index_groups=groups, tiled=True)  28.6 us
    dot_general x12, matrix products, product(): lax.dot_general(stacked, part, (((1,), (contract,)), ((), ())), preferred...  22.2 us
    ppermute x7, starting transfers between devices, swap(): return lax.ppermute(x, 'samp', swap_cores)  21.3 us
    ppermute x12, waiting for transfers between devices, unit_hop(): lax.ppermute(x, 'unit', [(i, i ^ mask) for i in range(lax.axis_size('unit...  20.6 us
    ppermute x12, starting transfers between devices, unit_hop(): lax.ppermute(x, 'unit', [(i, i ^ mask) for i in range(lax.axis_size('unit...  12.3 us
    all_to_all x3, starting transfers between devices, exchange(): return lax.all_to_all(x, 'samp', 0, 0, axis_index_groups=groups, tiled=True)  11.6 us
    ppermute x7, waiting for transfers between devices, swap(): return lax.ppermute(x, 'samp', swap_cores)  8 us
  transfers between devices with their start and end apart: 22, of which 16 were waited for; matrix products, arithmetic and copies ran while one was open for 1% of the time, Pallas kernels for 0%

profile of v1, /device:TPU:1, one launch (start us, length us, event | category | flops | bytes accessed | tf_op | source)
XLA Modules:
  0.0 240.4 jit_solution(15337868969025603808)
XLA Ops:
  2.7 5.2 %fusion.1 = (bf16[1024,2048]{1,0:T(8,128)(2,1)S(1)}, bf16[1024,2048]{1,0:T(8,128)(2,1)S(1)}) fusion(f32[1024,2048]{1,0:T(8,128)} %param.2), kind=kLoop, calls=%fused_computation.3 | loop fusion | flops 10485760 | bytes 16777216 | tf_op jit(solution)/shard_map/convert_element_type | solution.py:17
  11.5 3.3 %collective-permute-start = (f32[32,17,128]{2,1,0:T(8,128)S(1)}, f32[32,17,128]{2,1,0:T(8,128)S(1)}, u32[]{:S(2)}, u32[]{:S(2)}) collective-permute-start(f32[32,17,128]{2,1,0:T(8,128)S(1)} %concatenate.81), channel_id=1, source_target_pairs={{0,1},{1,0},{2,3},{3,2},{4,5},{5,4},{6,7},{7,6},{8,9},{9,8},{10,11... | collective-permute-start | bytes 835592 | tf_op jit(solution)/shard_map/ppermute | solution.py:55
  14.8 1.3 collective-permute-done
  16.2 21.3 %all_to_all.35 = f32[544,1,128]{2,1,0:T(1,128)S(1)} all-to-all(f32[544,1,128]{2,1,0:T(1,128)S(1)} %bitcast.105), channel_id=1, replica_groups={{0,2,4,6,8,10,12,14,16,18,20,22,24,26,28,30,32,34,36,38,40,42,44,46,48,..., dimensions={0} | all-to-all | bytes 557056 | tf_op jit(solution)/shard_map/all_to_all | solution.py:58
  38.0 1.3 reduce.18
  39.4 14.7 %all_to_all.36 = f32[32,16,128]{2,1,0:T(8,128)S(1)} all-to-all(f32[32,16,128]{2,1,0:T(8,128)S(1)} %broadcast_in_dim.20), channel_id=1, replica_groups={{0,2,4,6,8,10,12,14,16,18,20,22,24,26,28,30,32,34,36,38,40,42,44,46,48,..., dimensions={0} | all-to-all | bytes 524288 | tf_op jit(solution)/shard_map/all_to_all | solution.py:58
  54.2 3.5 %collective-permute-start.1 = (f32[32,16,128]{2,1,0:T(8,128)S(1)}, f32[32,16,128]{2,1,0:T(8,128)S(1)}, u32[]{:S(2)}, u32[]{:S(2)}) collective-permute-start(f32[32,16,128]{2,1,0:T(8,128)S(1)} %all_to_all.36), channel_id=1, source_target_pairs={{0,1},{1,0},{2,3},{3,2},{4,5},{5,4},{6,7},{7,6},{8,9},{9,8},{10,11... | collective-permute-start | bytes 786440 | tf_op jit(solution)/shard_map/ppermute | solution.py:55
  57.7 1.1 collective-permute-done.1
  59.8 3.9 %fusion.19 = f32[192,1024]{1,0:T(8,128)S(1)} fusion(bf16[1024,2048]{1,0:T(8,128)(2,1)} %copy-done.6, bf16[64,2048]{1,0:T(8,128)(2,1)S(1)} %get-tuple-element.26, bf16[64,2048]{1,0:T(8,128)(2,1)S(1)} %get-tuple-element.25, bf16[64,2048]{1,0:T(8,128)(2,1)S(1)} %get-tuple-element.24), kind=kOutput, calls=%fused_computation.76 | convolution fusion | flops 807665664 | bytes 5767168 | tf_op jit(solution)/shard_map/dot_general | solution.py:32
  63.6 1.5 fusion.20
  66.1 1.3 collective-permute-start.2
  67.5 1.9 collective-permute-start.4
  69.4 1.7 collective-permute-done.2
  71.2 2.6 %collective-permute-start.3 = (f32[264,128]{1,0:T(8,128)S(1)}, f32[264,128]{1,0:T(8,128)S(1)}, u32[]{:S(2)}, u32[]{:S(2)}) collective-permute-start(f32[264,128]{1,0:T(8,128)S(1)} %fusion.53), channel_id=1, source_target_pairs={{0,192},{64,128},{128,64},{192,0},{1,193},{65,129},{129,65},{193,1... | collective-permute-start | bytes 405512 | tf_op jit(solution)/shard_map/ppermute | solution.py:61
  74.0 4.1 %collective-permute-done.5 = f32[256,128]{1,0:T(8,128)S(1)} collective-permute-done((f32[256,128]{1,0:T(8,128)S(1)}, f32[256,128]{1,0:T(8,128)S(1)}, u32[]{:S(2)}, u32[]{:S(2)}) %collective-permute-start.5) | collective-permute-done | bytes 131104 | tf_op jit(solution)/shard_map/ppermute | solution.py:61
  79.0 3.3 %fusion.33 = f32[192,2048]{1,0:T(8,128)S(1)} fusion(bf16[1024,2048]{1,0:T(8,128)(2,1)} %copy-done.6, bf16[64,1024]{1,0:T(8,128)(2,1)S(1)} %get-tuple-element.44, bf16[64,1024]{1,0:T(8,128)(2,1)S(1)} %get-tuple-element.45, bf16[64,1024]{1,0:T(8,128)(2,1)S(1)} %get-tuple-element.43), kind=kOutput, calls=%fused_computation.119 | convolution fusion | flops 806486016 | bytes 6160384 | tf_op jit(solution)/shard_map/dot_general | solution.py:32
  84.4 2.4 %collective-permute-start.6 = (f32[32,17,128]{2,1,0:T(8,128)S(1)}, f32[32,17,128]{2,1,0:T(8,128)S(1)}, u32[]{:S(2)}, u32[]{:S(2)}) collective-permute-start(f32[32,17,128]{2,1,0:T(8,128)S(1)} %concatenate.88), channel_id=1, source_target_pairs={{0,1},{1,0},{2,3},{3,2},{4,5},{5,4},{6,7},{7,6},{8,9},{9,8},{10,11... | collective-permute-start | bytes 835592 | tf_op jit(solution)/shard_map/ppermute | solution.py:55
  86.9 1.3 collective-permute-done.6
  89.6 3.9 %all-to-all-start.2 = ((f32[544,1,128]{2,1,0:T(1,128)}), f32[544,1,128]{2,1,0:T(1,128)S(1)}, u32[]{:S(2)}, u32[]{:S(2)}) async-start(f32[544,1,128]{2,1,0:T(1,128)} %bitcast.3), calls=%async_computation.2 | async-start | bytes 557056 | tf_op jit(solution)/shard_map/all_to_all | solution.py:58
  94.6 11.1 %all-to-all-done.2 = f32[544,1,128]{2,1,0:T(1,128)S(1)} async-done(((f32[544,1,128]{2,1,0:T(1,128)}), f32[544,1,128]{2,1,0:T(1,128)S(1)}, u32[]{:S(2)}, u32[]{:S(2)}) %all-to-all-start.2) | async-done | bytes 278560 | tf_op jit(solution)/shard_map/all_to_all | solution.py:58
  105.6 1.3 reduce.19
  108.8 14.8 %all_to_all.37 = f32[32,16,128]{2,1,0:T(8,128)S(1)} all-to-all(f32[32,16,128]{2,1,0:T(8,128)S(1)} %broadcast_in_dim.45), channel_id=1, replica_groups={{0,2,4,6,8,10,12,14,16,18,20,22,24,26,28,30,32,34,36,38,40,42,44,46,48,..., dimensions={0} | all-to-all | bytes 524288 | tf_op jit(solution)/shard_map/all_to_all | solution.py:58
  123.6 3.6 %collective-permute-start.7 = (f32[32,16,128]{2,1,0:T(8,128)S(1)}, f32[32,16,128]{2,1,0:T(8,128)S(1)}, u32[]{:S(2)}, u32[]{:S(2)}) collective-permute-start(f32[32,16,128]{2,1,0:T(8,128)S(1)} %all_to_all.37), channel_id=1, source_target_pairs={{0,1},{1,0},{2,3},{3,2},{4,5},{5,4},{6,7},{7,6},{8,9},{9,8},{10,11... | collective-permute-start | bytes 786440 | tf_op jit(solution)/shard_map/ppermute | solution.py:55
  129.3 1.5 fusion.17
  131.5 1.5 fusion.18
  134.9 1.4 collective-permute-start.10
  136.2 3.4 %collective-permute-done.8 = f32[264,128]{1,0:T(8,128)S(1)} collective-permute-done((f32[264,128]{1,0:T(8,128)S(1)}, f32[264,128]{1,0:T(8,128)S(1)}, u32[]{:S(2)}, u32[]{:S(2)}) %collective-permute-start.8) | collective-permute-done | bytes 135200 | tf_op jit(solution)/shard_map/ppermute | solution.py:61
  139.8 1.4 collective-permute-start.9
  141.5 4.1 %collective-permute-done.11 = f32[256,128]{1,0:T(8,128)S(1)} collective-permute-done((f32[256,128]{1,0:T(8,128)S(1)}, f32[256,128]{1,0:T(8,128)S(1)}, u32[]{:S(2)}, u32[]{:S(2)}) %collective-permute-start.11) | collective-permute-done | bytes 131104 | tf_op jit(solution)/shard_map/ppermute | solution.py:61
  148.3 3.3 %fusion.31 = f32[192,2048]{1,0:T(8,128)S(1)} fusion(bf16[1024,2048]{1,0:T(8,128)(2,1)} %copy-done.6, bf16[64,1024]{1,0:T(8,128)(2,1)S(1)} %get-tuple-element.38, bf16[64,1024]{1,0:T(8,128)(2,1)S(1)} %get-tuple-element.37, bf16[64,1024]{1,0:T(8,128)(2,1)S(1)} %get-tuple-element.6), kind=kOutput, calls=%fused_computation.117 | convolution fusion | flops 806486016 | bytes 6160384 | tf_op jit(solution)/shard_map/dot_general | solution.py:32
  153.7 2.4 %collective-permute-start.12 = (f32[32,17,128]{2,1,0:T(8,128)S(1)}, f32[32,17,128]{2,1,0:T(8,128)S(1)}, u32[]{:S(2)}, u32[]{:S(2)}) collective-permute-start(f32[32,17,128]{2,1,0:T(8,128)S(1)} %concatenate.95), channel_id=1, source_target_pairs={{0,1},{1,0},{2,3},{3,2},{4,5},{5,4},{6,7},{7,6},{8,9},{9,8},{10,11... | collective-permute-start | bytes 835592 | tf_op jit(solution)/shard_map/ppermute | solution.py:55
  156.1 1.3 collective-permute-done.12
  158.9 3.9 %all-to-all-start.4 = ((f32[544,1,128]{2,1,0:T(1,128)}), f32[544,1,128]{2,1,0:T(1,128)S(1)}, u32[]{:S(2)}, u32[]{:S(2)}) async-start(f32[544,1,128]{2,1,0:T(1,128)} %bitcast.6), calls=%async_computation.4 | async-start | bytes 557056 | tf_op jit(solution)/shard_map/all_to_all | solution.py:58
  164.5 10.3 %all-to-all-done.4 = f32[544,1,128]{2,1,0:T(1,128)S(1)} async-done(((f32[544,1,128]{2,1,0:T(1,128)}), f32[544,1,128]{2,1,0:T(1,128)S(1)}, u32[]{:S(2)}, u32[]{:S(2)}) %all-to-all-start.4) | async-done | bytes 278560 | tf_op jit(solution)/shard_map/all_to_all | solution.py:58
  174.9 1.3 reduce.20
  178.1 14.8 %all_to_all.38 = f32[32,16,128]{2,1,0:T(8,128)S(1)} all-to-all(f32[32,16,128]{2,1,0:T(8,128)S(1)} %broadcast_in_dim.48), channel_id=1, replica_groups={{0,2,4,6,8,10,12,14,16,18,20,22,24,26,28,30,32,34,36,38,40,42,44,46,48,..., dimensions={0} | all-to-all | bytes 524288 | tf_op jit(solution)/shard_map/all_to_all | solution.py:58
  192.9 3.6 %collective-permute-start.13 = (f32[32,16,128]{2,1,0:T(8,128)S(1)}, f32[32,16,128]{2,1,0:T(8,128)S(1)}, u32[]{:S(2)}, u32[]{:S(2)}) collective-permute-start(f32[32,16,128]{2,1,0:T(8,128)S(1)} %all_to_all.38), channel_id=1, source_target_pairs={{0,1},{1,0},{2,3},{3,2},{4,5},{5,4},{6,7},{7,6},{8,9},{9,8},{10,11... | collective-permute-start | bytes 786440 | tf_op jit(solution)/shard_map/ppermute | solution.py:55
  196.5 1.1 collective-permute-done.13
  198.6 1.5 fusion.15
  200.8 1.5 fusion.16
  204.6 1.5 collective-permute-start.16
  206.1 3.3 %collective-permute-done.14 = f32[264,128]{1,0:T(8,128)S(1)} collective-permute-done((f32[264,128]{1,0:T(8,128)S(1)}, f32[264,128]{1,0:T(8,128)S(1)}, u32[]{:S(2)}, u32[]{:S(2)}) %collective-permute-start.14) | collective-permute-done | bytes 135200 | tf_op jit(solution)/shard_map/ppermute | solution.py:61
  210.2 1.5 collective-permute-start.15
  211.8 4.1 %collective-permute-done.17 = f32[256,128]{1,0:T(8,128)S(1)} collective-permute-done((f32[256,128]{1,0:T(8,128)S(1)}, f32[256,128]{1,0:T(8,128)S(1)}, u32[]{:S(2)}, u32[]{:S(2)}) %collective-permute-start.17) | collective-permute-done | bytes 131104 | tf_op jit(solution)/shard_map/ppermute | solution.py:61
  219.2 2.4 %collective-permute-start.18 = (f32[32,1,128]{2,1,0:T(1,128)S(1)}, f32[32,1,128]{2,1,0:T(1,128)S(1)}, u32[]{:S(2)}, u32[]{:S(2)}) collective-permute-start(f32[32,1,128]{2,1,0:T(1,128)S(1)} %broadcast_in_dim.51), channel_id=1, source_target_pairs={{0,1},{1,0},{2,3},{3,2},{4,5},{5,4},{6,7},{7,6},{8,9},{9,8},{10,11... | collective-permute-start | bytes 49160 | tf_op jit(solution)/shard_map/ppermute | solution.py:55
  222.5 1.2 broadcast_add_fusion
  223.7 3.8 %all-to-all-start.6 = ((f32[32,1,128]{2,1,0:T(1,128)}), f32[32,1,128]{2,1,0:T(1,128)S(1)}, u32[]{:S(2)}, u32[]{:S(2)}) async-start(f32[32,1,128]{2,1,0:T(1,128)} %bitcast.98), calls=%async_computation.6 | async-start | bytes 32768 | tf_op jit(solution)/shard_map/all_to_all | solution.py:58
  228.9 7.2 %all-to-all-done.6 = f32[32,1,128]{2,1,0:T(1,128)S(1)} async-done(((f32[32,1,128]{2,1,0:T(1,128)}), f32[32,1,128]{2,1,0:T(1,128)S(1)}, u32[]{:S(2)}, u32[]{:S(2)}) %all-to-all-start.6) | async-done | bytes 16416 | tf_op jit(solution)/shard_map/all_to_all | solution.py:58
  (147 shorter events, 35.3 us)
Async XLA Ops:
  7.9 2.0 copy-start
  7.9 3.2 %copy-start.6 = (bf16[1024,2048]{1,0:T(8,128)(2,1)}, bf16[1024,2048]{1,0:T(8,128)(2,1)S(1)}, u32[]{:S(2)}) copy-start(bf16[1024,2048]{1,0:T(8,128)(2,1)S(1)} %get-tuple-element.11) | copy-start | bytes 12582916
  11.5 4.7 %collective-permute-start = (f32[32,17,128]{2,1,0:T(8,128)S(1)}, f32[32,17,128]{2,1,0:T(8,128)S(1)}, u32[]{:S(2)}, u32[]{:S(2)}) collective-permute-start(f32[32,17,128]{2,1,0:T(8,128)S(1)} %concatenate.81), channel_id=1, source_target_pairs={{0,1},{1,0},{2,3},{3,2},{4,5},{5,4},{6,7},{7,6},{8,9},{9,8},{10,11... | collective-permute-start | bytes 835592 | tf_op jit(solution)/shard_map/ppermute | solution.py:55
  54.2 4.6 %collective-permute-start.1 = (f32[32,16,128]{2,1,0:T(8,128)S(1)}, f32[32,16,128]{2,1,0:T(8,128)S(1)}, u32[]{:S(2)}, u32[]{:S(2)}) collective-permute-start(f32[32,16,128]{2,1,0:T(8,128)S(1)} %all_to_all.36), channel_id=1, source_target_pairs={{0,1},{1,0},{2,3},{3,2},{4,5},{5,4},{6,7},{7,6},{8,9},{9,8},{10,11... | collective-permute-start | bytes 786440 | tf_op jit(solution)/shard_map/ppermute | solution.py:55
  59.7 3.9 %copy-start.1 = (bf16[1024,2048]{1,0:T(8,128)(2,1)S(1)}, bf16[1024,2048]{1,0:T(8,128)(2,1)}, u32[]{:S(2)}) copy-start(bf16[1024,2048]{1,0:T(8,128)(2,1)} %copy-done) | copy-start | bytes 12582916
  66.1 4.9 %collective-permute-start.2 = (f32[264,128]{1,0:T(8,128)S(1)}, f32[264,128]{1,0:T(8,128)S(1)}, u32[]{:S(2)}, u32[]{:S(2)}) collective-permute-start(f32[264,128]{1,0:T(8,128)S(1)} %maximum_maximum_fusion), channel_id=1, source_target_pairs={{0,64},{64,0},{128,192},{192,128},{1,65},{65,1},{129,193},{193,129... | collective-permute-start | bytes 405512 | tf_op jit(solution)/shard_map/ppermute | solution.py:61
  67.5 6.3 %collective-permute-start.4 = (f32[256,128]{1,0:T(8,128)S(1)}, f32[256,128]{1,0:T(8,128)S(1)}, u32[]{:S(2)}, u32[]{:S(2)}) collective-permute-start(f32[256,128]{1,0:T(8,128)S(1)} %slice.264), channel_id=1, source_target_pairs={{0,192},{64,128},{128,64},{192,0},{1,193},{65,129},{129,65},{193,1... | collective-permute-start | bytes 393224 | tf_op jit(solution)/shard_map/ppermute | solution.py:61
  71.2 7.0 %collective-permute-start.3 = (f32[264,128]{1,0:T(8,128)S(1)}, f32[264,128]{1,0:T(8,128)S(1)}, u32[]{:S(2)}, u32[]{:S(2)}) collective-permute-start(f32[264,128]{1,0:T(8,128)S(1)} %fusion.53), channel_id=1, source_target_pairs={{0,192},{64,128},{128,64},{192,0},{1,193},{65,129},{129,65},{193,1... | collective-permute-start | bytes 405512 | tf_op jit(solution)/shard_map/ppermute | solution.py:61
  73.8 4.4 %collective-permute-start.5 = (f32[256,128]{1,0:T(8,128)S(1)}, f32[256,128]{1,0:T(8,128)S(1)}, u32[]{:S(2)}, u32[]{:S(2)}) collective-permute-start(f32[256,128]{1,0:T(8,128)S(1)} %add.226), channel_id=1, source_target_pairs={{0,64},{64,0},{128,192},{192,128},{1,65},{65,1},{129,193},{193,129... | collective-permute-start | bytes 393224 | tf_op jit(solution)/shard_map/ppermute | solution.py:61
  79.0 3.5 %copy-start.2 = (bf16[1024,2048]{1,0:T(8,128)(2,1)S(1)}, bf16[1024,2048]{1,0:T(8,128)(2,1)}, u32[]{:S(2)}) copy-start(bf16[1024,2048]{1,0:T(8,128)(2,1)} %copy-done) | copy-start | bytes 12582916
  84.4 3.8 %collective-permute-start.6 = (f32[32,17,128]{2,1,0:T(8,128)S(1)}, f32[32,17,128]{2,1,0:T(8,128)S(1)}, u32[]{:S(2)}, u32[]{:S(2)}) collective-permute-start(f32[32,17,128]{2,1,0:T(8,128)S(1)} %concatenate.88), channel_id=1, source_target_pairs={{0,1},{1,0},{2,3},{3,2},{4,5},{5,4},{6,7},{7,6},{8,9},{9,8},{10,11... | collective-permute-start | bytes 835592 | tf_op jit(solution)/shard_map/ppermute | solution.py:55
  89.6 16.0 %all-to-all-start.2 = ((f32[544,1,128]{2,1,0:T(1,128)}), f32[544,1,128]{2,1,0:T(1,128)S(1)}, u32[]{:S(2)}, u32[]{:S(2)}) async-start(f32[544,1,128]{2,1,0:T(1,128)} %bitcast.3), calls=%async_computation.2 | async-start | bytes 557056 | tf_op jit(solution)/shard_map/all_to_all | solution.py:58
  108.8 20.5 %copy-start.7 = (bf16[1024,2048]{1,0:T(8,128)(2,1)S(1)}, bf16[1024,2048]{1,0:T(8,128)(2,1)}, u32[]{:S(2)}) copy-start(bf16[1024,2048]{1,0:T(8,128)(2,1)} %copy-done.6) | copy-start | bytes 12582916
  123.6 4.8 %collective-permute-start.7 = (f32[32,16,128]{2,1,0:T(8,128)S(1)}, f32[32,16,128]{2,1,0:T(8,128)S(1)}, u32[]{:S(2)}, u32[]{:S(2)}) collective-permute-start(f32[32,16,128]{2,1,0:T(8,128)S(1)} %all_to_all.37), channel_id=1, source_target_pairs={{0,1},{1,0},{2,3},{3,2},{4,5},{5,4},{6,7},{7,6},{8,9},{9,8},{10,11... | collective-permute-start | bytes 786440 | tf_op jit(solution)/shard_map/ppermute | solution.py:55
  129.3 2.2 copy-start.3
  134.7 4.9 %collective-permute-start.8 = (f32[264,128]{1,0:T(8,128)S(1)}, f32[264,128]{1,0:T(8,128)S(1)}, u32[]{:S(2)}, u32[]{:S(2)}) collective-permute-start(f32[264,128]{1,0:T(8,128)S(1)} %maximum_maximum_fusion.1), channel_id=1, source_target_pairs={{0,64},{64,0},{128,192},{192,128},{1,65},{65,1},{129,193},{193,129... | collective-permute-start | bytes 405512 | tf_op jit(solution)/shard_map/ppermute | solution.py:61
  134.9 6.3 %collective-permute-start.10 = (f32[256,128]{1,0:T(8,128)S(1)}, f32[256,128]{1,0:T(8,128)S(1)}, u32[]{:S(2)}, u32[]{:S(2)}) collective-permute-start(f32[256,128]{1,0:T(8,128)S(1)} %slice.288), channel_id=1, source_target_pairs={{0,192},{64,128},{128,64},{192,0},{1,193},{65,129},{129,65},{193,1... | collective-permute-start | bytes 393224 | tf_op jit(solution)/shard_map/ppermute | solution.py:61
  139.8 5.8 %collective-permute-start.9 = (f32[264,128]{1,0:T(8,128)S(1)}, f32[264,128]{1,0:T(8,128)S(1)}, u32[]{:S(2)}, u32[]{:S(2)}) collective-permute-start(f32[264,128]{1,0:T(8,128)S(1)} %fusion.75), channel_id=1, source_target_pairs={{0,192},{64,128},{128,64},{192,0},{1,193},{65,129},{129,65},{193,1... | collective-permute-start | bytes 405512 | tf_op jit(solution)/shard_map/ppermute | solution.py:61
  141.2 4.4 %collective-permute-start.11 = (f32[256,128]{1,0:T(8,128)S(1)}, f32[256,128]{1,0:T(8,128)S(1)}, u32[]{:S(2)}, u32[]{:S(2)}) collective-permute-start(f32[256,128]{1,0:T(8,128)S(1)} %add.243), channel_id=1, source_target_pairs={{0,64},{64,0},{128,192},{192,128},{1,65},{65,1},{129,193},{193,129... | collective-permute-start | bytes 393224 | tf_op jit(solution)/shard_map/ppermute | solution.py:61
  148.2 3.5 %copy-start.4 = (bf16[1024,2048]{1,0:T(8,128)(2,1)S(1)}, bf16[1024,2048]{1,0:T(8,128)(2,1)}, u32[]{:S(2)}) copy-start(bf16[1024,2048]{1,0:T(8,128)(2,1)} %copy-done) | copy-start | bytes 12582916
  153.7 3.8 %collective-permute-start.12 = (f32[32,17,128]{2,1,0:T(8,128)S(1)}, f32[32,17,128]{2,1,0:T(8,128)S(1)}, u32[]{:S(2)}, u32[]{:S(2)}) collective-permute-start(f32[32,17,128]{2,1,0:T(8,128)S(1)} %concatenate.95), channel_id=1, source_target_pairs={{0,1},{1,0},{2,3},{3,2},{4,5},{5,4},{6,7},{7,6},{8,9},{9,8},{10,11... | collective-permute-start | bytes 835592 | tf_op jit(solution)/shard_map/ppermute | solution.py:55
  158.9 16.0 %all-to-all-start.4 = ((f32[544,1,128]{2,1,0:T(1,128)}), f32[544,1,128]{2,1,0:T(1,128)S(1)}, u32[]{:S(2)}, u32[]{:S(2)}) async-start(f32[544,1,128]{2,1,0:T(1,128)} %bitcast.6), calls=%async_computation.4 | async-start | bytes 557056 | tf_op jit(solution)/shard_map/all_to_all | solution.py:58
  178.1 20.5 %copy-start.8 = (bf16[1024,2048]{1,0:T(8,128)(2,1)S(1)}, bf16[1024,2048]{1,0:T(8,128)(2,1)}, u32[]{:S(2)}) copy-start(bf16[1024,2048]{1,0:T(8,128)(2,1)} %copy-done.6) | copy-start | bytes 12582916
  192.9 4.8 %collective-permute-start.13 = (f32[32,16,128]{2,1,0:T(8,128)S(1)}, f32[32,16,128]{2,1,0:T(8,128)S(1)}, u32[]{:S(2)}, u32[]{:S(2)}) collective-permute-start(f32[32,16,128]{2,1,0:T(8,128)S(1)} %all_to_all.38), channel_id=1, source_target_pairs={{0,1},{1,0},{2,3},{3,2},{4,5},{5,4},{6,7},{7,6},{8,9},{9,8},{10,11... | collective-permute-start | bytes 786440 | tf_op jit(solution)/shard_map/ppermute | solution.py:55
  198.6 2.2 copy-start.5
  203.7 0.6 copy-start.9
  204.5 4.9 %collective-permute-start.14 = (f32[264,128]{1,0:T(8,128)S(1)}, f32[264,128]{1,0:T(8,128)S(1)}, u32[]{:S(2)}, u32[]{:S(2)}) collective-permute-start(f32[264,128]{1,0:T(8,128)S(1)} %maximum_maximum_fusion.2), channel_id=1, source_target_pairs={{0,64},{64,0},{128,192},{192,128},{1,65},{65,1},{129,193},{193,129... | collective-permute-start | bytes 405512 | tf_op jit(solution)/shard_map/ppermute | solution.py:61
  204.6 7.1 %collective-permute-start.16 = (f32[256,128]{1,0:T(8,128)S(1)}, f32[256,128]{1,0:T(8,128)S(1)}, u32[]{:S(2)}, u32[]{:S(2)}) collective-permute-start(f32[256,128]{1,0:T(8,128)S(1)} %slice.313), channel_id=1, source_target_pairs={{0,192},{64,128},{128,64},{192,0},{1,193},{65,129},{129,65},{193,1... | collective-permute-start | bytes 393224 | tf_op jit(solution)/shard_map/ppermute | solution.py:61
  210.2 5.7 %collective-permute-start.15 = (f32[264,128]{1,0:T(8,128)S(1)}, f32[264,128]{1,0:T(8,128)S(1)}, u32[]{:S(2)}, u32[]{:S(2)}) collective-permute-start(f32[264,128]{1,0:T(8,128)S(1)} %fusion.74), channel_id=1, source_target_pairs={{0,192},{64,128},{128,64},{192,0},{1,193},{65,129},{129,65},{193,1... | collective-permute-start | bytes 405512 | tf_op jit(solution)/shard_map/ppermute | solution.py:61
  211.7 4.2 %collective-permute-start.17 = (f32[256,128]{1,0:T(8,128)S(1)}, f32[256,128]{1,0:T(8,128)S(1)}, u32[]{:S(2)}, u32[]{:S(2)}) collective-permute-start(f32[256,128]{1,0:T(8,128)S(1)} %add.268), channel_id=1, source_target_pairs={{0,64},{64,0},{128,192},{192,128},{1,65},{65,1},{129,193},{193,129... | collective-permute-start | bytes 393224 | tf_op jit(solution)/shard_map/ppermute | solution.py:61
  219.2 3.3 %collective-permute-start.18 = (f32[32,1,128]{2,1,0:T(1,128)S(1)}, f32[32,1,128]{2,1,0:T(1,128)S(1)}, u32[]{:S(2)}, u32[]{:S(2)}) collective-permute-start(f32[32,1,128]{2,1,0:T(1,128)S(1)} %broadcast_in_dim.51), channel_id=1, source_target_pairs={{0,1},{1,0},{2,3},{3,2},{4,5},{5,4},{6,7},{7,6},{8,9},{9,8},{10,11... | collective-permute-start | bytes 49160 | tf_op jit(solution)/shard_map/ppermute | solution.py:55
  223.7 12.4 %all-to-all-start.6 = ((f32[32,1,128]{2,1,0:T(1,128)}), f32[32,1,128]{2,1,0:T(1,128)S(1)}, u32[]{:S(2)}, u32[]{:S(2)}) async-start(f32[32,1,128]{2,1,0:T(1,128)} %bitcast.98), calls=%async_computation.6 | async-start | bytes 32768 | tf_op jit(solution)/shard_map/all_to_all | solution.py:58

commit v2 on v0

v2 whole, which is shorter than its diff:
```python
import functools

import jax
import jax.numpy as jnp
from jax import lax
from jax.experimental import pallas as pl
from jax.experimental.pallas import tpu as pltpu
from jax.sharding import PartitionSpec as P

ITERS = 3
ridge = 0.5
CORES, LANES, TILE = 2, 128, 8
WIDE = 256
MIB = 1 << 20
F32, BF16 = jnp.float32, jnp.bfloat16
VMEM = pl.BlockSpec(memory_space=pltpu.VMEM)
HBM = pl.BlockSpec(memory_space=pl.ANY)


def shape(*dims, dtype=F32):
    return jax.ShapeDtypeStruct(dims, dtype)


def here(x):
    return pltpu.with_memory_space_constraint(x, pltpu.VMEM)


def call(kernel, out_shape, *args, scratch=(), limit=24, specs=None, flops=0, **static):
    return pl.pallas_call(
        functools.partial(kernel, **static),
        in_specs=specs or [VMEM] * len(args),
        out_specs=jax.tree.map(lambda _: VMEM, out_shape),
        out_shape=out_shape,
        scratch_shapes=list(scratch),
        compiler_params=pltpu.CompilerParams(vmem_limit_bytes=limit * MIB),
        cost_estimate=pl.CostEstimate(flops=flops, bytes_accessed=MIB, transcendentals=0),
        name=kernel.__name__,
    )(*args)


def split3(x):
    high = x.astype(BF16)
    rest = x - high.astype(F32)
    middle = rest.astype(BF16)
    low = (rest - middle.astype(F32)).astype(BF16)
    return jnp.concatenate([high, middle, low], axis=0)


def dot(a, b, ca, cb):
    return lax.dot_general(a, b, (((ca,), (cb,)), ((), ())), preferred_element_type=F32)


def fold3(p):
    n = p.shape[0] // 3
    return p[2 * n :] + p[n : 2 * n] + p[:n]


def row(x):
    return jnp.broadcast_to(x, (1, LANES))


def store_pieces(mine, theirs, value, at, stride):
    half = value.shape[0] // CORES
    for i in range(WIDE // LANES):
        part = value[:, i * LANES : (i + 1) * LANES]
        j = at * (WIDE // LANES) + i
        mine[pl.ds(j, half, stride=stride), :] = part[:half]
        theirs[pl.ds(j, half, stride=stride), :] = part[half:]


def first(core, states, targets, high, low, turned, mine, theirs, buf, sems):
    steps = buf.shape[0]
    copies = [
        pltpu.make_async_copy(
            states.at[:, pl.ds(t * WIDE, WIDE)], buf.at[t], sems.at[t]
        )
        for t in range(steps)
    ]
    for c in copies:
        c.start()
    half = targets.shape[0] // CORES
    own = core[0, 0] == 0
    top, bottom = targets[:half, :], targets[half:, :]
    x = jnp.concatenate(
        [jnp.where(own, top, bottom), jnp.where(own, bottom, top)], axis=0
    )
    turned[...] = x
    x3 = split3(x)
    for t in range(steps):
        copies[t].wait()
        s = buf[t]
        h = s.astype(BF16)
        l = (s - h.astype(F32)).astype(BF16)
        high[:, pl.ds(t * WIDE, WIDE)] = h
        low[:, pl.ds(t * WIDE, WIDE)] = l
        store_pieces(mine, theirs, fold3(dot(x3, l, 1, 0) + dot(x3, h, 1, 0)), t, mine.shape[0] // half)


def combine(a, ra, b, rb):
    n = b.shape[0]
    image = jnp.concatenate([a[:n, :] + ra[:n, :], b[...] + rb[...]], axis=1)
    tail = a[n : n + TILE, :LANES] + ra[n : n + TILE, :LANES]
    return image, tail


def step_image(a, ra, b, rb, before, scal, image_out, scal_out):
    image, tail = combine(a, ra, b, rb)
    gamma = tail[0:1]
    if before is None:
        beta = jnp.zeros_like(gamma)
        square = gamma
    else:
        beta = gamma / scal[0:1, :]
        square = gamma + beta * (2.0 * tail[1:2] + beta * scal[2:3, :])
        image = image + beta[:, :1] * before[...]
    image_out[...] = image
    scal_out[0:1, :] = gamma
    scal_out[1:2, :] = beta
    scal_out[2:3, :] = square
    scal_out[3:, :] = jnp.zeros((TILE - 3, LANES), F32)
    return image, row(jnp.sum(image * image))


def back(*refs, later):
    if later:
        a, ra, b, rb, before, scal, high, low, image_out, scal_out, mine, theirs = refs
    else:
        a, ra, b, rb, high, low, image_out, scal_out, mine, theirs = refs
        before = scal = None
    image, image_sq = step_image(a, ra, b, rb, before, scal, image_out, scal_out)
    half = image.shape[0] // CORES
    stride = mine.shape[0] // half
    x3 = split3(image)
    for t in range(high.shape[1] // WIDE):
        at = pl.ds(t * WIDE, WIDE)
        p = dot(x3, low[:, at], 1, 0) + dot(x3, high[:, at], 1, 0)
        store_pieces(mine, theirs, fold3(p), t, stride)
    extra = jnp.broadcast_to(image_sq, (half, LANES))
    mine[pl.ds(stride - 1, half, stride=stride), :] = extra
    theirs[pl.ds(stride - 1, half, stride=stride), :] = extra


def last_image(a, ra, b, rb, before, scal, image_out, scal_out, squares):
    _, image_sq = step_image(a, ra, b, rb, before, scal, image_out, scal_out)
    squares[...] = jnp.broadcast_to(image_sq, squares.shape)


def step_size(image_sq, scal):
    return scal[0:1, :] / (image_sq + ridge * scal[2:3, :])


def reduce_pieces(*refs, rows, scalars):
    if scalars:
        got, scal, out, size = refs
    else:
        got, out = refs
    count = out.shape[0] // rows
    stride = got.shape[0] // count
    terms = [got[i * stride : (i + 1) * stride, :] for i in range(count)]
    while len(terms) > 1:
        terms = [terms[i] + terms[i + 1] for i in range(0, len(terms), 2)]
    total = terms[0]
    for i in range(count):
        out[i * rows : (i + 1) * rows, :] = total[:rows]
    if scalars:
        size[...] = jnp.broadcast_to(step_size(total[rows : rows + 1], scal), size.shape)


def forward(*refs, step):
    if step == 0:
        top, bottom, high, low, gradient, a, b = refs
        g = jnp.concatenate([top[...], bottom[...]], axis=0)
        cross = None
    else:
        if step == 1:
            top, bottom, size, scal, g_old, high, low, gradient, direction, a, b = refs
            d = g_old[...]
        else:
            top, bottom, size, scal, g_old, d_old, high, low, gradient, direction, a, b = refs
            d = g_old[...] + scal[1:2, :] * d_old[...]
        q = jnp.concatenate([top[...], bottom[...]], axis=0)
        direction[...] = d
        g = g_old[...] - size[0:1, :] * (q + ridge * d)
        cross = jnp.sum(g * d)
    gradient[...] = g
    n = b.shape[0]
    stride = g.shape[0] // n
    a[n : n + 1, :] = jnp.broadcast_to(jnp.sum(g * g), (1, a.shape[1]))
    rest = jnp.zeros((TILE - 1, a.shape[1]), F32)
    a[n + 1 : n + TILE, :] = rest if cross is None else rest + cross
    x3 = split3(
        jnp.concatenate([gradient[pl.ds(j, n, stride=stride), :] for j in range(stride)], axis=1)
    )
    for t in range(high.shape[0] // WIDE):
        at = pl.ds(t * WIDE, WIDE)
        p = fold3(dot(x3, low[at, :], 1, 1) + dot(x3, high[at, :], 1, 1))
        out, k = (a, t) if t < a.shape[1] // WIDE else (b, t - a.shape[1] // WIDE)
        out[0:n, k * WIDE : (k + 1) * WIDE] = p


def finish(core, got, other, scal, size0, size1, d0, d1, g2, i0, i1, i2, targets, readout, residual, sums):
    n = targets.shape[0]
    half = n // CORES
    stride = d0.shape[0] // n
    image_sq = jnp.sum(got[...] + other[...], axis=0, keepdims=True)
    size2 = step_size(image_sq, scal)
    own = core[0, 0] == 0
    s0, s1 = size0[0:1, :], size1[0:1, :]
    direction = g2[...] + scal[1:2, :] * d1[...]
    total = s0 * d0[...] + s1 * d1[...] + size2 * direction
    sums[...] = total
    for j in range(stride):
        x = sums[pl.ds(j, n, stride=stride), :]
        at = pl.ds(j * LANES, LANES)
        readout[:half, at] = jnp.where(own, x[:half], x[half:])
        readout[half:, at] = jnp.where(own, x[half:], x[:half])
    r = targets[...] - s0[:, :1] * i0[...] - s1[:, :1] * i1[...] - size2[:, :1] * i2[...]
    residual[:half, :] = jnp.where(own, r[:half], r[half:])
    residual[half:, :] = jnp.where(own, r[half:], r[:half])


def shards(states, targets):
    samples, units = states.shape
    outputs = targets.shape[1]
    samp_count = lax.axis_size("samp")
    unit_count = lax.axis_size("unit")
    chips = samp_count // CORES
    half = outputs // CORES
    rows = units // LANES
    core = jnp.full((1, 1), lax.axis_index("samp") % CORES, jnp.int32)

    swap_cores = [(i, i ^ 1) for i in range(samp_count)]
    groups = [[chip * CORES + c for chip in range(chips)] for c in range(CORES)]

    def swap(x):
        return lax.ppermute(x, "samp", swap_cores)

    def exchange(x):
        n = x.shape[0]
        x = x.reshape(n, 1, LANES)
        x = lax.all_to_all(x, "samp", 0, 0, axis_index_groups=groups, tiled=True)
        return x.reshape(n, LANES)

    def unit_hop(x, mask):
        return lax.ppermute(x, "unit", [(i, i ^ mask) for i in range(unit_count)])

    def unit_sum(a, b):
        a, b = a + unit_hop(a, 1), b + unit_hop(b, 3)
        return a, unit_hop(a, 3), b, unit_hop(b, 1)

    vector = shape(TILE, LANES)
    image_shape = shape(outputs, samples)
    whole = shape(outputs * rows, LANES)
    ab = [shape(outputs + TILE, samples // 2), shape(outputs, samples // 2)]
    flops = 2 * 6 * samples * units * outputs

    smem = pl.BlockSpec(memory_space=pltpu.SMEM)
    high, low, turned, mine, theirs = call(
        first,
        [shape(samples, units, dtype=BF16)] * 2 + [image_shape] + [shape(half * rows, LANES)] * 2,
        core,
        states,
        here(targets.T),
        specs=[smem, HBM, VMEM],
        scratch=[
            pltpu.VMEM((units // WIDE, samples, WIDE), F32),
            pltpu.SemaphoreType.DMA((units // WIDE,)),
        ],
        limit=32,
        flops=flops,
    )
    high, low = here(high), here(low)
    got = exchange(mine + swap(theirs))
    spread = call(reduce_pieces, shape(half * rows, LANES), got, rows=rows, scalars=False)

    gradients, directions, images, sizes = [], [], [], []
    scal = size = None
    for step in range(ITERS):
        top = exchange(spread)
        bottom = swap(top)
        if step == 0:
            g, a, b = call(forward, [whole] + ab, top, bottom, high, low, step=0, flops=flops)
        else:
            olds = [gradients[-1]] + ([directions[-1]] if step > 1 else [])
            g, d, a, b = call(
                forward,
                [whole, whole] + ab,
                top,
                bottom,
                size,
                scal,
                *olds,
                high,
                low,
                step=step,
                flops=flops,
            )
            directions.append(d)
        gradients.append(g)
        hops = unit_sum(a, b)
        olds = [images[-1], scal] if step else []
        if step + 1 < ITERS:
            piece = shape(half * (rows + 1), LANES)
            image, scal, mine, theirs = call(
                back,
                [image_shape, vector, piece, piece],
                *hops,
                *olds,
                high,
                low,
                later=step > 0,
                flops=flops,
            )
            images.append(image)
            got = exchange(mine + swap(theirs))
            spread, size = call(
                reduce_pieces,
                [shape(half * rows, LANES), vector],
                got,
                scal,
                rows=rows,
                scalars=True,
            )
            sizes.append(size)
        else:
            image, scal, squares = call(
                last_image, [image_shape, vector, shape(half, LANES)], *hops, *olds
            )
            images.append(image)
            got = exchange(squares)
            other = swap(got)
    readout, residual = call(
        finish,
        [shape(outputs, units), image_shape],
        core,
        got,
        other,
        scal,
        *sizes,
        *directions,
        gradients[-1],
        *images,
        turned,
        specs=[smem] + [VMEM] * 12,
        scratch=[pltpu.VMEM((outputs * rows, LANES), F32)],
    )
    return readout.T, residual.T


def solution(mesh):
    return jax.shard_map(
        shards,
        mesh=mesh,
        in_specs=(P("samp", "unit"), P("samp", None)),
        out_specs=(P("unit", None), P("samp", None)),
        check_vma=False,
    )
```

time: 1390 us -> 198 us (0.14)
  blocking collectives: 751 us -> 108 us
  waiting for transfers between devices: 536 us -> 29.4 us
  matrix products: 63 us -> 0 us
  starting transfers between devices: 0.25 us -> 34.4 us
  between operations: 26.1 us -> 0.78 us
  Pallas kernels: 0 us -> 20.5 us
  other arithmetic: 15.6 us -> 0.22 us
    psum x8 -> x0, blocking collectives: 751 us -> none  [the longest x3 374 us: shards(): image_sq = lax.psum(jnp.sum(image * image), 'samp')]
    psum x6 -> x0, waiting for transfers between devices: 536 us -> none  [the longest x3 536 us: gradient_of(): summed = lax.psum(transposed(states, residual), 'samp')]
    all_to_all x0 -> x7, blocking collectives: none -> 108 us  [exchange(): x = lax.all_to_all(x, 'samp', 0, 0, axis_index_groups=groups, tiled=True)]
    dot_general x6 -> x0, matrix products: 63 us -> none  [the longest x3 35.7 us: shards(): jnp.dot(states, whole_direction, precision=lax.Precision.HIGHEST, preferr...]
    ppermute x0 -> x19, starting transfers between devices: none -> 34.4 us  [the longest x7 22.4 us: swap(): return lax.ppermute(x, 'samp', swap_cores)]
    ppermute x0 -> x19, waiting for transfers between devices: none -> 29.4 us  [the longest x12 21.5 us: unit_hop(): return lax.ppermute(x, 'unit', [(i, i ^ mask) for i in range(unit_count)])]
    pallas_call x0 -> x11, Pallas kernels: none -> 20.5 us  [call(): pl.pallas_call(functools.partial(kernel, **static), in_specs=specs or [VM...]
  transfers between devices with their start and end apart: 6 -> 19, of which waited for: 3 -> 14; matrix products, arithmetic and copies ran while one was open for 0% -> 0% of each run, Pallas kernels for 0% -> 0%
where the time goes in v2:
time: 198 us
  blocking collectives  108 us (55%)
  starting transfers between devices  34.4 us (17%)
  waiting for transfers between devices  29.4 us (15%)
  Pallas kernels  20.5 us (10%)
  local copies, waits for them, and re-layouts  4.32 us (2%)
    all_to_all x7, blocking collectives, exchange(): x = lax.all_to_all(x, 'samp', 0, 0, axis_index_groups=groups, tiled=True)  108 us
    ppermute x7, starting transfers between devices, swap(): return lax.ppermute(x, 'samp', swap_cores)  22.4 us
    ppermute x12, waiting for transfers between devices, unit_hop(): return lax.ppermute(x, 'unit', [(i, i ^ mask) for i in range(unit_count)])  21.5 us
    pallas_call x11, Pallas kernels, call(): pl.pallas_call(functools.partial(kernel, **static), in_specs=specs or [VM...  20.5 us
    ppermute x12, starting transfers between devices, unit_hop(): return lax.ppermute(x, 'unit', [(i, i ^ mask) for i in range(unit_count)])  12 us
    ppermute x7, waiting for transfers between devices, swap(): return lax.ppermute(x, 'samp', swap_cores)  7.86 us
    unnamed x4, local copies, waits for them, and re-layouts  4.32 us
  transfers between devices with their start and end apart: 19, of which 14 were waited for; matrix products, arithmetic and copies ran while one was open for 0% of the time, Pallas kernels for 0%

profile of v2, /device:TPU:1, one launch (start us, length us, event | category | flops | bytes accessed | tf_op | source)
XLA Modules:
  0.0 197.7 jit_solution(17701465764796940677)
XLA Ops:
  0.6 3.4 %copy-done = f32[1024,2048]{1,0:T(8,128)S(1)} copy-done((f32[1024,2048]{1,0:T(8,128)S(1)}, f32[1024,2048]{1,0:T(8,128)}, u32[]{:S(2)}) %copy-start) | copy-done | bytes 8388632
  4.0 0.9 copy-done.1
  5.0 6.0 %first.1 = (bf16[1024,2048]{1,0:T(8,128)(2,1)S(1)}, bf16[1024,2048]{1,0:T(8,128)(2,1)S(1)}, f32[64,1024]{1,0:T(8,128)S(1)}, f32[512,128]{1,0:T(8,128)S(1)}, f32[512,128]{1,0:T(8,128)S(1)}) custom-call(s32[1,1]{1,0:T(1,128)} %bitcast.core, f32[1024,2048]{1,0:T(8,128)S(1)} %copy-done, f32[64,1024]{1,0:T(8,128)S(1)} %bitcast.42), custom_call_target="tpu_custom_call" | custom-call | flops 1610612736 | bytes 1048576 | tf_op jit(solution)/shard_map/first/pallas_call | solution.py:29
  10.9 3.3 %collective-permute-start = (f32[512,128]{1,0:T(8,128)S(1)}, f32[512,128]{1,0:T(8,128)S(1)}, u32[]{:S(2)}, u32[]{:S(2)}) collective-permute-start(f32[512,128]{1,0:T(8,128)S(1)} %get-tuple-element.36), channel_id=1, source_target_pairs={{0,1},{1,0},{2,3},{3,2},{4,5},{5,4},{6,7},{7,6},{8,9},{9,8},{10,11... | collective-permute-start | bytes 786440 | tf_op jit(solution)/shard_map/ppermute | solution.py:236
  14.3 1.2 collective-permute-done
  15.5 20.8 %all_to_all.35 = f32[512,1,128]{2,1,0:T(1,128)S(1)} all-to-all(f32[512,1,128]{2,1,0:T(1,128)S(1)} %bitcast.50), channel_id=1, replica_groups={{0,2,4,6,8,10,12,14,16,18,20,22,24,26,28,30,32,34,36,38,40,42,44,46,48,..., dimensions={0} | all-to-all | bytes 524288 | tf_op jit(solution)/shard_map/all_to_all | solution.py:241
  36.3 15.0 %all_to_all.36 = f32[512,1,128]{2,1,0:T(1,128)S(1)} all-to-all(f32[512,1,128]{2,1,0:T(1,128)S(1)} %bitcast.41), channel_id=1, replica_groups={{0,2,4,6,8,10,12,14,16,18,20,22,24,26,28,30,32,34,36,38,40,42,44,46,48,..., dimensions={0} | all-to-all | bytes 524288 | tf_op jit(solution)/shard_map/all_to_all | solution.py:241
  51.3 3.3 %collective-permute-start.1 = (f32[512,128]{1,0:T(8,128)S(1)}, f32[512,128]{1,0:T(8,128)S(1)}, u32[]{:S(2)}, u32[]{:S(2)}) collective-permute-start(f32[512,128]{1,0:T(8,128)S(1)} %bitcast.38), channel_id=1, source_target_pairs={{0,1},{1,0},{2,3},{3,2},{4,5},{5,4},{6,7},{7,6},{8,9},{9,8},{10,11... | collective-permute-start | bytes 786440 | tf_op jit(solution)/shard_map/ppermute | solution.py:236
  54.6 1.2 collective-permute-done.1.refs_1_
  55.8 2.9 %forward.3 = (f32[1024,128]{1,0:T(8,128)S(1)}, f32[72,512]{1,0:T(8,128)S(1)}, f32[64,512]{1,0:T(8,128)S(1)}) custom-call(f32[512,128]{1,0:T(8,128)S(1)} %bitcast.39, f32[512,128]{1,0:T(8,128)S(1)} %collective-permute-done.1.refs_1_, bf16[1024,2048]{1,0:T(8,128)(2,1)S(1)} %get-tuple-element.37.refs_2_.refs_4_.refs_5_.refs_6_, ...), custom_call_target="tpu_custom_call" | custom-call | flops 1610612736 | bytes 1048576 | tf_op jit(solution)/shard_map/forward/pallas_call | solution.py:29
  58.7 1.3 collective-permute-start.2
  60.0 1.8 collective-permute-start.4
  61.8 2.1 %collective-permute-done.2 = f32[72,512]{1,0:T(8,128)S(1)} collective-permute-done((f32[72,512]{1,0:T(8,128)S(1)}, f32[72,512]{1,0:T(8,128)S(1)}, u32[]{:S(2)}, u32[]{:S(2)}) %collective-permute-start.2) | collective-permute-done | bytes 147488 | tf_op jit(solution)/shard_map/ppermute | solution.py:245
  63.9 2.5 %collective-permute-start.3 = (f32[72,512]{1,0:T(8,128)S(1)}, f32[72,512]{1,0:T(8,128)S(1)}, u32[]{:S(2)}, u32[]{:S(2)}) collective-permute-start(f32[72,512]{1,0:T(8,128)S(1)} %add.33.refs_0_), channel_id=1, source_target_pairs={{0,192},{64,128},{128,64},{192,0},{1,193},{65,129},{129,65},{193,1... | collective-permute-start | bytes 442376 | tf_op jit(solution)/shard_map/ppermute | solution.py:245
  66.5 0.1 collective-permute-start.5
  66.6 4.1 %collective-permute-done.5.refs_3_ = f32[64,512]{1,0:T(8,128)S(1)} collective-permute-done((f32[64,512]{1,0:T(8,128)S(1)}, f32[64,512]{1,0:T(8,128)S(1)}, u32[]{:S(2)}, u32[]{:S(2)}) %collective-permute-start.5) | collective-permute-done | bytes 131104 | tf_op jit(solution)/shard_map/ppermute | solution.py:245
  70.7 1.9 back.2
  72.5 2.6 %collective-permute-start.6 = (f32[544,128]{1,0:T(8,128)S(1)}, f32[544,128]{1,0:T(8,128)S(1)}, u32[]{:S(2)}, u32[]{:S(2)}) collective-permute-start(f32[544,128]{1,0:T(8,128)S(1)} %get-tuple-element.42), channel_id=1, source_target_pairs={{0,1},{1,0},{2,3},{3,2},{4,5},{5,4},{6,7},{7,6},{8,9},{9,8},{10,11... | collective-permute-start | bytes 835592 | tf_op jit(solution)/shard_map/ppermute | solution.py:236
  75.1 1.2 collective-permute-done.6
  76.4 15.4 %all_to_all.37 = f32[544,1,128]{2,1,0:T(1,128)S(1)} all-to-all(f32[544,1,128]{2,1,0:T(1,128)S(1)} %bitcast.48), channel_id=1, replica_groups={{0,2,4,6,8,10,12,14,16,18,20,22,24,26,28,30,32,34,36,38,40,42,44,46,48,..., dimensions={0} | all-to-all | bytes 557056 | tf_op jit(solution)/shard_map/all_to_all | solution.py:241
  91.8 14.7 %all_to_all.38 = f32[512,1,128]{2,1,0:T(1,128)S(1)} all-to-all(f32[512,1,128]{2,1,0:T(1,128)S(1)} %bitcast.43), channel_id=1, replica_groups={{0,2,4,6,8,10,12,14,16,18,20,22,24,26,28,30,32,34,36,38,40,42,44,46,48,..., dimensions={0} | all-to-all | bytes 524288 | tf_op jit(solution)/shard_map/all_to_all | solution.py:241
  106.5 3.5 %collective-permute-start.7 = (f32[512,128]{1,0:T(8,128)S(1)}, f32[512,128]{1,0:T(8,128)S(1)}, u32[]{:S(2)}, u32[]{:S(2)}) collective-permute-start(f32[512,128]{1,0:T(8,128)S(1)} %bitcast.36), channel_id=1, source_target_pairs={{0,1},{1,0},{2,3},{3,2},{4,5},{5,4},{6,7},{7,6},{8,9},{9,8},{10,11... | collective-permute-start | bytes 786440 | tf_op jit(solution)/shard_map/ppermute | solution.py:236
  110.0 1.2 collective-permute-done.7.refs_1_
  111.1 3.1 %forward.4 = (f32[1024,128]{1,0:T(8,128)S(1)}, f32[1024,128]{1,0:T(8,128)S(1)}, f32[72,512]{1,0:T(8,128)S(1)}, f32[64,512]{1,0:T(8,128)S(1)}) custom-call(f32[512,128]{1,0:T(8,128)S(1)} %bitcast.37, f32[512,128]{1,0:T(8,128)S(1)} %collective-permute-done.7.refs_1_, f32[8,128]{1,0:T(8,128)S(1)} %get-tuple-element.45.refs_2_.size0, ...), custom_call_target="tpu_custom_call" | custom-call | flops 1610612736 | bytes 1048576 | tf_op jit(solution)/shard_map/forward/pallas_call | solution.py:29
  114.2 0.1 collective-permute-start.8
  114.3 1.1 collective-permute-start.10
  115.4 3.9 %collective-permute-done.8 = f32[72,512]{1,0:T(8,128)S(1)} collective-permute-done((f32[72,512]{1,0:T(8,128)S(1)}, f32[72,512]{1,0:T(8,128)S(1)}, u32[]{:S(2)}, u32[]{:S(2)}) %collective-permute-start.8) | collective-permute-done | bytes 147488 | tf_op jit(solution)/shard_map/ppermute | solution.py:245
  119.4 1.1 collective-permute-start.9
  120.5 0.1 collective-permute-start.11
  120.6 3.8 %collective-permute-done.11.refs_3_ = f32[64,512]{1,0:T(8,128)S(1)} collective-permute-done((f32[64,512]{1,0:T(8,128)S(1)}, f32[64,512]{1,0:T(8,128)S(1)}, u32[]{:S(2)}, u32[]{:S(2)}) %collective-permute-start.11) | collective-permute-done | bytes 131104 | tf_op jit(solution)/shard_map/ppermute | solution.py:245
  124.4 0.2 collective-permute-done.9.refs_1_
  124.7 1.9 back.3
  126.6 2.5 %collective-permute-start.12 = (f32[544,128]{1,0:T(8,128)S(1)}, f32[544,128]{1,0:T(8,128)S(1)}, u32[]{:S(2)}, u32[]{:S(2)}) collective-permute-start(f32[544,128]{1,0:T(8,128)S(1)} %get-tuple-element.51), channel_id=1, source_target_pairs={{0,1},{1,0},{2,3},{3,2},{4,5},{5,4},{6,7},{7,6},{8,9},{9,8},{10,11... | collective-permute-start | bytes 835592 | tf_op jit(solution)/shard_map/ppermute | solution.py:236
  129.1 1.2 collective-permute-done.12
  130.3 15.4 %all_to_all.39 = f32[544,1,128]{2,1,0:T(1,128)S(1)} all-to-all(f32[544,1,128]{2,1,0:T(1,128)S(1)} %bitcast.49), channel_id=1, replica_groups={{0,2,4,6,8,10,12,14,16,18,20,22,24,26,28,30,32,34,36,38,40,42,44,46,48,..., dimensions={0} | all-to-all | bytes 557056 | tf_op jit(solution)/shard_map/all_to_all | solution.py:241
  145.7 14.7 %all_to_all.40 = f32[512,1,128]{2,1,0:T(1,128)S(1)} all-to-all(f32[512,1,128]{2,1,0:T(1,128)S(1)} %bitcast.44), channel_id=1, replica_groups={{0,2,4,6,8,10,12,14,16,18,20,22,24,26,28,30,32,34,36,38,40,42,44,46,48,..., dimensions={0} | all-to-all | bytes 524288 | tf_op jit(solution)/shard_map/all_to_all | solution.py:241
  160.4 3.5 %collective-permute-start.13 = (f32[512,128]{1,0:T(8,128)S(1)}, f32[512,128]{1,0:T(8,128)S(1)}, u32[]{:S(2)}, u32[]{:S(2)}) collective-permute-start(f32[512,128]{1,0:T(8,128)S(1)} %bitcast.34), channel_id=1, source_target_pairs={{0,1},{1,0},{2,3},{3,2},{4,5},{5,4},{6,7},{7,6},{8,9},{9,8},{10,11... | collective-permute-start | bytes 786440 | tf_op jit(solution)/shard_map/ppermute | solution.py:236
  163.9 1.2 collective-permute-done.13.refs_1_
  165.1 3.1 %forward.5 = (f32[1024,128]{1,0:T(8,128)S(1)}, f32[1024,128]{1,0:T(8,128)S(1)}, f32[72,512]{1,0:T(8,128)S(1)}, f32[64,512]{1,0:T(8,128)S(1)}) custom-call(f32[512,128]{1,0:T(8,128)S(1)} %bitcast.35, f32[512,128]{1,0:T(8,128)S(1)} %collective-permute-done.13.refs_1_, f32[8,128]{1,0:T(8,128)S(1)} %get-tuple-element.54.refs_2_.size1, ...), custom_call_target="tpu_custom_call" | custom-call | flops 1610612736 | bytes 1048576 | tf_op jit(solution)/shard_map/forward/pallas_call | solution.py:29
  168.2 1.7 collective-permute-start.16
  170.0 3.3 %collective-permute-done.14 = f32[72,512]{1,0:T(8,128)S(1)} collective-permute-done((f32[72,512]{1,0:T(8,128)S(1)}, f32[72,512]{1,0:T(8,128)S(1)}, u32[]{:S(2)}, u32[]{:S(2)}) %collective-permute-start.14) | collective-permute-done | bytes 147488 | tf_op jit(solution)/shard_map/ppermute | solution.py:245
  173.3 2.0 collective-permute-start.15
  175.4 4.1 %collective-permute-done.17.rb = f32[64,512]{1,0:T(8,128)S(1)} collective-permute-done((f32[64,512]{1,0:T(8,128)S(1)}, f32[64,512]{1,0:T(8,128)S(1)}, u32[]{:S(2)}, u32[]{:S(2)}) %collective-permute-start.17) | collective-permute-done | bytes 131104 | tf_op jit(solution)/shard_map/ppermute | solution.py:245
  179.5 0.3 last_image.1
  179.8 11.9 %all_to_all.41 = f32[32,1,128]{2,1,0:T(1,128)S(1)} all-to-all(f32[32,1,128]{2,1,0:T(1,128)S(1)} %bitcast.47), channel_id=1, replica_groups={{0,2,4,6,8,10,12,14,16,18,20,22,24,26,28,30,32,34,36,38,40,42,44,46,48,..., dimensions={0} | all-to-all | bytes 32768 | tf_op jit(solution)/shard_map/all_to_all | solution.py:241
  191.7 3.8 %collective-permute-start.18 = (f32[32,128]{1,0:T(8,128)S(1)}, f32[32,128]{1,0:T(8,128)S(1)}, u32[]{:S(2)}, u32[]{:S(2)}) collective-permute-start(f32[32,128]{1,0:T(8,128)S(1)} %bitcast.45), channel_id=1, source_target_pairs={{0,1},{1,0},{2,3},{3,2},{4,5},{5,4},{6,7},{7,6},{8,9},{9,8},{10,11... | collective-permute-start | bytes 49160 | tf_op jit(solution)/shard_map/ppermute | solution.py:236
  195.5 0.8 collective-permute-done.18.other
  196.3 1.4 finish.1
  (21 shorter events, 0.5 us)
Async XLA Ops:
  0.6 3.4 %copy-start = (f32[1024,2048]{1,0:T(8,128)S(1)}, f32[1024,2048]{1,0:T(8,128)}, u32[]{:S(2)}) copy-start(f32[1024,2048]{1,0:T(8,128)} %states.1) | copy-start | bytes 25165828
  4.0 0.9 copy-start.1
  10.9 4.5 %collective-permute-start = (f32[512,128]{1,0:T(8,128)S(1)}, f32[512,128]{1,0:T(8,128)S(1)}, u32[]{:S(2)}, u32[]{:S(2)}) collective-permute-start(f32[512,128]{1,0:T(8,128)S(1)} %get-tuple-element.36), channel_id=1, source_target_pairs={{0,1},{1,0},{2,3},{3,2},{4,5},{5,4},{6,7},{7,6},{8,9},{9,8},{10,11... | collective-permute-start | bytes 786440 | tf_op jit(solution)/shard_map/ppermute | solution.py:236
  51.3 4.5 %collective-permute-start.1 = (f32[512,128]{1,0:T(8,128)S(1)}, f32[512,128]{1,0:T(8,128)S(1)}, u32[]{:S(2)}, u32[]{:S(2)}) collective-permute-start(f32[512,128]{1,0:T(8,128)S(1)} %bitcast.38), channel_id=1, source_target_pairs={{0,1},{1,0},{2,3},{3,2},{4,5},{5,4},{6,7},{7,6},{8,9},{9,8},{10,11... | collective-permute-start | bytes 786440 | tf_op jit(solution)/shard_map/ppermute | solution.py:236
  58.7 5.2 %collective-permute-start.2 = (f32[72,512]{1,0:T(8,128)S(1)}, f32[72,512]{1,0:T(8,128)S(1)}, u32[]{:S(2)}, u32[]{:S(2)}) collective-permute-start(f32[72,512]{1,0:T(8,128)S(1)} %get-tuple-element.39), channel_id=1, source_target_pairs={{0,64},{64,0},{128,192},{192,128},{1,65},{65,1},{129,193},{193,129... | collective-permute-start | bytes 442376 | tf_op jit(solution)/shard_map/ppermute | solution.py:245
  60.0 6.4 %collective-permute-start.4 = (f32[64,512]{1,0:T(8,128)S(1)}, f32[64,512]{1,0:T(8,128)S(1)}, u32[]{:S(2)}, u32[]{:S(2)}) collective-permute-start(f32[64,512]{1,0:T(8,128)S(1)} %get-tuple-element.40), channel_id=1, source_target_pairs={{0,192},{64,128},{128,64},{192,0},{1,193},{65,129},{129,65},{193,1... | collective-permute-start | bytes 393224 | tf_op jit(solution)/shard_map/ppermute | solution.py:245
  63.9 6.8 %collective-permute-start.3 = (f32[72,512]{1,0:T(8,128)S(1)}, f32[72,512]{1,0:T(8,128)S(1)}, u32[]{:S(2)}, u32[]{:S(2)}) collective-permute-start(f32[72,512]{1,0:T(8,128)S(1)} %add.33.refs_0_), channel_id=1, source_target_pairs={{0,192},{64,128},{128,64},{192,0},{1,193},{65,129},{129,65},{193,1... | collective-permute-start | bytes 442376 | tf_op jit(solution)/shard_map/ppermute | solution.py:245
  66.5 4.2 %collective-permute-start.5 = (f32[64,512]{1,0:T(8,128)S(1)}, f32[64,512]{1,0:T(8,128)S(1)}, u32[]{:S(2)}, u32[]{:S(2)}) collective-permute-start(f32[64,512]{1,0:T(8,128)S(1)} %add.34.refs_2_), channel_id=1, source_target_pairs={{0,64},{64,0},{128,192},{192,128},{1,65},{65,1},{129,193},{193,129... | collective-permute-start | bytes 393224 | tf_op jit(solution)/shard_map/ppermute | solution.py:245
  72.5 3.8 %collective-permute-start.6 = (f32[544,128]{1,0:T(8,128)S(1)}, f32[544,128]{1,0:T(8,128)S(1)}, u32[]{:S(2)}, u32[]{:S(2)}) collective-permute-start(f32[544,128]{1,0:T(8,128)S(1)} %get-tuple-element.42), channel_id=1, source_target_pairs={{0,1},{1,0},{2,3},{3,2},{4,5},{5,4},{6,7},{7,6},{8,9},{9,8},{10,11... | collective-permute-start | bytes 835592 | tf_op jit(solution)/shard_map/ppermute | solution.py:236
  106.5 4.6 %collective-permute-start.7 = (f32[512,128]{1,0:T(8,128)S(1)}, f32[512,128]{1,0:T(8,128)S(1)}, u32[]{:S(2)}, u32[]{:S(2)}) collective-permute-start(f32[512,128]{1,0:T(8,128)S(1)} %bitcast.36), channel_id=1, source_target_pairs={{0,1},{1,0},{2,3},{3,2},{4,5},{5,4},{6,7},{7,6},{8,9},{9,8},{10,11... | collective-permute-start | bytes 786440 | tf_op jit(solution)/shard_map/ppermute | solution.py:236
  114.2 5.1 %collective-permute-start.8 = (f32[72,512]{1,0:T(8,128)S(1)}, f32[72,512]{1,0:T(8,128)S(1)}, u32[]{:S(2)}, u32[]{:S(2)}) collective-permute-start(f32[72,512]{1,0:T(8,128)S(1)} %get-tuple-element.47), channel_id=1, source_target_pairs={{0,64},{64,0},{128,192},{192,128},{1,65},{65,1},{129,193},{193,129... | collective-permute-start | bytes 442376 | tf_op jit(solution)/shard_map/ppermute | solution.py:245
  114.3 6.2 %collective-permute-start.10 = (f32[64,512]{1,0:T(8,128)S(1)}, f32[64,512]{1,0:T(8,128)S(1)}, u32[]{:S(2)}, u32[]{:S(2)}) collective-permute-start(f32[64,512]{1,0:T(8,128)S(1)} %get-tuple-element.48), channel_id=1, source_target_pairs={{0,192},{64,128},{128,64},{192,0},{1,193},{65,129},{129,65},{193,1... | collective-permute-start | bytes 393224 | tf_op jit(solution)/shard_map/ppermute | solution.py:245
  119.4 5.3 %collective-permute-start.9 = (f32[72,512]{1,0:T(8,128)S(1)}, f32[72,512]{1,0:T(8,128)S(1)}, u32[]{:S(2)}, u32[]{:S(2)}) collective-permute-start(f32[72,512]{1,0:T(8,128)S(1)} %add.36.refs_0_), channel_id=1, source_target_pairs={{0,192},{64,128},{128,64},{192,0},{1,193},{65,129},{129,65},{193,1... | collective-permute-start | bytes 442376 | tf_op jit(solution)/shard_map/ppermute | solution.py:245
  120.5 3.9 %collective-permute-start.11 = (f32[64,512]{1,0:T(8,128)S(1)}, f32[64,512]{1,0:T(8,128)S(1)}, u32[]{:S(2)}, u32[]{:S(2)}) collective-permute-start(f32[64,512]{1,0:T(8,128)S(1)} %add.37.refs_2_), channel_id=1, source_target_pairs={{0,64},{64,0},{128,192},{192,128},{1,65},{65,1},{129,193},{193,129... | collective-permute-start | bytes 393224 | tf_op jit(solution)/shard_map/ppermute | solution.py:245
  126.6 3.7 %collective-permute-start.12 = (f32[544,128]{1,0:T(8,128)S(1)}, f32[544,128]{1,0:T(8,128)S(1)}, u32[]{:S(2)}, u32[]{:S(2)}) collective-permute-start(f32[544,128]{1,0:T(8,128)S(1)} %get-tuple-element.51), channel_id=1, source_target_pairs={{0,1},{1,0},{2,3},{3,2},{4,5},{5,4},{6,7},{7,6},{8,9},{9,8},{10,11... | collective-permute-start | bytes 835592 | tf_op jit(solution)/shard_map/ppermute | solution.py:236
  160.4 4.6 %collective-permute-start.13 = (f32[512,128]{1,0:T(8,128)S(1)}, f32[512,128]{1,0:T(8,128)S(1)}, u32[]{:S(2)}, u32[]{:S(2)}) collective-permute-start(f32[512,128]{1,0:T(8,128)S(1)} %bitcast.34), channel_id=1, source_target_pairs={{0,1},{1,0},{2,3},{3,2},{4,5},{5,4},{6,7},{7,6},{8,9},{9,8},{10,11... | collective-permute-start | bytes 786440 | tf_op jit(solution)/shard_map/ppermute | solution.py:236
  168.2 5.1 %collective-permute-start.14 = (f32[72,512]{1,0:T(8,128)S(1)}, f32[72,512]{1,0:T(8,128)S(1)}, u32[]{:S(2)}, u32[]{:S(2)}) collective-permute-start(f32[72,512]{1,0:T(8,128)S(1)} %get-tuple-element.57), channel_id=1, source_target_pairs={{0,64},{64,0},{128,192},{192,128},{1,65},{65,1},{129,193},{193,129... | collective-permute-start | bytes 442376 | tf_op jit(solution)/shard_map/ppermute | solution.py:245
  168.2 7.0 %collective-permute-start.16 = (f32[64,512]{1,0:T(8,128)S(1)}, f32[64,512]{1,0:T(8,128)S(1)}, u32[]{:S(2)}, u32[]{:S(2)}) collective-permute-start(f32[64,512]{1,0:T(8,128)S(1)} %get-tuple-element.58), channel_id=1, source_target_pairs={{0,192},{64,128},{128,64},{192,0},{1,193},{65,129},{129,65},{193,1... | collective-permute-start | bytes 393224 | tf_op jit(solution)/shard_map/ppermute | solution.py:245
  173.3 6.2 %collective-permute-start.15 = (f32[72,512]{1,0:T(8,128)S(1)}, f32[72,512]{1,0:T(8,128)S(1)}, u32[]{:S(2)}, u32[]{:S(2)}) collective-permute-start(f32[72,512]{1,0:T(8,128)S(1)} %add.39.a), channel_id=1, source_target_pairs={{0,192},{64,128},{128,64},{192,0},{1,193},{65,129},{129,65},{193,1... | collective-permute-start | bytes 442376 | tf_op jit(solution)/shard_map/ppermute | solution.py:245
  175.3 4.2 %collective-permute-start.17 = (f32[64,512]{1,0:T(8,128)S(1)}, f32[64,512]{1,0:T(8,128)S(1)}, u32[]{:S(2)}, u32[]{:S(2)}) collective-permute-start(f32[64,512]{1,0:T(8,128)S(1)} %add.40.b), channel_id=1, source_target_pairs={{0,64},{64,0},{128,192},{192,128},{1,65},{65,1},{129,193},{193,129... | collective-permute-start | bytes 393224 | tf_op jit(solution)/shard_map/ppermute | solution.py:245
  191.7 4.6 %collective-permute-start.18 = (f32[32,128]{1,0:T(8,128)S(1)}, f32[32,128]{1,0:T(8,128)S(1)}, u32[]{:S(2)}, u32[]{:S(2)}) collective-permute-start(f32[32,128]{1,0:T(8,128)S(1)} %bitcast.45), channel_id=1, source_target_pairs={{0,1},{1,0},{2,3},{3,2},{4,5},{5,4},{6,7},{7,6},{8,9},{9,8},{10,11... | collective-permute-start | bytes 49160 | tf_op jit(solution)/shard_map/ppermute | solution.py:236

commit v3 on v2

v3 whole, which is shorter than its diff:
```python
import functools

import jax
import jax.numpy as jnp
from jax import lax
from jax.experimental import pallas as pl
from jax.experimental.pallas import tpu as pltpu
from jax.sharding import PartitionSpec as P

ITERS = 3
ridge = 0.5
CORES, LANES, TILE = 2, 128, 8
WIDE = 256
MIB = 1 << 20
F32, BF16 = jnp.float32, jnp.bfloat16
VMEM = pl.BlockSpec(memory_space=pltpu.VMEM)
HBM = pl.BlockSpec(memory_space=pl.ANY)


def shape(*dims, dtype=F32):
    return jax.ShapeDtypeStruct(dims, dtype)


def here(x):
    return pltpu.with_memory_space_constraint(x, pltpu.VMEM)


def call(kernel, out_shape, *args, scratch=(), limit=24, specs=None, flops=0, **static):
    return pl.pallas_call(
        functools.partial(kernel, **static),
        in_specs=specs or [VMEM] * len(args),
        out_specs=jax.tree.map(lambda _: VMEM, out_shape),
        out_shape=out_shape,
        scratch_shapes=list(scratch),
        compiler_params=pltpu.CompilerParams(vmem_limit_bytes=limit * MIB),
        cost_estimate=pl.CostEstimate(flops=flops, bytes_accessed=MIB, transcendentals=0),
        name=kernel.__name__,
    )(*args)


def split2(x):
    high = x.astype(BF16)
    return jnp.concatenate([high, (x - high.astype(F32)).astype(BF16)], axis=0)


def dot(a, b, ca, cb):
    return lax.dot_general(a, b, (((ca,), (cb,)), ((), ())), preferred_element_type=F32)


def fold(p):
    n = p.shape[0] // 2
    return p[n:] + p[:n]


def rows_product(x, high, low, at):
    x2 = split2(x) if x.dtype == F32 else x
    return fold(dot(x2, low[:, at], 1, 0) + dot(x2, high[:, at], 1, 0))


def row(x):
    return jnp.broadcast_to(x, (1, LANES))


def store_pieces(mine, theirs, value, at, stride):
    half = value.shape[0] // CORES
    for i in range(WIDE // LANES):
        part = value[:, i * LANES : (i + 1) * LANES]
        j = at * (WIDE // LANES) + i
        mine[pl.ds(j, half, stride=stride), :] = part[:half]
        theirs[pl.ds(j, half, stride=stride), :] = part[half:]


def own_half_first(x, own):
    half = x.shape[0] // CORES
    top, bottom = x[:half], x[half:]
    return jnp.concatenate(
        [jnp.where(own, top, bottom), jnp.where(own, bottom, top)], axis=0
    )


def first(core, states, targets, high, low, turned, mine, theirs, buf, target_buf, sems):
    steps = buf.shape[0]
    fetch = pltpu.make_async_copy(targets, target_buf, sems.at[steps])
    fetch.start()
    copies = [
        pltpu.make_async_copy(
            states.at[:, pl.ds(t * WIDE, WIDE)], buf.at[t], sems.at[t]
        )
        for t in range(steps)
    ]
    for c in copies:
        c.start()
    fetch.wait()
    x = own_half_first(target_buf[...], core[0, 0] == 0)
    turned[...] = x
    x2 = split2(x)
    half = x.shape[0] // CORES
    for t in range(steps):
        copies[t].wait()
        s = buf[t]
        h = s.astype(BF16)
        l = (s - h.astype(F32)).astype(BF16)
        high[:, pl.ds(t * WIDE, WIDE)] = h
        low[:, pl.ds(t * WIDE, WIDE)] = l
        p = fold(dot(x2, l, 1, 0) + dot(x2, h, 1, 0))
        store_pieces(mine, theirs, p, t, mine.shape[0] // half)


def turn_states(high, low, high_turned, low_turned):
    high_turned[...] = high[...].T
    low_turned[...] = low[...].T


def combine(hops):
    p = hops[0][...] + hops[1][...] + (hops[2][...] + hops[3][...])
    n = p.shape[0] - TILE
    return p[:n], p[n:, :LANES]


def step_image(hops, before, scal, image_out, scal_out):
    image, tail = combine(hops)
    gamma = tail[0:1]
    if before is None:
        beta = jnp.zeros_like(gamma)
        square = gamma
    else:
        beta = gamma / scal[0:1, :]
        square = gamma + beta * (2.0 * tail[1:2] + beta * scal[2:3, :])
        image = image + beta[:, :1] * before[...]
    image_out[...] = image
    scal_out[0:1, :] = gamma
    scal_out[1:2, :] = beta
    scal_out[2:3, :] = square
    scal_out[3:, :] = jnp.zeros((TILE - 3, LANES), F32)
    return image, row(jnp.sum(image * image))


def back(*refs, later):
    hops = refs[:4]
    before, scal = refs[4:6] if later else (None, None)
    high, low, image_out, scal_out, mine, theirs = refs[-6:]
    image, image_sq = step_image(hops, before, scal, image_out, scal_out)
    half = image.shape[0] // CORES
    stride = mine.shape[0] // half
    x2 = split2(image)
    for t in range(high.shape[1] // WIDE):
        p = rows_product(x2, high, low, pl.ds(t * WIDE, WIDE))
        store_pieces(mine, theirs, p, t, stride)
    extra = jnp.broadcast_to(image_sq, (half, LANES))
    mine[pl.ds(stride - 1, half, stride=stride), :] = extra
    theirs[pl.ds(stride - 1, half, stride=stride), :] = extra


def last_image(h0, h1, h2, h3, before, scal, image_out, scal_out, squares):
    _, image_sq = step_image((h0, h1, h2, h3), before, scal, image_out, scal_out)
    squares[...] = jnp.broadcast_to(image_sq, squares.shape)


def step_size(image_sq, scal):
    return scal[0:1, :] / (image_sq + ridge * scal[2:3, :])


def reduce_pieces(*refs, rows, scalars):
    if scalars:
        got, scal, out, size = refs
    else:
        got, out = refs
    count = out.shape[0] // rows
    stride = got.shape[0] // count
    terms = [got[i * stride : (i + 1) * stride, :] for i in range(count)]
    while len(terms) > 1:
        terms = [terms[i] + terms[i + 1] for i in range(0, len(terms), 2)]
    total = terms[0]
    for i in range(count):
        out[i * rows : (i + 1) * rows, :] = total[:rows]
    if scalars:
        size[...] = jnp.broadcast_to(step_size(total[rows : rows + 1], scal), size.shape)


def forward(*refs, step):
    if step == 0:
        top, bottom, high, low, gradient, out = refs
        g = jnp.concatenate([top[...], bottom[...]], axis=0)
        cross = None
    else:
        if step == 1:
            top, bottom, size, scal, g_old, high, low, gradient, direction, out = refs
            d = g_old[...]
        else:
            top, bottom, size, scal, g_old, d_old, high, low, gradient, direction, out = refs
            d = g_old[...] + scal[1:2, :] * d_old[...]
        q = jnp.concatenate([top[...], bottom[...]], axis=0)
        direction[...] = d
        g = g_old[...] - size[0:1, :] * (q + ridge * d)
        cross = jnp.sum(g * d)
    gradient[...] = g
    n = out.shape[0] - TILE
    stride = g.shape[0] // n
    x2 = split2(
        jnp.concatenate([gradient[pl.ds(j, n, stride=stride), :] for j in range(stride)], axis=1)
    )
    for t in range(high.shape[1] // WIDE):
        at = pl.ds(t * WIDE, WIDE)
        out[0:n, at] = rows_product(x2, high, low, at)
    out[n : n + 1, :] = jnp.broadcast_to(jnp.sum(g * g), (1, out.shape[1]))
    rest = jnp.zeros((TILE - 1, out.shape[1]), F32)
    out[n + 1 :, :] = rest if cross is None else rest + cross


def prepare(core, scal, size0, size1, d0, d1, g2, i0, i1, i2, targets, readout, direction, residual, image, sums):
    own = core[0, 0] == 0
    n = targets.shape[0]
    stride = d0.shape[0] // n
    s0, s1 = size0[0:1, :], size1[0:1, :]
    for value, out in (
        (s0 * d0[...] + s1 * d1[...], readout),
        (g2[...] + scal[1:2, :] * d1[...], direction),
    ):
        sums[...] = value
        for j in range(stride):
            out[:, pl.ds(j * LANES, LANES)] = own_half_first(
                sums[pl.ds(j, n, stride=stride), :], own
            )
    r = targets[...] - s0[:, :1] * i0[...] - s1[:, :1] * i1[...]
    residual[...] = own_half_first(r, own)
    image[...] = own_half_first(i2[...], own)


def finish(got, other, scal, readout_part, direction, residual_part, image, readout, residual):
    image_sq = jnp.sum(got[...] + other[...], axis=0, keepdims=True)
    size = step_size(image_sq, scal)[:, :1]
    readout[...] = readout_part[...] + size * direction[...]
    residual[...] = residual_part[...] - size * image[...]


def shards(states, targets):
    samples, units = states.shape
    outputs = targets.shape[1]
    samp_count = lax.axis_size("samp")
    unit_count = lax.axis_size("unit")
    chips = samp_count // CORES
    half = outputs // CORES
    rows = units // LANES
    core = jnp.full((1, 1), lax.axis_index("samp") % CORES, jnp.int32)

    swap_cores = [(i, i ^ 1) for i in range(samp_count)]
    groups = [[chip * CORES + c for chip in range(chips)] for c in range(CORES)]

    def swap(x):
        return lax.ppermute(x, "samp", swap_cores)

    def exchange(x):
        n = x.shape[0]
        x = x.reshape(n, 1, LANES)
        x = lax.all_to_all(x, "samp", 0, 0, axis_index_groups=groups, tiled=True)
        return x.reshape(n, LANES)

    def unit_terms(x):
        hops = [
            lax.ppermute(x, "unit", [(i, (i + d) % unit_count) for i in range(unit_count)])
            for d in range(1, unit_count)
        ]
        return [x] + hops

    vector = shape(TILE, LANES)
    image_shape = shape(outputs, samples)
    whole = shape(outputs * rows, LANES)
    partial = shape(outputs + TILE, samples)
    flops = 2 * 4 * samples * units * outputs

    smem = pl.BlockSpec(memory_space=pltpu.SMEM)
    high, low, turned, mine, theirs = call(
        first,
        [shape(samples, units, dtype=BF16)] * 2 + [image_shape] + [shape(half * rows, LANES)] * 2,
        core,
        pltpu.with_memory_space_constraint(states, pltpu.HBM),
        pltpu.with_memory_space_constraint(targets.T, pltpu.HBM),
        specs=[smem, HBM, HBM],
        scratch=[
            pltpu.VMEM((units // WIDE, samples, WIDE), F32),
            pltpu.VMEM((outputs, samples), F32),
            pltpu.SemaphoreType.DMA((units // WIDE + 1,)),
        ],
        limit=32,
        flops=flops,
    )
    high, low = here(high), here(low)
    high_turned, low_turned = call(
        turn_states, [shape(units, samples, dtype=BF16)] * 2, high, low, flops=flops
    )
    high_turned, low_turned = here(high_turned), here(low_turned)
    got = exchange(mine + swap(theirs))
    spread = call(reduce_pieces, shape(half * rows, LANES), got, rows=rows, scalars=False)

    gradients, directions, images, sizes = [], [], [], []
    scal = size = None
    for step in range(ITERS):
        top = exchange(spread)
        bottom = swap(top)
        if step == 0:
            g, out = call(
                forward,
                [whole, partial],
                top,
                bottom,
                high_turned,
                low_turned,
                step=0,
                flops=flops,
            )
        else:
            olds = [gradients[-1]] + ([directions[-1]] if step > 1 else [])
            g, d, out = call(
                forward,
                [whole, whole, partial],
                top,
                bottom,
                size,
                scal,
                *olds,
                high_turned,
                low_turned,
                step=step,
                flops=flops,
            )
            directions.append(d)
        gradients.append(g)
        hops = unit_terms(out)
        olds = [images[-1], scal] if step else []
        if step + 1 < ITERS:
            piece = shape(half * (rows + 1), LANES)
            image, scal, mine, theirs = call(
                back,
                [image_shape, vector, piece, piece],
                *hops,
                *olds,
                high,
                low,
                later=step > 0,
                flops=flops,
            )
            images.append(image)
            got = exchange(mine + swap(theirs))
            spread, size = call(
                reduce_pieces,
                [shape(half * rows, LANES), vector],
                got,
                scal,
                rows=rows,
                scalars=True,
            )
            sizes.append(size)
        else:
            image, scal, squares = call(
                last_image, [image_shape, vector, shape(half, LANES)], *hops, *olds
            )
            images.append(image)
            got = exchange(squares)
            other = swap(got)
    parts = call(
        prepare,
        [shape(outputs, units)] * 2 + [image_shape] * 2,
        core,
        scal,
        *sizes,
        *directions,
        gradients[-1],
        *images,
        turned,
        specs=[smem] + [VMEM] * 10,
        scratch=[pltpu.VMEM((outputs * rows, LANES), F32)],
        flops=flops,
    )
    readout, residual = call(
        finish, [shape(outputs, units), image_shape], got, other, scal, *parts
    )
    return readout.T, residual.T


def solution(mesh):
    return jax.shard_map(
        shards,
        mesh=mesh,
        in_specs=(P("samp", "unit"), P("samp", None)),
        out_specs=(P("unit", None), P("samp", None)),
        check_vma=False,
    )
```

time: 198 us -> 203 us (1.025)
  waiting for transfers between devices: 29.4 us -> 53.1 us
  starting transfers between devices: 34.4 us -> 23.6 us
  local copies, waits for them, and re-layouts: 4.32 us -> 0 us
  Pallas kernels: 20.5 us -> 17.1 us
    ppermute x12 -> x9, waiting for transfers between devices: 21.5 us -> 47.1 us  [unit_terms(): lax.ppermute(x, 'unit', [(i, (i + d) % unit_count) for i in range(unit_co...]
    ppermute x7, starting transfers between devices: 22.4 us -> 16.8 us  [swap(): return lax.ppermute(x, 'samp', swap_cores)]
    ppermute x12 -> x9, starting transfers between devices: 12 us -> 6.77 us  [unit_terms(): lax.ppermute(x, 'unit', [(i, (i + d) % unit_count) for i in range(unit_co...]
    unnamed x4 -> x0, local copies, waits for them, and re-layouts: 4.32 us -> none
    pallas_call x11 -> x13, Pallas kernels: 20.5 us -> 17.1 us  [call(): pl.pallas_call(functools.partial(kernel, **static), in_specs=specs or [VM...]
  transfers between devices with their start and end apart: 19 -> 16, of which waited for: 14 -> 14; matrix products, arithmetic and copies ran while one was open for 0% -> 0% of each run, Pallas kernels for 0% -> 2%
where the time goes in v3:
time: 203 us
  blocking collectives  108 us (53%)
  waiting for transfers between devices  53.1 us (26%)
  starting transfers between devices  23.6 us (12%)
  Pallas kernels  17.1 us (8%)
    all_to_all x7, blocking collectives, exchange(): x = lax.all_to_all(x, 'samp', 0, 0, axis_index_groups=groups, tiled=True)  108 us
    ppermute x9, waiting for transfers between devices, unit_terms(): lax.ppermute(x, 'unit', [(i, (i + d) % unit_count) for i in range(unit_co...  47.1 us
    pallas_call x13, Pallas kernels, call(): pl.pallas_call(functools.partial(kernel, **static), in_specs=specs or [VM...  17.1 us
    ppermute x7, starting transfers between devices, swap(): return lax.ppermute(x, 'samp', swap_cores)  16.8 us
    ppermute x9, starting transfers between devices, unit_terms(): lax.ppermute(x, 'unit', [(i, (i + d) % unit_count) for i in range(unit_co...  6.77 us
    ppermute x7, waiting for transfers between devices, swap(): return lax.ppermute(x, 'samp', swap_cores)  5.99 us
  transfers between devices with their start and end apart: 16, of which 14 were waited for; matrix products, arithmetic and copies ran while one was open for 0% of the time, Pallas kernels for 2%

profile of v3, /device:TPU:1, one launch (start us, length us, event | category | flops | bytes accessed | tf_op | source)
XLA Modules:
  0.0 202.6 jit_solution(766380101522487723)
XLA Ops:
  0.6 5.3 %first.1 = (bf16[1024,2048]{1,0:T(8,128)(2,1)S(1)}, bf16[1024,2048]{1,0:T(8,128)(2,1)S(1)}, f32[64,1024]{1,0:T(8,128)S(1)}, f32[512,128]{1,0:T(8,128)S(1)}, f32[512,128]{1,0:T(8,128)S(1)}) custom-call(s32[1,1]{1,0:T(1,128)} %bitcast.core, f32[1024,2048]{1,0:T(8,128)} %states.1, f32[64,1024]{1,0:T(8,128)} %bitcast.50), custom_call_target="tpu_custom_call" | custom-call | flops 1073741824 | bytes 1048576 | tf_op jit(solution)/shard_map/first/pallas_call | solution.py:29
  5.9 3.3 %collective-permute-start = (f32[512,128]{1,0:T(8,128)S(1)}, f32[512,128]{1,0:T(8,128)S(1)}, u32[]{:S(2)}, u32[]{:S(2)}) collective-permute-start(f32[512,128]{1,0:T(8,128)S(1)} %get-tuple-element.39), channel_id=1, source_target_pairs={{0,1},{1,0},{2,3},{3,2},{4,5},{5,4},{6,7},{7,6},{8,9},{9,8},{10,11... | collective-permute-start | bytes 786440 | tf_op jit(solution)/shard_map/ppermute | solution.py:250
  9.2 1.2 collective-permute-done
  10.4 20.8 %all_to_all.35 = f32[512,1,128]{2,1,0:T(1,128)S(1)} all-to-all(f32[512,1,128]{2,1,0:T(1,128)S(1)} %bitcast.49), channel_id=1, replica_groups={{0,2,4,6,8,10,12,14,16,18,20,22,24,26,28,30,32,34,36,38,40,42,44,46,48,..., dimensions={0} | all-to-all | bytes 524288 | tf_op jit(solution)/shard_map/all_to_all | solution.py:255
  31.3 15.0 %all_to_all.36 = f32[512,1,128]{2,1,0:T(1,128)S(1)} all-to-all(f32[512,1,128]{2,1,0:T(1,128)S(1)} %bitcast.41), channel_id=1, replica_groups={{0,2,4,6,8,10,12,14,16,18,20,22,24,26,28,30,32,34,36,38,40,42,44,46,48,..., dimensions={0} | all-to-all | bytes 524288 | tf_op jit(solution)/shard_map/all_to_all | solution.py:255
  46.3 3.3 %collective-permute-start.1 = (f32[512,128]{1,0:T(8,128)S(1)}, f32[512,128]{1,0:T(8,128)S(1)}, u32[]{:S(2)}, u32[]{:S(2)}) collective-permute-start(f32[512,128]{1,0:T(8,128)S(1)} %bitcast.36), channel_id=1, source_target_pairs={{0,1},{1,0},{2,3},{3,2},{4,5},{5,4},{6,7},{7,6},{8,9},{9,8},{10,11... | collective-permute-start | bytes 786440 | tf_op jit(solution)/shard_map/ppermute | solution.py:250
  49.6 2.4 %turn_states.1 = (bf16[2048,1024]{1,0:T(8,128)(2,1)S(1)}, bf16[2048,1024]{1,0:T(8,128)(2,1)S(1)}) custom-call(bf16[1024,2048]{1,0:T(8,128)(2,1)S(1)} %get-tuple-element.40.high.refs_4_.refs_6_, bf16[1024,2048]{1,0:T(8,128)(2,1)S(1)} %get-tuple-element.41.low.refs_5_.refs_7_), custom_call_target="tpu_custom_call" | custom-call | flops 1073741824 | bytes 1048576 | tf_op jit(solution)/shard_map/turn_states/pallas_call | solution.py:29
  52.1 0.0 collective-permute-done.1.refs_1_
  52.1 1.4 forward.3
  53.5 2.6 %collective-permute-start.4 = (f32[72,1024]{1,0:T(8,128)S(1)}, f32[72,1024]{1,0:T(8,128)S(1)}, u32[]{:S(2)}, u32[]{:S(2)}) collective-permute-start(f32[72,1024]{1,0:T(8,128)S(1)} %get-tuple-element.44.refs_0_), channel_id=1, source_target_pairs={{0,192},{64,0},{128,64},{192,128},{1,193},{65,1},{129,65},{193,129... | collective-permute-start | bytes 884744 | tf_op jit(solution)/shard_map/ppermute | solution.py:260
  56.0 0.5 collective-permute-start.3
  56.5 0.6 collective-permute-start.2
  57.2 11.5 %collective-permute-done.4.refs_3_ = f32[72,1024]{1,0:T(8,128)S(1)} collective-permute-done((f32[72,1024]{1,0:T(8,128)S(1)}, f32[72,1024]{1,0:T(8,128)S(1)}, u32[]{:S(2)}, u32[]{:S(2)}) %collective-permute-start.4) | collective-permute-done | bytes 294944 | tf_op jit(solution)/shard_map/ppermute | solution.py:260
  68.7 4.1 %collective-permute-done.2.refs_1_ = f32[72,1024]{1,0:T(8,128)S(1)} collective-permute-done((f32[72,1024]{1,0:T(8,128)S(1)}, f32[72,1024]{1,0:T(8,128)S(1)}, u32[]{:S(2)}, u32[]{:S(2)}) %collective-permute-start.2) | collective-permute-done | bytes 294944 | tf_op jit(solution)/shard_map/ppermute | solution.py:260
  72.8 1.3 back.2
  74.1 0.8 collective-permute-start.5
  74.9 1.2 collective-permute-done.5
  76.1 15.4 %all_to_all.37 = f32[544,1,128]{2,1,0:T(1,128)S(1)} all-to-all(f32[544,1,128]{2,1,0:T(1,128)S(1)} %bitcast.47), channel_id=1, replica_groups={{0,2,4,6,8,10,12,14,16,18,20,22,24,26,28,30,32,34,36,38,40,42,44,46,48,..., dimensions={0} | all-to-all | bytes 557056 | tf_op jit(solution)/shard_map/all_to_all | solution.py:255
  91.5 14.7 %all_to_all.38 = f32[512,1,128]{2,1,0:T(1,128)S(1)} all-to-all(f32[512,1,128]{2,1,0:T(1,128)S(1)} %bitcast.42), channel_id=1, replica_groups={{0,2,4,6,8,10,12,14,16,18,20,22,24,26,28,30,32,34,36,38,40,42,44,46,48,..., dimensions={0} | all-to-all | bytes 524288 | tf_op jit(solution)/shard_map/all_to_all | solution.py:255
  106.2 3.5 %collective-permute-start.6 = (f32[512,128]{1,0:T(8,128)S(1)}, f32[512,128]{1,0:T(8,128)S(1)}, u32[]{:S(2)}, u32[]{:S(2)}) collective-permute-start(f32[512,128]{1,0:T(8,128)S(1)} %bitcast.38), channel_id=1, source_target_pairs={{0,1},{1,0},{2,3},{3,2},{4,5},{5,4},{6,7},{7,6},{8,9},{9,8},{10,11... | collective-permute-start | bytes 786440 | tf_op jit(solution)/shard_map/ppermute | solution.py:250
  109.7 1.2 collective-permute-done.6.refs_1_
  110.9 1.6 forward.4
  112.4 0.4 collective-permute-start.9
  112.8 0.5 collective-permute-start.8
  113.4 0.6 collective-permute-start.7
  114.0 6.7 %collective-permute-done.9.refs_3_ = f32[72,1024]{1,0:T(8,128)S(1)} collective-permute-done((f32[72,1024]{1,0:T(8,128)S(1)}, f32[72,1024]{1,0:T(8,128)S(1)}, u32[]{:S(2)}, u32[]{:S(2)}) %collective-permute-start.9) | collective-permute-done | bytes 294944 | tf_op jit(solution)/shard_map/ppermute | solution.py:260
  120.7 1.6 collective-permute-done.8.refs_2_
  122.3 7.3 %collective-permute-done.7.refs_1_ = f32[72,1024]{1,0:T(8,128)S(1)} collective-permute-done((f32[72,1024]{1,0:T(8,128)S(1)}, f32[72,1024]{1,0:T(8,128)S(1)}, u32[]{:S(2)}, u32[]{:S(2)}) %collective-permute-start.7) | collective-permute-done | bytes 294944 | tf_op jit(solution)/shard_map/ppermute | solution.py:260
  129.6 1.4 back.3
  131.0 0.6 collective-permute-start.10
  131.6 1.2 collective-permute-done.10
  132.8 15.4 %all_to_all.39 = f32[544,1,128]{2,1,0:T(1,128)S(1)} all-to-all(f32[544,1,128]{2,1,0:T(1,128)S(1)} %bitcast.48), channel_id=1, replica_groups={{0,2,4,6,8,10,12,14,16,18,20,22,24,26,28,30,32,34,36,38,40,42,44,46,48,..., dimensions={0} | all-to-all | bytes 557056 | tf_op jit(solution)/shard_map/all_to_all | solution.py:255
  148.2 14.7 %all_to_all.40 = f32[512,1,128]{2,1,0:T(1,128)S(1)} all-to-all(f32[512,1,128]{2,1,0:T(1,128)S(1)} %bitcast.43), channel_id=1, replica_groups={{0,2,4,6,8,10,12,14,16,18,20,22,24,26,28,30,32,34,36,38,40,42,44,46,48,..., dimensions={0} | all-to-all | bytes 524288 | tf_op jit(solution)/shard_map/all_to_all | solution.py:255
  162.9 3.5 %collective-permute-start.11 = (f32[512,128]{1,0:T(8,128)S(1)}, f32[512,128]{1,0:T(8,128)S(1)}, u32[]{:S(2)}, u32[]{:S(2)}) collective-permute-start(f32[512,128]{1,0:T(8,128)S(1)} %bitcast.34), channel_id=1, source_target_pairs={{0,1},{1,0},{2,3},{3,2},{4,5},{5,4},{6,7},{7,6},{8,9},{9,8},{10,11... | collective-permute-start | bytes 786440 | tf_op jit(solution)/shard_map/ppermute | solution.py:250
  166.4 1.2 collective-permute-done.11.refs_1_
  167.6 1.6 forward.5
  169.2 0.6 collective-permute-start.14
  169.8 0.3 collective-permute-start.13
  170.1 0.6 collective-permute-start.12
  170.8 6.8 %collective-permute-done.14.h3 = f32[72,1024]{1,0:T(8,128)S(1)} collective-permute-done((f32[72,1024]{1,0:T(8,128)S(1)}, f32[72,1024]{1,0:T(8,128)S(1)}, u32[]{:S(2)}, u32[]{:S(2)}) %collective-permute-start.14) | collective-permute-done | bytes 294944 | tf_op jit(solution)/shard_map/ppermute | solution.py:260
  177.5 1.8 collective-permute-done.13.h2
  179.3 7.3 %collective-permute-done.12.h1 = f32[72,1024]{1,0:T(8,128)S(1)} collective-permute-done((f32[72,1024]{1,0:T(8,128)S(1)}, f32[72,1024]{1,0:T(8,128)S(1)}, u32[]{:S(2)}, u32[]{:S(2)}) %collective-permute-start.12) | collective-permute-done | bytes 294944 | tf_op jit(solution)/shard_map/ppermute | solution.py:260
  186.6 0.3 last_image.1
  186.9 11.9 %all_to_all.41 = f32[32,1,128]{2,1,0:T(1,128)S(1)} all-to-all(f32[32,1,128]{2,1,0:T(1,128)S(1)} %bitcast.46), channel_id=1, replica_groups={{0,2,4,6,8,10,12,14,16,18,20,22,24,26,28,30,32,34,36,38,40,42,44,46,48,..., dimensions={0} | all-to-all | bytes 32768 | tf_op jit(solution)/shard_map/all_to_all | solution.py:255
  198.8 1.9 collective-permute-start.15
  200.8 0.7 prepare.1
  201.5 0.1 collective-permute-done.15.other
  201.6 1.0 finish.1
  (7 shorter events, 0.2 us)
Async XLA Ops:
  5.9 4.5 %collective-permute-start = (f32[512,128]{1,0:T(8,128)S(1)}, f32[512,128]{1,0:T(8,128)S(1)}, u32[]{:S(2)}, u32[]{:S(2)}) collective-permute-start(f32[512,128]{1,0:T(8,128)S(1)} %get-tuple-element.39), channel_id=1, source_target_pairs={{0,1},{1,0},{2,3},{3,2},{4,5},{5,4},{6,7},{7,6},{8,9},{9,8},{10,11... | collective-permute-start | bytes 786440 | tf_op jit(solution)/shard_map/ppermute | solution.py:250
  46.3 5.7 %collective-permute-start.1 = (f32[512,128]{1,0:T(8,128)S(1)}, f32[512,128]{1,0:T(8,128)S(1)}, u32[]{:S(2)}, u32[]{:S(2)}) collective-permute-start(f32[512,128]{1,0:T(8,128)S(1)} %bitcast.36), channel_id=1, source_target_pairs={{0,1},{1,0},{2,3},{3,2},{4,5},{5,4},{6,7},{7,6},{8,9},{9,8},{10,11... | collective-permute-start | bytes 786440 | tf_op jit(solution)/shard_map/ppermute | solution.py:250
  53.5 15.2 %collective-permute-start.4 = (f32[72,1024]{1,0:T(8,128)S(1)}, f32[72,1024]{1,0:T(8,128)S(1)}, u32[]{:S(2)}, u32[]{:S(2)}) collective-permute-start(f32[72,1024]{1,0:T(8,128)S(1)} %get-tuple-element.44.refs_0_), channel_id=1, source_target_pairs={{0,192},{64,0},{128,64},{192,128},{1,193},{65,1},{129,65},{193,129... | collective-permute-start | bytes 884744 | tf_op jit(solution)/shard_map/ppermute | solution.py:260
  56.0 12.6 %collective-permute-start.3 = (f32[72,1024]{1,0:T(8,128)S(1)}, f32[72,1024]{1,0:T(8,128)S(1)}, u32[]{:S(2)}, u32[]{:S(2)}) collective-permute-start(f32[72,1024]{1,0:T(8,128)S(1)} %get-tuple-element.44.refs_0_), channel_id=1, source_target_pairs={{0,128},{64,192},{128,0},{192,64},{1,129},{65,193},{129,1},{193,65... | collective-permute-start | bytes 884744 | tf_op jit(solution)/shard_map/ppermute | solution.py:260
  56.5 16.2 %collective-permute-start.2 = (f32[72,1024]{1,0:T(8,128)S(1)}, f32[72,1024]{1,0:T(8,128)S(1)}, u32[]{:S(2)}, u32[]{:S(2)}) collective-permute-start(f32[72,1024]{1,0:T(8,128)S(1)} %get-tuple-element.44.refs_0_), channel_id=1, source_target_pairs={{0,64},{64,128},{128,192},{192,0},{1,65},{65,129},{129,193},{193,1... | collective-permute-start | bytes 884744 | tf_op jit(solution)/shard_map/ppermute | solution.py:260
  74.1 1.9 collective-permute-start.5
  106.2 4.6 %collective-permute-start.6 = (f32[512,128]{1,0:T(8,128)S(1)}, f32[512,128]{1,0:T(8,128)S(1)}, u32[]{:S(2)}, u32[]{:S(2)}) collective-permute-start(f32[512,128]{1,0:T(8,128)S(1)} %bitcast.38), channel_id=1, source_target_pairs={{0,1},{1,0},{2,3},{3,2},{4,5},{5,4},{6,7},{7,6},{8,9},{9,8},{10,11... | collective-permute-start | bytes 786440 | tf_op jit(solution)/shard_map/ppermute | solution.py:250
  112.4 8.3 %collective-permute-start.9 = (f32[72,1024]{1,0:T(8,128)S(1)}, f32[72,1024]{1,0:T(8,128)S(1)}, u32[]{:S(2)}, u32[]{:S(2)}) collective-permute-start(f32[72,1024]{1,0:T(8,128)S(1)} %get-tuple-element.51.refs_0_), channel_id=1, source_target_pairs={{0,192},{64,0},{128,64},{192,128},{1,193},{65,1},{129,65},{193,129... | collective-permute-start | bytes 884744 | tf_op jit(solution)/shard_map/ppermute | solution.py:260
  112.8 9.5 %collective-permute-start.8 = (f32[72,1024]{1,0:T(8,128)S(1)}, f32[72,1024]{1,0:T(8,128)S(1)}, u32[]{:S(2)}, u32[]{:S(2)}) collective-permute-start(f32[72,1024]{1,0:T(8,128)S(1)} %get-tuple-element.51.refs_0_), channel_id=1, source_target_pairs={{0,128},{64,192},{128,0},{192,64},{1,129},{65,193},{129,1},{193,65... | collective-permute-start | bytes 884744 | tf_op jit(solution)/shard_map/ppermute | solution.py:260
  113.4 16.2 %collective-permute-start.7 = (f32[72,1024]{1,0:T(8,128)S(1)}, f32[72,1024]{1,0:T(8,128)S(1)}, u32[]{:S(2)}, u32[]{:S(2)}) collective-permute-start(f32[72,1024]{1,0:T(8,128)S(1)} %get-tuple-element.51.refs_0_), channel_id=1, source_target_pairs={{0,64},{64,128},{128,192},{192,0},{1,65},{65,129},{129,193},{193,1... | collective-permute-start | bytes 884744 | tf_op jit(solution)/shard_map/ppermute | solution.py:260
  131.0 1.8 collective-permute-start.10
  162.9 4.6 %collective-permute-start.11 = (f32[512,128]{1,0:T(8,128)S(1)}, f32[512,128]{1,0:T(8,128)S(1)}, u32[]{:S(2)}, u32[]{:S(2)}) collective-permute-start(f32[512,128]{1,0:T(8,128)S(1)} %bitcast.34), channel_id=1, source_target_pairs={{0,1},{1,0},{2,3},{3,2},{4,5},{5,4},{6,7},{7,6},{8,9},{9,8},{10,11... | collective-permute-start | bytes 786440 | tf_op jit(solution)/shard_map/ppermute | solution.py:250
  169.2 8.3 %collective-permute-start.14 = (f32[72,1024]{1,0:T(8,128)S(1)}, f32[72,1024]{1,0:T(8,128)S(1)}, u32[]{:S(2)}, u32[]{:S(2)}) collective-permute-start(f32[72,1024]{1,0:T(8,128)S(1)} %get-tuple-element.60.h0), channel_id=1, source_target_pairs={{0,192},{64,0},{128,64},{192,128},{1,193},{65,1},{129,65},{193,129... | collective-permute-start | bytes 884744 | tf_op jit(solution)/shard_map/ppermute | solution.py:260
  169.8 9.4 %collective-permute-start.13 = (f32[72,1024]{1,0:T(8,128)S(1)}, f32[72,1024]{1,0:T(8,128)S(1)}, u32[]{:S(2)}, u32[]{:S(2)}) collective-permute-start(f32[72,1024]{1,0:T(8,128)S(1)} %get-tuple-element.60.h0), channel_id=1, source_target_pairs={{0,128},{64,192},{128,0},{192,64},{1,129},{65,193},{129,1},{193,65... | collective-permute-start | bytes 884744 | tf_op jit(solution)/shard_map/ppermute | solution.py:260
  170.1 16.5 %collective-permute-start.12 = (f32[72,1024]{1,0:T(8,128)S(1)}, f32[72,1024]{1,0:T(8,128)S(1)}, u32[]{:S(2)}, u32[]{:S(2)}) collective-permute-start(f32[72,1024]{1,0:T(8,128)S(1)} %get-tuple-element.60.h0), channel_id=1, source_target_pairs={{0,64},{64,128},{128,192},{192,0},{1,65},{65,129},{129,193},{193,1... | collective-permute-start | bytes 884744 | tf_op jit(solution)/shard_map/ppermute | solution.py:260
  198.8 2.8 %collective-permute-start.15 = (f32[32,128]{1,0:T(8,128)S(1)}, f32[32,128]{1,0:T(8,128)S(1)}, u32[]{:S(2)}, u32[]{:S(2)}) collective-permute-start(f32[32,128]{1,0:T(8,128)S(1)} %bitcast.44), channel_id=1, source_target_pairs={{0,1},{1,0},{2,3},{3,2},{4,5},{5,4},{6,7},{7,6},{8,9},{9,8},{10,11... | collective-permute-start | bytes 49160 | tf_op jit(solution)/shard_map/ppermute | solution.py:250

commit v4 on v3

--- a/solution.py
+++ b/solution.py
@@ -106,19 +106,18 @@
         store_pieces(mine, theirs, p, t, mine.shape[0] // half)
 
 
-def turn_states(high, low, high_turned, low_turned):
-    high_turned[...] = high[...].T
-    low_turned[...] = low[...].T
-
-
-def combine(hops):
-    p = hops[0][...] + hops[1][...] + (hops[2][...] + hops[3][...])
-    n = p.shape[0] - TILE
-    return p[:n], p[n:, :LANES]
+def turn_states(x, turned):
+    turned[...] = x[...].T
+
+
+def combine(a, ra, b, rb):
+    n = b.shape[0]
+    image = jnp.concatenate([a[:n, :] + ra[:n, :], b[...] + rb[...]], axis=1)
+    return image, a[n : n + TILE, :LANES] + ra[n : n + TILE, :LANES]
 
 
 def step_image(hops, before, scal, image_out, scal_out):
-    image, tail = combine(hops)
+    image, tail = combine(*hops)
     gamma = tail[0:1]
     if before is None:
         beta = jnp.zeros_like(gamma)
@@ -179,32 +178,34 @@
 
 def forward(*refs, step):
     if step == 0:
-        top, bottom, high, low, gradient, out = refs
+        top, bottom, high, low, gradient, a, b = refs
         g = jnp.concatenate([top[...], bottom[...]], axis=0)
         cross = None
     else:
         if step == 1:
-            top, bottom, size, scal, g_old, high, low, gradient, direction, out = refs
+            top, bottom, size, scal, g_old, high, low, gradient, direction, a, b = refs
             d = g_old[...]
         else:
-            top, bottom, size, scal, g_old, d_old, high, low, gradient, direction, out = refs
+            top, bottom, size, scal, g_old, d_old, high, low, gradient, direction, a, b = refs
             d = g_old[...] + scal[1:2, :] * d_old[...]
         q = jnp.concatenate([top[...], bottom[...]], axis=0)
         direction[...] = d
         g = g_old[...] - size[0:1, :] * (q + ridge * d)
         cross = jnp.sum(g * d)
     gradient[...] = g
-    n = out.shape[0] - TILE
+    n = b.shape[0]
     stride = g.shape[0] // n
     x2 = split2(
         jnp.concatenate([gradient[pl.ds(j, n, stride=stride), :] for j in range(stride)], axis=1)
     )
-    for t in range(high.shape[1] // WIDE):
-        at = pl.ds(t * WIDE, WIDE)
-        out[0:n, at] = rows_product(x2, high, low, at)
-    out[n : n + 1, :] = jnp.broadcast_to(jnp.sum(g * g), (1, out.shape[1]))
-    rest = jnp.zeros((TILE - 1, out.shape[1]), F32)
-    out[n + 1 :, :] = rest if cross is None else rest + cross
+    steps = high.shape[1] // WIDE
+    for t in range(steps):
+        p = rows_product(x2, high, low, pl.ds(t * WIDE, WIDE))
+        out, k = (a, t) if t < steps // 2 else (b, t - steps // 2)
+        out[0:n, k * WIDE : (k + 1) * WIDE] = p
+    a[n : n + 1, :] = jnp.broadcast_to(jnp.sum(g * g), (1, a.shape[1]))
+    rest = jnp.zeros((TILE - 1, a.shape[1]), F32)
+    a[n + 1 :, :] = rest if cross is None else rest + cross
 
 
 def prepare(core, scal, size0, size1, d0, d1, g2, i0, i1, i2, targets, readout, direction, residual, image, sums):
@@ -251,21 +252,22 @@
 
     def exchange(x):
         n = x.shape[0]
-        x = x.reshape(n, 1, LANES)
+        parts = (half, rows, LANES) if n == half * rows else (half, 1, n // half * LANES)
+        x = x.reshape(parts)
         x = lax.all_to_all(x, "samp", 0, 0, axis_index_groups=groups, tiled=True)
         return x.reshape(n, LANES)
 
-    def unit_terms(x):
-        hops = [
-            lax.ppermute(x, "unit", [(i, (i + d) % unit_count) for i in range(unit_count)])
-            for d in range(1, unit_count)
-        ]
-        return [x] + hops
+    def unit_hop(x, mask):
+        return lax.ppermute(x, "unit", [(i, i ^ mask) for i in range(unit_count)])
+
+    def unit_terms(a, b):
+        a, b = a + unit_hop(a, 1), b + unit_hop(b, 3)
+        return a, unit_hop(a, 3), b, unit_hop(b, 1)
 
     vector = shape(TILE, LANES)
     image_shape = shape(outputs, samples)
     whole = shape(outputs * rows, LANES)
-    partial = shape(outputs + TILE, samples)
+    partial = [shape(outputs + TILE, samples // 2), shape(outputs, samples // 2)]
     flops = 2 * 4 * samples * units * outputs
 
     smem = pl.BlockSpec(memory_space=pltpu.SMEM)
@@ -285,10 +287,10 @@
         flops=flops,
     )
     high, low = here(high), here(low)
-    high_turned, low_turned = call(
-        turn_states, [shape(units, samples, dtype=BF16)] * 2, high, low, flops=flops
-    )
-    high_turned, low_turned = here(high_turned), here(low_turned)
+    high_turned, low_turned = [
+        here(call(turn_states, shape(units, samples, dtype=BF16), x, flops=flops))
+        for x in (high, low)
+    ]
     got = exchange(mine + swap(theirs))
     spread = call(reduce_pieces, shape(half * rows, LANES), got, rows=rows, scalars=False)
 
@@ -298,9 +300,9 @@
         top = exchange(spread)
         bottom = swap(top)
         if step == 0:
-            g, out = call(
+            g, *terms = call(
                 forward,
-                [whole, partial],
+                [whole] + partial,
                 top,
                 bottom,
                 high_turned,
@@ -310,9 +312,9 @@
             )
         else:
             olds = [gradients[-1]] + ([directions[-1]] if step > 1 else [])
-            g, d, out = call(
+            g, d, *terms = call(
                 forward,
-                [whole, whole, partial],
+                [whole, whole] + partial,
                 top,
                 bottom,
                 size,
@@ -325,7 +327,7 @@
             )
             directions.append(d)
         gradients.append(g)
-        hops = unit_terms(out)
+        hops = unit_terms(*terms)
         olds = [images[-1], scal] if step else []
         if step + 1 < ITERS:
             piece = shape(half * (rows + 1), LANES)

time: 203 us -> 188 us (0.926)
  waiting for transfers between devices: 53.1 us -> 27.4 us
  starting transfers between devices: 23.6 us -> 34.1 us
    ppermute x9 -> x12, waiting for transfers between devices: 47.1 us -> 21.4 us  [unit_hop(): return lax.ppermute(x, 'unit', [(i, i ^ mask) for i in range(unit_count)])]
    ppermute x7, starting transfers between devices: 16.8 us -> 22.2 us  [swap(): return lax.ppermute(x, 'samp', swap_cores)]
    ppermute x9 -> x12, starting transfers between devices: 6.77 us -> 11.8 us  [unit_hop(): return lax.ppermute(x, 'unit', [(i, i ^ mask) for i in range(unit_count)])]
    pallas_call x13 -> x14, Pallas kernels: 17.1 us -> 17.1 us  [call(): pl.pallas_call(functools.partial(kernel, **static), in_specs=specs or [VM...]
  transfers between devices with their start and end apart: 16 -> 19, of which waited for: 14 -> 12; matrix products, arithmetic and copies ran while one was open for 0% -> 0% of each run, Pallas kernels for 2% -> 2%
where the time goes in v4:
time: 188 us
  blocking collectives  108 us (57%)
  starting transfers between devices  34.1 us (18%)
  waiting for transfers between devices  27.4 us (15%)
  Pallas kernels  17.1 us (9%)
    all_to_all x7, blocking collectives, exchange(): x = lax.all_to_all(x, 'samp', 0, 0, axis_index_groups=groups, tiled=True)  108 us
    ppermute x7, starting transfers between devices, swap(): return lax.ppermute(x, 'samp', swap_cores)  22.2 us
    ppermute x12, waiting for transfers between devices, unit_hop(): return lax.ppermute(x, 'unit', [(i, i ^ mask) for i in range(unit_count)])  21.4 us
    pallas_call x14, Pallas kernels, call(): pl.pallas_call(functools.partial(kernel, **static), in_specs=specs or [VM...  17.1 us
    ppermute x12, starting transfers between devices, unit_hop(): return lax.ppermute(x, 'unit', [(i, i ^ mask) for i in range(unit_count)])  11.8 us
    ppermute x7, waiting for transfers between devices, swap(): return lax.ppermute(x, 'samp', swap_cores)  5.99 us
  transfers between devices with their start and end apart: 19, of which 12 were waited for; matrix products, arithmetic and copies ran while one was open for 0% of the time, Pallas kernels for 2%

profile of v4, /device:TPU:1, one launch (start us, length us, event | category | flops | bytes accessed | tf_op | source)
XLA Modules:
  0.0 187.9 jit_solution(14057620649136932092)
XLA Ops:
  0.6 5.3 %first.1 = (bf16[1024,2048]{1,0:T(8,128)(2,1)S(1)}, bf16[1024,2048]{1,0:T(8,128)(2,1)S(1)}, f32[64,1024]{1,0:T(8,128)S(1)}, f32[512,128]{1,0:T(8,128)S(1)}, f32[512,128]{1,0:T(8,128)S(1)}) custom-call(s32[1,1]{1,0:T(1,128)} %bitcast.core, f32[1024,2048]{1,0:T(8,128)} %states.1, f32[64,1024]{1,0:T(8,128)} %bitcast.38), custom_call_target="tpu_custom_call" | custom-call | flops 1073741824 | bytes 1048576 | tf_op jit(solution)/shard_map/first/pallas_call | solution.py:29
  5.9 3.3 %collective-permute-start = (f32[512,128]{1,0:T(8,128)S(1)}, f32[512,128]{1,0:T(8,128)S(1)}, u32[]{:S(2)}, u32[]{:S(2)}) collective-permute-start(f32[512,128]{1,0:T(8,128)S(1)} %get-tuple-element.40), channel_id=1, source_target_pairs={{0,1},{1,0},{2,3},{3,2},{4,5},{5,4},{6,7},{7,6},{8,9},{9,8},{10,11... | collective-permute-start | bytes 786440 | tf_op jit(solution)/shard_map/ppermute | solution.py:251
  9.2 1.2 collective-permute-done
  10.4 20.8 %all_to_all.35 = f32[32,16,128]{2,1,0:T(8,128)S(1)} all-to-all(f32[32,16,128]{2,1,0:T(8,128)S(1)} %bitcast.37), channel_id=1, replica_groups={{0,2,4,6,8,10,12,14,16,18,20,22,24,26,28,30,32,34,36,38,40,42,44,46,48,..., dimensions={0} | all-to-all | bytes 524288 | tf_op jit(solution)/shard_map/all_to_all | solution.py:257
  31.3 15.0 %all_to_all.36 = f32[32,16,128]{2,1,0:T(8,128)S(1)} all-to-all(f32[32,16,128]{2,1,0:T(8,128)S(1)} %bitcast.29), channel_id=1, replica_groups={{0,2,4,6,8,10,12,14,16,18,20,22,24,26,28,30,32,34,36,38,40,42,44,46,48,..., dimensions={0} | all-to-all | bytes 524288 | tf_op jit(solution)/shard_map/all_to_all | solution.py:257
  46.3 3.3 %collective-permute-start.1 = (f32[512,128]{1,0:T(8,128)S(1)}, f32[512,128]{1,0:T(8,128)S(1)}, u32[]{:S(2)}, u32[]{:S(2)}) collective-permute-start(f32[512,128]{1,0:T(8,128)S(1)} %bitcast.26), channel_id=1, source_target_pairs={{0,1},{1,0},{2,3},{3,2},{4,5},{5,4},{6,7},{7,6},{8,9},{9,8},{10,11... | collective-permute-start | bytes 786440 | tf_op jit(solution)/shard_map/ppermute | solution.py:251
  49.6 1.2 turn_states.2.refs_2_.refs_5_.refs_6_
  50.9 1.2 turn_states.3.refs_3_.refs_6_.refs_7_
  52.1 1.4 forward.3
  53.5 1.3 collective-permute-start.2
  54.8 1.8 collective-permute-start.4
  56.6 2.5 %collective-permute-done.2 = f32[72,512]{1,0:T(8,128)S(1)} collective-permute-done((f32[72,512]{1,0:T(8,128)S(1)}, f32[72,512]{1,0:T(8,128)S(1)}, u32[]{:S(2)}, u32[]{:S(2)}) %collective-permute-start.2) | collective-permute-done | bytes 147488 | tf_op jit(solution)/shard_map/ppermute | solution.py:261
  59.1 2.6 %collective-permute-start.3 = (f32[72,512]{1,0:T(8,128)S(1)}, f32[72,512]{1,0:T(8,128)S(1)}, u32[]{:S(2)}, u32[]{:S(2)}) collective-permute-start(f32[72,512]{1,0:T(8,128)S(1)} %add.33.refs_0_), channel_id=1, source_target_pairs={{0,192},{64,128},{128,64},{192,0},{1,193},{65,129},{129,65},{193,1... | collective-permute-start | bytes 442376 | tf_op jit(solution)/shard_map/ppermute | solution.py:261
  61.7 0.1 collective-permute-start.5
  61.8 4.1 %collective-permute-done.5.refs_3_ = f32[64,512]{1,0:T(8,128)S(1)} collective-permute-done((f32[64,512]{1,0:T(8,128)S(1)}, f32[64,512]{1,0:T(8,128)S(1)}, u32[]{:S(2)}, u32[]{:S(2)}) %collective-permute-start.5) | collective-permute-done | bytes 131104 | tf_op jit(solution)/shard_map/ppermute | solution.py:261
  65.9 1.3 back.2
  67.2 2.2 %collective-permute-start.6 = (f32[544,128]{1,0:T(8,128)S(1)}, f32[544,128]{1,0:T(8,128)S(1)}, u32[]{:S(2)}, u32[]{:S(2)}) collective-permute-start(f32[544,128]{1,0:T(8,128)S(1)} %get-tuple-element.46), channel_id=1, source_target_pairs={{0,1},{1,0},{2,3},{3,2},{4,5},{5,4},{6,7},{7,6},{8,9},{9,8},{10,11... | collective-permute-start | bytes 835592 | tf_op jit(solution)/shard_map/ppermute | solution.py:251
  69.4 1.2 collective-permute-done.6
  70.6 15.4 %all_to_all.37 = f32[32,1,2176]{2,1,0:T(1,128)S(1)} all-to-all(f32[32,1,2176]{2,1,0:T(1,128)S(1)} %bitcast.35), channel_id=1, replica_groups={{0,2,4,6,8,10,12,14,16,18,20,22,24,26,28,30,32,34,36,38,40,42,44,46,48,..., dimensions={0} | all-to-all | bytes 557056 | tf_op jit(solution)/shard_map/all_to_all | solution.py:257
  86.0 14.7 %all_to_all.38 = f32[32,16,128]{2,1,0:T(8,128)S(1)} all-to-all(f32[32,16,128]{2,1,0:T(8,128)S(1)} %bitcast.30), channel_id=1, replica_groups={{0,2,4,6,8,10,12,14,16,18,20,22,24,26,28,30,32,34,36,38,40,42,44,46,48,..., dimensions={0} | all-to-all | bytes 524288 | tf_op jit(solution)/shard_map/all_to_all | solution.py:257
  100.7 3.5 %collective-permute-start.7 = (f32[512,128]{1,0:T(8,128)S(1)}, f32[512,128]{1,0:T(8,128)S(1)}, u32[]{:S(2)}, u32[]{:S(2)}) collective-permute-start(f32[512,128]{1,0:T(8,128)S(1)} %bitcast.24), channel_id=1, source_target_pairs={{0,1},{1,0},{2,3},{3,2},{4,5},{5,4},{6,7},{7,6},{8,9},{9,8},{10,11... | collective-permute-start | bytes 786440 | tf_op jit(solution)/shard_map/ppermute | solution.py:251
  104.2 1.2 collective-permute-done.7.refs_1_
  105.4 1.6 forward.4
  107.1 1.4 collective-permute-start.10
  108.5 3.6 %collective-permute-done.8 = f32[72,512]{1,0:T(8,128)S(1)} collective-permute-done((f32[72,512]{1,0:T(8,128)S(1)}, f32[72,512]{1,0:T(8,128)S(1)}, u32[]{:S(2)}, u32[]{:S(2)}) %collective-permute-start.8) | collective-permute-done | bytes 147488 | tf_op jit(solution)/shard_map/ppermute | solution.py:261
  112.1 1.4 collective-permute-start.9
  113.6 0.1 collective-permute-start.11
  113.7 3.8 %collective-permute-done.11.refs_3_ = f32[64,512]{1,0:T(8,128)S(1)} collective-permute-done((f32[64,512]{1,0:T(8,128)S(1)}, f32[64,512]{1,0:T(8,128)S(1)}, u32[]{:S(2)}, u32[]{:S(2)}) %collective-permute-start.11) | collective-permute-done | bytes 131104 | tf_op jit(solution)/shard_map/ppermute | solution.py:261
  117.5 1.3 back.3
  118.8 2.7 %collective-permute-start.12 = (f32[544,128]{1,0:T(8,128)S(1)}, f32[544,128]{1,0:T(8,128)S(1)}, u32[]{:S(2)}, u32[]{:S(2)}) collective-permute-start(f32[544,128]{1,0:T(8,128)S(1)} %get-tuple-element.55), channel_id=1, source_target_pairs={{0,1},{1,0},{2,3},{3,2},{4,5},{5,4},{6,7},{7,6},{8,9},{9,8},{10,11... | collective-permute-start | bytes 835592 | tf_op jit(solution)/shard_map/ppermute | solution.py:251
  121.6 1.2 collective-permute-done.12
  122.8 15.4 %all_to_all.39 = f32[32,1,2176]{2,1,0:T(1,128)S(1)} all-to-all(f32[32,1,2176]{2,1,0:T(1,128)S(1)} %bitcast.36), channel_id=1, replica_groups={{0,2,4,6,8,10,12,14,16,18,20,22,24,26,28,30,32,34,36,38,40,42,44,46,48,..., dimensions={0} | all-to-all | bytes 557056 | tf_op jit(solution)/shard_map/all_to_all | solution.py:257
  138.2 14.7 %all_to_all.40 = f32[32,16,128]{2,1,0:T(8,128)S(1)} all-to-all(f32[32,16,128]{2,1,0:T(8,128)S(1)} %bitcast.31), channel_id=1, replica_groups={{0,2,4,6,8,10,12,14,16,18,20,22,24,26,28,30,32,34,36,38,40,42,44,46,48,..., dimensions={0} | all-to-all | bytes 524288 | tf_op jit(solution)/shard_map/all_to_all | solution.py:257
  152.9 3.5 %collective-permute-start.13 = (f32[512,128]{1,0:T(8,128)S(1)}, f32[512,128]{1,0:T(8,128)S(1)}, u32[]{:S(2)}, u32[]{:S(2)}) collective-permute-start(f32[512,128]{1,0:T(8,128)S(1)} %bitcast.22), channel_id=1, source_target_pairs={{0,1},{1,0},{2,3},{3,2},{4,5},{5,4},{6,7},{7,6},{8,9},{9,8},{10,11... | collective-permute-start | bytes 786440 | tf_op jit(solution)/shard_map/ppermute | solution.py:251
  156.4 1.2 collective-permute-done.13.refs_1_
  157.5 1.6 forward.5
  159.2 0.1 collective-permute-start.14
  159.3 1.4 collective-permute-start.16
  160.7 3.6 %collective-permute-done.14 = f32[72,512]{1,0:T(8,128)S(1)} collective-permute-done((f32[72,512]{1,0:T(8,128)S(1)}, f32[72,512]{1,0:T(8,128)S(1)}, u32[]{:S(2)}, u32[]{:S(2)}) %collective-permute-start.14) | collective-permute-done | bytes 147488 | tf_op jit(solution)/shard_map/ppermute | solution.py:261
  164.4 1.4 collective-permute-start.15
  165.8 0.1 collective-permute-start.17
  165.9 3.8 %collective-permute-done.17.h3 = f32[64,512]{1,0:T(8,128)S(1)} collective-permute-done((f32[64,512]{1,0:T(8,128)S(1)}, f32[64,512]{1,0:T(8,128)S(1)}, u32[]{:S(2)}, u32[]{:S(2)}) %collective-permute-start.17) | collective-permute-done | bytes 131104 | tf_op jit(solution)/shard_map/ppermute | solution.py:261
  169.7 0.3 last_image.1
  170.0 12.2 %all_to_all.41 = f32[32,1,128]{2,1,0:T(1,128)S(1)} all-to-all(f32[32,1,128]{2,1,0:T(1,128)S(1)} %bitcast.34), channel_id=1, replica_groups={{0,2,4,6,8,10,12,14,16,18,20,22,24,26,28,30,32,34,36,38,40,42,44,46,48,..., dimensions={0} | all-to-all | bytes 32768 | tf_op jit(solution)/shard_map/all_to_all | solution.py:257
  182.3 3.8 %collective-permute-start.18 = (f32[32,128]{1,0:T(8,128)S(1)}, f32[32,128]{1,0:T(8,128)S(1)}, u32[]{:S(2)}, u32[]{:S(2)}) collective-permute-start(f32[32,128]{1,0:T(8,128)S(1)} %bitcast.32), channel_id=1, source_target_pairs={{0,1},{1,0},{2,3},{3,2},{4,5},{5,4},{6,7},{7,6},{8,9},{9,8},{10,11... | collective-permute-start | bytes 49160 | tf_op jit(solution)/shard_map/ppermute | solution.py:251
  186.0 0.7 prepare.1
  186.7 0.1 collective-permute-done.18.other
  186.9 1.0 finish.1
  (20 shorter events, 0.4 us)
Async XLA Ops:
  5.9 4.5 %collective-permute-start = (f32[512,128]{1,0:T(8,128)S(1)}, f32[512,128]{1,0:T(8,128)S(1)}, u32[]{:S(2)}, u32[]{:S(2)}) collective-permute-start(f32[512,128]{1,0:T(8,128)S(1)} %get-tuple-element.40), channel_id=1, source_target_pairs={{0,1},{1,0},{2,3},{3,2},{4,5},{5,4},{6,7},{7,6},{8,9},{9,8},{10,11... | collective-permute-start | bytes 786440 | tf_op jit(solution)/shard_map/ppermute | solution.py:251
  46.3 5.8 %collective-permute-start.1 = (f32[512,128]{1,0:T(8,128)S(1)}, f32[512,128]{1,0:T(8,128)S(1)}, u32[]{:S(2)}, u32[]{:S(2)}) collective-permute-start(f32[512,128]{1,0:T(8,128)S(1)} %bitcast.26), channel_id=1, source_target_pairs={{0,1},{1,0},{2,3},{3,2},{4,5},{5,4},{6,7},{7,6},{8,9},{9,8},{10,11... | collective-permute-start | bytes 786440 | tf_op jit(solution)/shard_map/ppermute | solution.py:251
  53.5 5.6 %collective-permute-start.2 = (f32[72,512]{1,0:T(8,128)S(1)}, f32[72,512]{1,0:T(8,128)S(1)}, u32[]{:S(2)}, u32[]{:S(2)}) collective-permute-start(f32[72,512]{1,0:T(8,128)S(1)} %get-tuple-element.43), channel_id=1, source_target_pairs={{0,64},{64,0},{128,192},{192,128},{1,65},{65,1},{129,193},{193,129... | collective-permute-start | bytes 442376 | tf_op jit(solution)/shard_map/ppermute | solution.py:261
  54.8 6.9 %collective-permute-start.4 = (f32[64,512]{1,0:T(8,128)S(1)}, f32[64,512]{1,0:T(8,128)S(1)}, u32[]{:S(2)}, u32[]{:S(2)}) collective-permute-start(f32[64,512]{1,0:T(8,128)S(1)} %get-tuple-element.44), channel_id=1, source_target_pairs={{0,192},{64,128},{128,64},{192,0},{1,193},{65,129},{129,65},{193,1... | collective-permute-start | bytes 393224 | tf_op jit(solution)/shard_map/ppermute | solution.py:261
  59.1 6.8 %collective-permute-start.3 = (f32[72,512]{1,0:T(8,128)S(1)}, f32[72,512]{1,0:T(8,128)S(1)}, u32[]{:S(2)}, u32[]{:S(2)}) collective-permute-start(f32[72,512]{1,0:T(8,128)S(1)} %add.33.refs_0_), channel_id=1, source_target_pairs={{0,192},{64,128},{128,64},{192,0},{1,193},{65,129},{129,65},{193,1... | collective-permute-start | bytes 442376 | tf_op jit(solution)/shard_map/ppermute | solution.py:261
  61.7 4.2 %collective-permute-start.5 = (f32[64,512]{1,0:T(8,128)S(1)}, f32[64,512]{1,0:T(8,128)S(1)}, u32[]{:S(2)}, u32[]{:S(2)}) collective-permute-start(f32[64,512]{1,0:T(8,128)S(1)} %add.34.refs_2_), channel_id=1, source_target_pairs={{0,64},{64,0},{128,192},{192,128},{1,65},{65,1},{129,193},{193,129... | collective-permute-start | bytes 393224 | tf_op jit(solution)/shard_map/ppermute | solution.py:261
  67.2 3.4 %collective-permute-start.6 = (f32[544,128]{1,0:T(8,128)S(1)}, f32[544,128]{1,0:T(8,128)S(1)}, u32[]{:S(2)}, u32[]{:S(2)}) collective-permute-start(f32[544,128]{1,0:T(8,128)S(1)} %get-tuple-element.46), channel_id=1, source_target_pairs={{0,1},{1,0},{2,3},{3,2},{4,5},{5,4},{6,7},{7,6},{8,9},{9,8},{10,11... | collective-permute-start | bytes 835592 | tf_op jit(solution)/shard_map/ppermute | solution.py:251
  100.7 4.6 %collective-permute-start.7 = (f32[512,128]{1,0:T(8,128)S(1)}, f32[512,128]{1,0:T(8,128)S(1)}, u32[]{:S(2)}, u32[]{:S(2)}) collective-permute-start(f32[512,128]{1,0:T(8,128)S(1)} %bitcast.24), channel_id=1, source_target_pairs={{0,1},{1,0},{2,3},{3,2},{4,5},{5,4},{6,7},{7,6},{8,9},{9,8},{10,11... | collective-permute-start | bytes 786440 | tf_op jit(solution)/shard_map/ppermute | solution.py:251
  107.0 5.1 %collective-permute-start.8 = (f32[72,512]{1,0:T(8,128)S(1)}, f32[72,512]{1,0:T(8,128)S(1)}, u32[]{:S(2)}, u32[]{:S(2)}) collective-permute-start(f32[72,512]{1,0:T(8,128)S(1)} %get-tuple-element.51), channel_id=1, source_target_pairs={{0,64},{64,0},{128,192},{192,128},{1,65},{65,1},{129,193},{193,129... | collective-permute-start | bytes 442376 | tf_op jit(solution)/shard_map/ppermute | solution.py:261
  107.1 6.5 %collective-permute-start.10 = (f32[64,512]{1,0:T(8,128)S(1)}, f32[64,512]{1,0:T(8,128)S(1)}, u32[]{:S(2)}, u32[]{:S(2)}) collective-permute-start(f32[64,512]{1,0:T(8,128)S(1)} %get-tuple-element.52), channel_id=1, source_target_pairs={{0,192},{64,128},{128,64},{192,0},{1,193},{65,129},{129,65},{193,1... | collective-permute-start | bytes 393224 | tf_op jit(solution)/shard_map/ppermute | solution.py:261
  112.1 5.3 %collective-permute-start.9 = (f32[72,512]{1,0:T(8,128)S(1)}, f32[72,512]{1,0:T(8,128)S(1)}, u32[]{:S(2)}, u32[]{:S(2)}) collective-permute-start(f32[72,512]{1,0:T(8,128)S(1)} %add.36.refs_0_), channel_id=1, source_target_pairs={{0,192},{64,128},{128,64},{192,0},{1,193},{65,129},{129,65},{193,1... | collective-permute-start | bytes 442376 | tf_op jit(solution)/shard_map/ppermute | solution.py:261
  113.6 3.9 %collective-permute-start.11 = (f32[64,512]{1,0:T(8,128)S(1)}, f32[64,512]{1,0:T(8,128)S(1)}, u32[]{:S(2)}, u32[]{:S(2)}) collective-permute-start(f32[64,512]{1,0:T(8,128)S(1)} %add.37.refs_2_), channel_id=1, source_target_pairs={{0,64},{64,0},{128,192},{192,128},{1,65},{65,1},{129,193},{193,129... | collective-permute-start | bytes 393224 | tf_op jit(solution)/shard_map/ppermute | solution.py:261
  118.8 3.9 %collective-permute-start.12 = (f32[544,128]{1,0:T(8,128)S(1)}, f32[544,128]{1,0:T(8,128)S(1)}, u32[]{:S(2)}, u32[]{:S(2)}) collective-permute-start(f32[544,128]{1,0:T(8,128)S(1)} %get-tuple-element.55), channel_id=1, source_target_pairs={{0,1},{1,0},{2,3},{3,2},{4,5},{5,4},{6,7},{7,6},{8,9},{9,8},{10,11... | collective-permute-start | bytes 835592 | tf_op jit(solution)/shard_map/ppermute | solution.py:251
  152.9 4.6 %collective-permute-start.13 = (f32[512,128]{1,0:T(8,128)S(1)}, f32[512,128]{1,0:T(8,128)S(1)}, u32[]{:S(2)}, u32[]{:S(2)}) collective-permute-start(f32[512,128]{1,0:T(8,128)S(1)} %bitcast.22), channel_id=1, source_target_pairs={{0,1},{1,0},{2,3},{3,2},{4,5},{5,4},{6,7},{7,6},{8,9},{9,8},{10,11... | collective-permute-start | bytes 786440 | tf_op jit(solution)/shard_map/ppermute | solution.py:251
  159.2 5.1 %collective-permute-start.14 = (f32[72,512]{1,0:T(8,128)S(1)}, f32[72,512]{1,0:T(8,128)S(1)}, u32[]{:S(2)}, u32[]{:S(2)}) collective-permute-start(f32[72,512]{1,0:T(8,128)S(1)} %get-tuple-element.61), channel_id=1, source_target_pairs={{0,64},{64,0},{128,192},{192,128},{1,65},{65,1},{129,193},{193,129... | collective-permute-start | bytes 442376 | tf_op jit(solution)/shard_map/ppermute | solution.py:261
  159.3 6.5 %collective-permute-start.16 = (f32[64,512]{1,0:T(8,128)S(1)}, f32[64,512]{1,0:T(8,128)S(1)}, u32[]{:S(2)}, u32[]{:S(2)}) collective-permute-start(f32[64,512]{1,0:T(8,128)S(1)} %get-tuple-element.62), channel_id=1, source_target_pairs={{0,192},{64,128},{128,64},{192,0},{1,193},{65,129},{129,65},{193,1... | collective-permute-start | bytes 393224 | tf_op jit(solution)/shard_map/ppermute | solution.py:261
  164.4 5.4 %collective-permute-start.15 = (f32[72,512]{1,0:T(8,128)S(1)}, f32[72,512]{1,0:T(8,128)S(1)}, u32[]{:S(2)}, u32[]{:S(2)}) collective-permute-start(f32[72,512]{1,0:T(8,128)S(1)} %add.39.h0), channel_id=1, source_target_pairs={{0,192},{64,128},{128,64},{192,0},{1,193},{65,129},{129,65},{193,1... | collective-permute-start | bytes 442376 | tf_op jit(solution)/shard_map/ppermute | solution.py:261
  165.8 3.9 %collective-permute-start.17 = (f32[64,512]{1,0:T(8,128)S(1)}, f32[64,512]{1,0:T(8,128)S(1)}, u32[]{:S(2)}, u32[]{:S(2)}) collective-permute-start(f32[64,512]{1,0:T(8,128)S(1)} %add.40.h2), channel_id=1, source_target_pairs={{0,64},{64,0},{128,192},{192,128},{1,65},{65,1},{129,193},{193,129... | collective-permute-start | bytes 393224 | tf_op jit(solution)/shard_map/ppermute | solution.py:261
  182.3 4.6 %collective-permute-start.18 = (f32[32,128]{1,0:T(8,128)S(1)}, f32[32,128]{1,0:T(8,128)S(1)}, u32[]{:S(2)}, u32[]{:S(2)}) collective-permute-start(f32[32,128]{1,0:T(8,128)S(1)} %bitcast.32), channel_id=1, source_target_pairs={{0,1},{1,0},{2,3},{3,2},{4,5},{5,4},{6,7},{7,6},{8,9},{9,8},{10,11... | collective-permute-start | bytes 49160 | tf_op jit(solution)/shard_map/ppermute | solution.py:251

commit v5 on v4

--- a/solution.py
+++ b/solution.py
@@ -10,7 +10,7 @@
 ITERS = 3
 ridge = 0.5
 CORES, LANES, TILE = 2, 128, 8
-WIDE = 256
+WIDE, FETCH = 256, 512
 MIB = 1 << 20
 F32, BF16 = jnp.float32, jnp.bfloat16
 VMEM = pl.BlockSpec(memory_space=pltpu.VMEM)
@@ -84,7 +84,7 @@
     fetch.start()
     copies = [
         pltpu.make_async_copy(
-            states.at[:, pl.ds(t * WIDE, WIDE)], buf.at[t], sems.at[t]
+            states.at[:, pl.ds(t * FETCH, FETCH)], buf.at[t], sems.at[t]
         )
         for t in range(steps)
     ]
@@ -100,14 +100,17 @@
         s = buf[t]
         h = s.astype(BF16)
         l = (s - h.astype(F32)).astype(BF16)
-        high[:, pl.ds(t * WIDE, WIDE)] = h
-        low[:, pl.ds(t * WIDE, WIDE)] = l
+        high[:, pl.ds(t * FETCH, FETCH)] = h
+        low[:, pl.ds(t * FETCH, FETCH)] = l
         p = fold(dot(x2, l, 1, 0) + dot(x2, h, 1, 0))
-        store_pieces(mine, theirs, p, t, mine.shape[0] // half)
-
-
-def turn_states(x, turned):
+        for i in range(FETCH // WIDE):
+            part = p[:, i * WIDE : (i + 1) * WIDE]
+            store_pieces(mine, theirs, part, t * (FETCH // WIDE) + i, mine.shape[0] // half)
+
+
+def turn_states(x, turned, token):
     turned[...] = x[...].T
+    token[...] = jnp.zeros(token.shape, F32)
 
 
 def combine(a, ra, b, rb):
@@ -159,11 +162,7 @@
     return scal[0:1, :] / (image_sq + ridge * scal[2:3, :])
 
 
-def reduce_pieces(*refs, rows, scalars):
-    if scalars:
-        got, scal, out, size = refs
-    else:
-        got, out = refs
+def sum_pieces(got, out, rows):
     count = out.shape[0] // rows
     stride = got.shape[0] // count
     terms = [got[i * stride : (i + 1) * stride, :] for i in range(count)]
@@ -172,8 +171,20 @@
     total = terms[0]
     for i in range(count):
         out[i * rows : (i + 1) * rows, :] = total[:rows]
-    if scalars:
-        size[...] = jnp.broadcast_to(step_size(total[rows : rows + 1], scal), size.shape)
+    return total
+
+
+def add_pieces(a, b, token, out):
+    out[...] = a[...] + b[...]
+
+
+def reduce_first(got, out, rows):
+    sum_pieces(got, out, rows)
+
+
+def reduce_pieces(got, scal, out, size, rows):
+    total = sum_pieces(got, out, rows)
+    size[...] = jnp.broadcast_to(step_size(total[rows : rows + 1], scal), size.shape)
 
 
 def forward(*refs, step):
@@ -279,20 +290,22 @@
         pltpu.with_memory_space_constraint(targets.T, pltpu.HBM),
         specs=[smem, HBM, HBM],
         scratch=[
-            pltpu.VMEM((units // WIDE, samples, WIDE), F32),
+            pltpu.VMEM((units // FETCH, samples, FETCH), F32),
             pltpu.VMEM((outputs, samples), F32),
-            pltpu.SemaphoreType.DMA((units // WIDE + 1,)),
+            pltpu.SemaphoreType.DMA((units // FETCH + 1,)),
         ],
         limit=32,
         flops=flops,
     )
     high, low = here(high), here(low)
-    high_turned, low_turned = [
-        here(call(turn_states, shape(units, samples, dtype=BF16), x, flops=flops))
+    (high_turned, token), (low_turned, _) = [
+        call(turn_states, [shape(units, samples, dtype=BF16), vector], x, flops=flops)
         for x in (high, low)
     ]
-    got = exchange(mine + swap(theirs))
-    spread = call(reduce_pieces, shape(half * rows, LANES), got, rows=rows, scalars=False)
+    high_turned, low_turned = here(high_turned), here(low_turned)
+    pieces = call(add_pieces, shape(half * rows, LANES), mine, swap(theirs), token)
+    got = exchange(pieces)
+    spread = call(reduce_first, shape(half * rows, LANES), got, rows=rows)
 
     gradients, directions, images, sizes = [], [], [], []
     scal = size = None
@@ -349,7 +362,6 @@
                 got,
                 scal,
                 rows=rows,
-                scalars=True,
             )
             sizes.append(size)
         else:

time: 188 us -> 187 us (level)
    pallas_call x14 -> x15, Pallas kernels: 17.1 us -> 16.6 us  [call(): pl.pallas_call(functools.partial(kernel, **static), in_specs=specs or [VM...]
  transfers between devices with their start and end apart: 19 -> 19, of which waited for: 12 -> 11; matrix products, arithmetic and copies ran while one was open for 0% -> 0% of each run, Pallas kernels for 2% -> 2%
where the time goes in v5:
time: 187 us; the launch traced here: 186 us
  blocking collectives  108 us (58%)
  starting transfers between devices  34.2 us (18%)
  waiting for transfers between devices  26.3 us (14%)
  Pallas kernels  16.6 us (9%)
    all_to_all x7, blocking collectives, exchange(): x = lax.all_to_all(x, 'samp', 0, 0, axis_index_groups=groups, tiled=True)  108 us
    ppermute x7, starting transfers between devices, swap(): return lax.ppermute(x, 'samp', swap_cores)  22.4 us
    ppermute x12, waiting for transfers between devices, unit_hop(): return lax.ppermute(x, 'unit', [(i, i ^ mask) for i in range(unit_count)])  21.4 us
    pallas_call x15, Pallas kernels, call(): pl.pallas_call(functools.partial(kernel, **static), in_specs=specs or [VM...  16.6 us
    ppermute x12, starting transfers between devices, unit_hop(): return lax.ppermute(x, 'unit', [(i, i ^ mask) for i in range(unit_count)])  11.8 us
    ppermute x7, waiting for transfers between devices, swap(): return lax.ppermute(x, 'samp', swap_cores)  4.84 us
  transfers between devices with their start and end apart: 19, of which 11 were waited for; matrix products, arithmetic and copies ran while one was open for 0% of the time, Pallas kernels for 2%

profile of v5, /device:TPU:1, one launch (start us, length us, event | category | flops | bytes accessed | tf_op | source)
XLA Modules:
  0.0 186.2 jit_solution(7917900655042992067)
XLA Ops:
  0.6 4.2 %first.1 = (bf16[1024,2048]{1,0:T(8,128)(2,1)S(1)}, bf16[1024,2048]{1,0:T(8,128)(2,1)S(1)}, f32[64,1024]{1,0:T(8,128)S(1)}, f32[512,128]{1,0:T(8,128)S(1)}, f32[512,128]{1,0:T(8,128)S(1)}) custom-call(s32[1,1]{1,0:T(1,128)} %bitcast.core, f32[1024,2048]{1,0:T(8,128)} %states.1, f32[64,1024]{1,0:T(8,128)} %bitcast.38), custom_call_target="tpu_custom_call" | custom-call | flops 1073741824 | bytes 1048576 | tf_op jit(solution)/shard_map/first/pallas_call | solution.py:29
  4.8 3.3 %collective-permute-start = (f32[512,128]{1,0:T(8,128)S(1)}, f32[512,128]{1,0:T(8,128)S(1)}, u32[]{:S(2)}, u32[]{:S(2)}) collective-permute-start(f32[512,128]{1,0:T(8,128)S(1)} %get-tuple-element.43), channel_id=1, source_target_pairs={{0,1},{1,0},{2,3},{3,2},{4,5},{5,4},{6,7},{7,6},{8,9},{9,8},{10,11... | collective-permute-start | bytes 786440 | tf_op jit(solution)/shard_map/ppermute | solution.py:262
  8.2 1.2 turn_states.2
  9.5 20.9 %all_to_all.35 = f32[32,16,128]{2,1,0:T(8,128)S(1)} all-to-all(f32[32,16,128]{2,1,0:T(8,128)S(1)} %bitcast.28), channel_id=1, replica_groups={{0,2,4,6,8,10,12,14,16,18,20,22,24,26,28,30,32,34,36,38,40,42,44,46,48,..., dimensions={0} | all-to-all | bytes 524288 | tf_op jit(solution)/shard_map/all_to_all | solution.py:268
  30.5 14.9 %all_to_all.36 = f32[32,16,128]{2,1,0:T(8,128)S(1)} all-to-all(f32[32,16,128]{2,1,0:T(8,128)S(1)} %bitcast.30), channel_id=1, replica_groups={{0,2,4,6,8,10,12,14,16,18,20,22,24,26,28,30,32,34,36,38,40,42,44,46,48,..., dimensions={0} | all-to-all | bytes 524288 | tf_op jit(solution)/shard_map/all_to_all | solution.py:268
  45.4 3.3 %collective-permute-start.1 = (f32[512,128]{1,0:T(8,128)S(1)}, f32[512,128]{1,0:T(8,128)S(1)}, u32[]{:S(2)}, u32[]{:S(2)}) collective-permute-start(f32[512,128]{1,0:T(8,128)S(1)} %bitcast.22), channel_id=1, source_target_pairs={{0,1},{1,0},{2,3},{3,2},{4,5},{5,4},{6,7},{7,6},{8,9},{9,8},{10,11... | collective-permute-start | bytes 786440 | tf_op jit(solution)/shard_map/ppermute | solution.py:262
  48.7 1.8 turn_states.3
  50.4 1.4 forward.3
  51.8 1.3 collective-permute-start.2
  53.1 1.8 collective-permute-start.4
  54.9 2.5 %collective-permute-done.2 = f32[72,512]{1,0:T(8,128)S(1)} collective-permute-done((f32[72,512]{1,0:T(8,128)S(1)}, f32[72,512]{1,0:T(8,128)S(1)}, u32[]{:S(2)}, u32[]{:S(2)}) %collective-permute-start.2) | collective-permute-done | bytes 147488 | tf_op jit(solution)/shard_map/ppermute | solution.py:272
  57.4 2.6 %collective-permute-start.3 = (f32[72,512]{1,0:T(8,128)S(1)}, f32[72,512]{1,0:T(8,128)S(1)}, u32[]{:S(2)}, u32[]{:S(2)}) collective-permute-start(f32[72,512]{1,0:T(8,128)S(1)} %add.29.refs_0_), channel_id=1, source_target_pairs={{0,192},{64,128},{128,64},{192,0},{1,193},{65,129},{129,65},{193,1... | collective-permute-start | bytes 442376 | tf_op jit(solution)/shard_map/ppermute | solution.py:272
  60.0 0.1 collective-permute-start.5
  60.1 4.1 %collective-permute-done.5.refs_3_ = f32[64,512]{1,0:T(8,128)S(1)} collective-permute-done((f32[64,512]{1,0:T(8,128)S(1)}, f32[64,512]{1,0:T(8,128)S(1)}, u32[]{:S(2)}, u32[]{:S(2)}) %collective-permute-start.5) | collective-permute-done | bytes 131104 | tf_op jit(solution)/shard_map/ppermute | solution.py:272
  64.2 1.3 back.2
  65.5 2.0 %collective-permute-start.6 = (f32[544,128]{1,0:T(8,128)S(1)}, f32[544,128]{1,0:T(8,128)S(1)}, u32[]{:S(2)}, u32[]{:S(2)}) collective-permute-start(f32[544,128]{1,0:T(8,128)S(1)} %get-tuple-element.52), channel_id=1, source_target_pairs={{0,1},{1,0},{2,3},{3,2},{4,5},{5,4},{6,7},{7,6},{8,9},{9,8},{10,11... | collective-permute-start | bytes 835592 | tf_op jit(solution)/shard_map/ppermute | solution.py:262
  67.5 1.2 collective-permute-done.6
  68.7 15.4 %all_to_all.37 = f32[32,1,2176]{2,1,0:T(1,128)S(1)} all-to-all(f32[32,1,2176]{2,1,0:T(1,128)S(1)} %bitcast.36), channel_id=1, replica_groups={{0,2,4,6,8,10,12,14,16,18,20,22,24,26,28,30,32,34,36,38,40,42,44,46,48,..., dimensions={0} | all-to-all | bytes 557056 | tf_op jit(solution)/shard_map/all_to_all | solution.py:268
  84.1 14.9 %all_to_all.38 = f32[32,16,128]{2,1,0:T(8,128)S(1)} all-to-all(f32[32,16,128]{2,1,0:T(8,128)S(1)} %bitcast.31), channel_id=1, replica_groups={{0,2,4,6,8,10,12,14,16,18,20,22,24,26,28,30,32,34,36,38,40,42,44,46,48,..., dimensions={0} | all-to-all | bytes 524288 | tf_op jit(solution)/shard_map/all_to_all | solution.py:268
  99.0 3.5 %collective-permute-start.7 = (f32[512,128]{1,0:T(8,128)S(1)}, f32[512,128]{1,0:T(8,128)S(1)}, u32[]{:S(2)}, u32[]{:S(2)}) collective-permute-start(f32[512,128]{1,0:T(8,128)S(1)} %bitcast.26), channel_id=1, source_target_pairs={{0,1},{1,0},{2,3},{3,2},{4,5},{5,4},{6,7},{7,6},{8,9},{9,8},{10,11... | collective-permute-start | bytes 786440 | tf_op jit(solution)/shard_map/ppermute | solution.py:262
  102.5 1.2 collective-permute-done.7.refs_1_
  103.7 1.6 forward.4
  105.3 0.1 collective-permute-start.8
  105.4 1.4 collective-permute-start.10
  106.8 3.6 %collective-permute-done.8 = f32[72,512]{1,0:T(8,128)S(1)} collective-permute-done((f32[72,512]{1,0:T(8,128)S(1)}, f32[72,512]{1,0:T(8,128)S(1)}, u32[]{:S(2)}, u32[]{:S(2)}) %collective-permute-start.8) | collective-permute-done | bytes 147488 | tf_op jit(solution)/shard_map/ppermute | solution.py:272
  110.5 1.4 collective-permute-start.9
  111.9 0.1 collective-permute-start.11
  112.0 3.8 %collective-permute-done.11.refs_3_ = f32[64,512]{1,0:T(8,128)S(1)} collective-permute-done((f32[64,512]{1,0:T(8,128)S(1)}, f32[64,512]{1,0:T(8,128)S(1)}, u32[]{:S(2)}, u32[]{:S(2)}) %collective-permute-start.11) | collective-permute-done | bytes 131104 | tf_op jit(solution)/shard_map/ppermute | solution.py:272
  115.8 1.3 back.3
  117.2 2.7 %collective-permute-start.12 = (f32[544,128]{1,0:T(8,128)S(1)}, f32[544,128]{1,0:T(8,128)S(1)}, u32[]{:S(2)}, u32[]{:S(2)}) collective-permute-start(f32[544,128]{1,0:T(8,128)S(1)} %get-tuple-element.61), channel_id=1, source_target_pairs={{0,1},{1,0},{2,3},{3,2},{4,5},{5,4},{6,7},{7,6},{8,9},{9,8},{10,11... | collective-permute-start | bytes 835592 | tf_op jit(solution)/shard_map/ppermute | solution.py:262
  119.9 1.2 collective-permute-done.12
  121.1 15.4 %all_to_all.39 = f32[32,1,2176]{2,1,0:T(1,128)S(1)} all-to-all(f32[32,1,2176]{2,1,0:T(1,128)S(1)} %bitcast.37), channel_id=1, replica_groups={{0,2,4,6,8,10,12,14,16,18,20,22,24,26,28,30,32,34,36,38,40,42,44,46,48,..., dimensions={0} | all-to-all | bytes 557056 | tf_op jit(solution)/shard_map/all_to_all | solution.py:268
  136.5 14.7 %all_to_all.40 = f32[32,16,128]{2,1,0:T(8,128)S(1)} all-to-all(f32[32,16,128]{2,1,0:T(8,128)S(1)} %bitcast.32), channel_id=1, replica_groups={{0,2,4,6,8,10,12,14,16,18,20,22,24,26,28,30,32,34,36,38,40,42,44,46,48,..., dimensions={0} | all-to-all | bytes 524288 | tf_op jit(solution)/shard_map/all_to_all | solution.py:268
  151.2 3.5 %collective-permute-start.13 = (f32[512,128]{1,0:T(8,128)S(1)}, f32[512,128]{1,0:T(8,128)S(1)}, u32[]{:S(2)}, u32[]{:S(2)}) collective-permute-start(f32[512,128]{1,0:T(8,128)S(1)} %bitcast.24), channel_id=1, source_target_pairs={{0,1},{1,0},{2,3},{3,2},{4,5},{5,4},{6,7},{7,6},{8,9},{9,8},{10,11... | collective-permute-start | bytes 786440 | tf_op jit(solution)/shard_map/ppermute | solution.py:262
  154.7 1.2 collective-permute-done.13.refs_1_
  155.9 1.6 forward.5
  157.5 0.1 collective-permute-start.14
  157.6 1.4 collective-permute-start.16
  159.1 3.6 %collective-permute-done.14 = f32[72,512]{1,0:T(8,128)S(1)} collective-permute-done((f32[72,512]{1,0:T(8,128)S(1)}, f32[72,512]{1,0:T(8,128)S(1)}, u32[]{:S(2)}, u32[]{:S(2)}) %collective-permute-start.14) | collective-permute-done | bytes 147488 | tf_op jit(solution)/shard_map/ppermute | solution.py:272
  162.7 1.4 collective-permute-start.15
  164.2 0.1 collective-permute-start.17
  164.3 3.8 %collective-permute-done.17.h3 = f32[64,512]{1,0:T(8,128)S(1)} collective-permute-done((f32[64,512]{1,0:T(8,128)S(1)}, f32[64,512]{1,0:T(8,128)S(1)}, u32[]{:S(2)}, u32[]{:S(2)}) %collective-permute-start.17) | collective-permute-done | bytes 131104 | tf_op jit(solution)/shard_map/ppermute | solution.py:272
  168.1 0.3 last_image.1
  168.3 11.9 %all_to_all.41 = f32[32,1,128]{2,1,0:T(1,128)S(1)} all-to-all(f32[32,1,128]{2,1,0:T(1,128)S(1)} %bitcast.35), channel_id=1, replica_groups={{0,2,4,6,8,10,12,14,16,18,20,22,24,26,28,30,32,34,36,38,40,42,44,46,48,..., dimensions={0} | all-to-all | bytes 32768 | tf_op jit(solution)/shard_map/all_to_all | solution.py:268
  180.3 4.1 %collective-permute-start.18 = (f32[32,128]{1,0:T(8,128)S(1)}, f32[32,128]{1,0:T(8,128)S(1)}, u32[]{:S(2)}, u32[]{:S(2)}) collective-permute-start(f32[32,128]{1,0:T(8,128)S(1)} %bitcast.33), channel_id=1, source_target_pairs={{0,1},{1,0},{2,3},{3,2},{4,5},{5,4},{6,7},{7,6},{8,9},{9,8},{10,11... | collective-permute-start | bytes 49160 | tf_op jit(solution)/shard_map/ppermute | solution.py:262
  184.3 0.7 prepare.1
  185.0 0.1 collective-permute-done.18.other
  185.2 1.0 finish.1
  (20 shorter events, 0.3 us)
Async XLA Ops:
  4.8 4.6 %collective-permute-start = (f32[512,128]{1,0:T(8,128)S(1)}, f32[512,128]{1,0:T(8,128)S(1)}, u32[]{:S(2)}, u32[]{:S(2)}) collective-permute-start(f32[512,128]{1,0:T(8,128)S(1)} %get-tuple-element.43), channel_id=1, source_target_pairs={{0,1},{1,0},{2,3},{3,2},{4,5},{5,4},{6,7},{7,6},{8,9},{9,8},{10,11... | collective-permute-start | bytes 786440 | tf_op jit(solution)/shard_map/ppermute | solution.py:262
  45.4 5.0 %collective-permute-start.1 = (f32[512,128]{1,0:T(8,128)S(1)}, f32[512,128]{1,0:T(8,128)S(1)}, u32[]{:S(2)}, u32[]{:S(2)}) collective-permute-start(f32[512,128]{1,0:T(8,128)S(1)} %bitcast.22), channel_id=1, source_target_pairs={{0,1},{1,0},{2,3},{3,2},{4,5},{5,4},{6,7},{7,6},{8,9},{9,8},{10,11... | collective-permute-start | bytes 786440 | tf_op jit(solution)/shard_map/ppermute | solution.py:262
  51.8 5.6 %collective-permute-start.2 = (f32[72,512]{1,0:T(8,128)S(1)}, f32[72,512]{1,0:T(8,128)S(1)}, u32[]{:S(2)}, u32[]{:S(2)}) collective-permute-start(f32[72,512]{1,0:T(8,128)S(1)} %get-tuple-element.49), channel_id=1, source_target_pairs={{0,64},{64,0},{128,192},{192,128},{1,65},{65,1},{129,193},{193,129... | collective-permute-start | bytes 442376 | tf_op jit(solution)/shard_map/ppermute | solution.py:272
  53.1 6.9 %collective-permute-start.4 = (f32[64,512]{1,0:T(8,128)S(1)}, f32[64,512]{1,0:T(8,128)S(1)}, u32[]{:S(2)}, u32[]{:S(2)}) collective-permute-start(f32[64,512]{1,0:T(8,128)S(1)} %get-tuple-element.50), channel_id=1, source_target_pairs={{0,192},{64,128},{128,64},{192,0},{1,193},{65,129},{129,65},{193,1... | collective-permute-start | bytes 393224 | tf_op jit(solution)/shard_map/ppermute | solution.py:272
  57.4 6.8 %collective-permute-start.3 = (f32[72,512]{1,0:T(8,128)S(1)}, f32[72,512]{1,0:T(8,128)S(1)}, u32[]{:S(2)}, u32[]{:S(2)}) collective-permute-start(f32[72,512]{1,0:T(8,128)S(1)} %add.29.refs_0_), channel_id=1, source_target_pairs={{0,192},{64,128},{128,64},{192,0},{1,193},{65,129},{129,65},{193,1... | collective-permute-start | bytes 442376 | tf_op jit(solution)/shard_map/ppermute | solution.py:272
  60.0 4.2 %collective-permute-start.5 = (f32[64,512]{1,0:T(8,128)S(1)}, f32[64,512]{1,0:T(8,128)S(1)}, u32[]{:S(2)}, u32[]{:S(2)}) collective-permute-start(f32[64,512]{1,0:T(8,128)S(1)} %add.30.refs_2_), channel_id=1, source_target_pairs={{0,64},{64,0},{128,192},{192,128},{1,65},{65,1},{129,193},{193,129... | collective-permute-start | bytes 393224 | tf_op jit(solution)/shard_map/ppermute | solution.py:272
  65.5 3.2 %collective-permute-start.6 = (f32[544,128]{1,0:T(8,128)S(1)}, f32[544,128]{1,0:T(8,128)S(1)}, u32[]{:S(2)}, u32[]{:S(2)}) collective-permute-start(f32[544,128]{1,0:T(8,128)S(1)} %get-tuple-element.52), channel_id=1, source_target_pairs={{0,1},{1,0},{2,3},{3,2},{4,5},{5,4},{6,7},{7,6},{8,9},{9,8},{10,11... | collective-permute-start | bytes 835592 | tf_op jit(solution)/shard_map/ppermute | solution.py:262
  99.0 4.6 %collective-permute-start.7 = (f32[512,128]{1,0:T(8,128)S(1)}, f32[512,128]{1,0:T(8,128)S(1)}, u32[]{:S(2)}, u32[]{:S(2)}) collective-permute-start(f32[512,128]{1,0:T(8,128)S(1)} %bitcast.26), channel_id=1, source_target_pairs={{0,1},{1,0},{2,3},{3,2},{4,5},{5,4},{6,7},{7,6},{8,9},{9,8},{10,11... | collective-permute-start | bytes 786440 | tf_op jit(solution)/shard_map/ppermute | solution.py:262
  105.3 5.1 %collective-permute-start.8 = (f32[72,512]{1,0:T(8,128)S(1)}, f32[72,512]{1,0:T(8,128)S(1)}, u32[]{:S(2)}, u32[]{:S(2)}) collective-permute-start(f32[72,512]{1,0:T(8,128)S(1)} %get-tuple-element.57), channel_id=1, source_target_pairs={{0,64},{64,0},{128,192},{192,128},{1,65},{65,1},{129,193},{193,129... | collective-permute-start | bytes 442376 | tf_op jit(solution)/shard_map/ppermute | solution.py:272
  105.4 6.5 %collective-permute-start.10 = (f32[64,512]{1,0:T(8,128)S(1)}, f32[64,512]{1,0:T(8,128)S(1)}, u32[]{:S(2)}, u32[]{:S(2)}) collective-permute-start(f32[64,512]{1,0:T(8,128)S(1)} %get-tuple-element.58), channel_id=1, source_target_pairs={{0,192},{64,128},{128,64},{192,0},{1,193},{65,129},{129,65},{193,1... | collective-permute-start | bytes 393224 | tf_op jit(solution)/shard_map/ppermute | solution.py:272
  110.5 5.4 %collective-permute-start.9 = (f32[72,512]{1,0:T(8,128)S(1)}, f32[72,512]{1,0:T(8,128)S(1)}, u32[]{:S(2)}, u32[]{:S(2)}) collective-permute-start(f32[72,512]{1,0:T(8,128)S(1)} %add.32.refs_0_), channel_id=1, source_target_pairs={{0,192},{64,128},{128,64},{192,0},{1,193},{65,129},{129,65},{193,1... | collective-permute-start | bytes 442376 | tf_op jit(solution)/shard_map/ppermute | solution.py:272
  111.9 3.9 %collective-permute-start.11 = (f32[64,512]{1,0:T(8,128)S(1)}, f32[64,512]{1,0:T(8,128)S(1)}, u32[]{:S(2)}, u32[]{:S(2)}) collective-permute-start(f32[64,512]{1,0:T(8,128)S(1)} %add.33.refs_2_), channel_id=1, source_target_pairs={{0,64},{64,0},{128,192},{192,128},{1,65},{65,1},{129,193},{193,129... | collective-permute-start | bytes 393224 | tf_op jit(solution)/shard_map/ppermute | solution.py:272
  117.2 3.9 %collective-permute-start.12 = (f32[544,128]{1,0:T(8,128)S(1)}, f32[544,128]{1,0:T(8,128)S(1)}, u32[]{:S(2)}, u32[]{:S(2)}) collective-permute-start(f32[544,128]{1,0:T(8,128)S(1)} %get-tuple-element.61), channel_id=1, source_target_pairs={{0,1},{1,0},{2,3},{3,2},{4,5},{5,4},{6,7},{7,6},{8,9},{9,8},{10,11... | collective-permute-start | bytes 835592 | tf_op jit(solution)/shard_map/ppermute | solution.py:262
  151.2 4.6 %collective-permute-start.13 = (f32[512,128]{1,0:T(8,128)S(1)}, f32[512,128]{1,0:T(8,128)S(1)}, u32[]{:S(2)}, u32[]{:S(2)}) collective-permute-start(f32[512,128]{1,0:T(8,128)S(1)} %bitcast.24), channel_id=1, source_target_pairs={{0,1},{1,0},{2,3},{3,2},{4,5},{5,4},{6,7},{7,6},{8,9},{9,8},{10,11... | collective-permute-start | bytes 786440 | tf_op jit(solution)/shard_map/ppermute | solution.py:262
  157.5 5.1 %collective-permute-start.14 = (f32[72,512]{1,0:T(8,128)S(1)}, f32[72,512]{1,0:T(8,128)S(1)}, u32[]{:S(2)}, u32[]{:S(2)}) collective-permute-start(f32[72,512]{1,0:T(8,128)S(1)} %get-tuple-element.67), channel_id=1, source_target_pairs={{0,64},{64,0},{128,192},{192,128},{1,65},{65,1},{129,193},{193,129... | collective-permute-start | bytes 442376 | tf_op jit(solution)/shard_map/ppermute | solution.py:272
  157.6 6.5 %collective-permute-start.16 = (f32[64,512]{1,0:T(8,128)S(1)}, f32[64,512]{1,0:T(8,128)S(1)}, u32[]{:S(2)}, u32[]{:S(2)}) collective-permute-start(f32[64,512]{1,0:T(8,128)S(1)} %get-tuple-element.68), channel_id=1, source_target_pairs={{0,192},{64,128},{128,64},{192,0},{1,193},{65,129},{129,65},{193,1... | collective-permute-start | bytes 393224 | tf_op jit(solution)/shard_map/ppermute | solution.py:272
  162.7 5.4 %collective-permute-start.15 = (f32[72,512]{1,0:T(8,128)S(1)}, f32[72,512]{1,0:T(8,128)S(1)}, u32[]{:S(2)}, u32[]{:S(2)}) collective-permute-start(f32[72,512]{1,0:T(8,128)S(1)} %add.35.h0), channel_id=1, source_target_pairs={{0,192},{64,128},{128,64},{192,0},{1,193},{65,129},{129,65},{193,1... | collective-permute-start | bytes 442376 | tf_op jit(solution)/shard_map/ppermute | solution.py:272
  164.2 3.9 %collective-permute-start.17 = (f32[64,512]{1,0:T(8,128)S(1)}, f32[64,512]{1,0:T(8,128)S(1)}, u32[]{:S(2)}, u32[]{:S(2)}) collective-permute-start(f32[64,512]{1,0:T(8,128)S(1)} %add.36.h2), channel_id=1, source_target_pairs={{0,64},{64,0},{128,192},{192,128},{1,65},{65,1},{129,193},{193,129... | collective-permute-start | bytes 393224 | tf_op jit(solution)/shard_map/ppermute | solution.py:272
  180.3 4.9 %collective-permute-start.18 = (f32[32,128]{1,0:T(8,128)S(1)}, f32[32,128]{1,0:T(8,128)S(1)}, u32[]{:S(2)}, u32[]{:S(2)}) collective-permute-start(f32[32,128]{1,0:T(8,128)S(1)} %bitcast.33), channel_id=1, source_target_pairs={{0,1},{1,0},{2,3},{3,2},{4,5},{5,4},{6,7},{7,6},{8,9},{9,8},{10,11... | collective-permute-start | bytes 49160 | tf_op jit(solution)/shard_map/ppermute | solution.py:262

commit v6 on v5

--- a/solution.py
+++ b/solution.py
@@ -9,7 +9,7 @@
 
 ITERS = 3
 ridge = 0.5
-CORES, LANES, TILE = 2, 128, 8
+CORES, BLOCK, LANES, TILE = 2, 8, 128, 8
 WIDE, FETCH = 256, 512
 MIB = 1 << 20
 F32, BF16 = jnp.float32, jnp.bfloat16
@@ -149,11 +149,12 @@
         p = rows_product(x2, high, low, pl.ds(t * WIDE, WIDE))
         store_pieces(mine, theirs, p, t, stride)
     extra = jnp.broadcast_to(image_sq, (half, LANES))
-    mine[pl.ds(stride - 1, half, stride=stride), :] = extra
-    theirs[pl.ds(stride - 1, half, stride=stride), :] = extra
-
-
-def last_image(h0, h1, h2, h3, before, scal, image_out, scal_out, squares):
+    for j in range(high.shape[1] // LANES, stride):
+        mine[pl.ds(j, half, stride=stride), :] = extra
+        theirs[pl.ds(j, half, stride=stride), :] = extra
+
+
+def last_image(h0, h1, h2, h3, before, scal, token, image_out, scal_out, squares):
     _, image_sq = step_image((h0, h1, h2, h3), before, scal, image_out, scal_out)
     squares[...] = jnp.broadcast_to(image_sq, squares.shape)
 
@@ -162,29 +163,31 @@
     return scal[0:1, :] / (image_sq + ridge * scal[2:3, :])
 
 
-def sum_pieces(got, out, rows):
-    count = out.shape[0] // rows
-    stride = got.shape[0] // count
-    terms = [got[i * stride : (i + 1) * stride, :] for i in range(count)]
+def add_pieces(a, b, token, out):
+    out[...] = a[...] + b[...]
+
+
+def sum_pieces(got, out):
+    n = out.shape[0]
+    terms = [got[i * n : (i + 1) * n, :] for i in range(got.shape[0] // n)]
     while len(terms) > 1:
         terms = [terms[i] + terms[i + 1] for i in range(0, len(terms), 2)]
-    total = terms[0]
-    for i in range(count):
-        out[i * rows : (i + 1) * rows, :] = total[:rows]
-    return total
-
-
-def add_pieces(a, b, token, out):
-    out[...] = a[...] + b[...]
-
-
-def reduce_first(got, out, rows):
-    sum_pieces(got, out, rows)
-
-
-def reduce_pieces(got, scal, out, size, rows):
-    total = sum_pieces(got, out, rows)
-    size[...] = jnp.broadcast_to(step_size(total[rows : rows + 1], scal), size.shape)
+    out[...] = terms[0]
+
+
+def sum_blocks(*refs, rows, copies):
+    a, b, *rest = refs
+    total = a[...] + b[...]
+    out = rest[-2] if len(rest) == 3 else rest[-1]
+    n = out.shape[0] // copies
+    stride = total.shape[0] // (n // rows)
+    for i in range(n // rows):
+        part = total[i * stride : i * stride + rows]
+        for k in range(copies):
+            out[k * n + i * rows : k * n + (i + 1) * rows, :] = part
+    if len(rest) == 3:
+        scal, _, size = rest
+        size[...] = jnp.broadcast_to(step_size(total[rows : rows + 1], scal), size.shape)
 
 
 def forward(*refs, step):
@@ -219,30 +222,29 @@
     a[n + 1 :, :] = rest if cross is None else rest + cross
 
 
-def prepare(core, scal, size0, size1, d0, d1, g2, i0, i1, i2, targets, readout, direction, residual, image, sums):
+def prepare(core, size0, size1, d0, d1, g2, i0, i1, targets, readout, before, gradient, residual, token, sums):
     own = core[0, 0] == 0
     n = targets.shape[0]
     stride = d0.shape[0] // n
     s0, s1 = size0[0:1, :], size1[0:1, :]
-    for value, out in (
-        (s0 * d0[...] + s1 * d1[...], readout),
-        (g2[...] + scal[1:2, :] * d1[...], direction),
-    ):
-        sums[...] = value
+    sums[...] = s0 * d0[...] + s1 * d1[...]
+    for source, out in ((sums, readout), (d1, before), (g2, gradient)):
         for j in range(stride):
             out[:, pl.ds(j * LANES, LANES)] = own_half_first(
-                sums[pl.ds(j, n, stride=stride), :], own
+                source[pl.ds(j, n, stride=stride), :], own
             )
     r = targets[...] - s0[:, :1] * i0[...] - s1[:, :1] * i1[...]
     residual[...] = own_half_first(r, own)
-    image[...] = own_half_first(i2[...], own)
-
-
-def finish(got, other, scal, readout_part, direction, residual_part, image, readout, residual):
-    image_sq = jnp.sum(got[...] + other[...], axis=0, keepdims=True)
+    token[...] = jnp.zeros(token.shape, F32)
+
+
+def finish(core, squares, others, scal, image, readout_part, before, gradient, residual_part, readout, residual):
+    image_sq = jnp.sum(squares[...] + others[...], axis=0, keepdims=True)
     size = step_size(image_sq, scal)[:, :1]
-    readout[...] = readout_part[...] + size * direction[...]
-    residual[...] = residual_part[...] - size * image[...]
+    beta = scal[1:2, :1]
+    readout[...] = readout_part[...] + size * (gradient[...] + beta * before[...])
+    last = own_half_first(image[...], core[0, 0] == 0)
+    residual[...] = residual_part[...] - size * last
 
 
 def shards(states, targets):
@@ -253,20 +255,42 @@
     chips = samp_count // CORES
     half = outputs // CORES
     rows = units // LANES
+    vector = shape(TILE, LANES)
     core = jnp.full((1, 1), lax.axis_index("samp") % CORES, jnp.int32)
 
     swap_cores = [(i, i ^ 1) for i in range(samp_count)]
-    groups = [[chip * CORES + c for chip in range(chips)] for c in range(CORES)]
+    blocks = chips // BLOCK
+    assert blocks == 4
+    groups = [
+        [(block * BLOCK + chip) * CORES + c for chip in range(BLOCK)]
+        for block in range(blocks)
+        for c in range(CORES)
+    ]
 
     def swap(x):
         return lax.ppermute(x, "samp", swap_cores)
 
     def exchange(x):
         n = x.shape[0]
-        parts = (half, rows, LANES) if n == half * rows else (half, 1, n // half * LANES)
-        x = x.reshape(parts)
+        x = x.reshape(BLOCK, n // BLOCK, LANES)
         x = lax.all_to_all(x, "samp", 0, 0, axis_index_groups=groups, tiled=True)
         return x.reshape(n, LANES)
+
+    def block_hop(x, mask):
+        step = BLOCK * CORES
+        return lax.ppermute(x, "samp", [(i, i ^ (mask * step)) for i in range(samp_count)])
+
+    def block_terms(x):
+        x = x + block_hop(x, 1)
+        return x, block_hop(x, 3)
+
+    def sum_samples(pieces, scal):
+        n = pieces.shape[0] // BLOCK
+        terms = block_terms(call(sum_pieces, shape(n, LANES), exchange(pieces)))
+        outs = [shape(half * rows, LANES)] + ([] if scal is None else [vector])
+        scals = [] if scal is None else [scal]
+        outs = call(sum_blocks, outs, *terms, *scals, rows=rows, copies=BLOCK)
+        return outs[0], outs[-1]
 
     def unit_hop(x, mask):
         return lax.ppermute(x, "unit", [(i, i ^ mask) for i in range(unit_count)])
@@ -275,7 +299,6 @@
         a, b = a + unit_hop(a, 1), b + unit_hop(b, 3)
         return a, unit_hop(a, 3), b, unit_hop(b, 1)
 
-    vector = shape(TILE, LANES)
     image_shape = shape(outputs, samples)
     whole = shape(outputs * rows, LANES)
     partial = [shape(outputs + TILE, samples // 2), shape(outputs, samples // 2)]
@@ -304,8 +327,7 @@
     ]
     high_turned, low_turned = here(high_turned), here(low_turned)
     pieces = call(add_pieces, shape(half * rows, LANES), mine, swap(theirs), token)
-    got = exchange(pieces)
-    spread = call(reduce_first, shape(half * rows, LANES), got, rows=rows)
+    spread, _ = sum_samples(pieces, None)
 
     gradients, directions, images, sizes = [], [], [], []
     scal = size = None
@@ -343,7 +365,7 @@
         hops = unit_terms(*terms)
         olds = [images[-1], scal] if step else []
         if step + 1 < ITERS:
-            piece = shape(half * (rows + 1), LANES)
+            piece = shape(half * (rows + 2), LANES)
             image, scal, mine, theirs = call(
                 back,
                 [image_shape, vector, piece, piece],
@@ -355,38 +377,44 @@
                 flops=flops,
             )
             images.append(image)
-            got = exchange(mine + swap(theirs))
-            spread, size = call(
-                reduce_pieces,
-                [shape(half * rows, LANES), vector],
-                got,
-                scal,
-                rows=rows,
-            )
+            spread, size = sum_samples(mine + swap(theirs), scal)
             sizes.append(size)
         else:
+            *parts, token = call(
+                prepare,
+                [shape(outputs, units)] * 3 + [image_shape, vector],
+                core,
+                *sizes,
+                *directions,
+                gradients[-1],
+                *images,
+                turned,
+                specs=[smem] + [VMEM] * 8,
+                scratch=[pltpu.VMEM((outputs * rows, LANES), F32)],
+                flops=flops // 4,
+            )
             image, scal, squares = call(
-                last_image, [image_shape, vector, shape(half, LANES)], *hops, *olds
-            )
-            images.append(image)
-            got = exchange(squares)
-            other = swap(got)
-    parts = call(
-        prepare,
-        [shape(outputs, units)] * 2 + [image_shape] * 2,
+                last_image, [image_shape, vector, shape(chips, LANES)], *hops, *olds, token
+            )
+    all_chips = [[chip * CORES + c for chip in range(chips)] for c in range(CORES)]
+    squares = lax.all_to_all(
+        squares.reshape(chips, 1, LANES),
+        "samp",
+        0,
+        0,
+        axis_index_groups=all_chips,
+        tiled=True,
+    ).reshape(chips, LANES)
+    readout, residual = call(
+        finish,
+        [shape(outputs, units), image_shape],
         core,
+        squares,
+        swap(squares),
         scal,
-        *sizes,
-        *directions,
-        gradients[-1],
-        *images,
-        turned,
-        specs=[smem] + [VMEM] * 10,
-        scratch=[pltpu.VMEM((outputs * rows, LANES), F32)],
-        flops=flops,
-    )
-    readout, residual = call(
-        finish, [shape(outputs, units), image_shape], got, other, scal, *parts
+        image,
+        *parts,
+        specs=[smem] + [VMEM] * 8,
     )
     return readout.T, residual.T
 

time: 187 us -> 182 us (0.973)
  blocking collectives: 108 us -> 71.2 us
  starting transfers between devices: 34.2 us -> 54.4 us
  waiting for transfers between devices: 26.3 us -> 38.7 us
    all_to_all x7 -> x6, blocking collectives: 108 us -> 56.7 us  [exchange(): x = lax.all_to_all(x, 'samp', 0, 0, axis_index_groups=groups, tiled=True)]
    ppermute x0 -> x6, starting transfers between devices: none -> 16.5 us  [block_hop(): lax.ppermute(x, 'samp', [(i, i ^ mask * step) for i in range(samp_count)])]
    all_to_all x0 -> x1, blocking collectives: none -> 14.5 us  [shards(): lax.all_to_all(squares.reshape(chips, 1, LANES), 'samp', 0, 0, axis_index...]
    ppermute x0 -> x6, waiting for transfers between devices: none -> 12.1 us  [block_hop(): lax.ppermute(x, 'samp', [(i, i ^ mask * step) for i in range(samp_count)])]
    ppermute x7, starting transfers between devices: 22.4 us -> 25.8 us  [swap(): return lax.ppermute(x, 'samp', swap_cores)]
    pallas_call x15 -> x18, Pallas kernels: 16.6 us -> 16.7 us  [call(): pl.pallas_call(functools.partial(kernel, **static), in_specs=specs or [VM...]
  transfers between devices with their start and end apart: 19 -> 25, of which waited for: 11 -> 17; matrix products, arithmetic and copies ran while one was open for 0% -> 0% of each run, Pallas kernels for 2% -> 2%
where the time goes in v6:
time: 182 us
  blocking collectives  71.2 us (39%)
  starting transfers between devices  54.4 us (30%)
  waiting for transfers between devices  38.7 us (21%)
  Pallas kernels  16.7 us (9%)
    all_to_all x6, blocking collectives, exchange(): x = lax.all_to_all(x, 'samp', 0, 0, axis_index_groups=groups, tiled=True)  56.7 us
    ppermute x7, starting transfers between devices, swap(): return lax.ppermute(x, 'samp', swap_cores)  25.8 us
    ppermute x12, waiting for transfers between devices, unit_hop(): return lax.ppermute(x, 'unit', [(i, i ^ mask) for i in range(unit_count)])  21 us
    pallas_call x18, Pallas kernels, call(): pl.pallas_call(functools.partial(kernel, **static), in_specs=specs or [VM...  16.7 us
    ppermute x6, starting transfers between devices, block_hop(): lax.ppermute(x, 'samp', [(i, i ^ mask * step) for i in range(samp_count)])  16.5 us
    all_to_all x1, blocking collectives, shards(): lax.all_to_all(squares.reshape(chips, 1, LANES), 'samp', 0, 0, axis_index...  14.5 us
    ppermute x6, waiting for transfers between devices, block_hop(): lax.ppermute(x, 'samp', [(i, i ^ mask * step) for i in range(samp_count)])  12.1 us
    ppermute x12, starting transfers between devices, unit_hop(): return lax.ppermute(x, 'unit', [(i, i ^ mask) for i in range(unit_count)])  12.1 us
  transfers between devices with their start and end apart: 25, of which 17 were waited for; matrix products, arithmetic and copies ran while one was open for 0% of the time, Pallas kernels for 2%

profile of v6, /device:TPU:1, one launch (start us, length us, event | category | flops | bytes accessed | tf_op | source)
XLA Modules:
  0.0 182.1 jit_solution(216740641144511688)
XLA Ops:
  0.6 4.2 %first.1 = (bf16[1024,2048]{1,0:T(8,128)(2,1)S(1)}, bf16[1024,2048]{1,0:T(8,128)(2,1)S(1)}, f32[64,1024]{1,0:T(8,128)S(1)}, f32[512,128]{1,0:T(8,128)S(1)}, f32[512,128]{1,0:T(8,128)S(1)}) custom-call(s32[1,1]{1,0:T(1,128)} %bitcast.core, f32[1024,2048]{1,0:T(8,128)} %states.1, f32[64,1024]{1,0:T(8,128)} %bitcast.38), custom_call_target="tpu_custom_call" | custom-call | flops 1073741824 | bytes 1048576 | tf_op jit(solution)/shard_map/first/pallas_call | solution.py:29
  4.8 3.3 %collective-permute-start = (f32[512,128]{1,0:T(8,128)S(1)}, f32[512,128]{1,0:T(8,128)S(1)}, u32[]{:S(2)}, u32[]{:S(2)}) collective-permute-start(f32[512,128]{1,0:T(8,128)S(1)} %get-tuple-element.44), channel_id=1, source_target_pairs={{0,1},{1,0},{2,3},{3,2},{4,5},{5,4},{6,7},{7,6},{8,9},{9,8},{10,11... | collective-permute-start | bytes 786440 | tf_op jit(solution)/shard_map/ppermute | solution.py:271
  8.2 1.2 turn_states.2
  9.5 9.8 %all_to_all.35 = f32[8,64,128]{2,1,0:T(8,128)S(1)} all-to-all(f32[8,64,128]{2,1,0:T(8,128)S(1)} %bitcast.28), channel_id=1, replica_groups={{0,2,4,6,8,10,12,14},{1,3,5,7,9,11,13,15},{16,18,20,22,24,26,28,30},{17..., dimensions={0} | all-to-all | bytes 524288 | tf_op jit(solution)/shard_map/all_to_all | solution.py:276
  19.3 3.1 %collective-permute-start.1 = (f32[64,128]{1,0:T(8,128)S(1)}, f32[64,128]{1,0:T(8,128)S(1)}, u32[]{:S(2)}, u32[]{:S(2)}) collective-permute-start(f32[64,128]{1,0:T(8,128)S(1)} %sum_pieces.3), channel_id=1, source_target_pairs={{0,16},{1,17},{2,18},{3,19},{4,20},{5,21},{6,22},{7,23},{8,24},{9,... | collective-permute-start | bytes 98312 | tf_op jit(solution)/shard_map/ppermute | solution.py:281
  22.4 1.6 collective-permute-done.1
  24.0 4.2 %collective-permute-start.2 = (f32[64,128]{1,0:T(8,128)S(1)}, f32[64,128]{1,0:T(8,128)S(1)}, u32[]{:S(2)}, u32[]{:S(2)}) collective-permute-start(f32[64,128]{1,0:T(8,128)S(1)} %add.38.refs_0_), channel_id=1, source_target_pairs={{0,48},{1,49},{2,50},{3,51},{4,52},{5,53},{6,54},{7,55},{8,56},{9,... | collective-permute-start | bytes 98312 | tf_op jit(solution)/shard_map/ppermute | solution.py:281
  28.2 1.6 collective-permute-done.2.refs_1_
  29.9 9.3 %all_to_all.36 = f32[8,64,128]{2,1,0:T(8,128)S(1)} all-to-all(f32[8,64,128]{2,1,0:T(8,128)S(1)} %bitcast.29), channel_id=1, replica_groups={{0,2,4,6,8,10,12,14},{1,3,5,7,9,11,13,15},{16,18,20,22,24,26,28,30},{17..., dimensions={0} | all-to-all | bytes 524288 | tf_op jit(solution)/shard_map/all_to_all | solution.py:276
  39.2 4.8 %collective-permute-start.3 = (f32[512,128]{1,0:T(8,128)S(1)}, f32[512,128]{1,0:T(8,128)S(1)}, u32[]{:S(2)}, u32[]{:S(2)}) collective-permute-start(f32[512,128]{1,0:T(8,128)S(1)} %bitcast.22), channel_id=1, source_target_pairs={{0,1},{1,0},{2,3},{3,2},{4,5},{5,4},{6,7},{7,6},{8,9},{9,8},{10,11... | collective-permute-start | bytes 786440 | tf_op jit(solution)/shard_map/ppermute | solution.py:271
  44.0 1.8 turn_states.3
  45.7 1.4 forward.3
  47.1 1.3 collective-permute-start.4
  48.4 1.8 collective-permute-start.6
  50.2 2.5 %collective-permute-done.4 = f32[72,512]{1,0:T(8,128)S(1)} collective-permute-done((f32[72,512]{1,0:T(8,128)S(1)}, f32[72,512]{1,0:T(8,128)S(1)}, u32[]{:S(2)}, u32[]{:S(2)}) %collective-permute-start.4) | collective-permute-done | bytes 147488 | tf_op jit(solution)/shard_map/ppermute | solution.py:296
  52.7 2.6 %collective-permute-start.5 = (f32[72,512]{1,0:T(8,128)S(1)}, f32[72,512]{1,0:T(8,128)S(1)}, u32[]{:S(2)}, u32[]{:S(2)}) collective-permute-start(f32[72,512]{1,0:T(8,128)S(1)} %add.39.refs_0_), channel_id=1, source_target_pairs={{0,192},{64,128},{128,64},{192,0},{1,193},{65,129},{129,65},{193,1... | collective-permute-start | bytes 442376 | tf_op jit(solution)/shard_map/ppermute | solution.py:296
  55.4 4.1 %collective-permute-done.7.refs_3_ = f32[64,512]{1,0:T(8,128)S(1)} collective-permute-done((f32[64,512]{1,0:T(8,128)S(1)}, f32[64,512]{1,0:T(8,128)S(1)}, u32[]{:S(2)}, u32[]{:S(2)}) %collective-permute-start.7) | collective-permute-done | bytes 131104 | tf_op jit(solution)/shard_map/ppermute | solution.py:296
  59.5 1.3 back.2
  60.8 2.0 %collective-permute-start.8 = (f32[576,128]{1,0:T(8,128)S(1)}, f32[576,128]{1,0:T(8,128)S(1)}, u32[]{:S(2)}, u32[]{:S(2)}) collective-permute-start(f32[576,128]{1,0:T(8,128)S(1)} %get-tuple-element.53), channel_id=1, source_target_pairs={{0,1},{1,0},{2,3},{3,2},{4,5},{5,4},{6,7},{7,6},{8,9},{9,8},{10,11... | collective-permute-start | bytes 884744 | tf_op jit(solution)/shard_map/ppermute | solution.py:271
  62.8 1.2 collective-permute-done.8
  64.1 9.8 %all_to_all.37 = f32[8,72,128]{2,1,0:T(8,128)S(1)} all-to-all(f32[8,72,128]{2,1,0:T(8,128)S(1)} %bitcast.36), channel_id=1, replica_groups={{0,2,4,6,8,10,12,14},{1,3,5,7,9,11,13,15},{16,18,20,22,24,26,28,30},{17..., dimensions={0} | all-to-all | bytes 589824 | tf_op jit(solution)/shard_map/all_to_all | solution.py:276
  73.9 1.5 collective-permute-start.9
  75.4 2.7 %collective-permute-done.9 = f32[72,128]{1,0:T(8,128)S(1)} collective-permute-done((f32[72,128]{1,0:T(8,128)S(1)}, f32[72,128]{1,0:T(8,128)S(1)}, u32[]{:S(2)}, u32[]{:S(2)}) %collective-permute-start.9) | collective-permute-done | bytes 36896 | tf_op jit(solution)/shard_map/ppermute | solution.py:281
  78.1 3.2 %collective-permute-start.10 = (f32[72,128]{1,0:T(8,128)S(1)}, f32[72,128]{1,0:T(8,128)S(1)}, u32[]{:S(2)}, u32[]{:S(2)}) collective-permute-start(f32[72,128]{1,0:T(8,128)S(1)} %add.42.refs_0_), channel_id=1, source_target_pairs={{0,48},{1,49},{2,50},{3,51},{4,52},{5,53},{6,54},{7,55},{8,56},{9,... | collective-permute-start | bytes 110600 | tf_op jit(solution)/shard_map/ppermute | solution.py:281
  81.2 1.8 collective-permute-done.10.refs_1_
  83.0 9.0 %all_to_all.38 = f32[8,64,128]{2,1,0:T(8,128)S(1)} all-to-all(f32[8,64,128]{2,1,0:T(8,128)S(1)} %bitcast.31), channel_id=1, replica_groups={{0,2,4,6,8,10,12,14},{1,3,5,7,9,11,13,15},{16,18,20,22,24,26,28,30},{17..., dimensions={0} | all-to-all | bytes 524288 | tf_op jit(solution)/shard_map/all_to_all | solution.py:276
  92.0 4.5 %collective-permute-start.11 = (f32[512,128]{1,0:T(8,128)S(1)}, f32[512,128]{1,0:T(8,128)S(1)}, u32[]{:S(2)}, u32[]{:S(2)}) collective-permute-start(f32[512,128]{1,0:T(8,128)S(1)} %bitcast.26), channel_id=1, source_target_pairs={{0,1},{1,0},{2,3},{3,2},{4,5},{5,4},{6,7},{7,6},{8,9},{9,8},{10,11... | collective-permute-start | bytes 786440 | tf_op jit(solution)/shard_map/ppermute | solution.py:271
  97.7 1.6 forward.4
  99.4 1.4 collective-permute-start.14
  100.8 3.6 %collective-permute-done.12 = f32[72,512]{1,0:T(8,128)S(1)} collective-permute-done((f32[72,512]{1,0:T(8,128)S(1)}, f32[72,512]{1,0:T(8,128)S(1)}, u32[]{:S(2)}, u32[]{:S(2)}) %collective-permute-start.12) | collective-permute-done | bytes 147488 | tf_op jit(solution)/shard_map/ppermute | solution.py:296
  104.5 1.4 collective-permute-start.13
  106.0 3.8 %collective-permute-done.15.refs_3_ = f32[64,512]{1,0:T(8,128)S(1)} collective-permute-done((f32[64,512]{1,0:T(8,128)S(1)}, f32[64,512]{1,0:T(8,128)S(1)}, u32[]{:S(2)}, u32[]{:S(2)}) %collective-permute-start.15) | collective-permute-done | bytes 131104 | tf_op jit(solution)/shard_map/ppermute | solution.py:296
  109.8 1.3 back.3
  111.1 2.7 %collective-permute-start.16 = (f32[576,128]{1,0:T(8,128)S(1)}, f32[576,128]{1,0:T(8,128)S(1)}, u32[]{:S(2)}, u32[]{:S(2)}) collective-permute-start(f32[576,128]{1,0:T(8,128)S(1)} %get-tuple-element.62), channel_id=1, source_target_pairs={{0,1},{1,0},{2,3},{3,2},{4,5},{5,4},{6,7},{7,6},{8,9},{9,8},{10,11... | collective-permute-start | bytes 884744 | tf_op jit(solution)/shard_map/ppermute | solution.py:271
  115.1 9.6 %all_to_all.39 = f32[8,72,128]{2,1,0:T(8,128)S(1)} all-to-all(f32[8,72,128]{2,1,0:T(8,128)S(1)} %bitcast.37), channel_id=1, replica_groups={{0,2,4,6,8,10,12,14},{1,3,5,7,9,11,13,15},{16,18,20,22,24,26,28,30},{17..., dimensions={0} | all-to-all | bytes 589824 | tf_op jit(solution)/shard_map/all_to_all | solution.py:276
  124.8 1.5 collective-permute-start.17
  126.3 2.7 %collective-permute-done.17 = f32[72,128]{1,0:T(8,128)S(1)} collective-permute-done((f32[72,128]{1,0:T(8,128)S(1)}, f32[72,128]{1,0:T(8,128)S(1)}, u32[]{:S(2)}, u32[]{:S(2)}) %collective-permute-start.17) | collective-permute-done | bytes 36896 | tf_op jit(solution)/shard_map/ppermute | solution.py:281
  128.9 3.2 %collective-permute-start.18 = (f32[72,128]{1,0:T(8,128)S(1)}, f32[72,128]{1,0:T(8,128)S(1)}, u32[]{:S(2)}, u32[]{:S(2)}) collective-permute-start(f32[72,128]{1,0:T(8,128)S(1)} %add.46.refs_0_), channel_id=1, source_target_pairs={{0,48},{1,49},{2,50},{3,51},{4,52},{5,53},{6,54},{7,55},{8,56},{9,... | collective-permute-start | bytes 110600 | tf_op jit(solution)/shard_map/ppermute | solution.py:281
  132.1 1.7 collective-permute-done.18.refs_1_
  133.9 9.0 %all_to_all.40 = f32[8,64,128]{2,1,0:T(8,128)S(1)} all-to-all(f32[8,64,128]{2,1,0:T(8,128)S(1)} %bitcast.32), channel_id=1, replica_groups={{0,2,4,6,8,10,12,14},{1,3,5,7,9,11,13,15},{16,18,20,22,24,26,28,30},{17..., dimensions={0} | all-to-all | bytes 524288 | tf_op jit(solution)/shard_map/all_to_all | solution.py:276
  142.9 4.5 %collective-permute-start.19 = (f32[512,128]{1,0:T(8,128)S(1)}, f32[512,128]{1,0:T(8,128)S(1)}, u32[]{:S(2)}, u32[]{:S(2)}) collective-permute-start(f32[512,128]{1,0:T(8,128)S(1)} %bitcast.24), channel_id=1, source_target_pairs={{0,1},{1,0},{2,3},{3,2},{4,5},{5,4},{6,7},{7,6},{8,9},{9,8},{10,11... | collective-permute-start | bytes 786440 | tf_op jit(solution)/shard_map/ppermute | solution.py:271
  148.5 1.6 forward.5
  150.3 1.4 collective-permute-start.22
  151.7 3.6 %collective-permute-done.20 = f32[72,512]{1,0:T(8,128)S(1)} collective-permute-done((f32[72,512]{1,0:T(8,128)S(1)}, f32[72,512]{1,0:T(8,128)S(1)}, u32[]{:S(2)}, u32[]{:S(2)}) %collective-permute-start.20) | collective-permute-done | bytes 147488 | tf_op jit(solution)/shard_map/ppermute | solution.py:296
  155.3 1.7 collective-permute-start.21
  157.8 3.4 %collective-permute-done.23.h3 = f32[64,512]{1,0:T(8,128)S(1)} collective-permute-done((f32[64,512]{1,0:T(8,128)S(1)}, f32[64,512]{1,0:T(8,128)S(1)}, u32[]{:S(2)}, u32[]{:S(2)}) %collective-permute-start.23) | collective-permute-done | bytes 131104 | tf_op jit(solution)/shard_map/ppermute | solution.py:296
  161.5 14.5 %all_to_all.41 = f32[32,1,128]{2,1,0:T(1,128)S(1)} all-to-all(f32[32,1,128]{2,1,0:T(1,128)S(1)} %bitcast.35), channel_id=1, replica_groups={{0,2,4,6,8,10,12,14,16,18,20,22,24,26,28,30,32,34,36,38,40,42,44,46,48,..., dimensions={0} | all-to-all | bytes 32768 | tf_op jit(solution)/shard_map/all_to_all | solution.py:400
  176.1 4.1 %collective-permute-start.24 = (f32[32,128]{1,0:T(8,128)S(1)}, f32[32,128]{1,0:T(8,128)S(1)}, u32[]{:S(2)}, u32[]{:S(2)}) collective-permute-start(f32[32,128]{1,0:T(8,128)S(1)} %bitcast.33), channel_id=1, source_target_pairs={{0,1},{1,0},{2,3},{3,2},{4,5},{5,4},{6,7},{7,6},{8,9},{9,8},{10,11... | collective-permute-start | bytes 49160 | tf_op jit(solution)/shard_map/ppermute | solution.py:271
  (38 shorter events, 7.3 us)
Async XLA Ops:
  4.8 4.6 %collective-permute-start = (f32[512,128]{1,0:T(8,128)S(1)}, f32[512,128]{1,0:T(8,128)S(1)}, u32[]{:S(2)}, u32[]{:S(2)}) collective-permute-start(f32[512,128]{1,0:T(8,128)S(1)} %get-tuple-element.44), channel_id=1, source_target_pairs={{0,1},{1,0},{2,3},{3,2},{4,5},{5,4},{6,7},{7,6},{8,9},{9,8},{10,11... | collective-permute-start | bytes 786440 | tf_op jit(solution)/shard_map/ppermute | solution.py:271
  19.3 4.7 %collective-permute-start.1 = (f32[64,128]{1,0:T(8,128)S(1)}, f32[64,128]{1,0:T(8,128)S(1)}, u32[]{:S(2)}, u32[]{:S(2)}) collective-permute-start(f32[64,128]{1,0:T(8,128)S(1)} %sum_pieces.3), channel_id=1, source_target_pairs={{0,16},{1,17},{2,18},{3,19},{4,20},{5,21},{6,22},{7,23},{8,24},{9,... | collective-permute-start | bytes 98312 | tf_op jit(solution)/shard_map/ppermute | solution.py:281
  24.0 5.8 %collective-permute-start.2 = (f32[64,128]{1,0:T(8,128)S(1)}, f32[64,128]{1,0:T(8,128)S(1)}, u32[]{:S(2)}, u32[]{:S(2)}) collective-permute-start(f32[64,128]{1,0:T(8,128)S(1)} %add.38.refs_0_), channel_id=1, source_target_pairs={{0,48},{1,49},{2,50},{3,51},{4,52},{5,53},{6,54},{7,55},{8,56},{9,... | collective-permute-start | bytes 98312 | tf_op jit(solution)/shard_map/ppermute | solution.py:281
  39.2 6.5 %collective-permute-start.3 = (f32[512,128]{1,0:T(8,128)S(1)}, f32[512,128]{1,0:T(8,128)S(1)}, u32[]{:S(2)}, u32[]{:S(2)}) collective-permute-start(f32[512,128]{1,0:T(8,128)S(1)} %bitcast.22), channel_id=1, source_target_pairs={{0,1},{1,0},{2,3},{3,2},{4,5},{5,4},{6,7},{7,6},{8,9},{9,8},{10,11... | collective-permute-start | bytes 786440 | tf_op jit(solution)/shard_map/ppermute | solution.py:271
  47.1 5.6 %collective-permute-start.4 = (f32[72,512]{1,0:T(8,128)S(1)}, f32[72,512]{1,0:T(8,128)S(1)}, u32[]{:S(2)}, u32[]{:S(2)}) collective-permute-start(f32[72,512]{1,0:T(8,128)S(1)} %get-tuple-element.50), channel_id=1, source_target_pairs={{0,64},{64,0},{128,192},{192,128},{1,65},{65,1},{129,193},{193,129... | collective-permute-start | bytes 442376 | tf_op jit(solution)/shard_map/ppermute | solution.py:296
  48.4 6.9 %collective-permute-start.6 = (f32[64,512]{1,0:T(8,128)S(1)}, f32[64,512]{1,0:T(8,128)S(1)}, u32[]{:S(2)}, u32[]{:S(2)}) collective-permute-start(f32[64,512]{1,0:T(8,128)S(1)} %get-tuple-element.51), channel_id=1, source_target_pairs={{0,192},{64,128},{128,64},{192,0},{1,193},{65,129},{129,65},{193,1... | collective-permute-start | bytes 393224 | tf_op jit(solution)/shard_map/ppermute | solution.py:296
  52.7 6.8 %collective-permute-start.5 = (f32[72,512]{1,0:T(8,128)S(1)}, f32[72,512]{1,0:T(8,128)S(1)}, u32[]{:S(2)}, u32[]{:S(2)}) collective-permute-start(f32[72,512]{1,0:T(8,128)S(1)} %add.39.refs_0_), channel_id=1, source_target_pairs={{0,192},{64,128},{128,64},{192,0},{1,193},{65,129},{129,65},{193,1... | collective-permute-start | bytes 442376 | tf_op jit(solution)/shard_map/ppermute | solution.py:296
  55.3 4.2 %collective-permute-start.7 = (f32[64,512]{1,0:T(8,128)S(1)}, f32[64,512]{1,0:T(8,128)S(1)}, u32[]{:S(2)}, u32[]{:S(2)}) collective-permute-start(f32[64,512]{1,0:T(8,128)S(1)} %add.40.refs_2_), channel_id=1, source_target_pairs={{0,64},{64,0},{128,192},{192,128},{1,65},{65,1},{129,193},{193,129... | collective-permute-start | bytes 393224 | tf_op jit(solution)/shard_map/ppermute | solution.py:296
  60.8 3.2 %collective-permute-start.8 = (f32[576,128]{1,0:T(8,128)S(1)}, f32[576,128]{1,0:T(8,128)S(1)}, u32[]{:S(2)}, u32[]{:S(2)}) collective-permute-start(f32[576,128]{1,0:T(8,128)S(1)} %get-tuple-element.53), channel_id=1, source_target_pairs={{0,1},{1,0},{2,3},{3,2},{4,5},{5,4},{6,7},{7,6},{8,9},{9,8},{10,11... | collective-permute-start | bytes 884744 | tf_op jit(solution)/shard_map/ppermute | solution.py:271
  73.9 4.2 %collective-permute-start.9 = (f32[72,128]{1,0:T(8,128)S(1)}, f32[72,128]{1,0:T(8,128)S(1)}, u32[]{:S(2)}, u32[]{:S(2)}) collective-permute-start(f32[72,128]{1,0:T(8,128)S(1)} %sum_pieces.4), channel_id=1, source_target_pairs={{0,16},{1,17},{2,18},{3,19},{4,20},{5,21},{6,22},{7,23},{8,24},{9,... | collective-permute-start | bytes 110600 | tf_op jit(solution)/shard_map/ppermute | solution.py:281
  78.1 4.9 %collective-permute-start.10 = (f32[72,128]{1,0:T(8,128)S(1)}, f32[72,128]{1,0:T(8,128)S(1)}, u32[]{:S(2)}, u32[]{:S(2)}) collective-permute-start(f32[72,128]{1,0:T(8,128)S(1)} %add.42.refs_0_), channel_id=1, source_target_pairs={{0,48},{1,49},{2,50},{3,51},{4,52},{5,53},{6,54},{7,55},{8,56},{9,... | collective-permute-start | bytes 110600 | tf_op jit(solution)/shard_map/ppermute | solution.py:281
  92.0 5.6 %collective-permute-start.11 = (f32[512,128]{1,0:T(8,128)S(1)}, f32[512,128]{1,0:T(8,128)S(1)}, u32[]{:S(2)}, u32[]{:S(2)}) collective-permute-start(f32[512,128]{1,0:T(8,128)S(1)} %bitcast.26), channel_id=1, source_target_pairs={{0,1},{1,0},{2,3},{3,2},{4,5},{5,4},{6,7},{7,6},{8,9},{9,8},{10,11... | collective-permute-start | bytes 786440 | tf_op jit(solution)/shard_map/ppermute | solution.py:271
  99.3 5.1 %collective-permute-start.12 = (f32[72,512]{1,0:T(8,128)S(1)}, f32[72,512]{1,0:T(8,128)S(1)}, u32[]{:S(2)}, u32[]{:S(2)}) collective-permute-start(f32[72,512]{1,0:T(8,128)S(1)} %get-tuple-element.58), channel_id=1, source_target_pairs={{0,64},{64,0},{128,192},{192,128},{1,65},{65,1},{129,193},{193,129... | collective-permute-start | bytes 442376 | tf_op jit(solution)/shard_map/ppermute | solution.py:296
  99.4 6.5 %collective-permute-start.14 = (f32[64,512]{1,0:T(8,128)S(1)}, f32[64,512]{1,0:T(8,128)S(1)}, u32[]{:S(2)}, u32[]{:S(2)}) collective-permute-start(f32[64,512]{1,0:T(8,128)S(1)} %get-tuple-element.59), channel_id=1, source_target_pairs={{0,192},{64,128},{128,64},{192,0},{1,193},{65,129},{129,65},{193,1... | collective-permute-start | bytes 393224 | tf_op jit(solution)/shard_map/ppermute | solution.py:296
  104.5 5.3 %collective-permute-start.13 = (f32[72,512]{1,0:T(8,128)S(1)}, f32[72,512]{1,0:T(8,128)S(1)}, u32[]{:S(2)}, u32[]{:S(2)}) collective-permute-start(f32[72,512]{1,0:T(8,128)S(1)} %add.43.refs_0_), channel_id=1, source_target_pairs={{0,192},{64,128},{128,64},{192,0},{1,193},{65,129},{129,65},{193,1... | collective-permute-start | bytes 442376 | tf_op jit(solution)/shard_map/ppermute | solution.py:296
  105.9 3.9 %collective-permute-start.15 = (f32[64,512]{1,0:T(8,128)S(1)}, f32[64,512]{1,0:T(8,128)S(1)}, u32[]{:S(2)}, u32[]{:S(2)}) collective-permute-start(f32[64,512]{1,0:T(8,128)S(1)} %add.44.refs_2_), channel_id=1, source_target_pairs={{0,64},{64,0},{128,192},{192,128},{1,65},{65,1},{129,193},{193,129... | collective-permute-start | bytes 393224 | tf_op jit(solution)/shard_map/ppermute | solution.py:296
  111.1 3.9 %collective-permute-start.16 = (f32[576,128]{1,0:T(8,128)S(1)}, f32[576,128]{1,0:T(8,128)S(1)}, u32[]{:S(2)}, u32[]{:S(2)}) collective-permute-start(f32[576,128]{1,0:T(8,128)S(1)} %get-tuple-element.62), channel_id=1, source_target_pairs={{0,1},{1,0},{2,3},{3,2},{4,5},{5,4},{6,7},{7,6},{8,9},{9,8},{10,11... | collective-permute-start | bytes 884744 | tf_op jit(solution)/shard_map/ppermute | solution.py:271
  124.8 4.2 %collective-permute-start.17 = (f32[72,128]{1,0:T(8,128)S(1)}, f32[72,128]{1,0:T(8,128)S(1)}, u32[]{:S(2)}, u32[]{:S(2)}) collective-permute-start(f32[72,128]{1,0:T(8,128)S(1)} %sum_pieces.5), channel_id=1, source_target_pairs={{0,16},{1,17},{2,18},{3,19},{4,20},{5,21},{6,22},{7,23},{8,24},{9,... | collective-permute-start | bytes 110600 | tf_op jit(solution)/shard_map/ppermute | solution.py:281
  128.9 4.9 %collective-permute-start.18 = (f32[72,128]{1,0:T(8,128)S(1)}, f32[72,128]{1,0:T(8,128)S(1)}, u32[]{:S(2)}, u32[]{:S(2)}) collective-permute-start(f32[72,128]{1,0:T(8,128)S(1)} %add.46.refs_0_), channel_id=1, source_target_pairs={{0,48},{1,49},{2,50},{3,51},{4,52},{5,53},{6,54},{7,55},{8,56},{9,... | collective-permute-start | bytes 110600 | tf_op jit(solution)/shard_map/ppermute | solution.py:281
  142.9 5.6 %collective-permute-start.19 = (f32[512,128]{1,0:T(8,128)S(1)}, f32[512,128]{1,0:T(8,128)S(1)}, u32[]{:S(2)}, u32[]{:S(2)}) collective-permute-start(f32[512,128]{1,0:T(8,128)S(1)} %bitcast.24), channel_id=1, source_target_pairs={{0,1},{1,0},{2,3},{3,2},{4,5},{5,4},{6,7},{7,6},{8,9},{9,8},{10,11... | collective-permute-start | bytes 786440 | tf_op jit(solution)/shard_map/ppermute | solution.py:271
  150.2 5.1 %collective-permute-start.20 = (f32[72,512]{1,0:T(8,128)S(1)}, f32[72,512]{1,0:T(8,128)S(1)}, u32[]{:S(2)}, u32[]{:S(2)}) collective-permute-start(f32[72,512]{1,0:T(8,128)S(1)} %get-tuple-element.68), channel_id=1, source_target_pairs={{0,64},{64,0},{128,192},{192,128},{1,65},{65,1},{129,193},{193,129... | collective-permute-start | bytes 442376 | tf_op jit(solution)/shard_map/ppermute | solution.py:296
  150.3 6.7 %collective-permute-start.22 = (f32[64,512]{1,0:T(8,128)S(1)}, f32[64,512]{1,0:T(8,128)S(1)}, u32[]{:S(2)}, u32[]{:S(2)}) collective-permute-start(f32[64,512]{1,0:T(8,128)S(1)} %get-tuple-element.69), channel_id=1, source_target_pairs={{0,192},{64,128},{128,64},{192,0},{1,193},{65,129},{129,65},{193,1... | collective-permute-start | bytes 393224 | tf_op jit(solution)/shard_map/ppermute | solution.py:296
  155.3 5.9 %collective-permute-start.21 = (f32[72,512]{1,0:T(8,128)S(1)}, f32[72,512]{1,0:T(8,128)S(1)}, u32[]{:S(2)}, u32[]{:S(2)}) collective-permute-start(f32[72,512]{1,0:T(8,128)S(1)} %add.47.h0), channel_id=1, source_target_pairs={{0,192},{64,128},{128,64},{192,0},{1,193},{65,129},{129,65},{193,1... | collective-permute-start | bytes 442376 | tf_op jit(solution)/shard_map/ppermute | solution.py:296
  157.0 4.2 %collective-permute-start.23 = (f32[64,512]{1,0:T(8,128)S(1)}, f32[64,512]{1,0:T(8,128)S(1)}, u32[]{:S(2)}, u32[]{:S(2)}) collective-permute-start(f32[64,512]{1,0:T(8,128)S(1)} %add.48.h2), channel_id=1, source_target_pairs={{0,64},{64,0},{128,192},{192,128},{1,65},{65,1},{129,193},{193,129... | collective-permute-start | bytes 393224 | tf_op jit(solution)/shard_map/ppermute | solution.py:296
  176.1 4.9 %collective-permute-start.24 = (f32[32,128]{1,0:T(8,128)S(1)}, f32[32,128]{1,0:T(8,128)S(1)}, u32[]{:S(2)}, u32[]{:S(2)}) collective-permute-start(f32[32,128]{1,0:T(8,128)S(1)} %bitcast.33), channel_id=1, source_target_pairs={{0,1},{1,0},{2,3},{3,2},{4,5},{5,4},{6,7},{7,6},{8,9},{9,8},{10,11... | collective-permute-start | bytes 49160 | tf_op jit(solution)/shard_map/ppermute | solution.py:271

commit v7 on v6

--- a/solution.py
+++ b/solution.py
@@ -176,8 +176,8 @@
 
 
 def sum_blocks(*refs, rows, copies):
-    a, b, *rest = refs
-    total = a[...] + b[...]
+    t0, t1, t2, t3, *rest = refs
+    total = (t0[...] + t2[...]) + (t1[...] + t3[...])
     out = rest[-2] if len(rest) == 3 else rest[-1]
     n = out.shape[0] // copies
     stride = total.shape[0] // (n // rows)
@@ -276,13 +276,14 @@
         x = lax.all_to_all(x, "samp", 0, 0, axis_index_groups=groups, tiled=True)
         return x.reshape(n, LANES)
 
-    def block_hop(x, mask):
+    def block_terms(x):
         step = BLOCK * CORES
-        return lax.ppermute(x, "samp", [(i, i ^ (mask * step)) for i in range(samp_count)])
-
-    def block_terms(x):
-        x = x + block_hop(x, 1)
-        return x, block_hop(x, 3)
+        return [x] + [
+            lax.ppermute(
+                x, "samp", [(i, (i + d * step) % samp_count) for i in range(samp_count)]
+            )
+            for d in range(1, blocks)
+        ]
 
     def sum_samples(pieces, scal):
         n = pieces.shape[0] // BLOCK

time: 182 us -> 181 us (level)
    ppermute x6 -> x9, starting transfers between devices: 16.5 us -> 21.1 us  [block_terms(): lax.ppermute(x, 'samp', [(i, (i + d * step) % samp_count) for i in range(...]
    ppermute x7, starting transfers between devices: 25.8 us -> 21.5 us  [swap(): return lax.ppermute(x, 'samp', swap_cores)]
    ppermute x6 -> x9, waiting for transfers between devices: 12.1 us -> 10.2 us  [block_terms(): lax.ppermute(x, 'samp', [(i, (i + d * step) % samp_count) for i in range(...]
  transfers between devices with their start and end apart: 25 -> 28, of which waited for: 17 -> 17; matrix products, arithmetic and copies ran while one was open for 0% -> 0% of each run, Pallas kernels for 2% -> 2%
where the time goes in v7:
time: 181 us; the launch traced here: 180 us
  blocking collectives  70.9 us (39%)
  starting transfers between devices  54.6 us (30%)
  waiting for transfers between devices  36.9 us (20%)
  Pallas kernels  16.7 us (9%)
    all_to_all x6, blocking collectives, exchange(): x = lax.all_to_all(x, 'samp', 0, 0, axis_index_groups=groups, tiled=True)  57.8 us
    ppermute x7, starting transfers between devices, swap(): return lax.ppermute(x, 'samp', swap_cores)  21.5 us
    ppermute x12, waiting for transfers between devices, unit_hop(): return lax.ppermute(x, 'unit', [(i, i ^ mask) for i in range(unit_count)])  21.2 us
    ppermute x9, starting transfers between devices, block_terms(): lax.ppermute(x, 'samp', [(i, (i + d * step) % samp_count) for i in range(...  21.1 us
    pallas_call x18, Pallas kernels, call(): pl.pallas_call(functools.partial(kernel, **static), in_specs=specs or [VM...  16.7 us
    all_to_all x1, blocking collectives, shards(): lax.all_to_all(squares.reshape(chips, 1, LANES), 'samp', 0, 0, axis_index...  13.1 us
    ppermute x12, starting transfers between devices, unit_hop(): return lax.ppermute(x, 'unit', [(i, i ^ mask) for i in range(unit_count)])  12 us
    ppermute x9, waiting for transfers between devices, block_terms(): lax.ppermute(x, 'samp', [(i, (i + d * step) % samp_count) for i in range(...  10.2 us
  transfers between devices with their start and end apart: 28, of which 17 were waited for; matrix products, arithmetic and copies ran while one was open for 0% of the time, Pallas kernels for 2%

profile of v7, /device:TPU:1, one launch (start us, length us, event | category | flops | bytes accessed | tf_op | source)
XLA Modules:
  0.0 180.2 jit_solution(5656004414371660140)
XLA Ops:
  0.6 4.2 %first.1 = (bf16[1024,2048]{1,0:T(8,128)(2,1)S(1)}, bf16[1024,2048]{1,0:T(8,128)(2,1)S(1)}, f32[64,1024]{1,0:T(8,128)S(1)}, f32[512,128]{1,0:T(8,128)S(1)}, f32[512,128]{1,0:T(8,128)S(1)}) custom-call(s32[1,1]{1,0:T(1,128)} %bitcast.core, f32[1024,2048]{1,0:T(8,128)} %states.1, f32[64,1024]{1,0:T(8,128)} %bitcast.38), custom_call_target="tpu_custom_call" | custom-call | flops 1073741824 | bytes 1048576 | tf_op jit(solution)/shard_map/first/pallas_call | solution.py:29
  4.8 3.3 %collective-permute-start = (f32[512,128]{1,0:T(8,128)S(1)}, f32[512,128]{1,0:T(8,128)S(1)}, u32[]{:S(2)}, u32[]{:S(2)}) collective-permute-start(f32[512,128]{1,0:T(8,128)S(1)} %get-tuple-element.44), channel_id=1, source_target_pairs={{0,1},{1,0},{2,3},{3,2},{4,5},{5,4},{6,7},{7,6},{8,9},{9,8},{10,11... | collective-permute-start | bytes 786440 | tf_op jit(solution)/shard_map/ppermute | solution.py:271
  8.2 1.2 turn_states.2
  9.5 9.8 %all_to_all.35 = f32[8,64,128]{2,1,0:T(8,128)S(1)} all-to-all(f32[8,64,128]{2,1,0:T(8,128)S(1)} %bitcast.28), channel_id=1, replica_groups={{0,2,4,6,8,10,12,14},{1,3,5,7,9,11,13,15},{16,18,20,22,24,26,28,30},{17..., dimensions={0} | all-to-all | bytes 524288 | tf_op jit(solution)/shard_map/all_to_all | solution.py:276
  19.3 5.2 %collective-permute-start.3 = (f32[64,128]{1,0:T(8,128)S(1)}, f32[64,128]{1,0:T(8,128)S(1)}, u32[]{:S(2)}, u32[]{:S(2)}) collective-permute-start(f32[64,128]{1,0:T(8,128)S(1)} %sum_pieces.3.refs_0_), channel_id=1, source_target_pairs={{0,48},{1,49},{2,50},{3,51},{4,52},{5,53},{6,54},{7,55},{8,56},{9,... | collective-permute-start | bytes 98312 | tf_op jit(solution)/shard_map/ppermute | solution.py:282
  25.7 2.1 %collective-permute-start.1 = (f32[64,128]{1,0:T(8,128)S(1)}, f32[64,128]{1,0:T(8,128)S(1)}, u32[]{:S(2)}, u32[]{:S(2)}) collective-permute-start(f32[64,128]{1,0:T(8,128)S(1)} %sum_pieces.3.refs_0_), channel_id=1, source_target_pairs={{0,16},{1,17},{2,18},{3,19},{4,20},{5,21},{6,22},{7,23},{8,24},{9,... | collective-permute-start | bytes 98312 | tf_op jit(solution)/shard_map/ppermute | solution.py:282
  27.8 3.4 %collective-permute-done.2.refs_2_ = f32[64,128]{1,0:T(8,128)S(1)} collective-permute-done((f32[64,128]{1,0:T(8,128)S(1)}, f32[64,128]{1,0:T(8,128)S(1)}, u32[]{:S(2)}, u32[]{:S(2)}) %collective-permute-start.2) | collective-permute-done | bytes 32800 | tf_op jit(solution)/shard_map/ppermute | solution.py:282
  31.2 9.6 %all_to_all.36 = f32[8,64,128]{2,1,0:T(8,128)S(1)} all-to-all(f32[8,64,128]{2,1,0:T(8,128)S(1)} %bitcast.29), channel_id=1, replica_groups={{0,2,4,6,8,10,12,14},{1,3,5,7,9,11,13,15},{16,18,20,22,24,26,28,30},{17..., dimensions={0} | all-to-all | bytes 524288 | tf_op jit(solution)/shard_map/all_to_all | solution.py:276
  40.8 3.6 %collective-permute-start.4 = (f32[512,128]{1,0:T(8,128)S(1)}, f32[512,128]{1,0:T(8,128)S(1)}, u32[]{:S(2)}, u32[]{:S(2)}) collective-permute-start(f32[512,128]{1,0:T(8,128)S(1)} %bitcast.22), channel_id=1, source_target_pairs={{0,1},{1,0},{2,3},{3,2},{4,5},{5,4},{6,7},{7,6},{8,9},{9,8},{10,11... | collective-permute-start | bytes 786440 | tf_op jit(solution)/shard_map/ppermute | solution.py:271
  44.4 1.8 turn_states.3
  46.2 1.4 forward.3
  47.6 1.3 collective-permute-start.5
  48.9 1.8 %collective-permute-start.7 = (f32[64,512]{1,0:T(8,128)S(1)}, f32[64,512]{1,0:T(8,128)S(1)}, u32[]{:S(2)}, u32[]{:S(2)}) collective-permute-start(f32[64,512]{1,0:T(8,128)S(1)} %get-tuple-element.51), channel_id=1, source_target_pairs={{0,192},{64,128},{128,64},{192,0},{1,193},{65,129},{129,65},{193,1... | collective-permute-start | bytes 393224 | tf_op jit(solution)/shard_map/ppermute | solution.py:297
  50.7 2.5 %collective-permute-done.5 = f32[72,512]{1,0:T(8,128)S(1)} collective-permute-done((f32[72,512]{1,0:T(8,128)S(1)}, f32[72,512]{1,0:T(8,128)S(1)}, u32[]{:S(2)}, u32[]{:S(2)}) %collective-permute-start.5) | collective-permute-done | bytes 147488 | tf_op jit(solution)/shard_map/ppermute | solution.py:297
  53.2 2.6 %collective-permute-start.6 = (f32[72,512]{1,0:T(8,128)S(1)}, f32[72,512]{1,0:T(8,128)S(1)}, u32[]{:S(2)}, u32[]{:S(2)}) collective-permute-start(f32[72,512]{1,0:T(8,128)S(1)} %add.29.refs_0_), channel_id=1, source_target_pairs={{0,192},{64,128},{128,64},{192,0},{1,193},{65,129},{129,65},{193,1... | collective-permute-start | bytes 442376 | tf_op jit(solution)/shard_map/ppermute | solution.py:297
  56.0 4.1 %collective-permute-done.8.refs_3_ = f32[64,512]{1,0:T(8,128)S(1)} collective-permute-done((f32[64,512]{1,0:T(8,128)S(1)}, f32[64,512]{1,0:T(8,128)S(1)}, u32[]{:S(2)}, u32[]{:S(2)}) %collective-permute-start.8) | collective-permute-done | bytes 131104 | tf_op jit(solution)/shard_map/ppermute | solution.py:297
  60.1 1.3 back.2
  61.4 2.0 %collective-permute-start.9 = (f32[576,128]{1,0:T(8,128)S(1)}, f32[576,128]{1,0:T(8,128)S(1)}, u32[]{:S(2)}, u32[]{:S(2)}) collective-permute-start(f32[576,128]{1,0:T(8,128)S(1)} %get-tuple-element.53), channel_id=1, source_target_pairs={{0,1},{1,0},{2,3},{3,2},{4,5},{5,4},{6,7},{7,6},{8,9},{9,8},{10,11... | collective-permute-start | bytes 884744 | tf_op jit(solution)/shard_map/ppermute | solution.py:271
  63.4 1.2 collective-permute-done.9
  64.7 9.6 %all_to_all.37 = f32[8,72,128]{2,1,0:T(8,128)S(1)} all-to-all(f32[8,72,128]{2,1,0:T(8,128)S(1)} %bitcast.36), channel_id=1, replica_groups={{0,2,4,6,8,10,12,14},{1,3,5,7,9,11,13,15},{16,18,20,22,24,26,28,30},{17..., dimensions={0} | all-to-all | bytes 589824 | tf_op jit(solution)/shard_map/all_to_all | solution.py:276
  74.3 1.6 collective-permute-start.12
  76.0 2.7 %collective-permute-start.11 = (f32[72,128]{1,0:T(8,128)S(1)}, f32[72,128]{1,0:T(8,128)S(1)}, u32[]{:S(2)}, u32[]{:S(2)}) collective-permute-start(f32[72,128]{1,0:T(8,128)S(1)} %sum_pieces.4.refs_0_), channel_id=1, source_target_pairs={{0,32},{1,33},{2,34},{3,35},{4,36},{5,37},{6,38},{7,39},{8,40},{9,... | collective-permute-start | bytes 110600 | tf_op jit(solution)/shard_map/ppermute | solution.py:282
  78.7 2.3 %collective-permute-start.10 = (f32[72,128]{1,0:T(8,128)S(1)}, f32[72,128]{1,0:T(8,128)S(1)}, u32[]{:S(2)}, u32[]{:S(2)}) collective-permute-start(f32[72,128]{1,0:T(8,128)S(1)} %sum_pieces.4.refs_0_), channel_id=1, source_target_pairs={{0,16},{1,17},{2,18},{3,19},{4,20},{5,21},{6,22},{7,23},{8,24},{9,... | collective-permute-start | bytes 110600 | tf_op jit(solution)/shard_map/ppermute | solution.py:282
  81.0 1.9 %collective-permute-done.11.refs_2_ = f32[72,128]{1,0:T(8,128)S(1)} collective-permute-done((f32[72,128]{1,0:T(8,128)S(1)}, f32[72,128]{1,0:T(8,128)S(1)}, u32[]{:S(2)}, u32[]{:S(2)}) %collective-permute-start.11) | collective-permute-done | bytes 36896 | tf_op jit(solution)/shard_map/ppermute | solution.py:282
  84.0 9.5 %all_to_all.38 = f32[8,64,128]{2,1,0:T(8,128)S(1)} all-to-all(f32[8,64,128]{2,1,0:T(8,128)S(1)} %bitcast.31), channel_id=1, replica_groups={{0,2,4,6,8,10,12,14},{1,3,5,7,9,11,13,15},{16,18,20,22,24,26,28,30},{17..., dimensions={0} | all-to-all | bytes 524288 | tf_op jit(solution)/shard_map/all_to_all | solution.py:276
  93.5 3.0 %collective-permute-start.13 = (f32[512,128]{1,0:T(8,128)S(1)}, f32[512,128]{1,0:T(8,128)S(1)}, u32[]{:S(2)}, u32[]{:S(2)}) collective-permute-start(f32[512,128]{1,0:T(8,128)S(1)} %bitcast.26), channel_id=1, source_target_pairs={{0,1},{1,0},{2,3},{3,2},{4,5},{5,4},{6,7},{7,6},{8,9},{9,8},{10,11... | collective-permute-start | bytes 786440 | tf_op jit(solution)/shard_map/ppermute | solution.py:271
  97.7 1.6 forward.4
  99.5 1.2 collective-permute-start.16
  100.7 3.8 %collective-permute-done.14 = f32[72,512]{1,0:T(8,128)S(1)} collective-permute-done((f32[72,512]{1,0:T(8,128)S(1)}, f32[72,512]{1,0:T(8,128)S(1)}, u32[]{:S(2)}, u32[]{:S(2)}) %collective-permute-start.14) | collective-permute-done | bytes 147488 | tf_op jit(solution)/shard_map/ppermute | solution.py:297
  104.5 1.2 collective-permute-start.15
  105.9 3.8 %collective-permute-done.17.refs_3_ = f32[64,512]{1,0:T(8,128)S(1)} collective-permute-done((f32[64,512]{1,0:T(8,128)S(1)}, f32[64,512]{1,0:T(8,128)S(1)}, u32[]{:S(2)}, u32[]{:S(2)}) %collective-permute-start.17) | collective-permute-done | bytes 131104 | tf_op jit(solution)/shard_map/ppermute | solution.py:297
  109.8 1.3 back.3
  111.1 2.6 %collective-permute-start.18 = (f32[576,128]{1,0:T(8,128)S(1)}, f32[576,128]{1,0:T(8,128)S(1)}, u32[]{:S(2)}, u32[]{:S(2)}) collective-permute-start(f32[576,128]{1,0:T(8,128)S(1)} %get-tuple-element.62), channel_id=1, source_target_pairs={{0,1},{1,0},{2,3},{3,2},{4,5},{5,4},{6,7},{7,6},{8,9},{9,8},{10,11... | collective-permute-start | bytes 884744 | tf_op jit(solution)/shard_map/ppermute | solution.py:271
  113.7 1.2 collective-permute-done.18
  115.0 9.6 %all_to_all.39 = f32[8,72,128]{2,1,0:T(8,128)S(1)} all-to-all(f32[8,72,128]{2,1,0:T(8,128)S(1)} %bitcast.37), channel_id=1, replica_groups={{0,2,4,6,8,10,12,14},{1,3,5,7,9,11,13,15},{16,18,20,22,24,26,28,30},{17..., dimensions={0} | all-to-all | bytes 589824 | tf_op jit(solution)/shard_map/all_to_all | solution.py:276
  124.6 1.9 %collective-permute-start.21 = (f32[72,128]{1,0:T(8,128)S(1)}, f32[72,128]{1,0:T(8,128)S(1)}, u32[]{:S(2)}, u32[]{:S(2)}) collective-permute-start(f32[72,128]{1,0:T(8,128)S(1)} %sum_pieces.5.refs_0_), channel_id=1, source_target_pairs={{0,48},{1,49},{2,50},{3,51},{4,52},{5,53},{6,54},{7,55},{8,56},{9,... | collective-permute-start | bytes 110600 | tf_op jit(solution)/shard_map/ppermute | solution.py:282
  126.6 2.9 %collective-permute-start.20 = (f32[72,128]{1,0:T(8,128)S(1)}, f32[72,128]{1,0:T(8,128)S(1)}, u32[]{:S(2)}, u32[]{:S(2)}) collective-permute-start(f32[72,128]{1,0:T(8,128)S(1)} %sum_pieces.5.refs_0_), channel_id=1, source_target_pairs={{0,32},{1,33},{2,34},{3,35},{4,36},{5,37},{6,38},{7,39},{8,40},{9,... | collective-permute-start | bytes 110600 | tf_op jit(solution)/shard_map/ppermute | solution.py:282
  130.6 2.7 %collective-permute-done.20.refs_2_ = f32[72,128]{1,0:T(8,128)S(1)} collective-permute-done((f32[72,128]{1,0:T(8,128)S(1)}, f32[72,128]{1,0:T(8,128)S(1)}, u32[]{:S(2)}, u32[]{:S(2)}) %collective-permute-start.20) | collective-permute-done | bytes 36896 | tf_op jit(solution)/shard_map/ppermute | solution.py:282
  134.4 9.6 %all_to_all.40 = f32[8,64,128]{2,1,0:T(8,128)S(1)} all-to-all(f32[8,64,128]{2,1,0:T(8,128)S(1)} %bitcast.32), channel_id=1, replica_groups={{0,2,4,6,8,10,12,14},{1,3,5,7,9,11,13,15},{16,18,20,22,24,26,28,30},{17..., dimensions={0} | all-to-all | bytes 524288 | tf_op jit(solution)/shard_map/all_to_all | solution.py:276
  144.0 3.2 %collective-permute-start.22 = (f32[512,128]{1,0:T(8,128)S(1)}, f32[512,128]{1,0:T(8,128)S(1)}, u32[]{:S(2)}, u32[]{:S(2)}) collective-permute-start(f32[512,128]{1,0:T(8,128)S(1)} %bitcast.24), channel_id=1, source_target_pairs={{0,1},{1,0},{2,3},{3,2},{4,5},{5,4},{6,7},{7,6},{8,9},{9,8},{10,11... | collective-permute-start | bytes 786440 | tf_op jit(solution)/shard_map/ppermute | solution.py:271
  147.3 1.2 collective-permute-done.22.refs_1_
  148.4 1.6 forward.5
  150.2 1.6 collective-permute-start.25
  151.8 3.4 %collective-permute-done.23 = f32[72,512]{1,0:T(8,128)S(1)} collective-permute-done((f32[72,512]{1,0:T(8,128)S(1)}, f32[72,512]{1,0:T(8,128)S(1)}, u32[]{:S(2)}, u32[]{:S(2)}) %collective-permute-start.23) | collective-permute-done | bytes 147488 | tf_op jit(solution)/shard_map/ppermute | solution.py:297
  155.2 1.6 collective-permute-start.24
  157.7 3.4 %collective-permute-done.26.h3 = f32[64,512]{1,0:T(8,128)S(1)} collective-permute-done((f32[64,512]{1,0:T(8,128)S(1)}, f32[64,512]{1,0:T(8,128)S(1)}, u32[]{:S(2)}, u32[]{:S(2)}) %collective-permute-start.26) | collective-permute-done | bytes 131104 | tf_op jit(solution)/shard_map/ppermute | solution.py:297
  161.4 13.1 %all_to_all.41 = f32[32,1,128]{2,1,0:T(1,128)S(1)} all-to-all(f32[32,1,128]{2,1,0:T(1,128)S(1)} %bitcast.35), channel_id=1, replica_groups={{0,2,4,6,8,10,12,14,16,18,20,22,24,26,28,30,32,34,36,38,40,42,44,46,48,..., dimensions={0} | all-to-all | bytes 32768 | tf_op jit(solution)/shard_map/all_to_all | solution.py:401
  174.5 3.8 %collective-permute-start.27 = (f32[32,128]{1,0:T(8,128)S(1)}, f32[32,128]{1,0:T(8,128)S(1)}, u32[]{:S(2)}, u32[]{:S(2)}) collective-permute-start(f32[32,128]{1,0:T(8,128)S(1)} %bitcast.33), channel_id=1, source_target_pairs={{0,1},{1,0},{2,3},{3,2},{4,5},{5,4},{6,7},{7,6},{8,9},{9,8},{10,11... | collective-permute-start | bytes 49160 | tf_op jit(solution)/shard_map/ppermute | solution.py:271
  (41 shorter events, 9.7 us)
Async XLA Ops:
  4.8 4.6 %collective-permute-start = (f32[512,128]{1,0:T(8,128)S(1)}, f32[512,128]{1,0:T(8,128)S(1)}, u32[]{:S(2)}, u32[]{:S(2)}) collective-permute-start(f32[512,128]{1,0:T(8,128)S(1)} %get-tuple-element.44), channel_id=1, source_target_pairs={{0,1},{1,0},{2,3},{3,2},{4,5},{5,4},{6,7},{7,6},{8,9},{9,8},{10,11... | collective-permute-start | bytes 786440 | tf_op jit(solution)/shard_map/ppermute | solution.py:271
  19.3 8.5 %collective-permute-start.3 = (f32[64,128]{1,0:T(8,128)S(1)}, f32[64,128]{1,0:T(8,128)S(1)}, u32[]{:S(2)}, u32[]{:S(2)}) collective-permute-start(f32[64,128]{1,0:T(8,128)S(1)} %sum_pieces.3.refs_0_), channel_id=1, source_target_pairs={{0,48},{1,49},{2,50},{3,51},{4,52},{5,53},{6,54},{7,55},{8,56},{9,... | collective-permute-start | bytes 98312 | tf_op jit(solution)/shard_map/ppermute | solution.py:282
  24.5 6.7 %collective-permute-start.2 = (f32[64,128]{1,0:T(8,128)S(1)}, f32[64,128]{1,0:T(8,128)S(1)}, u32[]{:S(2)}, u32[]{:S(2)}) collective-permute-start(f32[64,128]{1,0:T(8,128)S(1)} %sum_pieces.3.refs_0_), channel_id=1, source_target_pairs={{0,32},{1,33},{2,34},{3,35},{4,36},{5,37},{6,38},{7,39},{8,40},{9,... | collective-permute-start | bytes 98312 | tf_op jit(solution)/shard_map/ppermute | solution.py:282
  25.7 5.5 %collective-permute-start.1 = (f32[64,128]{1,0:T(8,128)S(1)}, f32[64,128]{1,0:T(8,128)S(1)}, u32[]{:S(2)}, u32[]{:S(2)}) collective-permute-start(f32[64,128]{1,0:T(8,128)S(1)} %sum_pieces.3.refs_0_), channel_id=1, source_target_pairs={{0,16},{1,17},{2,18},{3,19},{4,20},{5,21},{6,22},{7,23},{8,24},{9,... | collective-permute-start | bytes 98312 | tf_op jit(solution)/shard_map/ppermute | solution.py:282
  40.8 5.3 %collective-permute-start.4 = (f32[512,128]{1,0:T(8,128)S(1)}, f32[512,128]{1,0:T(8,128)S(1)}, u32[]{:S(2)}, u32[]{:S(2)}) collective-permute-start(f32[512,128]{1,0:T(8,128)S(1)} %bitcast.22), channel_id=1, source_target_pairs={{0,1},{1,0},{2,3},{3,2},{4,5},{5,4},{6,7},{7,6},{8,9},{9,8},{10,11... | collective-permute-start | bytes 786440 | tf_op jit(solution)/shard_map/ppermute | solution.py:271
  47.6 5.6 %collective-permute-start.5 = (f32[72,512]{1,0:T(8,128)S(1)}, f32[72,512]{1,0:T(8,128)S(1)}, u32[]{:S(2)}, u32[]{:S(2)}) collective-permute-start(f32[72,512]{1,0:T(8,128)S(1)} %get-tuple-element.50), channel_id=1, source_target_pairs={{0,64},{64,0},{128,192},{192,128},{1,65},{65,1},{129,193},{193,129... | collective-permute-start | bytes 442376 | tf_op jit(solution)/shard_map/ppermute | solution.py:297
  48.9 6.9 %collective-permute-start.7 = (f32[64,512]{1,0:T(8,128)S(1)}, f32[64,512]{1,0:T(8,128)S(1)}, u32[]{:S(2)}, u32[]{:S(2)}) collective-permute-start(f32[64,512]{1,0:T(8,128)S(1)} %get-tuple-element.51), channel_id=1, source_target_pairs={{0,192},{64,128},{128,64},{192,0},{1,193},{65,129},{129,65},{193,1... | collective-permute-start | bytes 393224 | tf_op jit(solution)/shard_map/ppermute | solution.py:297
  53.2 7.0 %collective-permute-start.6 = (f32[72,512]{1,0:T(8,128)S(1)}, f32[72,512]{1,0:T(8,128)S(1)}, u32[]{:S(2)}, u32[]{:S(2)}) collective-permute-start(f32[72,512]{1,0:T(8,128)S(1)} %add.29.refs_0_), channel_id=1, source_target_pairs={{0,192},{64,128},{128,64},{192,0},{1,193},{65,129},{129,65},{193,1... | collective-permute-start | bytes 442376 | tf_op jit(solution)/shard_map/ppermute | solution.py:297
  55.8 4.4 %collective-permute-start.8 = (f32[64,512]{1,0:T(8,128)S(1)}, f32[64,512]{1,0:T(8,128)S(1)}, u32[]{:S(2)}, u32[]{:S(2)}) collective-permute-start(f32[64,512]{1,0:T(8,128)S(1)} %add.30.refs_2_), channel_id=1, source_target_pairs={{0,64},{64,0},{128,192},{192,128},{1,65},{65,1},{129,193},{193,129... | collective-permute-start | bytes 393224 | tf_op jit(solution)/shard_map/ppermute | solution.py:297
  61.4 3.2 %collective-permute-start.9 = (f32[576,128]{1,0:T(8,128)S(1)}, f32[576,128]{1,0:T(8,128)S(1)}, u32[]{:S(2)}, u32[]{:S(2)}) collective-permute-start(f32[576,128]{1,0:T(8,128)S(1)} %get-tuple-element.53), channel_id=1, source_target_pairs={{0,1},{1,0},{2,3},{3,2},{4,5},{5,4},{6,7},{7,6},{8,9},{9,8},{10,11... | collective-permute-start | bytes 884744 | tf_op jit(solution)/shard_map/ppermute | solution.py:271
  74.3 6.7 %collective-permute-start.12 = (f32[72,128]{1,0:T(8,128)S(1)}, f32[72,128]{1,0:T(8,128)S(1)}, u32[]{:S(2)}, u32[]{:S(2)}) collective-permute-start(f32[72,128]{1,0:T(8,128)S(1)} %sum_pieces.4.refs_0_), channel_id=1, source_target_pairs={{0,48},{1,49},{2,50},{3,51},{4,52},{5,53},{6,54},{7,55},{8,56},{9,... | collective-permute-start | bytes 110600 | tf_op jit(solution)/shard_map/ppermute | solution.py:282
  76.0 6.9 %collective-permute-start.11 = (f32[72,128]{1,0:T(8,128)S(1)}, f32[72,128]{1,0:T(8,128)S(1)}, u32[]{:S(2)}, u32[]{:S(2)}) collective-permute-start(f32[72,128]{1,0:T(8,128)S(1)} %sum_pieces.4.refs_0_), channel_id=1, source_target_pairs={{0,32},{1,33},{2,34},{3,35},{4,36},{5,37},{6,38},{7,39},{8,40},{9,... | collective-permute-start | bytes 110600 | tf_op jit(solution)/shard_map/ppermute | solution.py:282
  78.7 5.3 %collective-permute-start.10 = (f32[72,128]{1,0:T(8,128)S(1)}, f32[72,128]{1,0:T(8,128)S(1)}, u32[]{:S(2)}, u32[]{:S(2)}) collective-permute-start(f32[72,128]{1,0:T(8,128)S(1)} %sum_pieces.4.refs_0_), channel_id=1, source_target_pairs={{0,16},{1,17},{2,18},{3,19},{4,20},{5,21},{6,22},{7,23},{8,24},{9,... | collective-permute-start | bytes 110600 | tf_op jit(solution)/shard_map/ppermute | solution.py:282
  93.5 4.2 %collective-permute-start.13 = (f32[512,128]{1,0:T(8,128)S(1)}, f32[512,128]{1,0:T(8,128)S(1)}, u32[]{:S(2)}, u32[]{:S(2)}) collective-permute-start(f32[512,128]{1,0:T(8,128)S(1)} %bitcast.26), channel_id=1, source_target_pairs={{0,1},{1,0},{2,3},{3,2},{4,5},{5,4},{6,7},{7,6},{8,9},{9,8},{10,11... | collective-permute-start | bytes 786440 | tf_op jit(solution)/shard_map/ppermute | solution.py:271
  99.3 5.1 %collective-permute-start.14 = (f32[72,512]{1,0:T(8,128)S(1)}, f32[72,512]{1,0:T(8,128)S(1)}, u32[]{:S(2)}, u32[]{:S(2)}) collective-permute-start(f32[72,512]{1,0:T(8,128)S(1)} %get-tuple-element.58), channel_id=1, source_target_pairs={{0,64},{64,0},{128,192},{192,128},{1,65},{65,1},{129,193},{193,129... | collective-permute-start | bytes 442376 | tf_op jit(solution)/shard_map/ppermute | solution.py:297
  99.5 6.3 %collective-permute-start.16 = (f32[64,512]{1,0:T(8,128)S(1)}, f32[64,512]{1,0:T(8,128)S(1)}, u32[]{:S(2)}, u32[]{:S(2)}) collective-permute-start(f32[64,512]{1,0:T(8,128)S(1)} %get-tuple-element.59), channel_id=1, source_target_pairs={{0,192},{64,128},{128,64},{192,0},{1,193},{65,129},{129,65},{193,1... | collective-permute-start | bytes 393224 | tf_op jit(solution)/shard_map/ppermute | solution.py:297
  104.5 5.3 %collective-permute-start.15 = (f32[72,512]{1,0:T(8,128)S(1)}, f32[72,512]{1,0:T(8,128)S(1)}, u32[]{:S(2)}, u32[]{:S(2)}) collective-permute-start(f32[72,512]{1,0:T(8,128)S(1)} %add.32.refs_0_), channel_id=1, source_target_pairs={{0,192},{64,128},{128,64},{192,0},{1,193},{65,129},{129,65},{193,1... | collective-permute-start | bytes 442376 | tf_op jit(solution)/shard_map/ppermute | solution.py:297
  105.8 3.9 %collective-permute-start.17 = (f32[64,512]{1,0:T(8,128)S(1)}, f32[64,512]{1,0:T(8,128)S(1)}, u32[]{:S(2)}, u32[]{:S(2)}) collective-permute-start(f32[64,512]{1,0:T(8,128)S(1)} %add.33.refs_2_), channel_id=1, source_target_pairs={{0,64},{64,0},{128,192},{192,128},{1,65},{65,1},{129,193},{193,129... | collective-permute-start | bytes 393224 | tf_op jit(solution)/shard_map/ppermute | solution.py:297
  111.1 3.8 %collective-permute-start.18 = (f32[576,128]{1,0:T(8,128)S(1)}, f32[576,128]{1,0:T(8,128)S(1)}, u32[]{:S(2)}, u32[]{:S(2)}) collective-permute-start(f32[576,128]{1,0:T(8,128)S(1)} %get-tuple-element.62), channel_id=1, source_target_pairs={{0,1},{1,0},{2,3},{3,2},{4,5},{5,4},{6,7},{7,6},{8,9},{9,8},{10,11... | collective-permute-start | bytes 884744 | tf_op jit(solution)/shard_map/ppermute | solution.py:271
  124.6 6.0 %collective-permute-start.21 = (f32[72,128]{1,0:T(8,128)S(1)}, f32[72,128]{1,0:T(8,128)S(1)}, u32[]{:S(2)}, u32[]{:S(2)}) collective-permute-start(f32[72,128]{1,0:T(8,128)S(1)} %sum_pieces.5.refs_0_), channel_id=1, source_target_pairs={{0,48},{1,49},{2,50},{3,51},{4,52},{5,53},{6,54},{7,55},{8,56},{9,... | collective-permute-start | bytes 110600 | tf_op jit(solution)/shard_map/ppermute | solution.py:282
  126.6 6.7 %collective-permute-start.20 = (f32[72,128]{1,0:T(8,128)S(1)}, f32[72,128]{1,0:T(8,128)S(1)}, u32[]{:S(2)}, u32[]{:S(2)}) collective-permute-start(f32[72,128]{1,0:T(8,128)S(1)} %sum_pieces.5.refs_0_), channel_id=1, source_target_pairs={{0,32},{1,33},{2,34},{3,35},{4,36},{5,37},{6,38},{7,39},{8,40},{9,... | collective-permute-start | bytes 110600 | tf_op jit(solution)/shard_map/ppermute | solution.py:282
  129.5 4.9 %collective-permute-start.19 = (f32[72,128]{1,0:T(8,128)S(1)}, f32[72,128]{1,0:T(8,128)S(1)}, u32[]{:S(2)}, u32[]{:S(2)}) collective-permute-start(f32[72,128]{1,0:T(8,128)S(1)} %sum_pieces.5.refs_0_), channel_id=1, source_target_pairs={{0,16},{1,17},{2,18},{3,19},{4,20},{5,21},{6,22},{7,23},{8,24},{9,... | collective-permute-start | bytes 110600 | tf_op jit(solution)/shard_map/ppermute | solution.py:282
  144.0 4.4 %collective-permute-start.22 = (f32[512,128]{1,0:T(8,128)S(1)}, f32[512,128]{1,0:T(8,128)S(1)}, u32[]{:S(2)}, u32[]{:S(2)}) collective-permute-start(f32[512,128]{1,0:T(8,128)S(1)} %bitcast.24), channel_id=1, source_target_pairs={{0,1},{1,0},{2,3},{3,2},{4,5},{5,4},{6,7},{7,6},{8,9},{9,8},{10,11... | collective-permute-start | bytes 786440 | tf_op jit(solution)/shard_map/ppermute | solution.py:271
  150.1 5.1 %collective-permute-start.23 = (f32[72,512]{1,0:T(8,128)S(1)}, f32[72,512]{1,0:T(8,128)S(1)}, u32[]{:S(2)}, u32[]{:S(2)}) collective-permute-start(f32[72,512]{1,0:T(8,128)S(1)} %get-tuple-element.68), channel_id=1, source_target_pairs={{0,64},{64,0},{128,192},{192,128},{1,65},{65,1},{129,193},{193,129... | collective-permute-start | bytes 442376 | tf_op jit(solution)/shard_map/ppermute | solution.py:297
  150.2 6.7 %collective-permute-start.25 = (f32[64,512]{1,0:T(8,128)S(1)}, f32[64,512]{1,0:T(8,128)S(1)}, u32[]{:S(2)}, u32[]{:S(2)}) collective-permute-start(f32[64,512]{1,0:T(8,128)S(1)} %get-tuple-element.69), channel_id=1, source_target_pairs={{0,192},{64,128},{128,64},{192,0},{1,193},{65,129},{129,65},{193,1... | collective-permute-start | bytes 393224 | tf_op jit(solution)/shard_map/ppermute | solution.py:297
  155.2 5.9 %collective-permute-start.24 = (f32[72,512]{1,0:T(8,128)S(1)}, f32[72,512]{1,0:T(8,128)S(1)}, u32[]{:S(2)}, u32[]{:S(2)}) collective-permute-start(f32[72,512]{1,0:T(8,128)S(1)} %add.35.h0), channel_id=1, source_target_pairs={{0,192},{64,128},{128,64},{192,0},{1,193},{65,129},{129,65},{193,1... | collective-permute-start | bytes 442376 | tf_op jit(solution)/shard_map/ppermute | solution.py:297
  156.9 4.2 %collective-permute-start.26 = (f32[64,512]{1,0:T(8,128)S(1)}, f32[64,512]{1,0:T(8,128)S(1)}, u32[]{:S(2)}, u32[]{:S(2)}) collective-permute-start(f32[64,512]{1,0:T(8,128)S(1)} %add.36.h2), channel_id=1, source_target_pairs={{0,64},{64,0},{128,192},{192,128},{1,65},{65,1},{129,193},{193,129... | collective-permute-start | bytes 393224 | tf_op jit(solution)/shard_map/ppermute | solution.py:297
  174.5 4.6 %collective-permute-start.27 = (f32[32,128]{1,0:T(8,128)S(1)}, f32[32,128]{1,0:T(8,128)S(1)}, u32[]{:S(2)}, u32[]{:S(2)}) collective-permute-start(f32[32,128]{1,0:T(8,128)S(1)} %bitcast.33), channel_id=1, source_target_pairs={{0,1},{1,0},{2,3},{3,2},{4,5},{5,4},{6,7},{7,6},{8,9},{9,8},{10,11... | collective-permute-start | bytes 49160 | tf_op jit(solution)/shard_map/ppermute | solution.py:271

commit v8 on v7

--- a/solution.py
+++ b/solution.py
@@ -38,23 +38,23 @@
     )(*args)
 
 
-def split2(x):
-    high = x.astype(BF16)
-    return jnp.concatenate([high, (x - high.astype(F32)).astype(BF16)], axis=0)
+def split3(x):
+    terms = []
+    for _ in range(2):
+        terms.append(x.astype(BF16))
+        x = x - terms[-1].astype(F32)
+    return jnp.concatenate(terms + [x.astype(BF16)], axis=0)
 
 
 def dot(a, b, ca, cb):
     return lax.dot_general(a, b, (((ca,), (cb,)), ((), ())), preferred_element_type=F32)
 
 
-def fold(p):
-    n = p.shape[0] // 2
-    return p[n:] + p[:n]
-
-
-def rows_product(x, high, low, at):
-    x2 = split2(x) if x.dtype == F32 else x
-    return fold(dot(x2, low[:, at], 1, 0) + dot(x2, high[:, at], 1, 0))
+def rows_product(x3, high, low):
+    n = x3.shape[0] // 3
+    p = dot(x3[: 2 * n], low, 1, 0)
+    q = dot(x3, high, 1, 0)
+    return q[:n] + ((p[:n] + q[n : 2 * n]) + (p[n:] + q[2 * n :]))
 
 
 def row(x):
@@ -93,7 +93,7 @@
     fetch.wait()
     x = own_half_first(target_buf[...], core[0, 0] == 0)
     turned[...] = x
-    x2 = split2(x)
+    x3 = split3(x)
     half = x.shape[0] // CORES
     for t in range(steps):
         copies[t].wait()
@@ -102,7 +102,7 @@
         l = (s - h.astype(F32)).astype(BF16)
         high[:, pl.ds(t * FETCH, FETCH)] = h
         low[:, pl.ds(t * FETCH, FETCH)] = l
-        p = fold(dot(x2, l, 1, 0) + dot(x2, h, 1, 0))
+        p = rows_product(x3, h, l)
         for i in range(FETCH // WIDE):
             part = p[:, i * WIDE : (i + 1) * WIDE]
             store_pieces(mine, theirs, part, t * (FETCH // WIDE) + i, mine.shape[0] // half)
@@ -144,9 +144,10 @@
     image, image_sq = step_image(hops, before, scal, image_out, scal_out)
     half = image.shape[0] // CORES
     stride = mine.shape[0] // half
-    x2 = split2(image)
+    x3 = split3(image)
     for t in range(high.shape[1] // WIDE):
-        p = rows_product(x2, high, low, pl.ds(t * WIDE, WIDE))
+        at = pl.ds(t * WIDE, WIDE)
+        p = rows_product(x3, high[:, at], low[:, at])
         store_pieces(mine, theirs, p, t, stride)
     extra = jnp.broadcast_to(image_sq, (half, LANES))
     for j in range(high.shape[1] // LANES, stride):
@@ -209,12 +210,13 @@
     gradient[...] = g
     n = b.shape[0]
     stride = g.shape[0] // n
-    x2 = split2(
+    x3 = split3(
         jnp.concatenate([gradient[pl.ds(j, n, stride=stride), :] for j in range(stride)], axis=1)
     )
     steps = high.shape[1] // WIDE
     for t in range(steps):
-        p = rows_product(x2, high, low, pl.ds(t * WIDE, WIDE))
+        at = pl.ds(t * WIDE, WIDE)
+        p = rows_product(x3, high[:, at], low[:, at])
         out, k = (a, t) if t < steps // 2 else (b, t - steps // 2)
         out[0:n, k * WIDE : (k + 1) * WIDE] = p
     a[n : n + 1, :] = jnp.broadcast_to(jnp.sum(g * g), (1, a.shape[1]))

time: 181 us -> 182 us (level)
  Pallas kernels: 16.7 us -> 18.6 us
    pallas_call x18, Pallas kernels: 16.7 us -> 18.6 us  [call(): pl.pallas_call(functools.partial(kernel, **static), in_specs=specs or [VM...]
  transfers between devices with their start and end apart: 28 -> 28, of which waited for: 17 -> 16; matrix products, arithmetic and copies ran while one was open for 0% -> 0% of each run, Pallas kernels for 2% -> 2%
where the time goes in v8:
time: 182 us
  blocking collectives  70.9 us (39%)
  starting transfers between devices  54.9 us (30%)
  waiting for transfers between devices  36.8 us (20%)
  Pallas kernels  18.6 us (10%)
    all_to_all x6, blocking collectives, exchange(): x = lax.all_to_all(x, 'samp', 0, 0, axis_index_groups=groups, tiled=True)  57.8 us
    ppermute x7, starting transfers between devices, swap(): return lax.ppermute(x, 'samp', swap_cores)  21.6 us
    ppermute x9, starting transfers between devices, block_terms(): lax.ppermute(x, 'samp', [(i, (i + d * step) % samp_count) for i in range(...  21 us
    ppermute x12, waiting for transfers between devices, unit_hop(): return lax.ppermute(x, 'unit', [(i, i ^ mask) for i in range(unit_count)])  20.9 us
    pallas_call x18, Pallas kernels, call(): pl.pallas_call(functools.partial(kernel, **static), in_specs=specs or [VM...  18.6 us
    all_to_all x1, blocking collectives, shards(): lax.all_to_all(squares.reshape(chips, 1, LANES), 'samp', 0, 0, axis_index...  13 us
    ppermute x12, starting transfers between devices, unit_hop(): return lax.ppermute(x, 'unit', [(i, i ^ mask) for i in range(unit_count)])  12.2 us
    ppermute x9, waiting for transfers between devices, block_terms(): lax.ppermute(x, 'samp', [(i, (i + d * step) % samp_count) for i in range(...  10.2 us
  transfers between devices with their start and end apart: 28, of which 16 were waited for; matrix products, arithmetic and copies ran while one was open for 0% of the time, Pallas kernels for 2%

profile of v8, /device:TPU:1, one launch (start us, length us, event | category | flops | bytes accessed | tf_op | source)
XLA Modules:
  0.0 182.1 jit_solution(17979728048013838880)
XLA Ops:
  0.6 4.7 %first.1 = (bf16[1024,2048]{1,0:T(8,128)(2,1)S(1)}, bf16[1024,2048]{1,0:T(8,128)(2,1)S(1)}, f32[64,1024]{1,0:T(8,128)S(1)}, f32[512,128]{1,0:T(8,128)S(1)}, f32[512,128]{1,0:T(8,128)S(1)}) custom-call(s32[1,1]{1,0:T(1,128)} %bitcast.core, f32[1024,2048]{1,0:T(8,128)} %states.1, f32[64,1024]{1,0:T(8,128)} %bitcast.38), custom_call_target="tpu_custom_call" | custom-call | flops 1073741824 | bytes 1048576 | tf_op jit(solution)/shard_map/first/pallas_call | solution.py:29
  5.4 3.3 %collective-permute-start = (f32[512,128]{1,0:T(8,128)S(1)}, f32[512,128]{1,0:T(8,128)S(1)}, u32[]{:S(2)}, u32[]{:S(2)}) collective-permute-start(f32[512,128]{1,0:T(8,128)S(1)} %get-tuple-element.44), channel_id=1, source_target_pairs={{0,1},{1,0},{2,3},{3,2},{4,5},{5,4},{6,7},{7,6},{8,9},{9,8},{10,11... | collective-permute-start | bytes 786440 | tf_op jit(solution)/shard_map/ppermute | solution.py:273
  8.7 1.2 turn_states.2
  10.0 9.8 %all_to_all.35 = f32[8,64,128]{2,1,0:T(8,128)S(1)} all-to-all(f32[8,64,128]{2,1,0:T(8,128)S(1)} %bitcast.28), channel_id=1, replica_groups={{0,2,4,6,8,10,12,14},{1,3,5,7,9,11,13,15},{16,18,20,22,24,26,28,30},{17..., dimensions={0} | all-to-all | bytes 524288 | tf_op jit(solution)/shard_map/all_to_all | solution.py:278
  19.8 5.2 %collective-permute-start.3 = (f32[64,128]{1,0:T(8,128)S(1)}, f32[64,128]{1,0:T(8,128)S(1)}, u32[]{:S(2)}, u32[]{:S(2)}) collective-permute-start(f32[64,128]{1,0:T(8,128)S(1)} %sum_pieces.3.refs_0_), channel_id=1, source_target_pairs={{0,48},{1,49},{2,50},{3,51},{4,52},{5,53},{6,54},{7,55},{8,56},{9,... | collective-permute-start | bytes 98312 | tf_op jit(solution)/shard_map/ppermute | solution.py:284
  26.2 2.1 %collective-permute-start.1 = (f32[64,128]{1,0:T(8,128)S(1)}, f32[64,128]{1,0:T(8,128)S(1)}, u32[]{:S(2)}, u32[]{:S(2)}) collective-permute-start(f32[64,128]{1,0:T(8,128)S(1)} %sum_pieces.3.refs_0_), channel_id=1, source_target_pairs={{0,16},{1,17},{2,18},{3,19},{4,20},{5,21},{6,22},{7,23},{8,24},{9,... | collective-permute-start | bytes 98312 | tf_op jit(solution)/shard_map/ppermute | solution.py:284
  28.3 3.4 %collective-permute-done.2.refs_2_ = f32[64,128]{1,0:T(8,128)S(1)} collective-permute-done((f32[64,128]{1,0:T(8,128)S(1)}, f32[64,128]{1,0:T(8,128)S(1)}, u32[]{:S(2)}, u32[]{:S(2)}) %collective-permute-start.2) | collective-permute-done | bytes 32800 | tf_op jit(solution)/shard_map/ppermute | solution.py:284
  31.8 9.6 %all_to_all.36 = f32[8,64,128]{2,1,0:T(8,128)S(1)} all-to-all(f32[8,64,128]{2,1,0:T(8,128)S(1)} %bitcast.29), channel_id=1, replica_groups={{0,2,4,6,8,10,12,14},{1,3,5,7,9,11,13,15},{16,18,20,22,24,26,28,30},{17..., dimensions={0} | all-to-all | bytes 524288 | tf_op jit(solution)/shard_map/all_to_all | solution.py:278
  41.4 3.6 %collective-permute-start.4 = (f32[512,128]{1,0:T(8,128)S(1)}, f32[512,128]{1,0:T(8,128)S(1)}, u32[]{:S(2)}, u32[]{:S(2)}) collective-permute-start(f32[512,128]{1,0:T(8,128)S(1)} %bitcast.22), channel_id=1, source_target_pairs={{0,1},{1,0},{2,3},{3,2},{4,5},{5,4},{6,7},{7,6},{8,9},{9,8},{10,11... | collective-permute-start | bytes 786440 | tf_op jit(solution)/shard_map/ppermute | solution.py:273
  45.0 1.8 turn_states.3
  46.7 1.7 forward.3
  48.4 1.3 collective-permute-start.5
  49.7 1.8 %collective-permute-start.7 = (f32[64,512]{1,0:T(8,128)S(1)}, f32[64,512]{1,0:T(8,128)S(1)}, u32[]{:S(2)}, u32[]{:S(2)}) collective-permute-start(f32[64,512]{1,0:T(8,128)S(1)} %get-tuple-element.51), channel_id=1, source_target_pairs={{0,192},{64,128},{128,64},{192,0},{1,193},{65,129},{129,65},{193,1... | collective-permute-start | bytes 393224 | tf_op jit(solution)/shard_map/ppermute | solution.py:299
  51.5 2.5 %collective-permute-done.5 = f32[72,512]{1,0:T(8,128)S(1)} collective-permute-done((f32[72,512]{1,0:T(8,128)S(1)}, f32[72,512]{1,0:T(8,128)S(1)}, u32[]{:S(2)}, u32[]{:S(2)}) %collective-permute-start.5) | collective-permute-done | bytes 147488 | tf_op jit(solution)/shard_map/ppermute | solution.py:299
  54.0 2.6 %collective-permute-start.6 = (f32[72,512]{1,0:T(8,128)S(1)}, f32[72,512]{1,0:T(8,128)S(1)}, u32[]{:S(2)}, u32[]{:S(2)}) collective-permute-start(f32[72,512]{1,0:T(8,128)S(1)} %add.29.refs_0_), channel_id=1, source_target_pairs={{0,192},{64,128},{128,64},{192,0},{1,193},{65,129},{129,65},{193,1... | collective-permute-start | bytes 442376 | tf_op jit(solution)/shard_map/ppermute | solution.py:299
  56.9 4.1 %collective-permute-done.8.refs_3_ = f32[64,512]{1,0:T(8,128)S(1)} collective-permute-done((f32[64,512]{1,0:T(8,128)S(1)}, f32[64,512]{1,0:T(8,128)S(1)}, u32[]{:S(2)}, u32[]{:S(2)}) %collective-permute-start.8) | collective-permute-done | bytes 131104 | tf_op jit(solution)/shard_map/ppermute | solution.py:299
  61.0 1.6 back.2
  62.5 2.0 %collective-permute-start.9 = (f32[576,128]{1,0:T(8,128)S(1)}, f32[576,128]{1,0:T(8,128)S(1)}, u32[]{:S(2)}, u32[]{:S(2)}) collective-permute-start(f32[576,128]{1,0:T(8,128)S(1)} %get-tuple-element.53), channel_id=1, source_target_pairs={{0,1},{1,0},{2,3},{3,2},{4,5},{5,4},{6,7},{7,6},{8,9},{9,8},{10,11... | collective-permute-start | bytes 884744 | tf_op jit(solution)/shard_map/ppermute | solution.py:273
  64.6 1.2 collective-permute-done.9
  65.8 9.6 %all_to_all.37 = f32[8,72,128]{2,1,0:T(8,128)S(1)} all-to-all(f32[8,72,128]{2,1,0:T(8,128)S(1)} %bitcast.36), channel_id=1, replica_groups={{0,2,4,6,8,10,12,14},{1,3,5,7,9,11,13,15},{16,18,20,22,24,26,28,30},{17..., dimensions={0} | all-to-all | bytes 589824 | tf_op jit(solution)/shard_map/all_to_all | solution.py:278
  75.4 1.6 collective-permute-start.12
  77.1 2.7 %collective-permute-start.11 = (f32[72,128]{1,0:T(8,128)S(1)}, f32[72,128]{1,0:T(8,128)S(1)}, u32[]{:S(2)}, u32[]{:S(2)}) collective-permute-start(f32[72,128]{1,0:T(8,128)S(1)} %sum_pieces.4.refs_0_), channel_id=1, source_target_pairs={{0,32},{1,33},{2,34},{3,35},{4,36},{5,37},{6,38},{7,39},{8,40},{9,... | collective-permute-start | bytes 110600 | tf_op jit(solution)/shard_map/ppermute | solution.py:284
  79.8 2.3 %collective-permute-start.10 = (f32[72,128]{1,0:T(8,128)S(1)}, f32[72,128]{1,0:T(8,128)S(1)}, u32[]{:S(2)}, u32[]{:S(2)}) collective-permute-start(f32[72,128]{1,0:T(8,128)S(1)} %sum_pieces.4.refs_0_), channel_id=1, source_target_pairs={{0,16},{1,17},{2,18},{3,19},{4,20},{5,21},{6,22},{7,23},{8,24},{9,... | collective-permute-start | bytes 110600 | tf_op jit(solution)/shard_map/ppermute | solution.py:284
  82.1 1.9 %collective-permute-done.11.refs_2_ = f32[72,128]{1,0:T(8,128)S(1)} collective-permute-done((f32[72,128]{1,0:T(8,128)S(1)}, f32[72,128]{1,0:T(8,128)S(1)}, u32[]{:S(2)}, u32[]{:S(2)}) %collective-permute-start.11) | collective-permute-done | bytes 36896 | tf_op jit(solution)/shard_map/ppermute | solution.py:284
  85.1 9.5 %all_to_all.38 = f32[8,64,128]{2,1,0:T(8,128)S(1)} all-to-all(f32[8,64,128]{2,1,0:T(8,128)S(1)} %bitcast.31), channel_id=1, replica_groups={{0,2,4,6,8,10,12,14},{1,3,5,7,9,11,13,15},{16,18,20,22,24,26,28,30},{17..., dimensions={0} | all-to-all | bytes 524288 | tf_op jit(solution)/shard_map/all_to_all | solution.py:278
  94.6 3.0 %collective-permute-start.13 = (f32[512,128]{1,0:T(8,128)S(1)}, f32[512,128]{1,0:T(8,128)S(1)}, u32[]{:S(2)}, u32[]{:S(2)}) collective-permute-start(f32[512,128]{1,0:T(8,128)S(1)} %bitcast.26), channel_id=1, source_target_pairs={{0,1},{1,0},{2,3},{3,2},{4,5},{5,4},{6,7},{7,6},{8,9},{9,8},{10,11... | collective-permute-start | bytes 786440 | tf_op jit(solution)/shard_map/ppermute | solution.py:273
  98.8 1.9 %forward.4 = (f32[1024,128]{1,0:T(8,128)S(1)}, f32[1024,128]{1,0:T(8,128)S(1)}, f32[72,512]{1,0:T(8,128)S(1)}, f32[64,512]{1,0:T(8,128)S(1)}) custom-call(f32[512,128]{1,0:T(8,128)S(1)} %bitcast.27, f32[512,128]{1,0:T(8,128)S(1)} %collective-permute-done.13.refs_1_, f32[8,128]{1,0:T(8,128)S(1)} %get-tuple-element.56.refs_2_.size0, ...), custom_call_target="tpu_custom_call" | custom-call | flops 1073741824 | bytes 1048576 | tf_op jit(solution)/shard_map/forward/pallas_call | solution.py:29
  100.8 1.3 collective-permute-start.16
  102.1 3.7 %collective-permute-done.14 = f32[72,512]{1,0:T(8,128)S(1)} collective-permute-done((f32[72,512]{1,0:T(8,128)S(1)}, f32[72,512]{1,0:T(8,128)S(1)}, u32[]{:S(2)}, u32[]{:S(2)}) %collective-permute-start.14) | collective-permute-done | bytes 147488 | tf_op jit(solution)/shard_map/ppermute | solution.py:299
  105.9 1.3 collective-permute-start.15
  107.3 3.8 %collective-permute-done.17.refs_3_ = f32[64,512]{1,0:T(8,128)S(1)} collective-permute-done((f32[64,512]{1,0:T(8,128)S(1)}, f32[64,512]{1,0:T(8,128)S(1)}, u32[]{:S(2)}, u32[]{:S(2)}) %collective-permute-start.17) | collective-permute-done | bytes 131104 | tf_op jit(solution)/shard_map/ppermute | solution.py:299
  111.2 1.6 back.3
  112.8 2.7 %collective-permute-start.18 = (f32[576,128]{1,0:T(8,128)S(1)}, f32[576,128]{1,0:T(8,128)S(1)}, u32[]{:S(2)}, u32[]{:S(2)}) collective-permute-start(f32[576,128]{1,0:T(8,128)S(1)} %get-tuple-element.62), channel_id=1, source_target_pairs={{0,1},{1,0},{2,3},{3,2},{4,5},{5,4},{6,7},{7,6},{8,9},{9,8},{10,11... | collective-permute-start | bytes 884744 | tf_op jit(solution)/shard_map/ppermute | solution.py:273
  115.5 1.2 collective-permute-done.18
  116.7 9.6 %all_to_all.39 = f32[8,72,128]{2,1,0:T(8,128)S(1)} all-to-all(f32[8,72,128]{2,1,0:T(8,128)S(1)} %bitcast.37), channel_id=1, replica_groups={{0,2,4,6,8,10,12,14},{1,3,5,7,9,11,13,15},{16,18,20,22,24,26,28,30},{17..., dimensions={0} | all-to-all | bytes 589824 | tf_op jit(solution)/shard_map/all_to_all | solution.py:278
  126.4 1.9 %collective-permute-start.21 = (f32[72,128]{1,0:T(8,128)S(1)}, f32[72,128]{1,0:T(8,128)S(1)}, u32[]{:S(2)}, u32[]{:S(2)}) collective-permute-start(f32[72,128]{1,0:T(8,128)S(1)} %sum_pieces.5.refs_0_), channel_id=1, source_target_pairs={{0,48},{1,49},{2,50},{3,51},{4,52},{5,53},{6,54},{7,55},{8,56},{9,... | collective-permute-start | bytes 110600 | tf_op jit(solution)/shard_map/ppermute | solution.py:284
  128.3 2.8 %collective-permute-start.20 = (f32[72,128]{1,0:T(8,128)S(1)}, f32[72,128]{1,0:T(8,128)S(1)}, u32[]{:S(2)}, u32[]{:S(2)}) collective-permute-start(f32[72,128]{1,0:T(8,128)S(1)} %sum_pieces.5.refs_0_), channel_id=1, source_target_pairs={{0,32},{1,33},{2,34},{3,35},{4,36},{5,37},{6,38},{7,39},{8,40},{9,... | collective-permute-start | bytes 110600 | tf_op jit(solution)/shard_map/ppermute | solution.py:284
  131.1 1.2 collective-permute-start.19
  132.3 2.7 %collective-permute-done.20.refs_2_ = f32[72,128]{1,0:T(8,128)S(1)} collective-permute-done((f32[72,128]{1,0:T(8,128)S(1)}, f32[72,128]{1,0:T(8,128)S(1)}, u32[]{:S(2)}, u32[]{:S(2)}) %collective-permute-start.20) | collective-permute-done | bytes 36896 | tf_op jit(solution)/shard_map/ppermute | solution.py:284
  136.2 9.6 %all_to_all.40 = f32[8,64,128]{2,1,0:T(8,128)S(1)} all-to-all(f32[8,64,128]{2,1,0:T(8,128)S(1)} %bitcast.32), channel_id=1, replica_groups={{0,2,4,6,8,10,12,14},{1,3,5,7,9,11,13,15},{16,18,20,22,24,26,28,30},{17..., dimensions={0} | all-to-all | bytes 524288 | tf_op jit(solution)/shard_map/all_to_all | solution.py:278
  145.8 3.2 %collective-permute-start.22 = (f32[512,128]{1,0:T(8,128)S(1)}, f32[512,128]{1,0:T(8,128)S(1)}, u32[]{:S(2)}, u32[]{:S(2)}) collective-permute-start(f32[512,128]{1,0:T(8,128)S(1)} %bitcast.24), channel_id=1, source_target_pairs={{0,1},{1,0},{2,3},{3,2},{4,5},{5,4},{6,7},{7,6},{8,9},{9,8},{10,11... | collective-permute-start | bytes 786440 | tf_op jit(solution)/shard_map/ppermute | solution.py:273
  150.1 1.9 %forward.5 = (f32[1024,128]{1,0:T(8,128)S(1)}, f32[1024,128]{1,0:T(8,128)S(1)}, f32[72,512]{1,0:T(8,128)S(1)}, f32[64,512]{1,0:T(8,128)S(1)}) custom-call(f32[512,128]{1,0:T(8,128)S(1)} %bitcast.25, f32[512,128]{1,0:T(8,128)S(1)} %collective-permute-done.22.refs_1_, f32[8,128]{1,0:T(8,128)S(1)} %get-tuple-element.65.refs_2_.size1, ...), custom_call_target="tpu_custom_call" | custom-call | flops 1073741824 | bytes 1048576 | tf_op jit(solution)/shard_map/forward/pallas_call | solution.py:29
  152.1 1.6 collective-permute-start.25
  153.8 3.4 %collective-permute-done.23 = f32[72,512]{1,0:T(8,128)S(1)} collective-permute-done((f32[72,512]{1,0:T(8,128)S(1)}, f32[72,512]{1,0:T(8,128)S(1)}, u32[]{:S(2)}, u32[]{:S(2)}) %collective-permute-start.23) | collective-permute-done | bytes 147488 | tf_op jit(solution)/shard_map/ppermute | solution.py:299
  157.2 1.6 collective-permute-start.24
  159.6 3.4 %collective-permute-done.26.h3 = f32[64,512]{1,0:T(8,128)S(1)} collective-permute-done((f32[64,512]{1,0:T(8,128)S(1)}, f32[64,512]{1,0:T(8,128)S(1)}, u32[]{:S(2)}, u32[]{:S(2)}) %collective-permute-start.26) | collective-permute-done | bytes 131104 | tf_op jit(solution)/shard_map/ppermute | solution.py:299
  163.3 13.0 %all_to_all.41 = f32[32,1,128]{2,1,0:T(1,128)S(1)} all-to-all(f32[32,1,128]{2,1,0:T(1,128)S(1)} %bitcast.35), channel_id=1, replica_groups={{0,2,4,6,8,10,12,14,16,18,20,22,24,26,28,30,32,34,36,38,40,42,44,46,48,..., dimensions={0} | all-to-all | bytes 32768 | tf_op jit(solution)/shard_map/all_to_all | solution.py:403
  176.4 3.8 %collective-permute-start.27 = (f32[32,128]{1,0:T(8,128)S(1)}, f32[32,128]{1,0:T(8,128)S(1)}, u32[]{:S(2)}, u32[]{:S(2)}) collective-permute-start(f32[32,128]{1,0:T(8,128)S(1)} %bitcast.33), channel_id=1, source_target_pairs={{0,1},{1,0},{2,3},{3,2},{4,5},{5,4},{6,7},{7,6},{8,9},{9,8},{10,11... | collective-permute-start | bytes 49160 | tf_op jit(solution)/shard_map/ppermute | solution.py:273
  (41 shorter events, 9.6 us)
Async XLA Ops:
  5.4 4.6 %collective-permute-start = (f32[512,128]{1,0:T(8,128)S(1)}, f32[512,128]{1,0:T(8,128)S(1)}, u32[]{:S(2)}, u32[]{:S(2)}) collective-permute-start(f32[512,128]{1,0:T(8,128)S(1)} %get-tuple-element.44), channel_id=1, source_target_pairs={{0,1},{1,0},{2,3},{3,2},{4,5},{5,4},{6,7},{7,6},{8,9},{9,8},{10,11... | collective-permute-start | bytes 786440 | tf_op jit(solution)/shard_map/ppermute | solution.py:273
  19.8 8.5 %collective-permute-start.3 = (f32[64,128]{1,0:T(8,128)S(1)}, f32[64,128]{1,0:T(8,128)S(1)}, u32[]{:S(2)}, u32[]{:S(2)}) collective-permute-start(f32[64,128]{1,0:T(8,128)S(1)} %sum_pieces.3.refs_0_), channel_id=1, source_target_pairs={{0,48},{1,49},{2,50},{3,51},{4,52},{5,53},{6,54},{7,55},{8,56},{9,... | collective-permute-start | bytes 98312 | tf_op jit(solution)/shard_map/ppermute | solution.py:284
  25.1 6.7 %collective-permute-start.2 = (f32[64,128]{1,0:T(8,128)S(1)}, f32[64,128]{1,0:T(8,128)S(1)}, u32[]{:S(2)}, u32[]{:S(2)}) collective-permute-start(f32[64,128]{1,0:T(8,128)S(1)} %sum_pieces.3.refs_0_), channel_id=1, source_target_pairs={{0,32},{1,33},{2,34},{3,35},{4,36},{5,37},{6,38},{7,39},{8,40},{9,... | collective-permute-start | bytes 98312 | tf_op jit(solution)/shard_map/ppermute | solution.py:284
  26.2 5.5 %collective-permute-start.1 = (f32[64,128]{1,0:T(8,128)S(1)}, f32[64,128]{1,0:T(8,128)S(1)}, u32[]{:S(2)}, u32[]{:S(2)}) collective-permute-start(f32[64,128]{1,0:T(8,128)S(1)} %sum_pieces.3.refs_0_), channel_id=1, source_target_pairs={{0,16},{1,17},{2,18},{3,19},{4,20},{5,21},{6,22},{7,23},{8,24},{9,... | collective-permute-start | bytes 98312 | tf_op jit(solution)/shard_map/ppermute | solution.py:284
  41.4 5.3 %collective-permute-start.4 = (f32[512,128]{1,0:T(8,128)S(1)}, f32[512,128]{1,0:T(8,128)S(1)}, u32[]{:S(2)}, u32[]{:S(2)}) collective-permute-start(f32[512,128]{1,0:T(8,128)S(1)} %bitcast.22), channel_id=1, source_target_pairs={{0,1},{1,0},{2,3},{3,2},{4,5},{5,4},{6,7},{7,6},{8,9},{9,8},{10,11... | collective-permute-start | bytes 786440 | tf_op jit(solution)/shard_map/ppermute | solution.py:273
  48.4 5.6 %collective-permute-start.5 = (f32[72,512]{1,0:T(8,128)S(1)}, f32[72,512]{1,0:T(8,128)S(1)}, u32[]{:S(2)}, u32[]{:S(2)}) collective-permute-start(f32[72,512]{1,0:T(8,128)S(1)} %get-tuple-element.50), channel_id=1, source_target_pairs={{0,64},{64,0},{128,192},{192,128},{1,65},{65,1},{129,193},{193,129... | collective-permute-start | bytes 442376 | tf_op jit(solution)/shard_map/ppermute | solution.py:299
  49.7 6.9 %collective-permute-start.7 = (f32[64,512]{1,0:T(8,128)S(1)}, f32[64,512]{1,0:T(8,128)S(1)}, u32[]{:S(2)}, u32[]{:S(2)}) collective-permute-start(f32[64,512]{1,0:T(8,128)S(1)} %get-tuple-element.51), channel_id=1, source_target_pairs={{0,192},{64,128},{128,64},{192,0},{1,193},{65,129},{129,65},{193,1... | collective-permute-start | bytes 393224 | tf_op jit(solution)/shard_map/ppermute | solution.py:299
  54.0 7.0 %collective-permute-start.6 = (f32[72,512]{1,0:T(8,128)S(1)}, f32[72,512]{1,0:T(8,128)S(1)}, u32[]{:S(2)}, u32[]{:S(2)}) collective-permute-start(f32[72,512]{1,0:T(8,128)S(1)} %add.29.refs_0_), channel_id=1, source_target_pairs={{0,192},{64,128},{128,64},{192,0},{1,193},{65,129},{129,65},{193,1... | collective-permute-start | bytes 442376 | tf_op jit(solution)/shard_map/ppermute | solution.py:299
  56.6 4.4 %collective-permute-start.8 = (f32[64,512]{1,0:T(8,128)S(1)}, f32[64,512]{1,0:T(8,128)S(1)}, u32[]{:S(2)}, u32[]{:S(2)}) collective-permute-start(f32[64,512]{1,0:T(8,128)S(1)} %add.30.refs_2_), channel_id=1, source_target_pairs={{0,64},{64,0},{128,192},{192,128},{1,65},{65,1},{129,193},{193,129... | collective-permute-start | bytes 393224 | tf_op jit(solution)/shard_map/ppermute | solution.py:299
  62.5 3.2 %collective-permute-start.9 = (f32[576,128]{1,0:T(8,128)S(1)}, f32[576,128]{1,0:T(8,128)S(1)}, u32[]{:S(2)}, u32[]{:S(2)}) collective-permute-start(f32[576,128]{1,0:T(8,128)S(1)} %get-tuple-element.53), channel_id=1, source_target_pairs={{0,1},{1,0},{2,3},{3,2},{4,5},{5,4},{6,7},{7,6},{8,9},{9,8},{10,11... | collective-permute-start | bytes 884744 | tf_op jit(solution)/shard_map/ppermute | solution.py:273
  75.4 6.7 %collective-permute-start.12 = (f32[72,128]{1,0:T(8,128)S(1)}, f32[72,128]{1,0:T(8,128)S(1)}, u32[]{:S(2)}, u32[]{:S(2)}) collective-permute-start(f32[72,128]{1,0:T(8,128)S(1)} %sum_pieces.4.refs_0_), channel_id=1, source_target_pairs={{0,48},{1,49},{2,50},{3,51},{4,52},{5,53},{6,54},{7,55},{8,56},{9,... | collective-permute-start | bytes 110600 | tf_op jit(solution)/shard_map/ppermute | solution.py:284
  77.1 6.9 %collective-permute-start.11 = (f32[72,128]{1,0:T(8,128)S(1)}, f32[72,128]{1,0:T(8,128)S(1)}, u32[]{:S(2)}, u32[]{:S(2)}) collective-permute-start(f32[72,128]{1,0:T(8,128)S(1)} %sum_pieces.4.refs_0_), channel_id=1, source_target_pairs={{0,32},{1,33},{2,34},{3,35},{4,36},{5,37},{6,38},{7,39},{8,40},{9,... | collective-permute-start | bytes 110600 | tf_op jit(solution)/shard_map/ppermute | solution.py:284
  79.8 5.3 %collective-permute-start.10 = (f32[72,128]{1,0:T(8,128)S(1)}, f32[72,128]{1,0:T(8,128)S(1)}, u32[]{:S(2)}, u32[]{:S(2)}) collective-permute-start(f32[72,128]{1,0:T(8,128)S(1)} %sum_pieces.4.refs_0_), channel_id=1, source_target_pairs={{0,16},{1,17},{2,18},{3,19},{4,20},{5,21},{6,22},{7,23},{8,24},{9,... | collective-permute-start | bytes 110600 | tf_op jit(solution)/shard_map/ppermute | solution.py:284
  94.6 4.2 %collective-permute-start.13 = (f32[512,128]{1,0:T(8,128)S(1)}, f32[512,128]{1,0:T(8,128)S(1)}, u32[]{:S(2)}, u32[]{:S(2)}) collective-permute-start(f32[512,128]{1,0:T(8,128)S(1)} %bitcast.26), channel_id=1, source_target_pairs={{0,1},{1,0},{2,3},{3,2},{4,5},{5,4},{6,7},{7,6},{8,9},{9,8},{10,11... | collective-permute-start | bytes 786440 | tf_op jit(solution)/shard_map/ppermute | solution.py:273
  100.7 5.1 %collective-permute-start.14 = (f32[72,512]{1,0:T(8,128)S(1)}, f32[72,512]{1,0:T(8,128)S(1)}, u32[]{:S(2)}, u32[]{:S(2)}) collective-permute-start(f32[72,512]{1,0:T(8,128)S(1)} %get-tuple-element.58), channel_id=1, source_target_pairs={{0,64},{64,0},{128,192},{192,128},{1,65},{65,1},{129,193},{193,129... | collective-permute-start | bytes 442376 | tf_op jit(solution)/shard_map/ppermute | solution.py:299
  100.8 6.4 %collective-permute-start.16 = (f32[64,512]{1,0:T(8,128)S(1)}, f32[64,512]{1,0:T(8,128)S(1)}, u32[]{:S(2)}, u32[]{:S(2)}) collective-permute-start(f32[64,512]{1,0:T(8,128)S(1)} %get-tuple-element.59), channel_id=1, source_target_pairs={{0,192},{64,128},{128,64},{192,0},{1,193},{65,129},{129,65},{193,1... | collective-permute-start | bytes 393224 | tf_op jit(solution)/shard_map/ppermute | solution.py:299
  105.9 5.3 %collective-permute-start.15 = (f32[72,512]{1,0:T(8,128)S(1)}, f32[72,512]{1,0:T(8,128)S(1)}, u32[]{:S(2)}, u32[]{:S(2)}) collective-permute-start(f32[72,512]{1,0:T(8,128)S(1)} %add.32.refs_0_), channel_id=1, source_target_pairs={{0,192},{64,128},{128,64},{192,0},{1,193},{65,129},{129,65},{193,1... | collective-permute-start | bytes 442376 | tf_op jit(solution)/shard_map/ppermute | solution.py:299
  107.2 3.9 %collective-permute-start.17 = (f32[64,512]{1,0:T(8,128)S(1)}, f32[64,512]{1,0:T(8,128)S(1)}, u32[]{:S(2)}, u32[]{:S(2)}) collective-permute-start(f32[64,512]{1,0:T(8,128)S(1)} %add.33.refs_2_), channel_id=1, source_target_pairs={{0,64},{64,0},{128,192},{192,128},{1,65},{65,1},{129,193},{193,129... | collective-permute-start | bytes 393224 | tf_op jit(solution)/shard_map/ppermute | solution.py:299
  112.8 3.9 %collective-permute-start.18 = (f32[576,128]{1,0:T(8,128)S(1)}, f32[576,128]{1,0:T(8,128)S(1)}, u32[]{:S(2)}, u32[]{:S(2)}) collective-permute-start(f32[576,128]{1,0:T(8,128)S(1)} %get-tuple-element.62), channel_id=1, source_target_pairs={{0,1},{1,0},{2,3},{3,2},{4,5},{5,4},{6,7},{7,6},{8,9},{9,8},{10,11... | collective-permute-start | bytes 884744 | tf_op jit(solution)/shard_map/ppermute | solution.py:273
  126.4 5.9 %collective-permute-start.21 = (f32[72,128]{1,0:T(8,128)S(1)}, f32[72,128]{1,0:T(8,128)S(1)}, u32[]{:S(2)}, u32[]{:S(2)}) collective-permute-start(f32[72,128]{1,0:T(8,128)S(1)} %sum_pieces.5.refs_0_), channel_id=1, source_target_pairs={{0,48},{1,49},{2,50},{3,51},{4,52},{5,53},{6,54},{7,55},{8,56},{9,... | collective-permute-start | bytes 110600 | tf_op jit(solution)/shard_map/ppermute | solution.py:284
  128.3 6.8 %collective-permute-start.20 = (f32[72,128]{1,0:T(8,128)S(1)}, f32[72,128]{1,0:T(8,128)S(1)}, u32[]{:S(2)}, u32[]{:S(2)}) collective-permute-start(f32[72,128]{1,0:T(8,128)S(1)} %sum_pieces.5.refs_0_), channel_id=1, source_target_pairs={{0,32},{1,33},{2,34},{3,35},{4,36},{5,37},{6,38},{7,39},{8,40},{9,... | collective-permute-start | bytes 110600 | tf_op jit(solution)/shard_map/ppermute | solution.py:284
  131.1 5.0 %collective-permute-start.19 = (f32[72,128]{1,0:T(8,128)S(1)}, f32[72,128]{1,0:T(8,128)S(1)}, u32[]{:S(2)}, u32[]{:S(2)}) collective-permute-start(f32[72,128]{1,0:T(8,128)S(1)} %sum_pieces.5.refs_0_), channel_id=1, source_target_pairs={{0,16},{1,17},{2,18},{3,19},{4,20},{5,21},{6,22},{7,23},{8,24},{9,... | collective-permute-start | bytes 110600 | tf_op jit(solution)/shard_map/ppermute | solution.py:284
  145.8 4.3 %collective-permute-start.22 = (f32[512,128]{1,0:T(8,128)S(1)}, f32[512,128]{1,0:T(8,128)S(1)}, u32[]{:S(2)}, u32[]{:S(2)}) collective-permute-start(f32[512,128]{1,0:T(8,128)S(1)} %bitcast.24), channel_id=1, source_target_pairs={{0,1},{1,0},{2,3},{3,2},{4,5},{5,4},{6,7},{7,6},{8,9},{9,8},{10,11... | collective-permute-start | bytes 786440 | tf_op jit(solution)/shard_map/ppermute | solution.py:273
  152.0 5.1 %collective-permute-start.23 = (f32[72,512]{1,0:T(8,128)S(1)}, f32[72,512]{1,0:T(8,128)S(1)}, u32[]{:S(2)}, u32[]{:S(2)}) collective-permute-start(f32[72,512]{1,0:T(8,128)S(1)} %get-tuple-element.68), channel_id=1, source_target_pairs={{0,64},{64,0},{128,192},{192,128},{1,65},{65,1},{129,193},{193,129... | collective-permute-start | bytes 442376 | tf_op jit(solution)/shard_map/ppermute | solution.py:299
  152.1 6.7 %collective-permute-start.25 = (f32[64,512]{1,0:T(8,128)S(1)}, f32[64,512]{1,0:T(8,128)S(1)}, u32[]{:S(2)}, u32[]{:S(2)}) collective-permute-start(f32[64,512]{1,0:T(8,128)S(1)} %get-tuple-element.69), channel_id=1, source_target_pairs={{0,192},{64,128},{128,64},{192,0},{1,193},{65,129},{129,65},{193,1... | collective-permute-start | bytes 393224 | tf_op jit(solution)/shard_map/ppermute | solution.py:299
  157.2 5.9 %collective-permute-start.24 = (f32[72,512]{1,0:T(8,128)S(1)}, f32[72,512]{1,0:T(8,128)S(1)}, u32[]{:S(2)}, u32[]{:S(2)}) collective-permute-start(f32[72,512]{1,0:T(8,128)S(1)} %add.35.h0), channel_id=1, source_target_pairs={{0,192},{64,128},{128,64},{192,0},{1,193},{65,129},{129,65},{193,1... | collective-permute-start | bytes 442376 | tf_op jit(solution)/shard_map/ppermute | solution.py:299
  158.9 4.2 %collective-permute-start.26 = (f32[64,512]{1,0:T(8,128)S(1)}, f32[64,512]{1,0:T(8,128)S(1)}, u32[]{:S(2)}, u32[]{:S(2)}) collective-permute-start(f32[64,512]{1,0:T(8,128)S(1)} %add.36.h2), channel_id=1, source_target_pairs={{0,64},{64,0},{128,192},{192,128},{1,65},{65,1},{129,193},{193,129... | collective-permute-start | bytes 393224 | tf_op jit(solution)/shard_map/ppermute | solution.py:299
  176.4 4.6 %collective-permute-start.27 = (f32[32,128]{1,0:T(8,128)S(1)}, f32[32,128]{1,0:T(8,128)S(1)}, u32[]{:S(2)}, u32[]{:S(2)}) collective-permute-start(f32[32,128]{1,0:T(8,128)S(1)} %bitcast.33), channel_id=1, source_target_pairs={{0,1},{1,0},{2,3},{3,2},{4,5},{5,4},{6,7},{7,6},{8,9},{9,8},{10,11... | collective-permute-start | bytes 49160 | tf_op jit(solution)/shard_map/ppermute | solution.py:273

commit v9 on v8

--- a/solution.py
+++ b/solution.py
@@ -113,14 +113,17 @@
     token[...] = jnp.zeros(token.shape, F32)
 
 
-def combine(a, ra, b, rb):
-    n = b.shape[0]
-    image = jnp.concatenate([a[:n, :] + ra[:n, :], b[...] + rb[...]], axis=1)
-    return image, a[n : n + TILE, :LANES] + ra[n : n + TILE, :LANES]
+def combine(a, ra, b, rb, n):
+    tiles = b.shape[0] // n
+    parts = []
+    for x, rx in ((a, ra), (b, rb)):
+        parts += [x[j * n : (j + 1) * n, :] + rx[j * n : (j + 1) * n, :] for j in range(tiles)]
+    image = jnp.concatenate(parts, axis=1)
+    return image, a[tiles * n :, :] + ra[tiles * n :, :]
 
 
 def step_image(hops, before, scal, image_out, scal_out):
-    image, tail = combine(*hops)
+    image, tail = combine(*hops, image_out.shape[0])
     gamma = tail[0:1]
     if before is None:
         beta = jnp.zeros_like(gamma)
@@ -208,20 +211,24 @@
         g = g_old[...] - size[0:1, :] * (q + ridge * d)
         cross = jnp.sum(g * d)
     gradient[...] = g
-    n = b.shape[0]
-    stride = g.shape[0] // n
+    stride = high.shape[0] // LANES
+    n = g.shape[0] // stride
     x3 = split3(
         jnp.concatenate([gradient[pl.ds(j, n, stride=stride), :] for j in range(stride)], axis=1)
     )
-    steps = high.shape[1] // WIDE
-    for t in range(steps):
+    tiles = b.shape[0] // n
+    for t in range(high.shape[1] // WIDE):
         at = pl.ds(t * WIDE, WIDE)
         p = rows_product(x3, high[:, at], low[:, at])
-        out, k = (a, t) if t < steps // 2 else (b, t - steps // 2)
-        out[0:n, k * WIDE : (k + 1) * WIDE] = p
-    a[n : n + 1, :] = jnp.broadcast_to(jnp.sum(g * g), (1, a.shape[1]))
-    rest = jnp.zeros((TILE - 1, a.shape[1]), F32)
-    a[n + 1 :, :] = rest if cross is None else rest + cross
+        for i in range(WIDE // LANES):
+            j = t * (WIDE // LANES) + i
+            out = a if j < tiles else b
+            k = j % tiles
+            out[k * n : (k + 1) * n, :] = p[:, i * LANES : (i + 1) * LANES]
+    k = tiles * n
+    a[k : k + 1, :] = row(jnp.sum(g * g))
+    rest = jnp.zeros((TILE - 1, LANES), F32)
+    a[k + 1 :, :] = rest if cross is None else rest + cross
 
 
 def prepare(core, size0, size1, d0, d1, g2, i0, i1, targets, readout, before, gradient, residual, token, sums):
@@ -304,7 +311,8 @@
 
     image_shape = shape(outputs, samples)
     whole = shape(outputs * rows, LANES)
-    partial = [shape(outputs + TILE, samples // 2), shape(outputs, samples // 2)]
+    tiles = outputs * samples // 2 // LANES
+    partial = [shape(tiles + TILE, LANES), shape(tiles, LANES)]
     flops = 2 * 4 * samples * units * outputs
 
     smem = pl.BlockSpec(memory_space=pltpu.SMEM)

time: 182 us -> 182 us (level)
  no operation moved by 1% of the time
where the time goes in v9:
time: 182 us; the launch traced here: 181 us
  blocking collectives  70.9 us (39%)
  starting transfers between devices  54.9 us (30%)
  waiting for transfers between devices  36 us (20%)
  Pallas kernels  18.5 us (10%)
    all_to_all x6, blocking collectives, exchange(): x = lax.all_to_all(x, 'samp', 0, 0, axis_index_groups=groups, tiled=True)  57.8 us
    ppermute x7, starting transfers between devices, swap(): return lax.ppermute(x, 'samp', swap_cores)  21.7 us
    ppermute x9, starting transfers between devices, block_terms(): lax.ppermute(x, 'samp', [(i, (i + d * step) % samp_count) for i in range(...  21 us
    ppermute x12, waiting for transfers between devices, unit_hop(): return lax.ppermute(x, 'unit', [(i, i ^ mask) for i in range(unit_count)])  20.1 us
    pallas_call x18, Pallas kernels, call(): pl.pallas_call(functools.partial(kernel, **static), in_specs=specs or [VM...  18.5 us
    all_to_all x1, blocking collectives, shards(): lax.all_to_all(squares.reshape(chips, 1, LANES), 'samp', 0, 0, axis_index...  13.1 us
    ppermute x12, starting transfers between devices, unit_hop(): return lax.ppermute(x, 'unit', [(i, i ^ mask) for i in range(unit_count)])  12.2 us
    ppermute x9, waiting for transfers between devices, block_terms(): lax.ppermute(x, 'samp', [(i, (i + d * step) % samp_count) for i in range(...  10.3 us
  transfers between devices with their start and end apart: 28, of which 16 were waited for; matrix products, arithmetic and copies ran while one was open for 0% of the time, Pallas kernels for 2%

profile of v9, /device:TPU:1, one launch (start us, length us, event | category | flops | bytes accessed | tf_op | source)
XLA Modules:
  0.0 181.2 jit_solution(4916876532890228140)
XLA Ops:
  0.6 4.7 %first.1 = (bf16[1024,2048]{1,0:T(8,128)(2,1)S(1)}, bf16[1024,2048]{1,0:T(8,128)(2,1)S(1)}, f32[64,1024]{1,0:T(8,128)S(1)}, f32[512,128]{1,0:T(8,128)S(1)}, f32[512,128]{1,0:T(8,128)S(1)}) custom-call(s32[1,1]{1,0:T(1,128)} %bitcast.core, f32[1024,2048]{1,0:T(8,128)} %states.1, f32[64,1024]{1,0:T(8,128)} %bitcast.38), custom_call_target="tpu_custom_call" | custom-call | flops 1073741824 | bytes 1048576 | tf_op jit(solution)/shard_map/first/pallas_call | solution.py:29
  5.4 3.3 %collective-permute-start = (f32[512,128]{1,0:T(8,128)S(1)}, f32[512,128]{1,0:T(8,128)S(1)}, u32[]{:S(2)}, u32[]{:S(2)}) collective-permute-start(f32[512,128]{1,0:T(8,128)S(1)} %get-tuple-element.44), channel_id=1, source_target_pairs={{0,1},{1,0},{2,3},{3,2},{4,5},{5,4},{6,7},{7,6},{8,9},{9,8},{10,11... | collective-permute-start | bytes 786440 | tf_op jit(solution)/shard_map/ppermute | solution.py:280
  8.7 1.2 turn_states.2
  10.0 9.8 %all_to_all.35 = f32[8,64,128]{2,1,0:T(8,128)S(1)} all-to-all(f32[8,64,128]{2,1,0:T(8,128)S(1)} %bitcast.28), channel_id=1, replica_groups={{0,2,4,6,8,10,12,14},{1,3,5,7,9,11,13,15},{16,18,20,22,24,26,28,30},{17..., dimensions={0} | all-to-all | bytes 524288 | tf_op jit(solution)/shard_map/all_to_all | solution.py:285
  19.8 5.2 %collective-permute-start.3 = (f32[64,128]{1,0:T(8,128)S(1)}, f32[64,128]{1,0:T(8,128)S(1)}, u32[]{:S(2)}, u32[]{:S(2)}) collective-permute-start(f32[64,128]{1,0:T(8,128)S(1)} %sum_pieces.3.refs_0_), channel_id=1, source_target_pairs={{0,48},{1,49},{2,50},{3,51},{4,52},{5,53},{6,54},{7,55},{8,56},{9,... | collective-permute-start | bytes 98312 | tf_op jit(solution)/shard_map/ppermute | solution.py:291
  25.1 1.2 collective-permute-start.2
  26.2 2.1 %collective-permute-start.1 = (f32[64,128]{1,0:T(8,128)S(1)}, f32[64,128]{1,0:T(8,128)S(1)}, u32[]{:S(2)}, u32[]{:S(2)}) collective-permute-start(f32[64,128]{1,0:T(8,128)S(1)} %sum_pieces.3.refs_0_), channel_id=1, source_target_pairs={{0,16},{1,17},{2,18},{3,19},{4,20},{5,21},{6,22},{7,23},{8,24},{9,... | collective-permute-start | bytes 98312 | tf_op jit(solution)/shard_map/ppermute | solution.py:291
  28.3 3.4 %collective-permute-done.2.refs_2_ = f32[64,128]{1,0:T(8,128)S(1)} collective-permute-done((f32[64,128]{1,0:T(8,128)S(1)}, f32[64,128]{1,0:T(8,128)S(1)}, u32[]{:S(2)}, u32[]{:S(2)}) %collective-permute-start.2) | collective-permute-done | bytes 32800 | tf_op jit(solution)/shard_map/ppermute | solution.py:291
  31.8 9.6 %all_to_all.36 = f32[8,64,128]{2,1,0:T(8,128)S(1)} all-to-all(f32[8,64,128]{2,1,0:T(8,128)S(1)} %bitcast.29), channel_id=1, replica_groups={{0,2,4,6,8,10,12,14},{1,3,5,7,9,11,13,15},{16,18,20,22,24,26,28,30},{17..., dimensions={0} | all-to-all | bytes 524288 | tf_op jit(solution)/shard_map/all_to_all | solution.py:285
  41.4 3.6 %collective-permute-start.4 = (f32[512,128]{1,0:T(8,128)S(1)}, f32[512,128]{1,0:T(8,128)S(1)}, u32[]{:S(2)}, u32[]{:S(2)}) collective-permute-start(f32[512,128]{1,0:T(8,128)S(1)} %bitcast.22), channel_id=1, source_target_pairs={{0,1},{1,0},{2,3},{3,2},{4,5},{5,4},{6,7},{7,6},{8,9},{9,8},{10,11... | collective-permute-start | bytes 786440 | tf_op jit(solution)/shard_map/ppermute | solution.py:280
  45.0 1.8 turn_states.3
  46.7 1.7 forward.3
  48.4 1.3 collective-permute-start.5
  49.7 1.8 %collective-permute-start.7 = (f32[256,128]{1,0:T(8,128)S(1)}, f32[256,128]{1,0:T(8,128)S(1)}, u32[]{:S(2)}, u32[]{:S(2)}) collective-permute-start(f32[256,128]{1,0:T(8,128)S(1)} %get-tuple-element.51), channel_id=1, source_target_pairs={{0,192},{64,128},{128,64},{192,0},{1,193},{65,129},{129,65},{193,1... | collective-permute-start | bytes 393224 | tf_op jit(solution)/shard_map/ppermute | solution.py:306
  51.5 2.2 %collective-permute-done.5 = f32[264,128]{1,0:T(8,128)S(1)} collective-permute-done((f32[264,128]{1,0:T(8,128)S(1)}, f32[264,128]{1,0:T(8,128)S(1)}, u32[]{:S(2)}, u32[]{:S(2)}) %collective-permute-start.5) | collective-permute-done | bytes 135200 | tf_op jit(solution)/shard_map/ppermute | solution.py:306
  53.7 2.6 %collective-permute-start.6 = (f32[264,128]{1,0:T(8,128)S(1)}, f32[264,128]{1,0:T(8,128)S(1)}, u32[]{:S(2)}, u32[]{:S(2)}) collective-permute-start(f32[264,128]{1,0:T(8,128)S(1)} %add.29.refs_0_), channel_id=1, source_target_pairs={{0,192},{64,128},{128,64},{192,0},{1,193},{65,129},{129,65},{193,1... | collective-permute-start | bytes 405512 | tf_op jit(solution)/shard_map/ppermute | solution.py:306
  56.6 4.0 %collective-permute-done.8.refs_3_ = f32[256,128]{1,0:T(8,128)S(1)} collective-permute-done((f32[256,128]{1,0:T(8,128)S(1)}, f32[256,128]{1,0:T(8,128)S(1)}, u32[]{:S(2)}, u32[]{:S(2)}) %collective-permute-start.8) | collective-permute-done | bytes 131104 | tf_op jit(solution)/shard_map/ppermute | solution.py:306
  60.6 1.6 back.2
  62.2 2.1 %collective-permute-start.9 = (f32[576,128]{1,0:T(8,128)S(1)}, f32[576,128]{1,0:T(8,128)S(1)}, u32[]{:S(2)}, u32[]{:S(2)}) collective-permute-start(f32[576,128]{1,0:T(8,128)S(1)} %get-tuple-element.53), channel_id=1, source_target_pairs={{0,1},{1,0},{2,3},{3,2},{4,5},{5,4},{6,7},{7,6},{8,9},{9,8},{10,11... | collective-permute-start | bytes 884744 | tf_op jit(solution)/shard_map/ppermute | solution.py:280
  64.2 1.2 collective-permute-done.9
  65.5 9.6 %all_to_all.37 = f32[8,72,128]{2,1,0:T(8,128)S(1)} all-to-all(f32[8,72,128]{2,1,0:T(8,128)S(1)} %bitcast.36), channel_id=1, replica_groups={{0,2,4,6,8,10,12,14},{1,3,5,7,9,11,13,15},{16,18,20,22,24,26,28,30},{17..., dimensions={0} | all-to-all | bytes 589824 | tf_op jit(solution)/shard_map/all_to_all | solution.py:285
  75.1 1.6 collective-permute-start.12
  76.8 2.7 %collective-permute-start.11 = (f32[72,128]{1,0:T(8,128)S(1)}, f32[72,128]{1,0:T(8,128)S(1)}, u32[]{:S(2)}, u32[]{:S(2)}) collective-permute-start(f32[72,128]{1,0:T(8,128)S(1)} %sum_pieces.4.refs_0_), channel_id=1, source_target_pairs={{0,32},{1,33},{2,34},{3,35},{4,36},{5,37},{6,38},{7,39},{8,40},{9,... | collective-permute-start | bytes 110600 | tf_op jit(solution)/shard_map/ppermute | solution.py:291
  79.5 2.3 %collective-permute-start.10 = (f32[72,128]{1,0:T(8,128)S(1)}, f32[72,128]{1,0:T(8,128)S(1)}, u32[]{:S(2)}, u32[]{:S(2)}) collective-permute-start(f32[72,128]{1,0:T(8,128)S(1)} %sum_pieces.4.refs_0_), channel_id=1, source_target_pairs={{0,16},{1,17},{2,18},{3,19},{4,20},{5,21},{6,22},{7,23},{8,24},{9,... | collective-permute-start | bytes 110600 | tf_op jit(solution)/shard_map/ppermute | solution.py:291
  81.8 1.9 %collective-permute-done.11.refs_2_ = f32[72,128]{1,0:T(8,128)S(1)} collective-permute-done((f32[72,128]{1,0:T(8,128)S(1)}, f32[72,128]{1,0:T(8,128)S(1)}, u32[]{:S(2)}, u32[]{:S(2)}) %collective-permute-start.11) | collective-permute-done | bytes 36896 | tf_op jit(solution)/shard_map/ppermute | solution.py:291
  84.8 9.5 %all_to_all.38 = f32[8,64,128]{2,1,0:T(8,128)S(1)} all-to-all(f32[8,64,128]{2,1,0:T(8,128)S(1)} %bitcast.31), channel_id=1, replica_groups={{0,2,4,6,8,10,12,14},{1,3,5,7,9,11,13,15},{16,18,20,22,24,26,28,30},{17..., dimensions={0} | all-to-all | bytes 524288 | tf_op jit(solution)/shard_map/all_to_all | solution.py:285
  94.3 3.0 %collective-permute-start.13 = (f32[512,128]{1,0:T(8,128)S(1)}, f32[512,128]{1,0:T(8,128)S(1)}, u32[]{:S(2)}, u32[]{:S(2)}) collective-permute-start(f32[512,128]{1,0:T(8,128)S(1)} %bitcast.26), channel_id=1, source_target_pairs={{0,1},{1,0},{2,3},{3,2},{4,5},{5,4},{6,7},{7,6},{8,9},{9,8},{10,11... | collective-permute-start | bytes 786440 | tf_op jit(solution)/shard_map/ppermute | solution.py:280
  98.5 1.9 %forward.4 = (f32[1024,128]{1,0:T(8,128)S(1)}, f32[1024,128]{1,0:T(8,128)S(1)}, f32[264,128]{1,0:T(8,128)S(1)}, f32[256,128]{1,0:T(8,128)S(1)}) custom-call(f32[512,128]{1,0:T(8,128)S(1)} %bitcast.27, f32[512,128]{1,0:T(8,128)S(1)} %collective-permute-done.13.refs_1_, f32[8,128]{1,0:T(8,128)S(1)} %get-tuple-element.56.refs_2_.size0, ...), custom_call_target="tpu_custom_call" | custom-call | flops 1073741824 | bytes 1048576 | tf_op jit(solution)/shard_map/forward/pallas_call | solution.py:29
  100.5 1.4 collective-permute-start.16
  102.0 3.3 %collective-permute-done.14 = f32[264,128]{1,0:T(8,128)S(1)} collective-permute-done((f32[264,128]{1,0:T(8,128)S(1)}, f32[264,128]{1,0:T(8,128)S(1)}, u32[]{:S(2)}, u32[]{:S(2)}) %collective-permute-start.14) | collective-permute-done | bytes 135200 | tf_op jit(solution)/shard_map/ppermute | solution.py:306
  105.3 1.4 collective-permute-start.15
  106.9 3.8 %collective-permute-done.17.refs_3_ = f32[256,128]{1,0:T(8,128)S(1)} collective-permute-done((f32[256,128]{1,0:T(8,128)S(1)}, f32[256,128]{1,0:T(8,128)S(1)}, u32[]{:S(2)}, u32[]{:S(2)}) %collective-permute-start.17) | collective-permute-done | bytes 131104 | tf_op jit(solution)/shard_map/ppermute | solution.py:306
  110.7 1.6 back.3
  112.3 2.7 %collective-permute-start.18 = (f32[576,128]{1,0:T(8,128)S(1)}, f32[576,128]{1,0:T(8,128)S(1)}, u32[]{:S(2)}, u32[]{:S(2)}) collective-permute-start(f32[576,128]{1,0:T(8,128)S(1)} %get-tuple-element.62), channel_id=1, source_target_pairs={{0,1},{1,0},{2,3},{3,2},{4,5},{5,4},{6,7},{7,6},{8,9},{9,8},{10,11... | collective-permute-start | bytes 884744 | tf_op jit(solution)/shard_map/ppermute | solution.py:280
  115.0 1.2 collective-permute-done.18
  116.3 9.6 %all_to_all.39 = f32[8,72,128]{2,1,0:T(8,128)S(1)} all-to-all(f32[8,72,128]{2,1,0:T(8,128)S(1)} %bitcast.37), channel_id=1, replica_groups={{0,2,4,6,8,10,12,14},{1,3,5,7,9,11,13,15},{16,18,20,22,24,26,28,30},{17..., dimensions={0} | all-to-all | bytes 589824 | tf_op jit(solution)/shard_map/all_to_all | solution.py:285
  125.9 1.9 %collective-permute-start.21 = (f32[72,128]{1,0:T(8,128)S(1)}, f32[72,128]{1,0:T(8,128)S(1)}, u32[]{:S(2)}, u32[]{:S(2)}) collective-permute-start(f32[72,128]{1,0:T(8,128)S(1)} %sum_pieces.5.refs_0_), channel_id=1, source_target_pairs={{0,48},{1,49},{2,50},{3,51},{4,52},{5,53},{6,54},{7,55},{8,56},{9,... | collective-permute-start | bytes 110600 | tf_op jit(solution)/shard_map/ppermute | solution.py:291
  127.8 2.9 %collective-permute-start.20 = (f32[72,128]{1,0:T(8,128)S(1)}, f32[72,128]{1,0:T(8,128)S(1)}, u32[]{:S(2)}, u32[]{:S(2)}) collective-permute-start(f32[72,128]{1,0:T(8,128)S(1)} %sum_pieces.5.refs_0_), channel_id=1, source_target_pairs={{0,32},{1,33},{2,34},{3,35},{4,36},{5,37},{6,38},{7,39},{8,40},{9,... | collective-permute-start | bytes 110600 | tf_op jit(solution)/shard_map/ppermute | solution.py:291
  131.8 2.8 %collective-permute-done.20.refs_2_ = f32[72,128]{1,0:T(8,128)S(1)} collective-permute-done((f32[72,128]{1,0:T(8,128)S(1)}, f32[72,128]{1,0:T(8,128)S(1)}, u32[]{:S(2)}, u32[]{:S(2)}) %collective-permute-start.20) | collective-permute-done | bytes 36896 | tf_op jit(solution)/shard_map/ppermute | solution.py:291
  135.7 9.6 %all_to_all.40 = f32[8,64,128]{2,1,0:T(8,128)S(1)} all-to-all(f32[8,64,128]{2,1,0:T(8,128)S(1)} %bitcast.32), channel_id=1, replica_groups={{0,2,4,6,8,10,12,14},{1,3,5,7,9,11,13,15},{16,18,20,22,24,26,28,30},{17..., dimensions={0} | all-to-all | bytes 524288 | tf_op jit(solution)/shard_map/all_to_all | solution.py:285
  145.3 3.2 %collective-permute-start.22 = (f32[512,128]{1,0:T(8,128)S(1)}, f32[512,128]{1,0:T(8,128)S(1)}, u32[]{:S(2)}, u32[]{:S(2)}) collective-permute-start(f32[512,128]{1,0:T(8,128)S(1)} %bitcast.24), channel_id=1, source_target_pairs={{0,1},{1,0},{2,3},{3,2},{4,5},{5,4},{6,7},{7,6},{8,9},{9,8},{10,11... | collective-permute-start | bytes 786440 | tf_op jit(solution)/shard_map/ppermute | solution.py:280
  149.7 1.9 %forward.5 = (f32[1024,128]{1,0:T(8,128)S(1)}, f32[1024,128]{1,0:T(8,128)S(1)}, f32[264,128]{1,0:T(8,128)S(1)}, f32[256,128]{1,0:T(8,128)S(1)}) custom-call(f32[512,128]{1,0:T(8,128)S(1)} %bitcast.25, f32[512,128]{1,0:T(8,128)S(1)} %collective-permute-done.22.refs_1_, f32[8,128]{1,0:T(8,128)S(1)} %get-tuple-element.65.refs_2_.size1, ...), custom_call_target="tpu_custom_call" | custom-call | flops 1073741824 | bytes 1048576 | tf_op jit(solution)/shard_map/forward/pallas_call | solution.py:29
  151.7 1.5 collective-permute-start.25
  153.2 3.3 %collective-permute-done.23 = f32[264,128]{1,0:T(8,128)S(1)} collective-permute-done((f32[264,128]{1,0:T(8,128)S(1)}, f32[264,128]{1,0:T(8,128)S(1)}, u32[]{:S(2)}, u32[]{:S(2)}) %collective-permute-start.23) | collective-permute-done | bytes 135200 | tf_op jit(solution)/shard_map/ppermute | solution.py:306
  156.5 1.5 collective-permute-start.24
  158.8 3.4 %collective-permute-done.26.h3 = f32[256,128]{1,0:T(8,128)S(1)} collective-permute-done((f32[256,128]{1,0:T(8,128)S(1)}, f32[256,128]{1,0:T(8,128)S(1)}, u32[]{:S(2)}, u32[]{:S(2)}) %collective-permute-start.26) | collective-permute-done | bytes 131104 | tf_op jit(solution)/shard_map/ppermute | solution.py:306
  162.5 13.1 %all_to_all.41 = f32[32,1,128]{2,1,0:T(1,128)S(1)} all-to-all(f32[32,1,128]{2,1,0:T(1,128)S(1)} %bitcast.35), channel_id=1, replica_groups={{0,2,4,6,8,10,12,14,16,18,20,22,24,26,28,30,32,34,36,38,40,42,44,46,48,..., dimensions={0} | all-to-all | bytes 32768 | tf_op jit(solution)/shard_map/all_to_all | solution.py:411
  175.5 3.8 %collective-permute-start.27 = (f32[32,128]{1,0:T(8,128)S(1)}, f32[32,128]{1,0:T(8,128)S(1)}, u32[]{:S(2)}, u32[]{:S(2)}) collective-permute-start(f32[32,128]{1,0:T(8,128)S(1)} %bitcast.33), channel_id=1, source_target_pairs={{0,1},{1,0},{2,3},{3,2},{4,5},{5,4},{6,7},{7,6},{8,9},{9,8},{10,11... | collective-permute-start | bytes 49160 | tf_op jit(solution)/shard_map/ppermute | solution.py:280
  (41 shorter events, 9.6 us)
Async XLA Ops:
  5.4 4.6 %collective-permute-start = (f32[512,128]{1,0:T(8,128)S(1)}, f32[512,128]{1,0:T(8,128)S(1)}, u32[]{:S(2)}, u32[]{:S(2)}) collective-permute-start(f32[512,128]{1,0:T(8,128)S(1)} %get-tuple-element.44), channel_id=1, source_target_pairs={{0,1},{1,0},{2,3},{3,2},{4,5},{5,4},{6,7},{7,6},{8,9},{9,8},{10,11... | collective-permute-start | bytes 786440 | tf_op jit(solution)/shard_map/ppermute | solution.py:280
  19.8 8.5 %collective-permute-start.3 = (f32[64,128]{1,0:T(8,128)S(1)}, f32[64,128]{1,0:T(8,128)S(1)}, u32[]{:S(2)}, u32[]{:S(2)}) collective-permute-start(f32[64,128]{1,0:T(8,128)S(1)} %sum_pieces.3.refs_0_), channel_id=1, source_target_pairs={{0,48},{1,49},{2,50},{3,51},{4,52},{5,53},{6,54},{7,55},{8,56},{9,... | collective-permute-start | bytes 98312 | tf_op jit(solution)/shard_map/ppermute | solution.py:291
  25.1 6.7 %collective-permute-start.2 = (f32[64,128]{1,0:T(8,128)S(1)}, f32[64,128]{1,0:T(8,128)S(1)}, u32[]{:S(2)}, u32[]{:S(2)}) collective-permute-start(f32[64,128]{1,0:T(8,128)S(1)} %sum_pieces.3.refs_0_), channel_id=1, source_target_pairs={{0,32},{1,33},{2,34},{3,35},{4,36},{5,37},{6,38},{7,39},{8,40},{9,... | collective-permute-start | bytes 98312 | tf_op jit(solution)/shard_map/ppermute | solution.py:291
  26.2 5.5 %collective-permute-start.1 = (f32[64,128]{1,0:T(8,128)S(1)}, f32[64,128]{1,0:T(8,128)S(1)}, u32[]{:S(2)}, u32[]{:S(2)}) collective-permute-start(f32[64,128]{1,0:T(8,128)S(1)} %sum_pieces.3.refs_0_), channel_id=1, source_target_pairs={{0,16},{1,17},{2,18},{3,19},{4,20},{5,21},{6,22},{7,23},{8,24},{9,... | collective-permute-start | bytes 98312 | tf_op jit(solution)/shard_map/ppermute | solution.py:291
  41.4 5.3 %collective-permute-start.4 = (f32[512,128]{1,0:T(8,128)S(1)}, f32[512,128]{1,0:T(8,128)S(1)}, u32[]{:S(2)}, u32[]{:S(2)}) collective-permute-start(f32[512,128]{1,0:T(8,128)S(1)} %bitcast.22), channel_id=1, source_target_pairs={{0,1},{1,0},{2,3},{3,2},{4,5},{5,4},{6,7},{7,6},{8,9},{9,8},{10,11... | collective-permute-start | bytes 786440 | tf_op jit(solution)/shard_map/ppermute | solution.py:280
  48.4 5.3 %collective-permute-start.5 = (f32[264,128]{1,0:T(8,128)S(1)}, f32[264,128]{1,0:T(8,128)S(1)}, u32[]{:S(2)}, u32[]{:S(2)}) collective-permute-start(f32[264,128]{1,0:T(8,128)S(1)} %get-tuple-element.50), channel_id=1, source_target_pairs={{0,64},{64,0},{128,192},{192,128},{1,65},{65,1},{129,193},{193,129... | collective-permute-start | bytes 405512 | tf_op jit(solution)/shard_map/ppermute | solution.py:306
  49.7 6.6 %collective-permute-start.7 = (f32[256,128]{1,0:T(8,128)S(1)}, f32[256,128]{1,0:T(8,128)S(1)}, u32[]{:S(2)}, u32[]{:S(2)}) collective-permute-start(f32[256,128]{1,0:T(8,128)S(1)} %get-tuple-element.51), channel_id=1, source_target_pairs={{0,192},{64,128},{128,64},{192,0},{1,193},{65,129},{129,65},{193,1... | collective-permute-start | bytes 393224 | tf_op jit(solution)/shard_map/ppermute | solution.py:306
  53.7 6.9 %collective-permute-start.6 = (f32[264,128]{1,0:T(8,128)S(1)}, f32[264,128]{1,0:T(8,128)S(1)}, u32[]{:S(2)}, u32[]{:S(2)}) collective-permute-start(f32[264,128]{1,0:T(8,128)S(1)} %add.29.refs_0_), channel_id=1, source_target_pairs={{0,192},{64,128},{128,64},{192,0},{1,193},{65,129},{129,65},{193,1... | collective-permute-start | bytes 405512 | tf_op jit(solution)/shard_map/ppermute | solution.py:306
  56.3 4.3 %collective-permute-start.8 = (f32[256,128]{1,0:T(8,128)S(1)}, f32[256,128]{1,0:T(8,128)S(1)}, u32[]{:S(2)}, u32[]{:S(2)}) collective-permute-start(f32[256,128]{1,0:T(8,128)S(1)} %add.30.refs_2_), channel_id=1, source_target_pairs={{0,64},{64,0},{128,192},{192,128},{1,65},{65,1},{129,193},{193,129... | collective-permute-start | bytes 393224 | tf_op jit(solution)/shard_map/ppermute | solution.py:306
  62.2 3.3 %collective-permute-start.9 = (f32[576,128]{1,0:T(8,128)S(1)}, f32[576,128]{1,0:T(8,128)S(1)}, u32[]{:S(2)}, u32[]{:S(2)}) collective-permute-start(f32[576,128]{1,0:T(8,128)S(1)} %get-tuple-element.53), channel_id=1, source_target_pairs={{0,1},{1,0},{2,3},{3,2},{4,5},{5,4},{6,7},{7,6},{8,9},{9,8},{10,11... | collective-permute-start | bytes 884744 | tf_op jit(solution)/shard_map/ppermute | solution.py:280
  75.1 6.7 %collective-permute-start.12 = (f32[72,128]{1,0:T(8,128)S(1)}, f32[72,128]{1,0:T(8,128)S(1)}, u32[]{:S(2)}, u32[]{:S(2)}) collective-permute-start(f32[72,128]{1,0:T(8,128)S(1)} %sum_pieces.4.refs_0_), channel_id=1, source_target_pairs={{0,48},{1,49},{2,50},{3,51},{4,52},{5,53},{6,54},{7,55},{8,56},{9,... | collective-permute-start | bytes 110600 | tf_op jit(solution)/shard_map/ppermute | solution.py:291
  76.8 6.9 %collective-permute-start.11 = (f32[72,128]{1,0:T(8,128)S(1)}, f32[72,128]{1,0:T(8,128)S(1)}, u32[]{:S(2)}, u32[]{:S(2)}) collective-permute-start(f32[72,128]{1,0:T(8,128)S(1)} %sum_pieces.4.refs_0_), channel_id=1, source_target_pairs={{0,32},{1,33},{2,34},{3,35},{4,36},{5,37},{6,38},{7,39},{8,40},{9,... | collective-permute-start | bytes 110600 | tf_op jit(solution)/shard_map/ppermute | solution.py:291
  79.5 5.3 %collective-permute-start.10 = (f32[72,128]{1,0:T(8,128)S(1)}, f32[72,128]{1,0:T(8,128)S(1)}, u32[]{:S(2)}, u32[]{:S(2)}) collective-permute-start(f32[72,128]{1,0:T(8,128)S(1)} %sum_pieces.4.refs_0_), channel_id=1, source_target_pairs={{0,16},{1,17},{2,18},{3,19},{4,20},{5,21},{6,22},{7,23},{8,24},{9,... | collective-permute-start | bytes 110600 | tf_op jit(solution)/shard_map/ppermute | solution.py:291
  94.3 4.2 %collective-permute-start.13 = (f32[512,128]{1,0:T(8,128)S(1)}, f32[512,128]{1,0:T(8,128)S(1)}, u32[]{:S(2)}, u32[]{:S(2)}) collective-permute-start(f32[512,128]{1,0:T(8,128)S(1)} %bitcast.26), channel_id=1, source_target_pairs={{0,1},{1,0},{2,3},{3,2},{4,5},{5,4},{6,7},{7,6},{8,9},{9,8},{10,11... | collective-permute-start | bytes 786440 | tf_op jit(solution)/shard_map/ppermute | solution.py:280
  100.4 4.9 %collective-permute-start.14 = (f32[264,128]{1,0:T(8,128)S(1)}, f32[264,128]{1,0:T(8,128)S(1)}, u32[]{:S(2)}, u32[]{:S(2)}) collective-permute-start(f32[264,128]{1,0:T(8,128)S(1)} %get-tuple-element.58), channel_id=1, source_target_pairs={{0,64},{64,0},{128,192},{192,128},{1,65},{65,1},{129,193},{193,129... | collective-permute-start | bytes 405512 | tf_op jit(solution)/shard_map/ppermute | solution.py:306
  100.5 6.2 %collective-permute-start.16 = (f32[256,128]{1,0:T(8,128)S(1)}, f32[256,128]{1,0:T(8,128)S(1)}, u32[]{:S(2)}, u32[]{:S(2)}) collective-permute-start(f32[256,128]{1,0:T(8,128)S(1)} %get-tuple-element.59), channel_id=1, source_target_pairs={{0,192},{64,128},{128,64},{192,0},{1,193},{65,129},{129,65},{193,1... | collective-permute-start | bytes 393224 | tf_op jit(solution)/shard_map/ppermute | solution.py:306
  105.3 5.4 %collective-permute-start.15 = (f32[264,128]{1,0:T(8,128)S(1)}, f32[264,128]{1,0:T(8,128)S(1)}, u32[]{:S(2)}, u32[]{:S(2)}) collective-permute-start(f32[264,128]{1,0:T(8,128)S(1)} %add.32.refs_0_), channel_id=1, source_target_pairs={{0,192},{64,128},{128,64},{192,0},{1,193},{65,129},{129,65},{193,1... | collective-permute-start | bytes 405512 | tf_op jit(solution)/shard_map/ppermute | solution.py:306
  106.8 3.9 %collective-permute-start.17 = (f32[256,128]{1,0:T(8,128)S(1)}, f32[256,128]{1,0:T(8,128)S(1)}, u32[]{:S(2)}, u32[]{:S(2)}) collective-permute-start(f32[256,128]{1,0:T(8,128)S(1)} %add.33.refs_2_), channel_id=1, source_target_pairs={{0,64},{64,0},{128,192},{192,128},{1,65},{65,1},{129,193},{193,129... | collective-permute-start | bytes 393224 | tf_op jit(solution)/shard_map/ppermute | solution.py:306
  112.3 3.9 %collective-permute-start.18 = (f32[576,128]{1,0:T(8,128)S(1)}, f32[576,128]{1,0:T(8,128)S(1)}, u32[]{:S(2)}, u32[]{:S(2)}) collective-permute-start(f32[576,128]{1,0:T(8,128)S(1)} %get-tuple-element.62), channel_id=1, source_target_pairs={{0,1},{1,0},{2,3},{3,2},{4,5},{5,4},{6,7},{7,6},{8,9},{9,8},{10,11... | collective-permute-start | bytes 884744 | tf_op jit(solution)/shard_map/ppermute | solution.py:280
  125.9 5.9 %collective-permute-start.21 = (f32[72,128]{1,0:T(8,128)S(1)}, f32[72,128]{1,0:T(8,128)S(1)}, u32[]{:S(2)}, u32[]{:S(2)}) collective-permute-start(f32[72,128]{1,0:T(8,128)S(1)} %sum_pieces.5.refs_0_), channel_id=1, source_target_pairs={{0,48},{1,49},{2,50},{3,51},{4,52},{5,53},{6,54},{7,55},{8,56},{9,... | collective-permute-start | bytes 110600 | tf_op jit(solution)/shard_map/ppermute | solution.py:291
  127.8 6.8 %collective-permute-start.20 = (f32[72,128]{1,0:T(8,128)S(1)}, f32[72,128]{1,0:T(8,128)S(1)}, u32[]{:S(2)}, u32[]{:S(2)}) collective-permute-start(f32[72,128]{1,0:T(8,128)S(1)} %sum_pieces.5.refs_0_), channel_id=1, source_target_pairs={{0,32},{1,33},{2,34},{3,35},{4,36},{5,37},{6,38},{7,39},{8,40},{9,... | collective-permute-start | bytes 110600 | tf_op jit(solution)/shard_map/ppermute | solution.py:291
  130.7 5.0 %collective-permute-start.19 = (f32[72,128]{1,0:T(8,128)S(1)}, f32[72,128]{1,0:T(8,128)S(1)}, u32[]{:S(2)}, u32[]{:S(2)}) collective-permute-start(f32[72,128]{1,0:T(8,128)S(1)} %sum_pieces.5.refs_0_), channel_id=1, source_target_pairs={{0,16},{1,17},{2,18},{3,19},{4,20},{5,21},{6,22},{7,23},{8,24},{9,... | collective-permute-start | bytes 110600 | tf_op jit(solution)/shard_map/ppermute | solution.py:291
  145.3 4.3 %collective-permute-start.22 = (f32[512,128]{1,0:T(8,128)S(1)}, f32[512,128]{1,0:T(8,128)S(1)}, u32[]{:S(2)}, u32[]{:S(2)}) collective-permute-start(f32[512,128]{1,0:T(8,128)S(1)} %bitcast.24), channel_id=1, source_target_pairs={{0,1},{1,0},{2,3},{3,2},{4,5},{5,4},{6,7},{7,6},{8,9},{9,8},{10,11... | collective-permute-start | bytes 786440 | tf_op jit(solution)/shard_map/ppermute | solution.py:280
  151.6 4.9 %collective-permute-start.23 = (f32[264,128]{1,0:T(8,128)S(1)}, f32[264,128]{1,0:T(8,128)S(1)}, u32[]{:S(2)}, u32[]{:S(2)}) collective-permute-start(f32[264,128]{1,0:T(8,128)S(1)} %get-tuple-element.68), channel_id=1, source_target_pairs={{0,64},{64,0},{128,192},{192,128},{1,65},{65,1},{129,193},{193,129... | collective-permute-start | bytes 405512 | tf_op jit(solution)/shard_map/ppermute | solution.py:306
  151.7 6.3 %collective-permute-start.25 = (f32[256,128]{1,0:T(8,128)S(1)}, f32[256,128]{1,0:T(8,128)S(1)}, u32[]{:S(2)}, u32[]{:S(2)}) collective-permute-start(f32[256,128]{1,0:T(8,128)S(1)} %get-tuple-element.69), channel_id=1, source_target_pairs={{0,192},{64,128},{128,64},{192,0},{1,193},{65,129},{129,65},{193,1... | collective-permute-start | bytes 393224 | tf_op jit(solution)/shard_map/ppermute | solution.py:306
  156.5 5.7 %collective-permute-start.24 = (f32[264,128]{1,0:T(8,128)S(1)}, f32[264,128]{1,0:T(8,128)S(1)}, u32[]{:S(2)}, u32[]{:S(2)}) collective-permute-start(f32[264,128]{1,0:T(8,128)S(1)} %add.35.h0), channel_id=1, source_target_pairs={{0,192},{64,128},{128,64},{192,0},{1,193},{65,129},{129,65},{193,1... | collective-permute-start | bytes 405512 | tf_op jit(solution)/shard_map/ppermute | solution.py:306
  158.0 4.2 %collective-permute-start.26 = (f32[256,128]{1,0:T(8,128)S(1)}, f32[256,128]{1,0:T(8,128)S(1)}, u32[]{:S(2)}, u32[]{:S(2)}) collective-permute-start(f32[256,128]{1,0:T(8,128)S(1)} %add.36.h2), channel_id=1, source_target_pairs={{0,64},{64,0},{128,192},{192,128},{1,65},{65,1},{129,193},{193,129... | collective-permute-start | bytes 393224 | tf_op jit(solution)/shard_map/ppermute | solution.py:306
  175.5 4.6 %collective-permute-start.27 = (f32[32,128]{1,0:T(8,128)S(1)}, f32[32,128]{1,0:T(8,128)S(1)}, u32[]{:S(2)}, u32[]{:S(2)}) collective-permute-start(f32[32,128]{1,0:T(8,128)S(1)} %bitcast.33), channel_id=1, source_target_pairs={{0,1},{1,0},{2,3},{3,2},{4,5},{5,4},{6,7},{7,6},{8,9},{9,8},{10,11... | collective-permute-start | bytes 49160 | tf_op jit(solution)/shard_map/ppermute | solution.py:280

commit v10 on v9

--- a/solution.py
+++ b/solution.py
@@ -25,11 +25,11 @@
     return pltpu.with_memory_space_constraint(x, pltpu.VMEM)
 
 
-def call(kernel, out_shape, *args, scratch=(), limit=24, specs=None, flops=0, **static):
+def call(kernel, out_shape, *args, scratch=(), limit=24, specs=None, outs=None, flops=0, **static):
     return pl.pallas_call(
         functools.partial(kernel, **static),
         in_specs=specs or [VMEM] * len(args),
-        out_specs=jax.tree.map(lambda _: VMEM, out_shape),
+        out_specs=outs or jax.tree.map(lambda _: VMEM, out_shape),
         out_shape=out_shape,
         scratch_shapes=list(scratch),
         compiler_params=pltpu.CompilerParams(vmem_limit_bytes=limit * MIB),
@@ -247,13 +247,24 @@
     token[...] = jnp.zeros(token.shape, F32)
 
 
-def finish(core, squares, others, scal, image, readout_part, before, gradient, residual_part, readout, residual):
-    image_sq = jnp.sum(squares[...] + others[...], axis=0, keepdims=True)
+def finish(core, squares, scal, image, readout_part, before, gradient, residual_part, readout, residual, readout_buf, residual_buf, sems):
+    image_sq = jnp.sum(squares[...], axis=0, keepdims=True)
     size = step_size(image_sq, scal)[:, :1]
     beta = scal[1:2, :1]
-    readout[...] = readout_part[...] + size * (gradient[...] + beta * before[...])
+    parts = sems.shape[0] - 1
+    n = readout.shape[0] // parts
+    copies = []
+    for t in range(parts):
+        at = pl.ds(t * n, n)
+        readout_buf[at, :] = readout_part[at, :] + size * (gradient[at, :] + beta * before[at, :])
+        copies.append(pltpu.make_async_copy(readout_buf.at[at], readout.at[at], sems.at[t]))
+        copies[-1].start()
     last = own_half_first(image[...], core[0, 0] == 0)
-    residual[...] = residual_part[...] - size * last
+    residual_buf[...] = residual_part[...] - size * last
+    copies.append(pltpu.make_async_copy(residual_buf, residual, sems.at[parts]))
+    copies[-1].start()
+    for c in copies:
+        c.wait()
 
 
 def shards(states, targets):
@@ -405,27 +416,25 @@
                 flops=flops // 4,
             )
             image, scal, squares = call(
-                last_image, [image_shape, vector, shape(chips, LANES)], *hops, *olds, token
-            )
-    all_chips = [[chip * CORES + c for chip in range(chips)] for c in range(CORES)]
-    squares = lax.all_to_all(
-        squares.reshape(chips, 1, LANES),
-        "samp",
-        0,
-        0,
-        axis_index_groups=all_chips,
-        tiled=True,
-    ).reshape(chips, LANES)
+                last_image, [image_shape, vector, shape(samp_count, LANES)], *hops, *olds, token
+            )
+    squares = lax.all_to_all(squares.reshape(samp_count, 1, LANES), "samp", 0, 0, tiled=True)
+    squares = squares.reshape(samp_count, LANES)
     readout, residual = call(
         finish,
         [shape(outputs, units), image_shape],
         core,
         squares,
-        swap(squares),
         scal,
         image,
         *parts,
-        specs=[smem] + [VMEM] * 8,
+        specs=[smem] + [VMEM] * 7,
+        outs=[HBM] * 2,
+        scratch=[
+            pltpu.VMEM((outputs, units), F32),
+            pltpu.VMEM((outputs, samples), F32),
+            pltpu.SemaphoreType.DMA((5,)),
+        ],
     )
     return readout.T, residual.T
 

time: 182 us -> 181 us (level)
  starting transfers between devices: 54.9 us -> 51.1 us
  blocking collectives: 70.9 us -> 74.5 us
    ppermute x7 -> x6, starting transfers between devices: 21.7 us -> 17.9 us  [swap(): return lax.ppermute(x, 'samp', swap_cores)]
    all_to_all x1, blocking collectives: 13.1 us -> 16.6 us  [shards(): lax.all_to_all(squares.reshape(samp_count, 1, LANES), 'samp', 0, 0, tiled...]
    ppermute x7 -> x6, waiting for transfers between devices: 5.59 us -> 4.75 us  [swap(): return lax.ppermute(x, 'samp', swap_cores)]
  transfers between devices with their start and end apart: 28 -> 27, of which waited for: 16 -> 15; matrix products, arithmetic and copies ran while one was open for 0% -> 0% of each run, Pallas kernels for 2% -> 2%
where the time goes in v10:
time: 181 us; the launch traced here: 180 us
  blocking collectives  74.5 us (41%)
  starting transfers between devices  51.1 us (28%)
  waiting for transfers between devices  35.1 us (19%)
  Pallas kernels  18.5 us (10%)
    all_to_all x6, blocking collectives, exchange(): x = lax.all_to_all(x, 'samp', 0, 0, axis_index_groups=groups, tiled=True)  57.8 us
    ppermute x9, starting transfers between devices, block_terms(): lax.ppermute(x, 'samp', [(i, (i + d * step) % samp_count) for i in range(...  21 us
    ppermute x12, waiting for transfers between devices, unit_hop(): return lax.ppermute(x, 'unit', [(i, i ^ mask) for i in range(unit_count)])  20.1 us
    pallas_call x18, Pallas kernels, call(): pl.pallas_call(functools.partial(kernel, **static), in_specs=specs or [VM...  18.5 us
    ppermute x6, starting transfers between devices, swap(): return lax.ppermute(x, 'samp', swap_cores)  17.9 us
    all_to_all x1, blocking collectives, shards(): lax.all_to_all(squares.reshape(samp_count, 1, LANES), 'samp', 0, 0, tiled...  16.6 us
    ppermute x12, starting transfers between devices, unit_hop(): return lax.ppermute(x, 'unit', [(i, i ^ mask) for i in range(unit_count)])  12.2 us
    ppermute x9, waiting for transfers between devices, block_terms(): lax.ppermute(x, 'samp', [(i, (i + d * step) % samp_count) for i in range(...  10.3 us
  transfers between devices with their start and end apart: 27, of which 15 were waited for; matrix products, arithmetic and copies ran while one was open for 0% of the time, Pallas kernels for 2%

profile of v10, /device:TPU:1, one launch (start us, length us, event | category | flops | bytes accessed | tf_op | source)
XLA Modules:
  0.0 180.3 jit_solution(7798958400621606503)
XLA Ops:
  0.6 4.7 %first.1 = (bf16[1024,2048]{1,0:T(8,128)(2,1)S(1)}, bf16[1024,2048]{1,0:T(8,128)(2,1)S(1)}, f32[64,1024]{1,0:T(8,128)S(1)}, f32[512,128]{1,0:T(8,128)S(1)}, f32[512,128]{1,0:T(8,128)S(1)}) custom-call(s32[1,1]{1,0:T(1,128)} %bitcast.core, f32[1024,2048]{1,0:T(8,128)} %states.1, f32[64,1024]{1,0:T(8,128)} %bitcast.37), custom_call_target="tpu_custom_call" | custom-call | flops 1073741824 | bytes 1048576 | tf_op jit(solution)/shard_map/first/pallas_call | solution.py:29
  5.4 3.3 %collective-permute-start = (f32[512,128]{1,0:T(8,128)S(1)}, f32[512,128]{1,0:T(8,128)S(1)}, u32[]{:S(2)}, u32[]{:S(2)}) collective-permute-start(f32[512,128]{1,0:T(8,128)S(1)} %get-tuple-element.44), channel_id=1, source_target_pairs={{0,1},{1,0},{2,3},{3,2},{4,5},{5,4},{6,7},{7,6},{8,9},{9,8},{10,11... | collective-permute-start | bytes 786440 | tf_op jit(solution)/shard_map/ppermute | solution.py:291
  8.7 1.2 turn_states.2
  10.0 9.8 %all_to_all.35 = f32[8,64,128]{2,1,0:T(8,128)S(1)} all-to-all(f32[8,64,128]{2,1,0:T(8,128)S(1)} %bitcast.28), channel_id=1, replica_groups={{0,2,4,6,8,10,12,14},{1,3,5,7,9,11,13,15},{16,18,20,22,24,26,28,30},{17..., dimensions={0} | all-to-all | bytes 524288 | tf_op jit(solution)/shard_map/all_to_all | solution.py:296
  19.8 5.2 %collective-permute-start.3 = (f32[64,128]{1,0:T(8,128)S(1)}, f32[64,128]{1,0:T(8,128)S(1)}, u32[]{:S(2)}, u32[]{:S(2)}) collective-permute-start(f32[64,128]{1,0:T(8,128)S(1)} %sum_pieces.3.refs_0_), channel_id=1, source_target_pairs={{0,48},{1,49},{2,50},{3,51},{4,52},{5,53},{6,54},{7,55},{8,56},{9,... | collective-permute-start | bytes 98312 | tf_op jit(solution)/shard_map/ppermute | solution.py:302
  25.1 1.2 collective-permute-start.2
  26.2 2.1 %collective-permute-start.1 = (f32[64,128]{1,0:T(8,128)S(1)}, f32[64,128]{1,0:T(8,128)S(1)}, u32[]{:S(2)}, u32[]{:S(2)}) collective-permute-start(f32[64,128]{1,0:T(8,128)S(1)} %sum_pieces.3.refs_0_), channel_id=1, source_target_pairs={{0,16},{1,17},{2,18},{3,19},{4,20},{5,21},{6,22},{7,23},{8,24},{9,... | collective-permute-start | bytes 98312 | tf_op jit(solution)/shard_map/ppermute | solution.py:302
  28.3 3.4 %collective-permute-done.2.refs_2_ = f32[64,128]{1,0:T(8,128)S(1)} collective-permute-done((f32[64,128]{1,0:T(8,128)S(1)}, f32[64,128]{1,0:T(8,128)S(1)}, u32[]{:S(2)}, u32[]{:S(2)}) %collective-permute-start.2) | collective-permute-done | bytes 32800 | tf_op jit(solution)/shard_map/ppermute | solution.py:302
  31.8 9.6 %all_to_all.36 = f32[8,64,128]{2,1,0:T(8,128)S(1)} all-to-all(f32[8,64,128]{2,1,0:T(8,128)S(1)} %bitcast.29), channel_id=1, replica_groups={{0,2,4,6,8,10,12,14},{1,3,5,7,9,11,13,15},{16,18,20,22,24,26,28,30},{17..., dimensions={0} | all-to-all | bytes 524288 | tf_op jit(solution)/shard_map/all_to_all | solution.py:296
  41.4 3.6 %collective-permute-start.4 = (f32[512,128]{1,0:T(8,128)S(1)}, f32[512,128]{1,0:T(8,128)S(1)}, u32[]{:S(2)}, u32[]{:S(2)}) collective-permute-start(f32[512,128]{1,0:T(8,128)S(1)} %bitcast.22), channel_id=1, source_target_pairs={{0,1},{1,0},{2,3},{3,2},{4,5},{5,4},{6,7},{7,6},{8,9},{9,8},{10,11... | collective-permute-start | bytes 786440 | tf_op jit(solution)/shard_map/ppermute | solution.py:291
  45.0 1.8 turn_states.3
  46.7 1.7 forward.3
  48.4 1.3 collective-permute-start.5
  49.7 1.8 %collective-permute-start.7 = (f32[256,128]{1,0:T(8,128)S(1)}, f32[256,128]{1,0:T(8,128)S(1)}, u32[]{:S(2)}, u32[]{:S(2)}) collective-permute-start(f32[256,128]{1,0:T(8,128)S(1)} %get-tuple-element.51), channel_id=1, source_target_pairs={{0,192},{64,128},{128,64},{192,0},{1,193},{65,129},{129,65},{193,1... | collective-permute-start | bytes 393224 | tf_op jit(solution)/shard_map/ppermute | solution.py:317
  51.5 2.2 %collective-permute-done.5 = f32[264,128]{1,0:T(8,128)S(1)} collective-permute-done((f32[264,128]{1,0:T(8,128)S(1)}, f32[264,128]{1,0:T(8,128)S(1)}, u32[]{:S(2)}, u32[]{:S(2)}) %collective-permute-start.5) | collective-permute-done | bytes 135200 | tf_op jit(solution)/shard_map/ppermute | solution.py:317
  53.7 2.6 %collective-permute-start.6 = (f32[264,128]{1,0:T(8,128)S(1)}, f32[264,128]{1,0:T(8,128)S(1)}, u32[]{:S(2)}, u32[]{:S(2)}) collective-permute-start(f32[264,128]{1,0:T(8,128)S(1)} %add.29.refs_0_), channel_id=1, source_target_pairs={{0,192},{64,128},{128,64},{192,0},{1,193},{65,129},{129,65},{193,1... | collective-permute-start | bytes 405512 | tf_op jit(solution)/shard_map/ppermute | solution.py:317
  56.6 4.0 %collective-permute-done.8.refs_3_ = f32[256,128]{1,0:T(8,128)S(1)} collective-permute-done((f32[256,128]{1,0:T(8,128)S(1)}, f32[256,128]{1,0:T(8,128)S(1)}, u32[]{:S(2)}, u32[]{:S(2)}) %collective-permute-start.8) | collective-permute-done | bytes 131104 | tf_op jit(solution)/shard_map/ppermute | solution.py:317
  60.6 1.6 back.2
  62.2 2.1 %collective-permute-start.9 = (f32[576,128]{1,0:T(8,128)S(1)}, f32[576,128]{1,0:T(8,128)S(1)}, u32[]{:S(2)}, u32[]{:S(2)}) collective-permute-start(f32[576,128]{1,0:T(8,128)S(1)} %get-tuple-element.53), channel_id=1, source_target_pairs={{0,1},{1,0},{2,3},{3,2},{4,5},{5,4},{6,7},{7,6},{8,9},{9,8},{10,11... | collective-permute-start | bytes 884744 | tf_op jit(solution)/shard_map/ppermute | solution.py:291
  64.2 1.2 collective-permute-done.9
  65.5 9.6 %all_to_all.37 = f32[8,72,128]{2,1,0:T(8,128)S(1)} all-to-all(f32[8,72,128]{2,1,0:T(8,128)S(1)} %bitcast.35), channel_id=1, replica_groups={{0,2,4,6,8,10,12,14},{1,3,5,7,9,11,13,15},{16,18,20,22,24,26,28,30},{17..., dimensions={0} | all-to-all | bytes 589824 | tf_op jit(solution)/shard_map/all_to_all | solution.py:296
  75.1 1.6 collective-permute-start.12
  76.8 2.7 %collective-permute-start.11 = (f32[72,128]{1,0:T(8,128)S(1)}, f32[72,128]{1,0:T(8,128)S(1)}, u32[]{:S(2)}, u32[]{:S(2)}) collective-permute-start(f32[72,128]{1,0:T(8,128)S(1)} %sum_pieces.4.refs_0_), channel_id=1, source_target_pairs={{0,32},{1,33},{2,34},{3,35},{4,36},{5,37},{6,38},{7,39},{8,40},{9,... | collective-permute-start | bytes 110600 | tf_op jit(solution)/shard_map/ppermute | solution.py:302
  79.5 2.3 %collective-permute-start.10 = (f32[72,128]{1,0:T(8,128)S(1)}, f32[72,128]{1,0:T(8,128)S(1)}, u32[]{:S(2)}, u32[]{:S(2)}) collective-permute-start(f32[72,128]{1,0:T(8,128)S(1)} %sum_pieces.4.refs_0_), channel_id=1, source_target_pairs={{0,16},{1,17},{2,18},{3,19},{4,20},{5,21},{6,22},{7,23},{8,24},{9,... | collective-permute-start | bytes 110600 | tf_op jit(solution)/shard_map/ppermute | solution.py:302
  81.8 1.9 %collective-permute-done.11.refs_2_ = f32[72,128]{1,0:T(8,128)S(1)} collective-permute-done((f32[72,128]{1,0:T(8,128)S(1)}, f32[72,128]{1,0:T(8,128)S(1)}, u32[]{:S(2)}, u32[]{:S(2)}) %collective-permute-start.11) | collective-permute-done | bytes 36896 | tf_op jit(solution)/shard_map/ppermute | solution.py:302
  84.8 9.5 %all_to_all.38 = f32[8,64,128]{2,1,0:T(8,128)S(1)} all-to-all(f32[8,64,128]{2,1,0:T(8,128)S(1)} %bitcast.31), channel_id=1, replica_groups={{0,2,4,6,8,10,12,14},{1,3,5,7,9,11,13,15},{16,18,20,22,24,26,28,30},{17..., dimensions={0} | all-to-all | bytes 524288 | tf_op jit(solution)/shard_map/all_to_all | solution.py:296
  94.3 3.0 %collective-permute-start.13 = (f32[512,128]{1,0:T(8,128)S(1)}, f32[512,128]{1,0:T(8,128)S(1)}, u32[]{:S(2)}, u32[]{:S(2)}) collective-permute-start(f32[512,128]{1,0:T(8,128)S(1)} %bitcast.26), channel_id=1, source_target_pairs={{0,1},{1,0},{2,3},{3,2},{4,5},{5,4},{6,7},{7,6},{8,9},{9,8},{10,11... | collective-permute-start | bytes 786440 | tf_op jit(solution)/shard_map/ppermute | solution.py:291
  97.4 1.2 collective-permute-done.13.refs_1_
  98.5 1.9 %forward.4 = (f32[1024,128]{1,0:T(8,128)S(1)}, f32[1024,128]{1,0:T(8,128)S(1)}, f32[264,128]{1,0:T(8,128)S(1)}, f32[256,128]{1,0:T(8,128)S(1)}) custom-call(f32[512,128]{1,0:T(8,128)S(1)} %bitcast.27, f32[512,128]{1,0:T(8,128)S(1)} %collective-permute-done.13.refs_1_, f32[8,128]{1,0:T(8,128)S(1)} %get-tuple-element.56.refs_2_.size0, ...), custom_call_target="tpu_custom_call" | custom-call | flops 1073741824 | bytes 1048576 | tf_op jit(solution)/shard_map/forward/pallas_call | solution.py:29
  100.5 1.4 collective-permute-start.16
  102.0 3.3 %collective-permute-done.14 = f32[264,128]{1,0:T(8,128)S(1)} collective-permute-done((f32[264,128]{1,0:T(8,128)S(1)}, f32[264,128]{1,0:T(8,128)S(1)}, u32[]{:S(2)}, u32[]{:S(2)}) %collective-permute-start.14) | collective-permute-done | bytes 135200 | tf_op jit(solution)/shard_map/ppermute | solution.py:317
  105.3 1.4 collective-permute-start.15
  106.9 3.8 %collective-permute-done.17.refs_3_ = f32[256,128]{1,0:T(8,128)S(1)} collective-permute-done((f32[256,128]{1,0:T(8,128)S(1)}, f32[256,128]{1,0:T(8,128)S(1)}, u32[]{:S(2)}, u32[]{:S(2)}) %collective-permute-start.17) | collective-permute-done | bytes 131104 | tf_op jit(solution)/shard_map/ppermute | solution.py:317
  110.7 1.6 back.3
  112.3 2.7 %collective-permute-start.18 = (f32[576,128]{1,0:T(8,128)S(1)}, f32[576,128]{1,0:T(8,128)S(1)}, u32[]{:S(2)}, u32[]{:S(2)}) collective-permute-start(f32[576,128]{1,0:T(8,128)S(1)} %get-tuple-element.62), channel_id=1, source_target_pairs={{0,1},{1,0},{2,3},{3,2},{4,5},{5,4},{6,7},{7,6},{8,9},{9,8},{10,11... | collective-permute-start | bytes 884744 | tf_op jit(solution)/shard_map/ppermute | solution.py:291
  115.0 1.2 collective-permute-done.18
  116.3 9.6 %all_to_all.39 = f32[8,72,128]{2,1,0:T(8,128)S(1)} all-to-all(f32[8,72,128]{2,1,0:T(8,128)S(1)} %bitcast.36), channel_id=1, replica_groups={{0,2,4,6,8,10,12,14},{1,3,5,7,9,11,13,15},{16,18,20,22,24,26,28,30},{17..., dimensions={0} | all-to-all | bytes 589824 | tf_op jit(solution)/shard_map/all_to_all | solution.py:296
  125.9 1.9 %collective-permute-start.21 = (f32[72,128]{1,0:T(8,128)S(1)}, f32[72,128]{1,0:T(8,128)S(1)}, u32[]{:S(2)}, u32[]{:S(2)}) collective-permute-start(f32[72,128]{1,0:T(8,128)S(1)} %sum_pieces.5.refs_0_), channel_id=1, source_target_pairs={{0,48},{1,49},{2,50},{3,51},{4,52},{5,53},{6,54},{7,55},{8,56},{9,... | collective-permute-start | bytes 110600 | tf_op jit(solution)/shard_map/ppermute | solution.py:302
  127.8 2.9 %collective-permute-start.20 = (f32[72,128]{1,0:T(8,128)S(1)}, f32[72,128]{1,0:T(8,128)S(1)}, u32[]{:S(2)}, u32[]{:S(2)}) collective-permute-start(f32[72,128]{1,0:T(8,128)S(1)} %sum_pieces.5.refs_0_), channel_id=1, source_target_pairs={{0,32},{1,33},{2,34},{3,35},{4,36},{5,37},{6,38},{7,39},{8,40},{9,... | collective-permute-start | bytes 110600 | tf_op jit(solution)/shard_map/ppermute | solution.py:302
  131.8 2.8 %collective-permute-done.20.refs_2_ = f32[72,128]{1,0:T(8,128)S(1)} collective-permute-done((f32[72,128]{1,0:T(8,128)S(1)}, f32[72,128]{1,0:T(8,128)S(1)}, u32[]{:S(2)}, u32[]{:S(2)}) %collective-permute-start.20) | collective-permute-done | bytes 36896 | tf_op jit(solution)/shard_map/ppermute | solution.py:302
  135.7 9.6 %all_to_all.40 = f32[8,64,128]{2,1,0:T(8,128)S(1)} all-to-all(f32[8,64,128]{2,1,0:T(8,128)S(1)} %bitcast.32), channel_id=1, replica_groups={{0,2,4,6,8,10,12,14},{1,3,5,7,9,11,13,15},{16,18,20,22,24,26,28,30},{17..., dimensions={0} | all-to-all | bytes 524288 | tf_op jit(solution)/shard_map/all_to_all | solution.py:296
  145.3 3.2 %collective-permute-start.22 = (f32[512,128]{1,0:T(8,128)S(1)}, f32[512,128]{1,0:T(8,128)S(1)}, u32[]{:S(2)}, u32[]{:S(2)}) collective-permute-start(f32[512,128]{1,0:T(8,128)S(1)} %bitcast.24), channel_id=1, source_target_pairs={{0,1},{1,0},{2,3},{3,2},{4,5},{5,4},{6,7},{7,6},{8,9},{9,8},{10,11... | collective-permute-start | bytes 786440 | tf_op jit(solution)/shard_map/ppermute | solution.py:291
  149.7 1.9 %forward.5 = (f32[1024,128]{1,0:T(8,128)S(1)}, f32[1024,128]{1,0:T(8,128)S(1)}, f32[264,128]{1,0:T(8,128)S(1)}, f32[256,128]{1,0:T(8,128)S(1)}) custom-call(f32[512,128]{1,0:T(8,128)S(1)} %bitcast.25, f32[512,128]{1,0:T(8,128)S(1)} %collective-permute-done.22.refs_1_, f32[8,128]{1,0:T(8,128)S(1)} %get-tuple-element.65.refs_2_.size1, ...), custom_call_target="tpu_custom_call" | custom-call | flops 1073741824 | bytes 1048576 | tf_op jit(solution)/shard_map/forward/pallas_call | solution.py:29
  151.7 1.5 collective-permute-start.25
  153.2 3.3 %collective-permute-done.23 = f32[264,128]{1,0:T(8,128)S(1)} collective-permute-done((f32[264,128]{1,0:T(8,128)S(1)}, f32[264,128]{1,0:T(8,128)S(1)}, u32[]{:S(2)}, u32[]{:S(2)}) %collective-permute-start.23) | collective-permute-done | bytes 135200 | tf_op jit(solution)/shard_map/ppermute | solution.py:317
  156.5 1.5 collective-permute-start.24
  158.8 3.4 %collective-permute-done.26.h3 = f32[256,128]{1,0:T(8,128)S(1)} collective-permute-done((f32[256,128]{1,0:T(8,128)S(1)}, f32[256,128]{1,0:T(8,128)S(1)}, u32[]{:S(2)}, u32[]{:S(2)}) %collective-permute-start.26) | collective-permute-done | bytes 131104 | tf_op jit(solution)/shard_map/ppermute | solution.py:317
  162.5 16.6 %all_to_all.41 = f32[64,1,128]{2,1,0:T(1,128)S(1)} all-to-all(f32[64,1,128]{2,1,0:T(1,128)S(1)} %bitcast.34), channel_id=1, replica_groups=mesh['unit'=4,'samp'=64] {'samp'}, dimensions={0} | all-to-all | bytes 65536 | tf_op jit(solution)/shard_map/all_to_all | solution.py:421
  (39 shorter events, 7.5 us)
Async XLA Ops:
  5.4 4.6 %collective-permute-start = (f32[512,128]{1,0:T(8,128)S(1)}, f32[512,128]{1,0:T(8,128)S(1)}, u32[]{:S(2)}, u32[]{:S(2)}) collective-permute-start(f32[512,128]{1,0:T(8,128)S(1)} %get-tuple-element.44), channel_id=1, source_target_pairs={{0,1},{1,0},{2,3},{3,2},{4,5},{5,4},{6,7},{7,6},{8,9},{9,8},{10,11... | collective-permute-start | bytes 786440 | tf_op jit(solution)/shard_map/ppermute | solution.py:291
  19.8 8.5 %collective-permute-start.3 = (f32[64,128]{1,0:T(8,128)S(1)}, f32[64,128]{1,0:T(8,128)S(1)}, u32[]{:S(2)}, u32[]{:S(2)}) collective-permute-start(f32[64,128]{1,0:T(8,128)S(1)} %sum_pieces.3.refs_0_), channel_id=1, source_target_pairs={{0,48},{1,49},{2,50},{3,51},{4,52},{5,53},{6,54},{7,55},{8,56},{9,... | collective-permute-start | bytes 98312 | tf_op jit(solution)/shard_map/ppermute | solution.py:302
  25.1 6.7 %collective-permute-start.2 = (f32[64,128]{1,0:T(8,128)S(1)}, f32[64,128]{1,0:T(8,128)S(1)}, u32[]{:S(2)}, u32[]{:S(2)}) collective-permute-start(f32[64,128]{1,0:T(8,128)S(1)} %sum_pieces.3.refs_0_), channel_id=1, source_target_pairs={{0,32},{1,33},{2,34},{3,35},{4,36},{5,37},{6,38},{7,39},{8,40},{9,... | collective-permute-start | bytes 98312 | tf_op jit(solution)/shard_map/ppermute | solution.py:302
  26.2 5.5 %collective-permute-start.1 = (f32[64,128]{1,0:T(8,128)S(1)}, f32[64,128]{1,0:T(8,128)S(1)}, u32[]{:S(2)}, u32[]{:S(2)}) collective-permute-start(f32[64,128]{1,0:T(8,128)S(1)} %sum_pieces.3.refs_0_), channel_id=1, source_target_pairs={{0,16},{1,17},{2,18},{3,19},{4,20},{5,21},{6,22},{7,23},{8,24},{9,... | collective-permute-start | bytes 98312 | tf_op jit(solution)/shard_map/ppermute | solution.py:302
  41.4 5.3 %collective-permute-start.4 = (f32[512,128]{1,0:T(8,128)S(1)}, f32[512,128]{1,0:T(8,128)S(1)}, u32[]{:S(2)}, u32[]{:S(2)}) collective-permute-start(f32[512,128]{1,0:T(8,128)S(1)} %bitcast.22), channel_id=1, source_target_pairs={{0,1},{1,0},{2,3},{3,2},{4,5},{5,4},{6,7},{7,6},{8,9},{9,8},{10,11... | collective-permute-start | bytes 786440 | tf_op jit(solution)/shard_map/ppermute | solution.py:291
  48.4 5.3 %collective-permute-start.5 = (f32[264,128]{1,0:T(8,128)S(1)}, f32[264,128]{1,0:T(8,128)S(1)}, u32[]{:S(2)}, u32[]{:S(2)}) collective-permute-start(f32[264,128]{1,0:T(8,128)S(1)} %get-tuple-element.50), channel_id=1, source_target_pairs={{0,64},{64,0},{128,192},{192,128},{1,65},{65,1},{129,193},{193,129... | collective-permute-start | bytes 405512 | tf_op jit(solution)/shard_map/ppermute | solution.py:317
  49.7 6.6 %collective-permute-start.7 = (f32[256,128]{1,0:T(8,128)S(1)}, f32[256,128]{1,0:T(8,128)S(1)}, u32[]{:S(2)}, u32[]{:S(2)}) collective-permute-start(f32[256,128]{1,0:T(8,128)S(1)} %get-tuple-element.51), channel_id=1, source_target_pairs={{0,192},{64,128},{128,64},{192,0},{1,193},{65,129},{129,65},{193,1... | collective-permute-start | bytes 393224 | tf_op jit(solution)/shard_map/ppermute | solution.py:317
  53.7 6.9 %collective-permute-start.6 = (f32[264,128]{1,0:T(8,128)S(1)}, f32[264,128]{1,0:T(8,128)S(1)}, u32[]{:S(2)}, u32[]{:S(2)}) collective-permute-start(f32[264,128]{1,0:T(8,128)S(1)} %add.29.refs_0_), channel_id=1, source_target_pairs={{0,192},{64,128},{128,64},{192,0},{1,193},{65,129},{129,65},{193,1... | collective-permute-start | bytes 405512 | tf_op jit(solution)/shard_map/ppermute | solution.py:317
  56.3 4.3 %collective-permute-start.8 = (f32[256,128]{1,0:T(8,128)S(1)}, f32[256,128]{1,0:T(8,128)S(1)}, u32[]{:S(2)}, u32[]{:S(2)}) collective-permute-start(f32[256,128]{1,0:T(8,128)S(1)} %add.30.refs_2_), channel_id=1, source_target_pairs={{0,64},{64,0},{128,192},{192,128},{1,65},{65,1},{129,193},{193,129... | collective-permute-start | bytes 393224 | tf_op jit(solution)/shard_map/ppermute | solution.py:317
  62.2 3.3 %collective-permute-start.9 = (f32[576,128]{1,0:T(8,128)S(1)}, f32[576,128]{1,0:T(8,128)S(1)}, u32[]{:S(2)}, u32[]{:S(2)}) collective-permute-start(f32[576,128]{1,0:T(8,128)S(1)} %get-tuple-element.53), channel_id=1, source_target_pairs={{0,1},{1,0},{2,3},{3,2},{4,5},{5,4},{6,7},{7,6},{8,9},{9,8},{10,11... | collective-permute-start | bytes 884744 | tf_op jit(solution)/shard_map/ppermute | solution.py:291
  75.1 6.7 %collective-permute-start.12 = (f32[72,128]{1,0:T(8,128)S(1)}, f32[72,128]{1,0:T(8,128)S(1)}, u32[]{:S(2)}, u32[]{:S(2)}) collective-permute-start(f32[72,128]{1,0:T(8,128)S(1)} %sum_pieces.4.refs_0_), channel_id=1, source_target_pairs={{0,48},{1,49},{2,50},{3,51},{4,52},{5,53},{6,54},{7,55},{8,56},{9,... | collective-permute-start | bytes 110600 | tf_op jit(solution)/shard_map/ppermute | solution.py:302
  76.8 6.9 %collective-permute-start.11 = (f32[72,128]{1,0:T(8,128)S(1)}, f32[72,128]{1,0:T(8,128)S(1)}, u32[]{:S(2)}, u32[]{:S(2)}) collective-permute-start(f32[72,128]{1,0:T(8,128)S(1)} %sum_pieces.4.refs_0_), channel_id=1, source_target_pairs={{0,32},{1,33},{2,34},{3,35},{4,36},{5,37},{6,38},{7,39},{8,40},{9,... | collective-permute-start | bytes 110600 | tf_op jit(solution)/shard_map/ppermute | solution.py:302
  79.5 5.3 %collective-permute-start.10 = (f32[72,128]{1,0:T(8,128)S(1)}, f32[72,128]{1,0:T(8,128)S(1)}, u32[]{:S(2)}, u32[]{:S(2)}) collective-permute-start(f32[72,128]{1,0:T(8,128)S(1)} %sum_pieces.4.refs_0_), channel_id=1, source_target_pairs={{0,16},{1,17},{2,18},{3,19},{4,20},{5,21},{6,22},{7,23},{8,24},{9,... | collective-permute-start | bytes 110600 | tf_op jit(solution)/shard_map/ppermute | solution.py:302
  94.3 4.2 %collective-permute-start.13 = (f32[512,128]{1,0:T(8,128)S(1)}, f32[512,128]{1,0:T(8,128)S(1)}, u32[]{:S(2)}, u32[]{:S(2)}) collective-permute-start(f32[512,128]{1,0:T(8,128)S(1)} %bitcast.26), channel_id=1, source_target_pairs={{0,1},{1,0},{2,3},{3,2},{4,5},{5,4},{6,7},{7,6},{8,9},{9,8},{10,11... | collective-permute-start | bytes 786440 | tf_op jit(solution)/shard_map/ppermute | solution.py:291
  100.4 4.9 %collective-permute-start.14 = (f32[264,128]{1,0:T(8,128)S(1)}, f32[264,128]{1,0:T(8,128)S(1)}, u32[]{:S(2)}, u32[]{:S(2)}) collective-permute-start(f32[264,128]{1,0:T(8,128)S(1)} %get-tuple-element.58), channel_id=1, source_target_pairs={{0,64},{64,0},{128,192},{192,128},{1,65},{65,1},{129,193},{193,129... | collective-permute-start | bytes 405512 | tf_op jit(solution)/shard_map/ppermute | solution.py:317
  100.5 6.2 %collective-permute-start.16 = (f32[256,128]{1,0:T(8,128)S(1)}, f32[256,128]{1,0:T(8,128)S(1)}, u32[]{:S(2)}, u32[]{:S(2)}) collective-permute-start(f32[256,128]{1,0:T(8,128)S(1)} %get-tuple-element.59), channel_id=1, source_target_pairs={{0,192},{64,128},{128,64},{192,0},{1,193},{65,129},{129,65},{193,1... | collective-permute-start | bytes 393224 | tf_op jit(solution)/shard_map/ppermute | solution.py:317
  105.3 5.4 %collective-permute-start.15 = (f32[264,128]{1,0:T(8,128)S(1)}, f32[264,128]{1,0:T(8,128)S(1)}, u32[]{:S(2)}, u32[]{:S(2)}) collective-permute-start(f32[264,128]{1,0:T(8,128)S(1)} %add.32.refs_0_), channel_id=1, source_target_pairs={{0,192},{64,128},{128,64},{192,0},{1,193},{65,129},{129,65},{193,1... | collective-permute-start | bytes 405512 | tf_op jit(solution)/shard_map/ppermute | solution.py:317
  106.8 3.9 %collective-permute-start.17 = (f32[256,128]{1,0:T(8,128)S(1)}, f32[256,128]{1,0:T(8,128)S(1)}, u32[]{:S(2)}, u32[]{:S(2)}) collective-permute-start(f32[256,128]{1,0:T(8,128)S(1)} %add.33.refs_2_), channel_id=1, source_target_pairs={{0,64},{64,0},{128,192},{192,128},{1,65},{65,1},{129,193},{193,129... | collective-permute-start | bytes 393224 | tf_op jit(solution)/shard_map/ppermute | solution.py:317
  112.3 3.9 %collective-permute-start.18 = (f32[576,128]{1,0:T(8,128)S(1)}, f32[576,128]{1,0:T(8,128)S(1)}, u32[]{:S(2)}, u32[]{:S(2)}) collective-permute-start(f32[576,128]{1,0:T(8,128)S(1)} %get-tuple-element.62), channel_id=1, source_target_pairs={{0,1},{1,0},{2,3},{3,2},{4,5},{5,4},{6,7},{7,6},{8,9},{9,8},{10,11... | collective-permute-start | bytes 884744 | tf_op jit(solution)/shard_map/ppermute | solution.py:291
  125.9 5.9 %collective-permute-start.21 = (f32[72,128]{1,0:T(8,128)S(1)}, f32[72,128]{1,0:T(8,128)S(1)}, u32[]{:S(2)}, u32[]{:S(2)}) collective-permute-start(f32[72,128]{1,0:T(8,128)S(1)} %sum_pieces.5.refs_0_), channel_id=1, source_target_pairs={{0,48},{1,49},{2,50},{3,51},{4,52},{5,53},{6,54},{7,55},{8,56},{9,... | collective-permute-start | bytes 110600 | tf_op jit(solution)/shard_map/ppermute | solution.py:302
  127.8 6.8 %collective-permute-start.20 = (f32[72,128]{1,0:T(8,128)S(1)}, f32[72,128]{1,0:T(8,128)S(1)}, u32[]{:S(2)}, u32[]{:S(2)}) collective-permute-start(f32[72,128]{1,0:T(8,128)S(1)} %sum_pieces.5.refs_0_), channel_id=1, source_target_pairs={{0,32},{1,33},{2,34},{3,35},{4,36},{5,37},{6,38},{7,39},{8,40},{9,... | collective-permute-start | bytes 110600 | tf_op jit(solution)/shard_map/ppermute | solution.py:302
  130.7 5.0 %collective-permute-start.19 = (f32[72,128]{1,0:T(8,128)S(1)}, f32[72,128]{1,0:T(8,128)S(1)}, u32[]{:S(2)}, u32[]{:S(2)}) collective-permute-start(f32[72,128]{1,0:T(8,128)S(1)} %sum_pieces.5.refs_0_), channel_id=1, source_target_pairs={{0,16},{1,17},{2,18},{3,19},{4,20},{5,21},{6,22},{7,23},{8,24},{9,... | collective-permute-start | bytes 110600 | tf_op jit(solution)/shard_map/ppermute | solution.py:302
  145.3 4.3 %collective-permute-start.22 = (f32[512,128]{1,0:T(8,128)S(1)}, f32[512,128]{1,0:T(8,128)S(1)}, u32[]{:S(2)}, u32[]{:S(2)}) collective-permute-start(f32[512,128]{1,0:T(8,128)S(1)} %bitcast.24), channel_id=1, source_target_pairs={{0,1},{1,0},{2,3},{3,2},{4,5},{5,4},{6,7},{7,6},{8,9},{9,8},{10,11... | collective-permute-start | bytes 786440 | tf_op jit(solution)/shard_map/ppermute | solution.py:291
  151.6 4.9 %collective-permute-start.23 = (f32[264,128]{1,0:T(8,128)S(1)}, f32[264,128]{1,0:T(8,128)S(1)}, u32[]{:S(2)}, u32[]{:S(2)}) collective-permute-start(f32[264,128]{1,0:T(8,128)S(1)} %get-tuple-element.68), channel_id=1, source_target_pairs={{0,64},{64,0},{128,192},{192,128},{1,65},{65,1},{129,193},{193,129... | collective-permute-start | bytes 405512 | tf_op jit(solution)/shard_map/ppermute | solution.py:317
  151.7 6.3 %collective-permute-start.25 = (f32[256,128]{1,0:T(8,128)S(1)}, f32[256,128]{1,0:T(8,128)S(1)}, u32[]{:S(2)}, u32[]{:S(2)}) collective-permute-start(f32[256,128]{1,0:T(8,128)S(1)} %get-tuple-element.69), channel_id=1, source_target_pairs={{0,192},{64,128},{128,64},{192,0},{1,193},{65,129},{129,65},{193,1... | collective-permute-start | bytes 393224 | tf_op jit(solution)/shard_map/ppermute | solution.py:317
  156.5 5.7 %collective-permute-start.24 = (f32[264,128]{1,0:T(8,128)S(1)}, f32[264,128]{1,0:T(8,128)S(1)}, u32[]{:S(2)}, u32[]{:S(2)}) collective-permute-start(f32[264,128]{1,0:T(8,128)S(1)} %add.35.h0), channel_id=1, source_target_pairs={{0,192},{64,128},{128,64},{192,0},{1,193},{65,129},{129,65},{193,1... | collective-permute-start | bytes 405512 | tf_op jit(solution)/shard_map/ppermute | solution.py:317
  158.0 4.2 %collective-permute-start.26 = (f32[256,128]{1,0:T(8,128)S(1)}, f32[256,128]{1,0:T(8,128)S(1)}, u32[]{:S(2)}, u32[]{:S(2)}) collective-permute-start(f32[256,128]{1,0:T(8,128)S(1)} %add.36.h2), channel_id=1, source_target_pairs={{0,64},{64,0},{128,192},{192,128},{1,65},{65,1},{129,193},{193,129... | collective-permute-start | bytes 393224 | tf_op jit(solution)/shard_map/ppermute | solution.py:317

commit v11 on v10

--- a/solution.py
+++ b/solution.py
@@ -305,11 +305,11 @@
             for d in range(1, blocks)
         ]
 
-    def sum_samples(pieces, scal):
+    def sum_samples(pieces, scal, tokens=()):
         n = pieces.shape[0] // BLOCK
         terms = block_terms(call(sum_pieces, shape(n, LANES), exchange(pieces)))
         outs = [shape(half * rows, LANES)] + ([] if scal is None else [vector])
-        scals = [] if scal is None else [scal]
+        scals = list(tokens) if scal is None else [scal]
         outs = call(sum_blocks, outs, *terms, *scals, rows=rows, copies=BLOCK)
         return outs[0], outs[-1]
 
@@ -343,13 +343,13 @@
         flops=flops,
     )
     high, low = here(high), here(low)
-    (high_turned, token), (low_turned, _) = [
+    (high_turned, token), (low_turned, token_low) = [
         call(turn_states, [shape(units, samples, dtype=BF16), vector], x, flops=flops)
         for x in (high, low)
     ]
     high_turned, low_turned = here(high_turned), here(low_turned)
     pieces = call(add_pieces, shape(half * rows, LANES), mine, swap(theirs), token)
-    spread, _ = sum_samples(pieces, None)
+    spread, _ = sum_samples(pieces, None, [token_low])
 
     gradients, directions, images, sizes = [], [], [], []
     scal = size = None

time: 181 us -> 180 us (level)
  transfers between devices with their start and end apart: 27 -> 27, of which waited for: 15 -> 16; matrix products, arithmetic and copies ran while one was open for 0% -> 0% of each run, Pallas kernels for 2% -> 2%
where the time goes in v11:
time: 180 us
  blocking collectives  74.4 us (41%)
  starting transfers between devices  51.2 us (28%)
  waiting for transfers between devices  35 us (19%)
  Pallas kernels  18 us (10%)
    all_to_all x6, blocking collectives, exchange(): x = lax.all_to_all(x, 'samp', 0, 0, axis_index_groups=groups, tiled=True)  57.8 us
    ppermute x9, starting transfers between devices, block_terms(): lax.ppermute(x, 'samp', [(i, (i + d * step) % samp_count) for i in range(...  21 us
    ppermute x12, waiting for transfers between devices, unit_hop(): return lax.ppermute(x, 'unit', [(i, i ^ mask) for i in range(unit_count)])  20 us
    ppermute x6, starting transfers between devices, swap(): return lax.ppermute(x, 'samp', swap_cores)  18 us
    pallas_call x18, Pallas kernels, call(): pl.pallas_call(functools.partial(kernel, **static), in_specs=specs or [VM...  18 us
    all_to_all x1, blocking collectives, shards(): lax.all_to_all(squares.reshape(samp_count, 1, LANES), 'samp', 0, 0, tiled...  16.7 us
    ppermute x12, starting transfers between devices, unit_hop(): return lax.ppermute(x, 'unit', [(i, i ^ mask) for i in range(unit_count)])  12.2 us
    ppermute x9, waiting for transfers between devices, block_terms(): lax.ppermute(x, 'samp', [(i, (i + d * step) % samp_count) for i in range(...  9.01 us
  transfers between devices with their start and end apart: 27, of which 16 were waited for; matrix products, arithmetic and copies ran while one was open for 0% of the time, Pallas kernels for 2%

profile of v11, /device:TPU:1, one launch (start us, length us, event | category | flops | bytes accessed | tf_op | source)
XLA Modules:
  0.0 179.7 jit_solution(1444081966325819540)
XLA Ops:
  0.6 4.7 %first.1 = (bf16[1024,2048]{1,0:T(8,128)(2,1)S(1)}, bf16[1024,2048]{1,0:T(8,128)(2,1)S(1)}, f32[64,1024]{1,0:T(8,128)S(1)}, f32[512,128]{1,0:T(8,128)S(1)}, f32[512,128]{1,0:T(8,128)S(1)}) custom-call(s32[1,1]{1,0:T(1,128)} %bitcast.core, f32[1024,2048]{1,0:T(8,128)} %states.1, f32[64,1024]{1,0:T(8,128)} %bitcast.37), custom_call_target="tpu_custom_call" | custom-call | flops 1073741824 | bytes 1048576 | tf_op jit(solution)/shard_map/first/pallas_call | solution.py:29
  5.4 3.3 %collective-permute-start = (f32[512,128]{1,0:T(8,128)S(1)}, f32[512,128]{1,0:T(8,128)S(1)}, u32[]{:S(2)}, u32[]{:S(2)}) collective-permute-start(f32[512,128]{1,0:T(8,128)S(1)} %get-tuple-element.45), channel_id=1, source_target_pairs={{0,1},{1,0},{2,3},{3,2},{4,5},{5,4},{6,7},{7,6},{8,9},{9,8},{10,11... | collective-permute-start | bytes 786440 | tf_op jit(solution)/shard_map/ppermute | solution.py:291
  8.7 1.2 turn_states.2
  10.0 9.8 %all_to_all.35 = f32[8,64,128]{2,1,0:T(8,128)S(1)} all-to-all(f32[8,64,128]{2,1,0:T(8,128)S(1)} %bitcast.28), channel_id=1, replica_groups={{0,2,4,6,8,10,12,14},{1,3,5,7,9,11,13,15},{16,18,20,22,24,26,28,30},{17..., dimensions={0} | all-to-all | bytes 524288 | tf_op jit(solution)/shard_map/all_to_all | solution.py:296
  19.8 5.2 %collective-permute-start.3 = (f32[64,128]{1,0:T(8,128)S(1)}, f32[64,128]{1,0:T(8,128)S(1)}, u32[]{:S(2)}, u32[]{:S(2)}) collective-permute-start(f32[64,128]{1,0:T(8,128)S(1)} %sum_pieces.3.refs_0_), channel_id=1, source_target_pairs={{0,48},{1,49},{2,50},{3,51},{4,52},{5,53},{6,54},{7,55},{8,56},{9,... | collective-permute-start | bytes 98312 | tf_op jit(solution)/shard_map/ppermute | solution.py:302
  25.1 1.2 collective-permute-start.2
  26.2 2.1 %collective-permute-start.1 = (f32[64,128]{1,0:T(8,128)S(1)}, f32[64,128]{1,0:T(8,128)S(1)}, u32[]{:S(2)}, u32[]{:S(2)}) collective-permute-start(f32[64,128]{1,0:T(8,128)S(1)} %sum_pieces.3.refs_0_), channel_id=1, source_target_pairs={{0,16},{1,17},{2,18},{3,19},{4,20},{5,21},{6,22},{7,23},{8,24},{9,... | collective-permute-start | bytes 98312 | tf_op jit(solution)/shard_map/ppermute | solution.py:302
  28.3 1.2 turn_states.3
  29.6 2.2 %collective-permute-done.2.refs_2_ = f32[64,128]{1,0:T(8,128)S(1)} collective-permute-done((f32[64,128]{1,0:T(8,128)S(1)}, f32[64,128]{1,0:T(8,128)S(1)}, u32[]{:S(2)}, u32[]{:S(2)}) %collective-permute-start.2) | collective-permute-done | bytes 32800 | tf_op jit(solution)/shard_map/ppermute | solution.py:302
  31.8 9.6 %all_to_all.36 = f32[8,64,128]{2,1,0:T(8,128)S(1)} all-to-all(f32[8,64,128]{2,1,0:T(8,128)S(1)} %bitcast.29), channel_id=1, replica_groups={{0,2,4,6,8,10,12,14},{1,3,5,7,9,11,13,15},{16,18,20,22,24,26,28,30},{17..., dimensions={0} | all-to-all | bytes 524288 | tf_op jit(solution)/shard_map/all_to_all | solution.py:296
  41.4 3.6 %collective-permute-start.4 = (f32[512,128]{1,0:T(8,128)S(1)}, f32[512,128]{1,0:T(8,128)S(1)}, u32[]{:S(2)}, u32[]{:S(2)}) collective-permute-start(f32[512,128]{1,0:T(8,128)S(1)} %bitcast.26), channel_id=1, source_target_pairs={{0,1},{1,0},{2,3},{3,2},{4,5},{5,4},{6,7},{7,6},{8,9},{9,8},{10,11... | collective-permute-start | bytes 786440 | tf_op jit(solution)/shard_map/ppermute | solution.py:291
  45.0 1.2 collective-permute-done.4.refs_1_
  46.1 1.7 forward.3
  47.8 1.3 collective-permute-start.5
  49.1 1.8 %collective-permute-start.7 = (f32[256,128]{1,0:T(8,128)S(1)}, f32[256,128]{1,0:T(8,128)S(1)}, u32[]{:S(2)}, u32[]{:S(2)}) collective-permute-start(f32[256,128]{1,0:T(8,128)S(1)} %get-tuple-element.53), channel_id=1, source_target_pairs={{0,192},{64,128},{128,64},{192,0},{1,193},{65,129},{129,65},{193,1... | collective-permute-start | bytes 393224 | tf_op jit(solution)/shard_map/ppermute | solution.py:317
  50.9 1.8 collective-permute-done.5
  52.7 2.6 %collective-permute-start.6 = (f32[264,128]{1,0:T(8,128)S(1)}, f32[264,128]{1,0:T(8,128)S(1)}, u32[]{:S(2)}, u32[]{:S(2)}) collective-permute-start(f32[264,128]{1,0:T(8,128)S(1)} %add.29.refs_0_), channel_id=1, source_target_pairs={{0,192},{64,128},{128,64},{192,0},{1,193},{65,129},{129,65},{193,1... | collective-permute-start | bytes 405512 | tf_op jit(solution)/shard_map/ppermute | solution.py:317
  55.6 4.1 %collective-permute-done.8.refs_3_ = f32[256,128]{1,0:T(8,128)S(1)} collective-permute-done((f32[256,128]{1,0:T(8,128)S(1)}, f32[256,128]{1,0:T(8,128)S(1)}, u32[]{:S(2)}, u32[]{:S(2)}) %collective-permute-start.8) | collective-permute-done | bytes 131104 | tf_op jit(solution)/shard_map/ppermute | solution.py:317
  59.7 1.6 back.2
  61.2 2.4 %collective-permute-start.9 = (f32[576,128]{1,0:T(8,128)S(1)}, f32[576,128]{1,0:T(8,128)S(1)}, u32[]{:S(2)}, u32[]{:S(2)}) collective-permute-start(f32[576,128]{1,0:T(8,128)S(1)} %get-tuple-element.55), channel_id=1, source_target_pairs={{0,1},{1,0},{2,3},{3,2},{4,5},{5,4},{6,7},{7,6},{8,9},{9,8},{10,11... | collective-permute-start | bytes 884744 | tf_op jit(solution)/shard_map/ppermute | solution.py:291
  63.7 1.2 collective-permute-done.9
  64.9 9.6 %all_to_all.37 = f32[8,72,128]{2,1,0:T(8,128)S(1)} all-to-all(f32[8,72,128]{2,1,0:T(8,128)S(1)} %bitcast.35), channel_id=1, replica_groups={{0,2,4,6,8,10,12,14},{1,3,5,7,9,11,13,15},{16,18,20,22,24,26,28,30},{17..., dimensions={0} | all-to-all | bytes 589824 | tf_op jit(solution)/shard_map/all_to_all | solution.py:296
  74.5 1.6 collective-permute-start.12
  76.2 2.8 %collective-permute-start.11 = (f32[72,128]{1,0:T(8,128)S(1)}, f32[72,128]{1,0:T(8,128)S(1)}, u32[]{:S(2)}, u32[]{:S(2)}) collective-permute-start(f32[72,128]{1,0:T(8,128)S(1)} %sum_pieces.4.refs_0_), channel_id=1, source_target_pairs={{0,32},{1,33},{2,34},{3,35},{4,36},{5,37},{6,38},{7,39},{8,40},{9,... | collective-permute-start | bytes 110600 | tf_op jit(solution)/shard_map/ppermute | solution.py:302
  78.9 2.3 %collective-permute-start.10 = (f32[72,128]{1,0:T(8,128)S(1)}, f32[72,128]{1,0:T(8,128)S(1)}, u32[]{:S(2)}, u32[]{:S(2)}) collective-permute-start(f32[72,128]{1,0:T(8,128)S(1)} %sum_pieces.4.refs_0_), channel_id=1, source_target_pairs={{0,16},{1,17},{2,18},{3,19},{4,20},{5,21},{6,22},{7,23},{8,24},{9,... | collective-permute-start | bytes 110600 | tf_op jit(solution)/shard_map/ppermute | solution.py:302
  81.2 1.9 %collective-permute-done.11.refs_2_ = f32[72,128]{1,0:T(8,128)S(1)} collective-permute-done((f32[72,128]{1,0:T(8,128)S(1)}, f32[72,128]{1,0:T(8,128)S(1)}, u32[]{:S(2)}, u32[]{:S(2)}) %collective-permute-start.11) | collective-permute-done | bytes 36896 | tf_op jit(solution)/shard_map/ppermute | solution.py:302
  84.2 9.5 %all_to_all.38 = f32[8,64,128]{2,1,0:T(8,128)S(1)} all-to-all(f32[8,64,128]{2,1,0:T(8,128)S(1)} %bitcast.31), channel_id=1, replica_groups={{0,2,4,6,8,10,12,14},{1,3,5,7,9,11,13,15},{16,18,20,22,24,26,28,30},{17..., dimensions={0} | all-to-all | bytes 524288 | tf_op jit(solution)/shard_map/all_to_all | solution.py:296
  93.7 3.0 %collective-permute-start.13 = (f32[512,128]{1,0:T(8,128)S(1)}, f32[512,128]{1,0:T(8,128)S(1)}, u32[]{:S(2)}, u32[]{:S(2)}) collective-permute-start(f32[512,128]{1,0:T(8,128)S(1)} %bitcast.24), channel_id=1, source_target_pairs={{0,1},{1,0},{2,3},{3,2},{4,5},{5,4},{6,7},{7,6},{8,9},{9,8},{10,11... | collective-permute-start | bytes 786440 | tf_op jit(solution)/shard_map/ppermute | solution.py:291
  97.9 1.9 %forward.4 = (f32[1024,128]{1,0:T(8,128)S(1)}, f32[1024,128]{1,0:T(8,128)S(1)}, f32[264,128]{1,0:T(8,128)S(1)}, f32[256,128]{1,0:T(8,128)S(1)}) custom-call(f32[512,128]{1,0:T(8,128)S(1)} %bitcast.25, f32[512,128]{1,0:T(8,128)S(1)} %collective-permute-done.13.refs_1_, f32[8,128]{1,0:T(8,128)S(1)} %get-tuple-element.58.refs_2_.size0, ...), custom_call_target="tpu_custom_call" | custom-call | flops 1073741824 | bytes 1048576 | tf_op jit(solution)/shard_map/forward/pallas_call | solution.py:29
  99.9 1.4 collective-permute-start.16
  101.4 3.3 %collective-permute-done.14 = f32[264,128]{1,0:T(8,128)S(1)} collective-permute-done((f32[264,128]{1,0:T(8,128)S(1)}, f32[264,128]{1,0:T(8,128)S(1)}, u32[]{:S(2)}, u32[]{:S(2)}) %collective-permute-start.14) | collective-permute-done | bytes 135200 | tf_op jit(solution)/shard_map/ppermute | solution.py:317
  104.7 1.4 collective-permute-start.15
  106.3 4.1 %collective-permute-done.17.refs_3_ = f32[256,128]{1,0:T(8,128)S(1)} collective-permute-done((f32[256,128]{1,0:T(8,128)S(1)}, f32[256,128]{1,0:T(8,128)S(1)}, u32[]{:S(2)}, u32[]{:S(2)}) %collective-permute-start.17) | collective-permute-done | bytes 131104 | tf_op jit(solution)/shard_map/ppermute | solution.py:317
  110.4 1.6 back.3
  112.0 2.4 %collective-permute-start.18 = (f32[576,128]{1,0:T(8,128)S(1)}, f32[576,128]{1,0:T(8,128)S(1)}, u32[]{:S(2)}, u32[]{:S(2)}) collective-permute-start(f32[576,128]{1,0:T(8,128)S(1)} %get-tuple-element.64), channel_id=1, source_target_pairs={{0,1},{1,0},{2,3},{3,2},{4,5},{5,4},{6,7},{7,6},{8,9},{9,8},{10,11... | collective-permute-start | bytes 884744 | tf_op jit(solution)/shard_map/ppermute | solution.py:291
  114.4 1.2 collective-permute-done.18
  115.7 9.6 %all_to_all.39 = f32[8,72,128]{2,1,0:T(8,128)S(1)} all-to-all(f32[8,72,128]{2,1,0:T(8,128)S(1)} %bitcast.36), channel_id=1, replica_groups={{0,2,4,6,8,10,12,14},{1,3,5,7,9,11,13,15},{16,18,20,22,24,26,28,30},{17..., dimensions={0} | all-to-all | bytes 589824 | tf_op jit(solution)/shard_map/all_to_all | solution.py:296
  125.3 1.8 %collective-permute-start.21 = (f32[72,128]{1,0:T(8,128)S(1)}, f32[72,128]{1,0:T(8,128)S(1)}, u32[]{:S(2)}, u32[]{:S(2)}) collective-permute-start(f32[72,128]{1,0:T(8,128)S(1)} %sum_pieces.5.refs_0_), channel_id=1, source_target_pairs={{0,48},{1,49},{2,50},{3,51},{4,52},{5,53},{6,54},{7,55},{8,56},{9,... | collective-permute-start | bytes 110600 | tf_op jit(solution)/shard_map/ppermute | solution.py:302
  127.2 2.9 %collective-permute-start.20 = (f32[72,128]{1,0:T(8,128)S(1)}, f32[72,128]{1,0:T(8,128)S(1)}, u32[]{:S(2)}, u32[]{:S(2)}) collective-permute-start(f32[72,128]{1,0:T(8,128)S(1)} %sum_pieces.5.refs_0_), channel_id=1, source_target_pairs={{0,32},{1,33},{2,34},{3,35},{4,36},{5,37},{6,38},{7,39},{8,40},{9,... | collective-permute-start | bytes 110600 | tf_op jit(solution)/shard_map/ppermute | solution.py:302
  131.2 2.8 %collective-permute-done.20.refs_2_ = f32[72,128]{1,0:T(8,128)S(1)} collective-permute-done((f32[72,128]{1,0:T(8,128)S(1)}, f32[72,128]{1,0:T(8,128)S(1)}, u32[]{:S(2)}, u32[]{:S(2)}) %collective-permute-start.20) | collective-permute-done | bytes 36896 | tf_op jit(solution)/shard_map/ppermute | solution.py:302
  135.1 9.5 %all_to_all.40 = f32[8,64,128]{2,1,0:T(8,128)S(1)} all-to-all(f32[8,64,128]{2,1,0:T(8,128)S(1)} %bitcast.32), channel_id=1, replica_groups={{0,2,4,6,8,10,12,14},{1,3,5,7,9,11,13,15},{16,18,20,22,24,26,28,30},{17..., dimensions={0} | all-to-all | bytes 524288 | tf_op jit(solution)/shard_map/all_to_all | solution.py:296
  144.6 3.2 %collective-permute-start.22 = (f32[512,128]{1,0:T(8,128)S(1)}, f32[512,128]{1,0:T(8,128)S(1)}, u32[]{:S(2)}, u32[]{:S(2)}) collective-permute-start(f32[512,128]{1,0:T(8,128)S(1)} %bitcast.22), channel_id=1, source_target_pairs={{0,1},{1,0},{2,3},{3,2},{4,5},{5,4},{6,7},{7,6},{8,9},{9,8},{10,11... | collective-permute-start | bytes 786440 | tf_op jit(solution)/shard_map/ppermute | solution.py:291
  149.1 1.9 %forward.5 = (f32[1024,128]{1,0:T(8,128)S(1)}, f32[1024,128]{1,0:T(8,128)S(1)}, f32[264,128]{1,0:T(8,128)S(1)}, f32[256,128]{1,0:T(8,128)S(1)}) custom-call(f32[512,128]{1,0:T(8,128)S(1)} %bitcast.23, f32[512,128]{1,0:T(8,128)S(1)} %collective-permute-done.22.refs_1_, f32[8,128]{1,0:T(8,128)S(1)} %get-tuple-element.67.refs_2_.size1, ...), custom_call_target="tpu_custom_call" | custom-call | flops 1073741824 | bytes 1048576 | tf_op jit(solution)/shard_map/forward/pallas_call | solution.py:29
  151.1 1.5 collective-permute-start.25
  152.6 3.3 %collective-permute-done.23 = f32[264,128]{1,0:T(8,128)S(1)} collective-permute-done((f32[264,128]{1,0:T(8,128)S(1)}, f32[264,128]{1,0:T(8,128)S(1)}, u32[]{:S(2)}, u32[]{:S(2)}) %collective-permute-start.23) | collective-permute-done | bytes 135200 | tf_op jit(solution)/shard_map/ppermute | solution.py:317
  155.9 1.5 collective-permute-start.24
  158.2 3.4 %collective-permute-done.26.h3 = f32[256,128]{1,0:T(8,128)S(1)} collective-permute-done((f32[256,128]{1,0:T(8,128)S(1)}, f32[256,128]{1,0:T(8,128)S(1)}, u32[]{:S(2)}, u32[]{:S(2)}) %collective-permute-start.26) | collective-permute-done | bytes 131104 | tf_op jit(solution)/shard_map/ppermute | solution.py:317
  161.9 16.7 %all_to_all.41 = f32[64,1,128]{2,1,0:T(1,128)S(1)} all-to-all(f32[64,1,128]{2,1,0:T(1,128)S(1)} %bitcast.34), channel_id=1, replica_groups=mesh['unit'=4,'samp'=64] {'samp'}, dimensions={0} | all-to-all | bytes 65536 | tf_op jit(solution)/shard_map/all_to_all | solution.py:421
  (39 shorter events, 8.6 us)
Async XLA Ops:
  5.4 4.6 %collective-permute-start = (f32[512,128]{1,0:T(8,128)S(1)}, f32[512,128]{1,0:T(8,128)S(1)}, u32[]{:S(2)}, u32[]{:S(2)}) collective-permute-start(f32[512,128]{1,0:T(8,128)S(1)} %get-tuple-element.45), channel_id=1, source_target_pairs={{0,1},{1,0},{2,3},{3,2},{4,5},{5,4},{6,7},{7,6},{8,9},{9,8},{10,11... | collective-permute-start | bytes 786440 | tf_op jit(solution)/shard_map/ppermute | solution.py:291
  19.8 9.7 %collective-permute-start.3 = (f32[64,128]{1,0:T(8,128)S(1)}, f32[64,128]{1,0:T(8,128)S(1)}, u32[]{:S(2)}, u32[]{:S(2)}) collective-permute-start(f32[64,128]{1,0:T(8,128)S(1)} %sum_pieces.3.refs_0_), channel_id=1, source_target_pairs={{0,48},{1,49},{2,50},{3,51},{4,52},{5,53},{6,54},{7,55},{8,56},{9,... | collective-permute-start | bytes 98312 | tf_op jit(solution)/shard_map/ppermute | solution.py:302
  25.1 6.7 %collective-permute-start.2 = (f32[64,128]{1,0:T(8,128)S(1)}, f32[64,128]{1,0:T(8,128)S(1)}, u32[]{:S(2)}, u32[]{:S(2)}) collective-permute-start(f32[64,128]{1,0:T(8,128)S(1)} %sum_pieces.3.refs_0_), channel_id=1, source_target_pairs={{0,32},{1,33},{2,34},{3,35},{4,36},{5,37},{6,38},{7,39},{8,40},{9,... | collective-permute-start | bytes 98312 | tf_op jit(solution)/shard_map/ppermute | solution.py:302
  26.2 5.5 %collective-permute-start.1 = (f32[64,128]{1,0:T(8,128)S(1)}, f32[64,128]{1,0:T(8,128)S(1)}, u32[]{:S(2)}, u32[]{:S(2)}) collective-permute-start(f32[64,128]{1,0:T(8,128)S(1)} %sum_pieces.3.refs_0_), channel_id=1, source_target_pairs={{0,16},{1,17},{2,18},{3,19},{4,20},{5,21},{6,22},{7,23},{8,24},{9,... | collective-permute-start | bytes 98312 | tf_op jit(solution)/shard_map/ppermute | solution.py:302
  41.4 4.7 %collective-permute-start.4 = (f32[512,128]{1,0:T(8,128)S(1)}, f32[512,128]{1,0:T(8,128)S(1)}, u32[]{:S(2)}, u32[]{:S(2)}) collective-permute-start(f32[512,128]{1,0:T(8,128)S(1)} %bitcast.26), channel_id=1, source_target_pairs={{0,1},{1,0},{2,3},{3,2},{4,5},{5,4},{6,7},{7,6},{8,9},{9,8},{10,11... | collective-permute-start | bytes 786440 | tf_op jit(solution)/shard_map/ppermute | solution.py:291
  47.8 4.9 %collective-permute-start.5 = (f32[264,128]{1,0:T(8,128)S(1)}, f32[264,128]{1,0:T(8,128)S(1)}, u32[]{:S(2)}, u32[]{:S(2)}) collective-permute-start(f32[264,128]{1,0:T(8,128)S(1)} %get-tuple-element.52), channel_id=1, source_target_pairs={{0,64},{64,0},{128,192},{192,128},{1,65},{65,1},{129,193},{193,129... | collective-permute-start | bytes 405512 | tf_op jit(solution)/shard_map/ppermute | solution.py:317
  49.1 6.2 %collective-permute-start.7 = (f32[256,128]{1,0:T(8,128)S(1)}, f32[256,128]{1,0:T(8,128)S(1)}, u32[]{:S(2)}, u32[]{:S(2)}) collective-permute-start(f32[256,128]{1,0:T(8,128)S(1)} %get-tuple-element.53), channel_id=1, source_target_pairs={{0,192},{64,128},{128,64},{192,0},{1,193},{65,129},{129,65},{193,1... | collective-permute-start | bytes 393224 | tf_op jit(solution)/shard_map/ppermute | solution.py:317
  52.7 7.0 %collective-permute-start.6 = (f32[264,128]{1,0:T(8,128)S(1)}, f32[264,128]{1,0:T(8,128)S(1)}, u32[]{:S(2)}, u32[]{:S(2)}) collective-permute-start(f32[264,128]{1,0:T(8,128)S(1)} %add.29.refs_0_), channel_id=1, source_target_pairs={{0,192},{64,128},{128,64},{192,0},{1,193},{65,129},{129,65},{193,1... | collective-permute-start | bytes 405512 | tf_op jit(solution)/shard_map/ppermute | solution.py:317
  55.3 4.4 %collective-permute-start.8 = (f32[256,128]{1,0:T(8,128)S(1)}, f32[256,128]{1,0:T(8,128)S(1)}, u32[]{:S(2)}, u32[]{:S(2)}) collective-permute-start(f32[256,128]{1,0:T(8,128)S(1)} %add.30.refs_2_), channel_id=1, source_target_pairs={{0,64},{64,0},{128,192},{192,128},{1,65},{65,1},{129,193},{193,129... | collective-permute-start | bytes 393224 | tf_op jit(solution)/shard_map/ppermute | solution.py:317
  61.2 3.6 %collective-permute-start.9 = (f32[576,128]{1,0:T(8,128)S(1)}, f32[576,128]{1,0:T(8,128)S(1)}, u32[]{:S(2)}, u32[]{:S(2)}) collective-permute-start(f32[576,128]{1,0:T(8,128)S(1)} %get-tuple-element.55), channel_id=1, source_target_pairs={{0,1},{1,0},{2,3},{3,2},{4,5},{5,4},{6,7},{7,6},{8,9},{9,8},{10,11... | collective-permute-start | bytes 884744 | tf_op jit(solution)/shard_map/ppermute | solution.py:291
  74.5 6.7 %collective-permute-start.12 = (f32[72,128]{1,0:T(8,128)S(1)}, f32[72,128]{1,0:T(8,128)S(1)}, u32[]{:S(2)}, u32[]{:S(2)}) collective-permute-start(f32[72,128]{1,0:T(8,128)S(1)} %sum_pieces.4.refs_0_), channel_id=1, source_target_pairs={{0,48},{1,49},{2,50},{3,51},{4,52},{5,53},{6,54},{7,55},{8,56},{9,... | collective-permute-start | bytes 110600 | tf_op jit(solution)/shard_map/ppermute | solution.py:302
  76.2 6.9 %collective-permute-start.11 = (f32[72,128]{1,0:T(8,128)S(1)}, f32[72,128]{1,0:T(8,128)S(1)}, u32[]{:S(2)}, u32[]{:S(2)}) collective-permute-start(f32[72,128]{1,0:T(8,128)S(1)} %sum_pieces.4.refs_0_), channel_id=1, source_target_pairs={{0,32},{1,33},{2,34},{3,35},{4,36},{5,37},{6,38},{7,39},{8,40},{9,... | collective-permute-start | bytes 110600 | tf_op jit(solution)/shard_map/ppermute | solution.py:302
  78.9 5.3 %collective-permute-start.10 = (f32[72,128]{1,0:T(8,128)S(1)}, f32[72,128]{1,0:T(8,128)S(1)}, u32[]{:S(2)}, u32[]{:S(2)}) collective-permute-start(f32[72,128]{1,0:T(8,128)S(1)} %sum_pieces.4.refs_0_), channel_id=1, source_target_pairs={{0,16},{1,17},{2,18},{3,19},{4,20},{5,21},{6,22},{7,23},{8,24},{9,... | collective-permute-start | bytes 110600 | tf_op jit(solution)/shard_map/ppermute | solution.py:302
  93.7 4.2 %collective-permute-start.13 = (f32[512,128]{1,0:T(8,128)S(1)}, f32[512,128]{1,0:T(8,128)S(1)}, u32[]{:S(2)}, u32[]{:S(2)}) collective-permute-start(f32[512,128]{1,0:T(8,128)S(1)} %bitcast.24), channel_id=1, source_target_pairs={{0,1},{1,0},{2,3},{3,2},{4,5},{5,4},{6,7},{7,6},{8,9},{9,8},{10,11... | collective-permute-start | bytes 786440 | tf_op jit(solution)/shard_map/ppermute | solution.py:291
  99.8 4.9 %collective-permute-start.14 = (f32[264,128]{1,0:T(8,128)S(1)}, f32[264,128]{1,0:T(8,128)S(1)}, u32[]{:S(2)}, u32[]{:S(2)}) collective-permute-start(f32[264,128]{1,0:T(8,128)S(1)} %get-tuple-element.60), channel_id=1, source_target_pairs={{0,64},{64,0},{128,192},{192,128},{1,65},{65,1},{129,193},{193,129... | collective-permute-start | bytes 405512 | tf_op jit(solution)/shard_map/ppermute | solution.py:317
  99.9 6.2 %collective-permute-start.16 = (f32[256,128]{1,0:T(8,128)S(1)}, f32[256,128]{1,0:T(8,128)S(1)}, u32[]{:S(2)}, u32[]{:S(2)}) collective-permute-start(f32[256,128]{1,0:T(8,128)S(1)} %get-tuple-element.61), channel_id=1, source_target_pairs={{0,192},{64,128},{128,64},{192,0},{1,193},{65,129},{129,65},{193,1... | collective-permute-start | bytes 393224 | tf_op jit(solution)/shard_map/ppermute | solution.py:317
  104.7 5.7 %collective-permute-start.15 = (f32[264,128]{1,0:T(8,128)S(1)}, f32[264,128]{1,0:T(8,128)S(1)}, u32[]{:S(2)}, u32[]{:S(2)}) collective-permute-start(f32[264,128]{1,0:T(8,128)S(1)} %add.32.refs_0_), channel_id=1, source_target_pairs={{0,192},{64,128},{128,64},{192,0},{1,193},{65,129},{129,65},{193,1... | collective-permute-start | bytes 405512 | tf_op jit(solution)/shard_map/ppermute | solution.py:317
  106.2 4.2 %collective-permute-start.17 = (f32[256,128]{1,0:T(8,128)S(1)}, f32[256,128]{1,0:T(8,128)S(1)}, u32[]{:S(2)}, u32[]{:S(2)}) collective-permute-start(f32[256,128]{1,0:T(8,128)S(1)} %add.33.refs_2_), channel_id=1, source_target_pairs={{0,64},{64,0},{128,192},{192,128},{1,65},{65,1},{129,193},{193,129... | collective-permute-start | bytes 393224 | tf_op jit(solution)/shard_map/ppermute | solution.py:317
  112.0 3.6 %collective-permute-start.18 = (f32[576,128]{1,0:T(8,128)S(1)}, f32[576,128]{1,0:T(8,128)S(1)}, u32[]{:S(2)}, u32[]{:S(2)}) collective-permute-start(f32[576,128]{1,0:T(8,128)S(1)} %get-tuple-element.64), channel_id=1, source_target_pairs={{0,1},{1,0},{2,3},{3,2},{4,5},{5,4},{6,7},{7,6},{8,9},{9,8},{10,11... | collective-permute-start | bytes 884744 | tf_op jit(solution)/shard_map/ppermute | solution.py:291
  125.3 5.9 %collective-permute-start.21 = (f32[72,128]{1,0:T(8,128)S(1)}, f32[72,128]{1,0:T(8,128)S(1)}, u32[]{:S(2)}, u32[]{:S(2)}) collective-permute-start(f32[72,128]{1,0:T(8,128)S(1)} %sum_pieces.5.refs_0_), channel_id=1, source_target_pairs={{0,48},{1,49},{2,50},{3,51},{4,52},{5,53},{6,54},{7,55},{8,56},{9,... | collective-permute-start | bytes 110600 | tf_op jit(solution)/shard_map/ppermute | solution.py:302
  127.2 6.8 %collective-permute-start.20 = (f32[72,128]{1,0:T(8,128)S(1)}, f32[72,128]{1,0:T(8,128)S(1)}, u32[]{:S(2)}, u32[]{:S(2)}) collective-permute-start(f32[72,128]{1,0:T(8,128)S(1)} %sum_pieces.5.refs_0_), channel_id=1, source_target_pairs={{0,32},{1,33},{2,34},{3,35},{4,36},{5,37},{6,38},{7,39},{8,40},{9,... | collective-permute-start | bytes 110600 | tf_op jit(solution)/shard_map/ppermute | solution.py:302
  130.1 5.0 %collective-permute-start.19 = (f32[72,128]{1,0:T(8,128)S(1)}, f32[72,128]{1,0:T(8,128)S(1)}, u32[]{:S(2)}, u32[]{:S(2)}) collective-permute-start(f32[72,128]{1,0:T(8,128)S(1)} %sum_pieces.5.refs_0_), channel_id=1, source_target_pairs={{0,16},{1,17},{2,18},{3,19},{4,20},{5,21},{6,22},{7,23},{8,24},{9,... | collective-permute-start | bytes 110600 | tf_op jit(solution)/shard_map/ppermute | solution.py:302
  144.6 4.4 %collective-permute-start.22 = (f32[512,128]{1,0:T(8,128)S(1)}, f32[512,128]{1,0:T(8,128)S(1)}, u32[]{:S(2)}, u32[]{:S(2)}) collective-permute-start(f32[512,128]{1,0:T(8,128)S(1)} %bitcast.22), channel_id=1, source_target_pairs={{0,1},{1,0},{2,3},{3,2},{4,5},{5,4},{6,7},{7,6},{8,9},{9,8},{10,11... | collective-permute-start | bytes 786440 | tf_op jit(solution)/shard_map/ppermute | solution.py:291
  151.0 4.9 %collective-permute-start.23 = (f32[264,128]{1,0:T(8,128)S(1)}, f32[264,128]{1,0:T(8,128)S(1)}, u32[]{:S(2)}, u32[]{:S(2)}) collective-permute-start(f32[264,128]{1,0:T(8,128)S(1)} %get-tuple-element.70), channel_id=1, source_target_pairs={{0,64},{64,0},{128,192},{192,128},{1,65},{65,1},{129,193},{193,129... | collective-permute-start | bytes 405512 | tf_op jit(solution)/shard_map/ppermute | solution.py:317
  151.1 6.3 %collective-permute-start.25 = (f32[256,128]{1,0:T(8,128)S(1)}, f32[256,128]{1,0:T(8,128)S(1)}, u32[]{:S(2)}, u32[]{:S(2)}) collective-permute-start(f32[256,128]{1,0:T(8,128)S(1)} %get-tuple-element.71), channel_id=1, source_target_pairs={{0,192},{64,128},{128,64},{192,0},{1,193},{65,129},{129,65},{193,1... | collective-permute-start | bytes 393224 | tf_op jit(solution)/shard_map/ppermute | solution.py:317
  155.9 5.7 %collective-permute-start.24 = (f32[264,128]{1,0:T(8,128)S(1)}, f32[264,128]{1,0:T(8,128)S(1)}, u32[]{:S(2)}, u32[]{:S(2)}) collective-permute-start(f32[264,128]{1,0:T(8,128)S(1)} %add.35.h0), channel_id=1, source_target_pairs={{0,192},{64,128},{128,64},{192,0},{1,193},{65,129},{129,65},{193,1... | collective-permute-start | bytes 405512 | tf_op jit(solution)/shard_map/ppermute | solution.py:317
  157.4 4.2 %collective-permute-start.26 = (f32[256,128]{1,0:T(8,128)S(1)}, f32[256,128]{1,0:T(8,128)S(1)}, u32[]{:S(2)}, u32[]{:S(2)}) collective-permute-start(f32[256,128]{1,0:T(8,128)S(1)} %add.36.h2), channel_id=1, source_target_pairs={{0,64},{64,0},{128,192},{192,128},{1,65},{65,1},{129,193},{193,129... | collective-permute-start | bytes 393224 | tf_op jit(solution)/shard_map/ppermute | solution.py:317
